TPU v7x, 32 devices: a whole 2x2x4 slice. The times are simulated.
32 devices in a mesh: layer: 4 (over x, core), row: 8 (over z, y).
Axes of the slice: x: 2, y: 2, z: 4, core: 2. Of those that a mesh axis runs over, the one named last changes fastest.
Arguments:
- density: bfloat16 [5120, 2048], P('row', 'layer'), may hold values from -1 to 1, as said below
- pattern: int32 [80, 32], P('row', 'layer'), may hold values 0 or 1
Outputs:
- purified: float32 [5120, 2048], P('row', 'layer')
Inputs may be any that keep to these rules, and one draw needn't show every extreme that they name: `density`: entry (r, o * 64 + c) is P's entry in row r and column ((r // 64 + o - 16) mod 80) * 64 + c.
All inputs are finite; a program needn't handle non-finite values. No bound on the sum of `pattern` on one device may be relied on, other than what follows from the above.
Results may differ from a plain program's by a relative error of at most 0.0065.
Values may be sent and summed in bfloat16 or wider, within the bound.
No kernel may reach another device: no remote copies, remote signals or barrier semaphores. Data moves between devices by JAX's collectives and lax.ppermute only.
A program may use at most 192 MiB of HBM per device.

v0:
```python
import jax
import jax.numpy as jnp
from jax import lax
from jax.sharding import PartitionSpec as P


def shifted(value, axis, steps):
    count = lax.axis_size(axis)
    pairs = [(source, (source + steps) % count) for source in range(count)]
    return lax.ppermute(value, axis, pairs)


def body(density, pattern):
    rows_dev, slab_cols = density.shape
    block_rows, slab_offsets = pattern.shape
    tile_size = rows_dev // block_rows
    layers = lax.axis_size("layer")
    offsets = slab_offsets * layers
    half_band = offsets // 2
    reach_dev = (half_band + block_rows - 1) // block_rows
    layer_id = lax.axis_index("layer")
    keep = pattern.astype(jnp.bfloat16)[:, None, :, None]
    masked = (density.reshape(block_rows, tile_size, slab_offsets, tile_size) * keep).reshape(
        rows_dev, slab_cols
    )
    own_band = lax.all_gather(masked, "layer", axis=1, tiled=True)
    lower_parts = [shifted(own_band, "row", distance) for distance in range(reach_dev, 0, -1)]
    upper_parts = [shifted(own_band, "row", -distance) for distance in range(1, reach_dev + 1)]
    margin = jnp.concatenate(lower_parts + [own_band] + upper_parts, axis=0)
    padded = jnp.pad(
        margin.reshape(-1, tile_size, offsets, tile_size),
        ((0, 0), (0, 0), (half_band, half_band), (0, 0)),
    )
    row_base = reach_dev * block_rows - half_band
    own_start = reach_dev * rows_dev
    own_blocks = lax.slice_in_dim(margin, own_start, own_start + rows_dev, axis=0).reshape(
        block_rows, tile_size, offsets, tile_size
    )
    pattern_f = pattern.astype(jnp.float32)[:, None, :, None]
    row_ids = jnp.arange(block_rows, dtype=jnp.int32)

    def row_product(left_row, inner_count, first_offset, row_idx):

        def piece(inner_idx):
            start_row = row_base + row_idx + inner_idx
            start_col = first_offset - inner_idx + 2 * half_band
            return lax.dynamic_slice(
                padded, (start_row, 0, start_col, 0), (1, tile_size, slab_offsets, tile_size)
            )[0]

        inner_set = jnp.arange(inner_count, dtype=jnp.int32)
        windows = jax.vmap(piece)(inner_set)
        return jnp.einsum("xay,ayoz->xoz", left_row, windows, preferred_element_type=jnp.float32)

    def products(left_blocks):
        first_offset = layer_id * slab_offsets
        return lax.map(
            lambda row_idx: row_product(left_blocks[row_idx], offsets, first_offset, row_idx),
            row_ids,
        )

    square = (products(own_blocks) * pattern_f).astype(jnp.bfloat16)
    square_full = lax.all_gather(square.reshape(rows_dev, slab_cols), "layer", axis=1, tiled=True)
    cubic = products(square_full.reshape(block_rows, tile_size, offsets, tile_size)) * pattern_f
    purified = 3.0 * square.astype(jnp.float32) - 2.0 * cubic
    return purified.reshape(rows_dev, slab_cols)


def solution(mesh):
    placed = (P("row", "layer"), P("row", "layer"))
    return jax.shard_map(
        body, mesh=mesh, in_specs=placed, out_specs=P("row", "layer"), check_vma=False
    )
```

profile of v0, /device:TPU:0, one launch (start us, length us, event | category | flops | bytes accessed | tf_op | source)
XLA Modules:
  0.0 609.3 jit_solution(11274369258809490311)
XLA Ops:
  9.5 28.4 %all-gather.3.cloned.1.call-done = bf16[640,2048]{1,0:T(8,128)(2,1)} async-done(((bf16[640,512]{1,0:T(8,128)(2,1)}), bf16[640,2048]{1,0:T(8,128)(2,1)}) %all-gather.3.cloned.1.call-update) | async-done | bytes 2621456 | tf_op jit(solution)/shard_map/all_gather | solution.py:26
  40.8 3.2 collective-permute-start.2
  44.7 8.5 %reshape.90 = bf16[10,64,32,64]{3,2,1,0:T(8,128)(2,1)} reshape(bf16[640,2048]{1,0:T(8,128)(2,1)} %all-gather.3.cloned.1.call-done) | data formatting | bytes 5242880 | tf_op jit(solution)/shard_map/reshape | solution.py:36
  53.3 46.5 %collective-permute-done = bf16[640,2048]{1,0:T(8,128)(2,1)} collective-permute-done((bf16[640,2048]{1,0:T(8,128)(2,1)}, bf16[640,2048]{1,0:T(8,128)(2,1)}, u32[]{:S(2)}, u32[]{:S(2)}) %collective-permute-start) | collective-permute-done | bytes 2621472 | tf_op jit(solution)/shard_map/ppermute | solution.py:10
  99.7 3.5 constant_dynamic-update-slice_fusion.4
  103.3 53.6 %collective-permute-done.1 = bf16[640,2048]{1,0:T(8,128)(2,1)} collective-permute-done((bf16[640,2048]{1,0:T(8,128)(2,1)}, bf16[640,2048]{1,0:T(8,128)(2,1)}, u32[]{:S(2)}, u32[]{:S(2)}) %collective-permute-start.1) | collective-permute-done | bytes 2621472 | tf_op jit(solution)/shard_map/ppermute | solution.py:10
  156.8 3.6 constant_dynamic-update-slice_fusion.3
  162.2 3.5 constant_dynamic-update-slice_fusion.1
  165.8 45.5 %collective-permute-done.3 = bf16[640,2048]{1,0:T(8,128)(2,1)S(1)} collective-permute-done((bf16[640,2048]{1,0:T(8,128)(2,1)}, bf16[640,2048]{1,0:T(8,128)(2,1)S(1)}, u32[]{:S(2)}, u32[]{:S(2)}) %collective-permute-start.3) | collective-permute-done | bytes 2621472 | tf_op jit(solution)/shard_map/ppermute | solution.py:10
  212.9 37.5 %reshape.91 = bf16[50,64,32,64]{3,2,1,0:T(8,128)(2,1)} reshape(bf16[3200,2048]{1,0:T(8,128)(2,1)} %constant_dynamic-update-slice_fusion) | data formatting | bytes 26214400 | tf_op jit(solution)/shard_map/reshape | solution.py:31
  250.4 18.8 %copy.22 = bf16[50,64,32,64]{3,1,0,2:T(8,128)(2,1)} copy(bf16[50,64,32,64]{3,2,1,0:T(8,128)(2,1)} %reshape.91) | data formatting | bytes 26214400
  269.2 25.0 %pad.4.clone = bf16[50,64,64,64]{3,1,0,2:T(8,128)(2,1)} pad(bf16[50,64,32,64]{3,1,0,2:T(8,128)(2,1)} %copy.22, bf16[]{:T(256)} %constant.103.clone.1), padding=0_0x0_0x16_16x0_0 | pad | bytes 39321600 | tf_op jit(solution)/shard_map/jit(_pad)/pad | solution.py:30
  294.5 127.8 %while.24 = (s32[]{:T(128)}, f32[10,64,8,64]{3,1,2,0:T(8,128)S(1)}, s32[10]{0:T(128)S(1)}, bf16[10,64,32,64]{3,2,1,0:T(8,128)(2,1)}, s32[]{:T(128)}, /*index=5*/...) while((s32[]{:T(128)}, f32[10,64,8,64]{3,1,2,0:T(8,128)S(1)}, ...), condition=%wide.region_1.2_spmd, body=%wide.region_0.1_spmd.sunk | while | flops 134218176 | bytes 7602991 | solution.py:57
  299.1 5.1 gather_fusion
  304.1 3.2 fusion.30
  311.8 5.1 gather_fusion
  316.9 3.2 fusion.30
  324.6 5.1 gather_fusion
  337.4 5.1 gather_fusion
  350.2 5.1 gather_fusion
  363.0 5.1 gather_fusion
  375.7 5.1 gather_fusion
  388.5 5.1 gather_fusion
  401.3 5.1 gather_fusion
  414.1 5.1 gather_fusion
  427.4 24.0 %all-gather.5.cloned.1.call-done = bf16[640,2048]{1,0:T(8,128)(2,1)} async-done(((bf16[640,512]{1,0:T(8,128)(2,1)}), bf16[640,2048]{1,0:T(8,128)(2,1)}) %all-gather.5.cloned.1.call-update) | async-done | bytes 2621456 | tf_op jit(solution)/shard_map/all_gather | solution.py:63
  451.4 8.5 %reshape.93 = bf16[10,64,32,64]{3,2,1,0:T(8,128)(2,1)} reshape(bf16[640,2048]{1,0:T(8,128)(2,1)} %all-gather.5.cloned.1.call-done) | data formatting | bytes 5242880 | tf_op jit(solution)/shard_map/reshape | solution.py:64
  461.8 135.1 %while.25 = (s32[]{:T(128)}, f32[10,64,8,64]{3,1,2,0:T(8,128)}, s32[10]{0:T(128)S(1)}, bf16[10,64,32,64]{3,2,1,0:T(8,128)(2,1)}, s32[]{:T(128)}, /*index=5*/bf16...) while((s32[]{:T(128)}, f32[10,64,8,64]{3,1,2,0:T(8,128)}, s32[10]{0:T(128)S(1)}, ...), condition=%wide.region_3.4_spmd, body=%wide.region_2.3_spmd.sunk | while | flops 134218176 | bytes 9438507 | solution.py:57
  466.3 5.1 gather_fusion.1
  471.4 3.9 fusion.34
  479.9 5.1 gather_fusion.1
  484.9 3.9 fusion.34
  493.4 5.1 gather_fusion.1
  498.5 3.9 fusion.34
  506.9 5.1 gather_fusion.1
  512.0 3.9 fusion.34
  520.4 5.1 gather_fusion.1
  525.4 3.9 fusion.34
  533.9 5.1 gather_fusion.1
  538.9 3.9 fusion.34
  547.4 5.1 gather_fusion.1
  552.5 3.9 fusion.34
  560.9 5.1 gather_fusion.1
  566.0 3.9 fusion.34
  574.4 5.1 gather_fusion.1
  579.5 3.9 fusion.34
  587.9 5.1 gather_fusion.1
  593.0 3.9 fusion.34
  (98 shorter events, 83.2 us)
Async XLA Ops:
  6.5 1.9 copy-start.1
  6.5 31.3 %all-gather.3.cloned.1.call-start = ((), (), s32[]{:S(2)}) async-start(), calls=%async_computation | async-start | bytes 3276800 | tf_op jit(solution)/shard_map/all_gather | solution.py:26
  9.5 441.9 %all-gather.5.cloned.1.call-start = ((), (), s32[]{:S(2)}) async-start(), calls=%async_computation.1 | async-start | bytes 3276800 | tf_op jit(solution)/shard_map/all_gather | solution.py:63
  37.9 61.9 %collective-permute-start = (bf16[640,2048]{1,0:T(8,128)(2,1)}, bf16[640,2048]{1,0:T(8,128)(2,1)}, u32[]{:S(2)}, u32[]{:S(2)}) collective-permute-start(bf16[640,2048]{1,0:T(8,128)(2,1)} %all-gather.3.cloned.1.call-done), channel_id=1, source_target_pairs={{0,2},{1,3},{2,4},{3,5},{4,6},{5,7},{6,0},{7,1},{8,10},{9,11},{10,... | collective-permute-start | bytes 7864328 | tf_op jit(solution)/shard_map/ppermute | solution.py:10
  39.4 117.5 %collective-permute-start.1 = (bf16[640,2048]{1,0:T(8,128)(2,1)}, bf16[640,2048]{1,0:T(8,128)(2,1)}, u32[]{:S(2)}, u32[]{:S(2)}) collective-permute-start(bf16[640,2048]{1,0:T(8,128)(2,1)} %all-gather.3.cloned.1.call-done), channel_id=1, source_target_pairs={{0,1},{1,2},{2,3},{3,4},{4,5},{5,6},{6,7},{7,0},{8,9},{9,10},{10,1... | collective-permute-start | bytes 7864328 | tf_op jit(solution)/shard_map/ppermute | solution.py:10
  40.8 121.4 %collective-permute-start.2 = (bf16[640,2048]{1,0:T(8,128)(2,1)}, bf16[640,2048]{1,0:T(8,128)(2,1)}, u32[]{:S(2)}, u32[]{:S(2)}) collective-permute-start(bf16[640,2048]{1,0:T(8,128)(2,1)} %all-gather.3.cloned.1.call-done), channel_id=1, source_target_pairs={{0,7},{1,0},{2,1},{3,2},{4,3},{5,4},{6,5},{7,6},{8,15},{9,8},{10,9... | collective-permute-start | bytes 7864328 | tf_op jit(solution)/shard_map/ppermute | solution.py:10
  44.1 167.2 %collective-permute-start.3 = (bf16[640,2048]{1,0:T(8,128)(2,1)}, bf16[640,2048]{1,0:T(8,128)(2,1)S(1)}, u32[]{:S(2)}, u32[]{:S(2)}) collective-permute-start(bf16[640,2048]{1,0:T(8,128)(2,1)} %all-gather.3.cloned.1.call-done), channel_id=1, source_target_pairs={{0,6},{1,7},{2,0},{3,1},{4,2},{5,3},{6,4},{7,5},{8,14},{9,15},{10,... | collective-permute-start | bytes 7864328 | tf_op jit(solution)/shard_map/ppermute | solution.py:10
  103.3 57.1 %copy-start = (bf16[640,2048]{1,0:T(8,128)(2,1)S(1)}, bf16[640,2048]{1,0:T(8,128)(2,1)}, u32[]{:S(2)}) copy-start(bf16[640,2048]{1,0:T(8,128)(2,1)} %all-gather.3.cloned.1.call-done) | copy-start | bytes 7864324
Sparse Core Ops, SparseCore 0:
  9.6 28.2 all-gather.2
  427.6 23.7 all-gather.4
where the time goes:
time: 614 us; the launch traced here: 609 us
  local copies, waits for them, and re-layouts  260 us (42%)
  waiting for transfers between devices  198 us (32%)
  matrix products  70.5 us (11%)
  loops' own time  55.6 us (9%)
  between operations  13.5 us (2%)
  starting transfers between devices  6.79 us (1%)
    ppermute x4, waiting for transfers between devices, shifted(): return lax.ppermute(value, axis, pairs)  146 us
    gather x20, local copies, waits for them, and re-layouts, piece(): lax.dynamic_slice(padded, (start_row, 0, start_col, 0), (1, tile_size, sl...  102 us
    dot_general x20, matrix products, row_product(): jnp.einsum('xay,ayoz->xoz', left_row, windows, preferred_element_type=jnp...  70.5 us
    another operation x2, loops' own time, products(): lax.map(lambda row_idx: row_product(left_blocks[row_idx], offsets, first_...  55.6 us
    reshape x1, local copies, waits for them, and re-layouts, body(): margin.reshape(-1, tile_size, offsets, tile_size)  37.5 us
    unnamed x9, local copies, waits for them, and re-layouts  31.3 us
    all_gather x1, waiting for transfers between devices, body(): own_band = lax.all_gather(masked, 'layer', axis=1, tiled=True)  28.4 us
    pad x1, local copies, waits for them, and re-layouts, body(): jnp.pad(margin.reshape(-1, tile_size, offsets, tile_size), ((0, 0), (0, 0...  25 us
  transfers between devices with their start and end apart: 6, of which 5 were waited for; matrix products, arithmetic and copies ran while one was open for 3% of the time, Pallas kernels for 0%

commit v1 on v0

v1 whole, which is shorter than its diff:
```python
import functools

import jax
import jax.numpy as jnp
from jax import lax
from jax.experimental import pallas as pl
from jax.experimental.pallas import tpu as pltpu
from jax.sharding import PartitionSpec as P

VMEM = pl.BlockSpec(memory_space=pltpu.VMEM)
LIMIT = 48 * 1024 * 1024


class Geometry:
    def __init__(self, rows_dev, slab_cols, block_rows, slab_offsets, layers):
        self.rows, self.slab = block_rows, slab_offsets
        self.size = rows_dev // block_rows
        self.layers = layers
        self.offsets = slab_offsets * layers
        self.half = self.offsets // 2
        self.pair = 2 * slab_offsets
        self.reach_low, self.reach_high = self.half, self.half - 1
        self.span = self.even_up(self.pair + block_rows - 1)
        self.inner = self.reach_low + block_rows + self.reach_high

    @staticmethod
    def even_down(n):
        return n // 2 * 2

    @staticmethod
    def even_up(n):
        return (n + 1) // 2 * 2

    def valid(self, t, side):
        lo, hi = 0, self.pair + self.rows - 1
        shift = t - self.pair * side
        lo, hi = max(lo, shift), min(hi, self.offsets + shift)
        if t < 0:
            lo = max(lo, -t + shift)
        if t >= self.rows:
            hi = min(hi, self.offsets - (t - self.rows + 1) + shift)
        return lo, max(lo, hi)

    def message(self, side, step):
        first = step * self.rows
        rows = [
            t
            for t in range(first, first + self.rows)
            if -self.reach_low <= t < self.rows + self.reach_high
        ]
        spans = [self.valid(t, side) for t in rows]
        spans = [s for s in spans if s[1] > s[0]]
        lo = self.even_down(min(s[0] for s in spans))
        hi = self.even_up(max(s[1] for s in spans))
        return rows, lo, hi


def steps_of(side, name):
    sign = -1 if (name[1] == "wide") == (side == 0) else 1
    return sign * (1 if name[0] == "near" else 2)


NAMES = (("near", "wide"), ("near", "thin"), ("far", "wide"), ("far", "thin"))


def message_shape(g, name):
    found = [g.message(side, steps_of(side, name)) for side in (0, 1)]
    return max(len(f[0]) for f in found), max(f[2] - f[1] for f in found)


def expand_pattern(pattern_ref, slab_cols, size):
    rows, cols = pattern_ref.shape
    block = lax.broadcasted_iota(jnp.int32, (cols, slab_cols), 1) // size
    row = lax.broadcasted_iota(jnp.int32, (cols, slab_cols), 0)
    spread = jnp.where(block == row, 1.0, 0.0).astype(jnp.float32)
    return jnp.dot(
        pattern_ref[...].astype(jnp.float32), spread, preferred_element_type=jnp.float32
    )


def mask_kernel(g, density_ref, pattern_ref, out_ref):
    keep = expand_pattern(pattern_ref, density_ref.shape[1], g.size)
    for t in range(g.rows):
        rows = slice(t * g.size, (t + 1) * g.size)
        out_ref[rows, :] = density_ref[rows, :] * keep[t : t + 1, :].astype(jnp.bfloat16)


def place_row(dst_ref, dst_row, dst_lo, src_ref, src_row, height, lo, hi, shift, size, limit):
    first, last = max(lo, shift), min(hi, limit + shift)
    base = dst_lo - lo
    rows = slice(dst_row, dst_row + height)
    if first >= last:
        dst_ref[rows, dst_lo * size : (hi + base) * size] = jnp.zeros(
            (height, (hi - lo) * size), dst_ref.dtype
        )
        return
    value = src_ref[src_row : src_row + height, (first - shift) * size : (last - shift) * size]
    parts = []
    if first > lo:
        parts.append(jnp.zeros((height, (first - lo) * size), dst_ref.dtype))
    parts.append(value)
    if hi > last:
        parts.append(jnp.zeros((height, (hi - last) * size), dst_ref.dtype))
    if len(parts) > 1:
        value = jnp.concatenate(parts, axis=1)
    dst_ref[rows, dst_lo * size : (hi + base) * size] = value


def pack_kernel(g, names, count, layer_ref, *refs):
    slabs, outs, band = refs[:count], refs[count : count + len(names)], refs[-1]
    layer = layer_ref[0]
    side, core = layer // 2, layer % 2
    half = g.size // 2
    cols = g.slab * g.size
    for q, slab in enumerate(slabs):
        place = (layer ^ q) if count == g.layers else (core ^ q)
        start = pl.multiple_of(place * cols, cols)
        for t in range(g.rows):
            src = pl.multiple_of(t * g.size + half * core, half)
            band[t * half : (t + 1) * half, pl.ds(start, cols)] = slab[pl.ds(src, half), :]

    def write(side_value):
        first_block = 0 if count == g.layers else g.pair * side_value
        limit = g.offsets if count == g.layers else g.pair
        for name, out in zip(names, outs):
            step = steps_of(side_value, name)
            rows, lo, hi = g.message(side_value, step)
            width = out.shape[1] // g.size
            for n, t in enumerate(rows):
                own = t - step * g.rows
                shift = t - g.pair * side_value + first_block
                place_row(
                    out, n * half, 0, band, own * half, half, lo, lo + width, shift, g.size, limit
                )
            for n in range(len(rows), out.shape[0] // half):
                out[n * half : (n + 1) * half, :] = jnp.zeros((half, out.shape[1]), out.dtype)

    for side_value in (0, 1):
        pl.when(side == side_value)(functools.partial(write, side_value))


def fill_band(g, layer, slabs, band):
    cols = g.slab * g.size
    for q, slab in enumerate(slabs):
        band[:, pl.ds(pl.multiple_of((layer ^ q) * cols, cols), cols)] = slab[...]


def group_windows(g):
    size = (g.rows + 1) // 2
    found = []
    for first in range(0, g.rows, size):
        count = min(size, g.rows - first)
        lo = g.even_down(first)
        hi = g.even_up(first + count - 1 + g.slab)
        found.append((first, count, first, g.offsets + count - 1, lo, hi - lo))
    return found


def banded_product(g, core, band, left, inner, finish):
    for first, count, inner_first, inner_count, col, cols in group_windows(g):
        inner_pad = g.even_up(inner_count)
        for n in range(count):
            place_row(
                left, n * g.size, 0, band, (first + n) * g.size, g.size, 0, inner_pad, n, g.size, g.offsets
            )
        start = pl.multiple_of((core * g.slab + col) * g.size, 2 * g.size)
        product = jnp.dot(
            left[: count * g.size, : inner_count * g.size],
            inner[
                inner_first * g.size : (inner_first + inner_count) * g.size,
                pl.ds(start, cols * g.size),
            ],
            preferred_element_type=jnp.float32,
        )
        for n in range(count):
            at = (first + n - col) * g.size
            finish(
                first + n,
                product[n * g.size : (n + 1) * g.size, at : at + g.slab * g.size],
            )


def square_kernel(g, layer_ref, pattern_ref, *refs):
    slabs, refs = refs[: g.layers], refs[g.layers :]
    pieces, refs = refs[: 2 * len(NAMES)], refs[2 * len(NAMES) :]
    square_ref, inner, band, left = refs
    layer = layer_ref[0]
    side, core = layer // 2, layer % 2
    half = g.size // 2
    fill_band(g, layer, slabs, band)

    def gather(side_value):
        for t in range(g.rows):
            row = (t + g.reach_low) * g.size
            place_row(
                inner, row, 0, band, t * g.size, g.size, 0, g.span,
                t - g.pair * side_value, g.size, g.offsets,
            )
        for n, name in enumerate(NAMES):
            rows, lo, hi = g.message(side_value, steps_of(side_value, name))
            width = pieces[2 * n].shape[1] // g.size
            for m, t in enumerate(rows):
                row = (t + g.reach_low) * g.size
                block = slice(row, row + g.size)
                if lo > 0:
                    inner[block, : lo * g.size] = jnp.zeros((g.size, lo * g.size), inner.dtype)
                if lo + width < g.span:
                    inner[block, (lo + width) * g.size :] = jnp.zeros(
                        (g.size, (g.span - lo - width) * g.size), inner.dtype
                    )
                for q in range(2):
                    at = pl.multiple_of(row + half * (core ^ q), half)
                    inner[pl.ds(at, half), lo * g.size : (lo + width) * g.size] = pieces[2 * n + q][
                        m * half : (m + 1) * half, :
                    ]

    for side_value in (0, 1):
        pl.when(side == side_value)(functools.partial(gather, side_value))
    keep = expand_pattern(pattern_ref, square_ref.shape[1], g.size)

    def finish(t, value):
        rows = slice(t * g.size, (t + 1) * g.size)
        square_ref[rows, :] = (value * keep[t : t + 1, :]).astype(square_ref.dtype)

    banded_product(g, core, band, left, inner, finish)


def cubic_kernel(g, layer_ref, pattern_ref, *refs):
    slabs, refs = refs[: g.layers], refs[g.layers :]
    inner, out_ref, band, left = refs
    layer = layer_ref[0]
    core = layer % 2
    fill_band(g, layer, slabs, band)
    keep = expand_pattern(pattern_ref, out_ref.shape[1], g.size)

    def finish(t, value):
        rows = slice(t * g.size, (t + 1) * g.size)
        out_ref[rows, :] = 3.0 * slabs[0][rows, :].astype(jnp.float32) - 2.0 * (
            value * keep[t : t + 1, :]
        )

    banded_product(g, core, band, left, inner, finish)


def call(kernel, out_shape, scratch, smem, *args, flops=0):
    specs = [pl.BlockSpec(memory_space=pltpu.SMEM)] * smem + [VMEM] * (len(args) - smem)
    moved = sum(a.size * a.dtype.itemsize for a in args)
    return pl.pallas_call(
        kernel,
        out_shape=out_shape,
        in_specs=specs,
        out_specs=jax.tree.map(lambda _: VMEM, out_shape),
        scratch_shapes=scratch,
        compiler_params=pltpu.CompilerParams(vmem_limit_bytes=LIMIT),
        cost_estimate=pl.CostEstimate(flops=flops, bytes_accessed=moved, transcendentals=0),
    )(*args)


def body(density, pattern):
    layers, ring = lax.axis_size("layer"), lax.axis_size("row")
    g = Geometry(*density.shape, *pattern.shape, layers)
    rows_dev, cols = density.shape
    half_rows = g.size // 2
    layer = lax.axis_index("layer").astype(jnp.int32)
    layer_arg = layer[None]
    bf16 = functools.partial(jax.ShapeDtypeStruct, dtype=jnp.bfloat16)

    def swap(value, bit):
        return lax.ppermute(value, "layer", [(s, s ^ bit) for s in range(layers)])

    def send(value, name):
        pairs = []
        for r in range(ring):
            for l in range(layers):
                to = (r - steps_of(l // 2, name)) % ring
                pairs.append((l * ring + r, l * ring + to))
        return lax.ppermute(value, ("layer", "row"), pairs)

    def shape_of(name):
        rows, width = message_shape(g, name)
        return bf16((rows * half_rows, width * g.size))

    masked = call(functools.partial(mask_kernel, g), bf16((rows_dev, cols)), [], 0, density, pattern)
    across = swap(masked, 2)
    beside = swap(masked, 1)
    thin = [name for name in NAMES if name[1] == "thin"]
    wide = [name for name in NAMES if name[1] == "wide"]
    got = {}
    packed = call(
        functools.partial(pack_kernel, g, thin, 2),
        [shape_of(name) for name in thin],
        [pltpu.VMEM((rows_dev // 2, 2 * cols), jnp.bfloat16)],
        1, layer_arg, masked, beside,
    )
    for name, value in zip(thin, packed):
        got[name] = send(value, name)
    diagonal = swap(across, 1)
    slabs = (masked, beside, across, diagonal)
    packed = call(
        functools.partial(pack_kernel, g, wide, layers),
        [shape_of(name) for name in wide],
        [pltpu.VMEM((rows_dev // 2, layers * cols), jnp.bfloat16)],
        1, layer_arg, *slabs,
    )
    for name, value in zip(wide, packed):
        got[name] = send(value, name)
    pieces = []
    for name in NAMES:
        pieces += [got[name], swap(got[name], 1)]

    windows = group_windows(g)
    flops = sum(2 * w[1] * w[3] * w[5] * g.size**3 for w in windows)
    left = pltpu.VMEM(
        (max(w[1] for w in windows) * g.size, g.even_up(max(w[3] for w in windows)) * g.size), jnp.bfloat16
    )
    band = pltpu.VMEM((rows_dev, layers * cols), jnp.bfloat16)
    square, inner = call(
        functools.partial(square_kernel, g),
        [bf16((rows_dev, cols)), bf16((g.inner * g.size, g.span * g.size))],
        [band, left],
        1, layer_arg, pattern, *slabs, *pieces, flops=flops,
    )
    square_across, square_beside = swap(square, 2), swap(square, 1)
    square_slabs = (square, square_beside, square_across, swap(square_across, 1))
    return call(
        functools.partial(cubic_kernel, g),
        jax.ShapeDtypeStruct((rows_dev, cols), jnp.float32),
        [band, left],
        1, layer_arg, pattern, *square_slabs, inner, flops=flops,
    )


def solution(mesh):
    placed = (P("row", "layer"), P("row", "layer"))
    return jax.shard_map(
        body, mesh=mesh, in_specs=placed, out_specs=P("row", "layer"), check_vma=False
    )
```

time: 614 us -> 106 us (0.17)
  local copies, waits for them, and re-layouts: 260 us -> 2.84 us
  waiting for transfers between devices: 198 us -> 74.9 us
  matrix products: 70.5 us -> 0 us
  loops' own time: 55.6 us -> 0 us
  Pallas kernels: 0 us -> 14.7 us
  between operations: 13.5 us -> 0.06 us
  starting transfers between devices: 6.79 us -> 13.3 us
    gather x20 -> x0, local copies, waits for them, and re-layouts: 102 us -> none  [piece(): lax.dynamic_slice(padded, (start_row, 0, start_col, 0), (1, tile_size, sl...]
    ppermute x4 -> x14, waiting for transfers between devices: 146 us -> 74.9 us  [the longest x4 39.5 us: send(): return lax.ppermute(value, ('layer', 'row'), pairs)]
    dot_general x20 -> x0, matrix products: 70.5 us -> none  [row_product(): jnp.einsum('xay,ayoz->xoz', left_row, windows, preferred_element_type=jnp...]
    reshape x5 -> x0, local copies, waits for them, and re-layouts: 59 us -> none  [the longest x1 37.5 us: body(): margin.reshape(-1, tile_size, offsets, tile_size)]
    another operation x2 -> x0, loops' own time: 55.6 us -> none  [products(): lax.map(lambda row_idx: row_product(left_blocks[row_idx], offsets, first_...]
    all_gather x2 -> x0, waiting for transfers between devices: 52.3 us -> none  [the longest x1 28.4 us: body(): own_band = lax.all_gather(masked, 'layer', axis=1, tiled=True)]
    dynamic_slice x40 -> x0, local copies, waits for them, and re-layouts: 34.9 us -> none  [the longest x20 21.6 us: products(): left_blocks[row_idx]]
    unnamed x9 -> x7, local copies, waits for them, and re-layouts: 31.3 us -> 2.84 us
  transfers between devices with their start and end apart: 6 -> 14, of which waited for: 5 -> 8; matrix products, arithmetic and copies ran while one was open for 3% -> 0% of each run, Pallas kernels for 0% -> 0%
where the time goes in v1:
time: 106 us
  waiting for transfers between devices  74.9 us (71%)
  Pallas kernels  14.7 us (14%)
  starting transfers between devices  13.3 us (13%)
  local copies, waits for them, and re-layouts  2.84 us (3%)
    ppermute x4, waiting for transfers between devices, send(): return lax.ppermute(value, ('layer', 'row'), pairs)  39.5 us
    ppermute x10, waiting for transfers between devices, swap(): return lax.ppermute(value, 'layer', [(s, s ^ bit) for s in range(layers)])  35.3 us
    pallas_call x5, Pallas kernels, call(): pl.pallas_call(kernel, out_shape=out_shape, in_specs=specs, out_specs=jax...  14.7 us
    ppermute x4, starting transfers between devices, send(): return lax.ppermute(value, ('layer', 'row'), pairs)  7.93 us
    ppermute x10, starting transfers between devices, swap(): return lax.ppermute(value, 'layer', [(s, s ^ bit) for s in range(layers)])  5.32 us
    unnamed x7, local copies, waits for them, and re-layouts  2.84 us
  transfers between devices with their start and end apart: 14, of which 8 were waited for; matrix products, arithmetic and copies ran while one was open for 0% of the time, Pallas kernels for 0%

profile of v1, /device:TPU:0, one launch (start us, length us, event | category | flops | bytes accessed | tf_op | source)
XLA Modules:
  0.0 105.7 jit_solution(8849758642944747165)
XLA Ops:
  0.0 0.8 copy.5.pattern_ref
  0.8 0.0 copy-start
  0.8 1.1 %copy-done = bf16[640,512]{1,0:T(8,128)(2,1)S(1)} copy-done((bf16[640,512]{1,0:T(8,128)(2,1)S(1)}, bf16[640,512]{1,0:T(8,128)(2,1)}, u32[]{:S(2)}) %copy-start) | copy-done | bytes 655384
  1.9 0.2 shard_map.28.refs_0_
  2.0 3.0 %collective-permute-start.1 = (bf16[640,512]{1,0:T(8,128)(2,1)S(1)}, bf16[640,512]{1,0:T(8,128)(2,1)S(1)}, u32[]{:S(2)}, u32[]{:S(2)}) collective-permute-start(bf16[640,512]{1,0:T(8,128)(2,1)S(1)} %shard_map.28.refs_0_), channel_id=1, source_target_pairs={{0,16},{8,24},{16,0},{24,8},{1,17},{9,25},{17,1},{25,9},{2,18},{10... | collective-permute-start | bytes 1966088 | tf_op jit(solution)/shard_map/ppermute | solution.py:269
  5.0 0.0 collective-permute-start
  5.0 14.7 %collective-permute-done.1.refs_2_ = bf16[640,512]{1,0:T(8,128)(2,1)S(1)} collective-permute-done((bf16[640,512]{1,0:T(8,128)(2,1)S(1)}, bf16[640,512]{1,0:T(8,128)(2,1)S(1)}, u32[]{:S(2)}, u32[]{:S(2)}) %collective-permute-start.1) | collective-permute-done | bytes 655392 | tf_op jit(solution)/shard_map/ppermute | solution.py:269
  19.8 0.0 collective-permute-start.2
  19.8 0.0 collective-permute-done.refs_1_
  19.8 2.1 %collective-permute-done.2.refs_3_ = bf16[640,512]{1,0:T(8,128)(2,1)S(1)} collective-permute-done((bf16[640,512]{1,0:T(8,128)(2,1)S(1)}, bf16[640,512]{1,0:T(8,128)(2,1)S(1)}, u32[]{:S(2)}, u32[]{:S(2)}) %collective-permute-start.2) | collective-permute-done | bytes 655392 | tf_op jit(solution)/shard_map/ppermute | solution.py:269
  21.9 0.4 shard_map.29
  22.3 1.8 %collective-permute-start.3 = (bf16[320,1664]{1,0:T(8,128)(2,1)S(1)}, bf16[320,1664]{1,0:T(8,128)(2,1)S(1)}, u32[]{:S(2)}, u32[]{:S(2)}) collective-permute-start(bf16[320,1664]{1,0:T(8,128)(2,1)S(1)} %get-tuple-element.11), channel_id=1, source_target_pairs={{0,1},{8,9},{16,23},{24,31},{1,2},{9,10},{17,16},{25,24},{2,3},{10... | collective-permute-start | bytes 3194888 | tf_op jit(solution)/shard_map/ppermute | solution.py:277
  24.1 0.2 shard_map.30
  24.3 3.1 %collective-permute-start.5 = (bf16[320,1024]{1,0:T(8,128)(2,1)S(1)}, bf16[320,1024]{1,0:T(8,128)(2,1)S(1)}, u32[]{:S(2)}, u32[]{:S(2)}) collective-permute-start(bf16[320,1024]{1,0:T(8,128)(2,1)S(1)} %get-tuple-element.12), channel_id=1, source_target_pairs={{0,7},{8,15},{16,17},{24,25},{1,0},{9,8},{17,18},{25,26},{2,1},{10... | collective-permute-start | bytes 1966088 | tf_op jit(solution)/shard_map/ppermute | solution.py:277
  27.5 0.0 collective-permute-start.7
  27.5 33.8 %collective-permute-done.3.refs_4_ = bf16[320,1664]{1,0:T(8,128)(2,1)S(1)} collective-permute-done((bf16[320,1664]{1,0:T(8,128)(2,1)S(1)}, bf16[320,1664]{1,0:T(8,128)(2,1)S(1)}, u32[]{:S(2)}, u32[]{:S(2)}) %collective-permute-start.3) | collective-permute-done | bytes 1064992 | tf_op jit(solution)/shard_map/ppermute | solution.py:277
  61.2 0.0 copy-start.1
  61.2 0.0 collective-permute-start.4
  61.2 2.5 %collective-permute-done.5.refs_6_ = bf16[320,1024]{1,0:T(8,128)(2,1)S(1)} collective-permute-done((bf16[320,1024]{1,0:T(8,128)(2,1)S(1)}, bf16[320,1024]{1,0:T(8,128)(2,1)S(1)}, u32[]{:S(2)}, u32[]{:S(2)}) %collective-permute-start.5) | collective-permute-done | bytes 655392 | tf_op jit(solution)/shard_map/ppermute | solution.py:277
  63.7 0.0 collective-permute-start.6
  63.7 0.0 collective-permute-done.7.refs_8_
  63.7 0.5 collective-permute-start.8
  64.2 3.0 %collective-permute-start.9 = (bf16[192,384]{1,0:T(8,128)(2,1)S(1)}, bf16[192,384]{1,0:T(8,128)(2,1)S(1)}, u32[]{:S(2)}, u32[]{:S(2)}) collective-permute-start(bf16[192,384]{1,0:T(8,128)(2,1)S(1)} %get-tuple-element.14), channel_id=1, source_target_pairs={{0,6},{8,14},{16,18},{24,26},{1,7},{9,15},{17,19},{25,27},{2,0},{1... | collective-permute-start | bytes 442376 | tf_op jit(solution)/shard_map/ppermute | solution.py:277
  67.2 3.3 %collective-permute-done.9.refs_10_ = bf16[192,384]{1,0:T(8,128)(2,1)S(1)} collective-permute-done((bf16[192,384]{1,0:T(8,128)(2,1)S(1)}, bf16[192,384]{1,0:T(8,128)(2,1)S(1)}, u32[]{:S(2)}, u32[]{:S(2)}) %collective-permute-start.9) | collective-permute-done | bytes 147488 | tf_op jit(solution)/shard_map/ppermute | solution.py:277
  70.5 0.0 collective-permute-start.10
  70.5 1.4 %collective-permute-done.10.refs_11_ = bf16[192,384]{1,0:T(8,128)(2,1)S(1)} collective-permute-done((bf16[192,384]{1,0:T(8,128)(2,1)S(1)}, bf16[192,384]{1,0:T(8,128)(2,1)S(1)}, u32[]{:S(2)}, u32[]{:S(2)}) %collective-permute-start.10) | collective-permute-done | bytes 147488 | tf_op jit(solution)/shard_map/ppermute | solution.py:269
  71.9 0.0 collective-permute-done.6.refs_7_
  71.9 0.0 collective-permute-done.8.refs_9_
  71.9 0.0 collective-permute-done.4.refs_5_
  71.9 0.0 copy-done.1
  71.9 0.0 copy-start.2
  71.9 1.0 copy-done.2
  72.9 6.1 %shard_map.31 = (bf16[640,512]{1,0:T(8,128)(2,1)S(1)}, bf16[2624,1664]{1,0:T(8,128)(2,1)}) custom-call(s32[1]{0:T(128)} %bitcast.layer_ref, s32[10,8]{1,0:T(8,128)S(1)} %copy.5.pattern_ref, bf16[640,512]{1,0:T(8,128)(2,1)S(1)} %shard_map.28.refs_0_, bf16[640,512]{1,0:T(8,128)(2,1)S(1)} %collective-permute-done.refs_1_, ...), custom_call_target="tpu_custom_call" | custom-call | flops 2453667840 | bytes 7438660 | tf_op jit(solution)/shard_map/pallas_call | solution.py:248
  79.0 1.8 %collective-permute-start.12 = (bf16[640,512]{1,0:T(8,128)(2,1)S(1)}, bf16[640,512]{1,0:T(8,128)(2,1)S(1)}, u32[]{:S(2)}, u32[]{:S(2)}) collective-permute-start(bf16[640,512]{1,0:T(8,128)(2,1)S(1)} %get-tuple-element.15.refs_0_), channel_id=1, source_target_pairs={{0,16},{8,24},{16,0},{24,8},{1,17},{9,25},{17,1},{25,9},{2,18},{10... | collective-permute-start | bytes 1966088 | tf_op jit(solution)/shard_map/ppermute | solution.py:269
  80.8 0.0 collective-permute-start.11
  80.8 15.0 %collective-permute-done.12.refs_2_ = bf16[640,512]{1,0:T(8,128)(2,1)S(1)} collective-permute-done((bf16[640,512]{1,0:T(8,128)(2,1)S(1)}, bf16[640,512]{1,0:T(8,128)(2,1)S(1)}, u32[]{:S(2)}, u32[]{:S(2)}) %collective-permute-start.12) | collective-permute-done | bytes 655392 | tf_op jit(solution)/shard_map/ppermute | solution.py:269
  95.8 0.0 collective-permute-start.13
  95.8 0.0 collective-permute-done.11.refs_1_
  95.8 2.1 %collective-permute-done.13.refs_3_ = bf16[640,512]{1,0:T(8,128)(2,1)S(1)} collective-permute-done((bf16[640,512]{1,0:T(8,128)(2,1)S(1)}, bf16[640,512]{1,0:T(8,128)(2,1)S(1)}, u32[]{:S(2)}, u32[]{:S(2)}) %collective-permute-start.13) | collective-permute-done | bytes 655392 | tf_op jit(solution)/shard_map/ppermute | solution.py:269
  97.9 7.8 %shard_map.32 = f32[640,512]{1,0:T(8,128)} custom-call(s32[1]{0:T(128)} %bitcast.layer_ref, s32[10,8]{1,0:T(8,128)S(1)} %copy.5.pattern_ref, bf16[640,512]{1,0:T(8,128)(2,1)S(1)} %get-tuple-element.15.refs_0_, bf16[640,512]{1,0:T(8,128)(2,1)S(1)} %collective-permute-done.11.refs_1_, bf16[640,512]{1,0:T(8,128)(2,1)S(1)} %collective-permute-done.12.refs_2_, ...), custom_call_target="tpu_custom_call" | custom-call | flops 2453667840 | bytes 11354436 | tf_op jit(solution)/shard_map/pallas_call | solution.py:248
Async XLA Ops:
  0.8 1.1 %copy-start = (bf16[640,512]{1,0:T(8,128)(2,1)S(1)}, bf16[640,512]{1,0:T(8,128)(2,1)}, u32[]{:S(2)}) copy-start(bf16[640,512]{1,0:T(8,128)(2,1)} %density_ref.1) | copy-start | bytes 1966084
  2.0 17.7 %collective-permute-start.1 = (bf16[640,512]{1,0:T(8,128)(2,1)S(1)}, bf16[640,512]{1,0:T(8,128)(2,1)S(1)}, u32[]{:S(2)}, u32[]{:S(2)}) collective-permute-start(bf16[640,512]{1,0:T(8,128)(2,1)S(1)} %shard_map.28.refs_0_), channel_id=1, source_target_pairs={{0,16},{8,24},{16,0},{24,8},{1,17},{9,25},{17,1},{25,9},{2,18},{10... | collective-permute-start | bytes 1966088 | tf_op jit(solution)/shard_map/ppermute | solution.py:269
  5.0 14.7 %collective-permute-start = (bf16[640,512]{1,0:T(8,128)(2,1)S(1)}, bf16[640,512]{1,0:T(8,128)(2,1)S(1)}, u32[]{:S(2)}, u32[]{:S(2)}) collective-permute-start(bf16[640,512]{1,0:T(8,128)(2,1)S(1)} %shard_map.28.refs_0_), channel_id=1, source_target_pairs={{0,8},{8,0},{16,24},{24,16},{1,9},{9,1},{17,25},{25,17},{2,10},{10... | collective-permute-start | bytes 1966088 | tf_op jit(solution)/shard_map/ppermute | solution.py:269
  19.8 2.1 %collective-permute-start.2 = (bf16[640,512]{1,0:T(8,128)(2,1)S(1)}, bf16[640,512]{1,0:T(8,128)(2,1)S(1)}, u32[]{:S(2)}, u32[]{:S(2)}) collective-permute-start(bf16[640,512]{1,0:T(8,128)(2,1)S(1)} %collective-permute-done.1.refs_2_), channel_id=1, source_target_pairs={{0,8},{8,0},{16,24},{24,16},{1,9},{9,1},{17,25},{25,17},{2,10},{10... | collective-permute-start | bytes 1966088 | tf_op jit(solution)/shard_map/ppermute | solution.py:269
  22.3 38.9 %collective-permute-start.3 = (bf16[320,1664]{1,0:T(8,128)(2,1)S(1)}, bf16[320,1664]{1,0:T(8,128)(2,1)S(1)}, u32[]{:S(2)}, u32[]{:S(2)}) collective-permute-start(bf16[320,1664]{1,0:T(8,128)(2,1)S(1)} %get-tuple-element.11), channel_id=1, source_target_pairs={{0,1},{8,9},{16,23},{24,31},{1,2},{9,10},{17,16},{25,24},{2,3},{10... | collective-permute-start | bytes 3194888 | tf_op jit(solution)/shard_map/ppermute | solution.py:277
  24.3 39.4 %collective-permute-start.5 = (bf16[320,1024]{1,0:T(8,128)(2,1)S(1)}, bf16[320,1024]{1,0:T(8,128)(2,1)S(1)}, u32[]{:S(2)}, u32[]{:S(2)}) collective-permute-start(bf16[320,1024]{1,0:T(8,128)(2,1)S(1)} %get-tuple-element.12), channel_id=1, source_target_pairs={{0,7},{8,15},{16,17},{24,25},{1,0},{9,8},{17,18},{25,26},{2,1},{10... | collective-permute-start | bytes 1966088 | tf_op jit(solution)/shard_map/ppermute | solution.py:277
  27.5 36.3 %collective-permute-start.7 = (bf16[192,1408]{1,0:T(8,128)(2,1)S(1)}, bf16[192,1408]{1,0:T(8,128)(2,1)S(1)}, u32[]{:S(2)}, u32[]{:S(2)}) collective-permute-start(bf16[192,1408]{1,0:T(8,128)(2,1)S(1)} %get-tuple-element.13), channel_id=1, source_target_pairs={{0,2},{8,10},{16,22},{24,30},{1,3},{9,11},{17,23},{25,31},{2,4},{1... | collective-permute-start | bytes 1622024 | tf_op jit(solution)/shard_map/ppermute | solution.py:277
  61.2 10.7 %copy-start.1 = (bf16[320,1664]{1,0:T(8,128)(2,1)}, bf16[320,1664]{1,0:T(8,128)(2,1)S(1)}, u32[]{:S(2)}) copy-start(bf16[320,1664]{1,0:T(8,128)(2,1)S(1)} %collective-permute-done.3.refs_4_) | copy-start | bytes 3194884
  61.2 10.6 %collective-permute-start.4 = (bf16[320,1664]{1,0:T(8,128)(2,1)S(1)}, bf16[320,1664]{1,0:T(8,128)(2,1)S(1)}, u32[]{:S(2)}, u32[]{:S(2)}) collective-permute-start(bf16[320,1664]{1,0:T(8,128)(2,1)S(1)} %collective-permute-done.3.refs_4_), channel_id=1, source_target_pairs={{0,8},{8,0},{16,24},{24,16},{1,9},{9,1},{17,25},{25,17},{2,10},{10... | collective-permute-start | bytes 3194888 | tf_op jit(solution)/shard_map/ppermute | solution.py:269
  63.7 8.2 %collective-permute-start.6 = (bf16[320,1024]{1,0:T(8,128)(2,1)S(1)}, bf16[320,1024]{1,0:T(8,128)(2,1)S(1)}, u32[]{:S(2)}, u32[]{:S(2)}) collective-permute-start(bf16[320,1024]{1,0:T(8,128)(2,1)S(1)} %collective-permute-done.5.refs_6_), channel_id=1, source_target_pairs={{0,8},{8,0},{16,24},{24,16},{1,9},{9,1},{17,25},{25,17},{2,10},{10... | collective-permute-start | bytes 1966088 | tf_op jit(solution)/shard_map/ppermute | solution.py:269
  63.7 8.2 %collective-permute-start.8 = (bf16[192,1408]{1,0:T(8,128)(2,1)S(1)}, bf16[192,1408]{1,0:T(8,128)(2,1)S(1)}, u32[]{:S(2)}, u32[]{:S(2)}) collective-permute-start(bf16[192,1408]{1,0:T(8,128)(2,1)S(1)} %collective-permute-done.7.refs_8_), channel_id=1, source_target_pairs={{0,8},{8,0},{16,24},{24,16},{1,9},{9,1},{17,25},{25,17},{2,10},{10... | collective-permute-start | bytes 1622024 | tf_op jit(solution)/shard_map/ppermute | solution.py:269
  64.2 6.3 %collective-permute-start.9 = (bf16[192,384]{1,0:T(8,128)(2,1)S(1)}, bf16[192,384]{1,0:T(8,128)(2,1)S(1)}, u32[]{:S(2)}, u32[]{:S(2)}) collective-permute-start(bf16[192,384]{1,0:T(8,128)(2,1)S(1)} %get-tuple-element.14), channel_id=1, source_target_pairs={{0,6},{8,14},{16,18},{24,26},{1,7},{9,15},{17,19},{25,27},{2,0},{1... | collective-permute-start | bytes 442376 | tf_op jit(solution)/shard_map/ppermute | solution.py:277
  70.5 1.4 %collective-permute-start.10 = (bf16[192,384]{1,0:T(8,128)(2,1)S(1)}, bf16[192,384]{1,0:T(8,128)(2,1)S(1)}, u32[]{:S(2)}, u32[]{:S(2)}) collective-permute-start(bf16[192,384]{1,0:T(8,128)(2,1)S(1)} %collective-permute-done.9.refs_10_), channel_id=1, source_target_pairs={{0,8},{8,0},{16,24},{24,16},{1,9},{9,1},{17,25},{25,17},{2,10},{10... | collective-permute-start | bytes 442376 | tf_op jit(solution)/shard_map/ppermute | solution.py:269
  71.9 1.0 copy-start.2
  79.0 16.8 %collective-permute-start.12 = (bf16[640,512]{1,0:T(8,128)(2,1)S(1)}, bf16[640,512]{1,0:T(8,128)(2,1)S(1)}, u32[]{:S(2)}, u32[]{:S(2)}) collective-permute-start(bf16[640,512]{1,0:T(8,128)(2,1)S(1)} %get-tuple-element.15.refs_0_), channel_id=1, source_target_pairs={{0,16},{8,24},{16,0},{24,8},{1,17},{9,25},{17,1},{25,9},{2,18},{10... | collective-permute-start | bytes 1966088 | tf_op jit(solution)/shard_map/ppermute | solution.py:269
  80.8 15.0 %collective-permute-start.11 = (bf16[640,512]{1,0:T(8,128)(2,1)S(1)}, bf16[640,512]{1,0:T(8,128)(2,1)S(1)}, u32[]{:S(2)}, u32[]{:S(2)}) collective-permute-start(bf16[640,512]{1,0:T(8,128)(2,1)S(1)} %get-tuple-element.15.refs_0_), channel_id=1, source_target_pairs={{0,8},{8,0},{16,24},{24,16},{1,9},{9,1},{17,25},{25,17},{2,10},{10... | collective-permute-start | bytes 1966088 | tf_op jit(solution)/shard_map/ppermute | solution.py:269
  95.8 2.1 %collective-permute-start.13 = (bf16[640,512]{1,0:T(8,128)(2,1)S(1)}, bf16[640,512]{1,0:T(8,128)(2,1)S(1)}, u32[]{:S(2)}, u32[]{:S(2)}) collective-permute-start(bf16[640,512]{1,0:T(8,128)(2,1)S(1)} %collective-permute-done.12.refs_2_), channel_id=1, source_target_pairs={{0,8},{8,0},{16,24},{24,16},{1,9},{9,1},{17,25},{25,17},{2,10},{10... | collective-permute-start | bytes 1966088 | tf_op jit(solution)/shard_map/ppermute | solution.py:269

commit v2 on v0

v2 whole, which is shorter than its diff:
```python
import functools

import jax
import jax.numpy as jnp
from jax import lax
from jax.experimental import pallas as pl
from jax.experimental.pallas import tpu as pltpu
from jax.sharding import PartitionSpec as P

VMEM = pl.BlockSpec(memory_space=pltpu.VMEM)
LIMIT = 12 * 1024 * 1024


class Geometry:
    def __init__(self, rows_dev, slab_cols, block_rows, slab_offsets, layers):
        self.rows, self.slab = block_rows, slab_offsets
        self.size = rows_dev // block_rows
        self.layers = layers
        self.offsets = slab_offsets * layers
        self.half = self.offsets // 2
        self.pair = 2 * slab_offsets
        self.reach_low, self.reach_high = self.half, self.half - 1
        self.columns = self.pair + block_rows - 1
        self.span = even_up(self.columns)
        self.far = even_up(max(len(self.reached(step)) for step in (-2, 2)))

    def needed(self, t, side):
        lo, hi = self.pair * side - t, self.pair * side - t + self.columns
        if t < 0:
            lo = max(lo, -t)
        if t >= self.rows:
            hi = min(hi, self.offsets - (t - self.rows + 1))
        lo, hi = max(lo, 0), min(hi, self.offsets)
        return lo, max(lo, hi)

    def reached(self, step):
        first = step * self.rows
        return [
            t
            for t in range(first, first + self.rows)
            if -self.reach_low <= t < self.rows + self.reach_high
        ]

    def inner_rows(self, side, part):
        if part == "early":
            return sorted(list(range(self.rows)) + self.reached(step_of(side, NEAR_THIN)))
        rows = []
        for name in ([NEAR_WIDE, FAR_WIDE] if part == "late" else [FAR_THIN]):
            reached = self.reached(step_of(side, name))
            rows += reached + [None] * (0 if name[0] == "near" else self.far - len(reached))
        return rows

    def inner_count(self, part):
        return len(self.inner_rows(0, part))

    def group(self, name):
        first = even_up(2 * self.rows // 5)
        count = first if name == "A" else self.rows - first
        return count, even_up(count - 1 + self.slab)

    def first(self, side, name):
        return 0 if (side == 0) == (name == "A") else self.rows - self.group(name)[0]

    def layout(self, side, name):
        step = step_of(side, name)
        found = []
        for t in self.reached(step):
            lo, hi = self.needed(t, side)
            lo, hi = max(lo, self.pair * side), min(hi, self.pair * (side + 1))
            if hi > lo:
                found.append((even_up(hi) - even_down(lo), t, even_down(lo), even_up(hi)))
        found.sort(reverse=True)
        slots = (len(found) + 1) // 2
        used = [0] * slots
        places = {}
        for n, (width, t, lo, hi) in enumerate(found):
            slot = n if n < slots else 2 * slots - 1 - n
            places[t] = (slot, used[slot], lo, hi)
            used[slot] += width
        return places, slots, max(used)


def even_down(n):
    return n // 2 * 2


def even_up(n):
    return (n + 1) // 2 * 2


def step_of(side, name):
    sign = 1 if (name[1] == "thin") == (side == 0) else -1
    return sign * (1 if name[0] == "near" else 2)


NEAR_WIDE, NEAR_THIN = ("near", "wide"), ("near", "thin")
FAR_WIDE, FAR_THIN = ("far", "wide"), ("far", "thin")


def message_shape(g, name):
    layouts = [g.layout(side, name) for side in (0, 1)]
    rows, cols = max(f[1] for f in layouts) * g.size // 2, max(f[2] for f in layouts) * g.size
    if name == FAR_WIDE:
        return rows + g.far * g.size, g.slab * g.size
    return (2 * rows, cols) if name == FAR_THIN else (rows, cols)


def expand_pattern(pattern_ref, slab_cols, size):
    offsets = pattern_ref.shape[0]
    block = lax.broadcasted_iota(jnp.int32, (offsets, slab_cols), 1) // size
    row = lax.broadcasted_iota(jnp.int32, (offsets, slab_cols), 0)
    spread = jnp.where(block == row, 1.0, 0.0).astype(jnp.float32)
    return lax.dot_general(
        pattern_ref[...].astype(jnp.float32), spread, (((0,), (0,)), ((), ())),
        preferred_element_type=jnp.float32,
    )


def cross_rows(g, side):
    rows = [t - step_of(side, FAR_WIDE) * g.rows for t in g.reached(step_of(side, FAR_WIDE))]
    count = g.far
    return min(rows[0], g.rows - count), count


def mask_kernel(g, density_ref, pattern_ref, out_ref):
    keep = expand_pattern(pattern_ref, density_ref.shape[1], g.size)
    for t in range(g.rows):
        rows = slice(t * g.size, (t + 1) * g.size)
        out_ref[rows, :] = density_ref[rows, :] * keep[t : t + 1, :].astype(jnp.bfloat16)


def place_row(dst_ref, dst_row, dst_lo, src_ref, src_row, height, lo, hi, shift, size, limit):
    first, last = max(lo, shift), min(hi, limit + shift)
    base = dst_lo - lo
    rows = slice(dst_row, dst_row + height)
    if first >= last:
        dst_ref[rows, dst_lo * size : (hi + base) * size] = jnp.zeros(
            (height, (hi - lo) * size), dst_ref.dtype
        )
        return
    value = src_ref[src_row : src_row + height, (first - shift) * size : (last - shift) * size]
    parts = []
    if first > lo:
        parts.append(jnp.zeros((height, (first - lo) * size), dst_ref.dtype))
    parts.append(value)
    if hi > last:
        parts.append(jnp.zeros((height, (hi - last) * size), dst_ref.dtype))
    if len(parts) > 1:
        value = jnp.concatenate(parts, axis=1)
    dst_ref[rows, dst_lo * size : (hi + base) * size] = value


def pack(g, side, name, source, row_of, lead, height, out):
    places, slots, _ = g.layout(side, name)
    filled = [0] * slots
    for t, (slot, col, lo, hi) in places.items():
        out[slot * height : (slot + 1) * height, col * g.size : (col + hi - lo) * g.size] = source[
            pl.ds(row_of(t - step_of(side, name) * g.rows), height), (lo - lead) * g.size : (hi - lead) * g.size
        ]
        filled[slot] = max(filled[slot], col + hi - lo)
    for slot, count in enumerate(filled):
        if count * g.size < out.shape[1]:
            out[slot * height : (slot + 1) * height, count * g.size :] = jnp.zeros(
                (height, out.shape[1] - count * g.size), out.dtype
            )
    if slots * height < out.shape[0] and name != FAR_WIDE:
        out[slots * height :, :] = jnp.zeros((out.shape[0] - slots * height, out.shape[1]), out.dtype)


def fill_near(g, core, slabs, near):
    half, cols = g.size // 2, g.slab * g.size
    for q, slab in enumerate(slabs):
        start = pl.multiple_of((core ^ q) * cols, cols)
        for t in range(g.rows):
            src = pl.multiple_of(t * g.size + half * core, half)
            near[t * half : (t + 1) * half, pl.ds(start, cols)] = slab[pl.ds(src, half), :]


def pack_far_kernel(g, layer_ref, own_ref, beside_ref, other_ref, message, near):
    side, core = layer_ref[0] // 2, layer_ref[0] % 2
    half = g.size // 2
    fill_near(g, core, (own_ref, beside_ref), near)

    def fill(side):
        pack(g, side, FAR_WIDE, near, lambda row: row * half, side * g.pair, half, message)
        first, count = cross_rows(g, side)
        message[message.shape[0] - count * g.size :, :] = other_ref[first * g.size : (first + count) * g.size, :]

    for value in (0, 1):
        pl.when(side == value)(functools.partial(fill, value))


def relay_kernel(g, device_ref, own_ref, relayed_ref, after_ref, out_ref):
    side, row = device_ref[0] // 2, device_ref[1]
    pick((row % 2) == side, own_ref, relayed_ref, out_ref)


def pass_kernel(in_ref, *refs):
    refs[-1][...] = in_ref[...]


def pass_far_kernel(g, layer_ref, in_ref, after_ref, out_ref, message):
    out_ref[...] = in_ref[...]

    def fill(side):
        first, count = cross_rows(g, side)
        start = in_ref.shape[0] - (count + first) * g.size
        lead = (1 - side) * (g.offsets - g.slab)
        pack(g, 1 - side, FAR_THIN, in_ref, lambda row: start + row * g.size, lead, g.size, message)

    for value in (0, 1):
        pl.when(layer_ref[0] // 2 == value)(functools.partial(fill, value))


def fill_pair(g, core, slabs, pair):
    cols = g.slab * g.size
    for q, slab in enumerate(slabs):
        pair[:, pl.ds(pl.multiple_of((core ^ q) * cols, cols), cols)] = slab[...]


def place_parts(g, dst, at, height, t, side, parts):
    shift = t - g.pair * side
    values, done = [], 0
    for lo, hi, load in parts:
        lo, hi = max(lo, done - shift), min(hi, g.span - shift)
        if lo >= hi:
            continue
        if lo + shift > done:
            values.append(jnp.zeros((height, (lo + shift - done) * g.size), dst.dtype))
        values.append(load(lo, hi))
        done = hi + shift
    if done < g.span:
        values.append(jnp.zeros((height, (g.span - done) * g.size), dst.dtype))
    dst[pl.ds(at, height), :] = jnp.concatenate(values, axis=1) if len(values) > 1 else values[0]


def left_rows(g, dst, inner_rows, rows, band, band_first, lead, limit):
    runs = []
    for k, t in enumerate(inner_rows):
        offset = None if t is None else t - k
        if runs and runs[-1][0] == offset:
            runs[-1][2] = k + 1
        else:
            runs.append([offset, k, k + 1])
    for n, i in enumerate(rows):
        for offset, lo, hi in runs:
            shift = hi if offset is None else i - g.reach_low - offset + lead
            place_row(
                dst, n * g.size, lo, band, (band_first + n) * g.size, g.size, lo, hi, shift, g.size, limit
            )


def window_of(g, core, inner, col, cols):
    start = pl.multiple_of((core * g.slab + col) * g.size, 2 * g.size)
    return inner[:, pl.ds(start, cols * g.size)]


def dot(left, right):
    return jnp.dot(left, right, preferred_element_type=jnp.float32)


def own_columns(g, product, n):
    return product[n * g.size : (n + 1) * g.size, n * g.size : (n + g.slab) * g.size]


def by_side(side, values):
    return jnp.where(side == 0, values[0], values[1])


def group_first(g, side, name):
    return by_side(side, [g.first(value, name) for value in (0, 1)])


def message_part(g, side, name, t, piece, height):
    places, _, _ = g.layout(side, name)
    if t not in places:
        return []
    slot, col, lo, hi = places[t]
    rows = slice(slot * height, (slot + 1) * height)
    return [(lo, hi, lambda a, b: piece[rows, (col + a - lo) * g.size : (col + b - lo) * g.size])]


def pair_part(g, pair_index, ref, row, height):
    base = g.pair * pair_index
    return (
        base,
        base + g.pair,
        lambda a, b: ref[pl.ds(row, height), (a - base) * g.size : (b - base) * g.size],
    )


def pick(condition, first, second, out):
    pl.when(condition)(lambda: out.__setitem__(..., first[...]))
    pl.when(jnp.logical_not(condition))(lambda: out.__setitem__(..., second[...]))


def group_rows(g, side, name):
    first = g.first(side, name)
    return range(first, first + g.group(name)[0])


def early_kernel(g, layer_ref, own, beside, *refs):
    others, thins = refs[:2], refs[2:4]
    inner, sum_a, sum_b, late_a, late_b, far_b, band, left_a, left_b, pair = refs[4:]
    layer = layer_ref[0]
    side, core = layer // 2, layer % 2
    cols = g.slab * g.size
    for q, slab in enumerate((own, beside, *others)):
        band[:, pl.ds(pl.multiple_of((layer ^ q) * cols, cols), cols)] = slab[...]
    fill_pair(g, core, thins, pair)

    def gather(side):
        near = g.reached(step_of(side, NEAR_THIN))
        early, late, far = (g.inner_rows(side, part) for part in ("early", "late", "far"))
        for k, t in enumerate(early):
            if 0 <= t < g.rows:
                part = (0, g.offsets, lambda a, b, t=t: band[
                    t * g.size : (t + 1) * g.size, a * g.size : b * g.size
                ])
            else:
                part = pair_part(g, side, pair, (t - near[0]) * g.size, g.size)
            place_parts(g, inner, k * g.size, g.size, t, side, [part])
        for name, lefts in (("A", ((left_a, early), (late_a, late))), ("B", ((left_b, early), (late_b, late), (far_b, far)))):
            rows = group_rows(g, side, name)
            for left, inner_rows in lefts:
                left_rows(g, left, inner_rows, rows, band, rows[0], 0, g.offsets)

    for value in (0, 1):
        pl.when(side == value)(functools.partial(gather, value))
    for name, left, out in (("A", left_a, sum_a), ("B", left_b, sum_b)):
        col, (_, cols) = group_first(g, side, name), g.group(name)
        out[...] = dot(left[...], window_of(g, core, inner, col, cols))


def square_of(g, name, side, core, pattern_ref, total, lefts, inners, keep):
    keep[: g.rows, :] = expand_pattern(pattern_ref, keep.shape[1], g.size)
    first, (_, cols) = group_first(g, side, name), g.group(name)
    product = total[...]
    for left, inner in zip(lefts, inners):
        product += dot(left[...], window_of(g, core, inner, first, cols))
    return lambda n: (own_columns(g, product, n) * keep[pl.ds(first + n, 1), :]).astype(jnp.bfloat16)


def late_kernel(g, layer_ref, pattern_ref, *refs):
    crossed, wides, wide_fars = (refs[2 * n : 2 * n + 2] for n in range(3))
    total, left, square, inner, pair, own_pair, far_pair, keep = refs[6:]
    layer = layer_ref[0]
    side, core = layer // 2, layer % 2
    half = g.size // 2
    fill_pair(g, core, crossed, pair)
    fill_pair(g, core, wides, own_pair)
    tail = far_pair.shape[0]
    fill_pair(g, core, [piece.at[piece.shape[0] - tail :, :] for piece in wide_fars], far_pair)

    def gather(side):
        near = g.reached(step_of(side, NEAR_WIDE))
        for k, t in enumerate(g.inner_rows(side, "late")):
            if t is None:
                inner[k * g.size : (k + 1) * g.size, :] = jnp.zeros((g.size, inner.shape[1]), inner.dtype)
            elif t in near:
                row = (t - near[0]) * g.size
                parts = [pair_part(g, value, own_pair if value == side else pair, row, g.size) for value in (0, 1)]
                place_parts(g, inner, k * g.size, g.size, t, side, parts)
            else:
                row = (t - step_of(side, FAR_WIDE) * g.rows - cross_rows(g, side)[0]) * g.size
                for q, piece in enumerate(wide_fars):
                    at = half * (core ^ q)
                    parts = message_part(g, side, FAR_WIDE, t, piece, half)
                    parts.append(pair_part(g, 1 - side, far_pair, pl.multiple_of(row + at, half), half))
                    parts.sort(key=lambda part: part[0])
                    place_parts(g, inner, pl.multiple_of(k * g.size + at, half), half, t, side, parts)

    for value in (0, 1):
        pl.when(side == value)(functools.partial(gather, value))
    row_of = square_of(g, "A", side, core, pattern_ref, total, [left], [inner], keep)
    for n in range(g.group("A")[0]):
        square[n * g.size : (n + 1) * g.size, :] = row_of(n)


def square_kernel(g, layer_ref, pattern_ref, far, total, left, far_left, late, *refs):
    square, inner, keep = refs
    side, core = layer_ref[0] // 2, layer_ref[0] % 2

    def gather(side):
        for k, t in enumerate(g.inner_rows(side, "far")):
            parts = [] if t is None else message_part(g, side, FAR_THIN, t, far, g.size)
            place_parts(g, inner, k * g.size, g.size, t or 0, side, parts)

    for value in (0, 1):
        pl.when(side == value)(functools.partial(gather, value))
    row_of = square_of(g, "B", side, core, pattern_ref, total, [left, far_left], [late, inner], keep)
    for n in range(g.group("B")[0]):
        square[n * g.size : (n + 1) * g.size, :] = row_of(n)


def band_rows(g, side, name):
    return pl.ds(pl.multiple_of(group_first(g, side, name) * g.size, 2 * g.size), g.group(name)[0] * g.size)


def block_rows(g, t):
    return pl.ds(pl.multiple_of(t * g.size, g.size), g.size)


def early_span(g, part):
    spans = []
    for side in (0, 1):
        rows, pair = (range(g.rows), side) if part == "own" else (group_rows(g, 1 - side, part), 1 - side)
        lo = rows[0] - g.reach_low + g.pair * pair
        hi = rows[-1] - g.reach_low + g.pair * (pair + 1)
        met = [k for k, t in enumerate(g.inner_rows(side, "early")) if lo <= t < hi]
        spans.append((even_down(met[0]), met[-1] + 1))
    count = even_up(max(hi - lo for lo, hi in spans))
    total = len(g.inner_rows(0, "early"))
    return [min(lo, total - count) for lo, _ in spans], count


def cubic_left(g, side, part, rows, band, band_first, lefts):
    pair = side if part == "own" else 1 - side
    starts, count = early_span(g, part)
    early = g.inner_rows(side, "early")[starts[side] : starts[side] + count]
    rest = g.inner_rows(side, "late" if part == "own" else "far")
    for dst, inner_rows in zip(lefts, (early, rest)):
        left_rows(g, dst, inner_rows, rows, band, band_first, g.pair * pair, g.pair)


def cubic_right(g, side, part, inners):
    starts, count = early_span(g, part)
    start = pl.multiple_of(by_side(side, starts) * g.size, 2 * g.size)
    return [inners[0].at[pl.ds(start, count * g.size), :], inners[1]]


def left_scratch(g, part, count):
    sizes = [early_span(g, part)[1], g.inner_count("late" if part == "own" else "far")]
    return [pltpu.VMEM((count * g.size, n * g.size), jnp.bfloat16) for n in sizes]


def cubic_kernel(g, layer_ref, pattern_ref, *refs):
    squares, inners, (out, band, own, keep, *lefts) = refs[:4], refs[4:6], refs[6:]
    layer = layer_ref[0]
    side, core = layer // 2, layer % 2
    cols = g.slab * g.size
    for n, name in enumerate("AB"):
        rows = band_rows(g, side, name)
        own[rows, :] = squares[2 * n][...]
        for q in range(2):
            column = pl.ds(pl.multiple_of((core ^ q) * cols, cols), cols)
            band[rows, column] = squares[2 * n + q][...]
    keep[: g.rows, :] = expand_pattern(pattern_ref, cols, g.size)
    rights = cubic_right(g, side, "own", inners)
    size = (g.rows + 1) // 2
    for n, first in enumerate(range(0, g.rows, size)):
        rows = range(first, min(first + size, g.rows))
        col = even_down(first)
        width = even_up(rows[-1] + g.slab) - col
        used = lefts[2 * n : 2 * n + 2]
        for value in (0, 1):
            pl.when(side == value)(functools.partial(cubic_left, g, value, "own", rows, band, first, used))
        product = sum(
            dot(left[: len(rows) * g.size, :], window_of(g, core, right, col, width))
            for left, right in zip(used, rights)
        )
        for k, t in enumerate(rows):
            at = (t - col) * g.size
            here = slice(t * g.size, (t + 1) * g.size)
            out[here, :] = 3.0 * own[here, :].astype(jnp.float32) - 2.0 * (
                product[k * g.size : (k + 1) * g.size, at : at + cols] * keep[t : t + 1, :]
            )


def other_part(g, layer, name, squares, inners, band, lefts):
    side, core = layer // 2, layer % 2
    cols = g.slab * g.size
    _, width = g.group(name)
    for q in range(2):
        band[:, pl.ds(pl.multiple_of((core ^ q) * cols, cols), cols)] = squares[q][...]
    for value in (0, 1):
        rows = group_rows(g, 1 - value, name)
        pl.when(side == value)(functools.partial(cubic_left, g, value, name, rows, band, 0, lefts))
    first = group_first(g, 1 - side, name)
    rights = cubic_right(g, side, name, inners)
    return first, sum(
        dot(left[...], window_of(g, core, right, first, width)) for left, right in zip(lefts, rights)
    )


def other_kernel(g, layer_ref, pattern_ref, *refs):
    squares, inners, (partial, out, band, keep, *lefts) = refs[:2], refs[2:4], refs[4:]
    keep[: g.rows, :] = expand_pattern(pattern_ref, out.shape[1], g.size)
    first, product = other_part(g, layer_ref[0], "A", squares, inners, band, lefts)
    for n in range(g.group("A")[0]):
        out[n * g.size : (n + 1) * g.size, :] = partial[block_rows(g, first + n), :] - 2.0 * (
            own_columns(g, product, n) * keep[pl.ds(first + n, 1), :]
        )


def last_kernel(g, layer_ref, pattern_ref, *refs):
    squares, inners, (partial, done, out, band, keep, *lefts) = refs[:2], refs[2:4], refs[4:]
    keep[: g.rows, :] = expand_pattern(pattern_ref, out.shape[1], g.size)
    out[band_rows(g, 1 - layer_ref[0] // 2, "A"), :] = done[...]
    first, product = other_part(g, layer_ref[0], "B", squares, inners, band, lefts)
    for n in range(g.group("B")[0]):
        rows = block_rows(g, first + n)
        out[rows, :] = partial[rows, :] - 2.0 * (own_columns(g, product, n) * keep[pl.ds(first + n, 1), :])


def call(kernel, out_shape, scratch, smem, *args, flops=0, after=()):
    specs = [pl.BlockSpec(memory_space=pltpu.SMEM)] * smem + [VMEM] * (len(args) - smem)
    specs += [pl.BlockSpec(memory_space=pl.ANY)] * len(after)
    return pl.pallas_call(
        kernel,
        out_shape=out_shape,
        in_specs=specs,
        out_specs=jax.tree.map(lambda _: VMEM, out_shape),
        scratch_shapes=scratch,
        compiler_params=pltpu.CompilerParams(vmem_limit_bytes=LIMIT),
        cost_estimate=pl.CostEstimate(flops=0, bytes_accessed=0, transcendentals=0),
    )(*args, *after)


def body(density, pattern):
    layers, ring = lax.axis_size("layer"), lax.axis_size("row")
    g = Geometry(*density.shape, *pattern.shape, layers)
    pattern = pattern.T
    rows_dev, cols = density.shape
    layer_arg = lax.axis_index("layer").astype(jnp.int32)[None]
    bf16 = functools.partial(jax.ShapeDtypeStruct, dtype=jnp.bfloat16)
    scratch = lambda *shape: pltpu.VMEM(shape, jnp.bfloat16)

    def swap(value, bit):
        return lax.ppermute(value, "layer", [(s, s ^ bit) for s in range(layers)])

    def send(value, name, keep=lambda layer, row: True):
        pairs = []
        for l in range(layers):
            step = step_of(l // 2, name)
            pairs += [
                (l * ring + r, l * ring + (r - step) % ring) for r in range(ring) if keep(l, r)
            ]
        return lax.ppermute(value, ("layer", "row"), pairs)

    half_rows, slab = rows_dev // 2, (rows_dev, cols)
    cross_shape = (g.far * g.size, cols)
    device_arg = jnp.stack([layer_arg[0], lax.axis_index("row").astype(jnp.int32)])

    def put_after(value, *after):
        return call(pass_kernel, bf16(value.shape), [], 0, value, after=after)

    masked = call(functools.partial(mask_kernel, g), bf16(slab), [], 0, density, pattern)
    thin = send(masked, NEAR_THIN)
    other = swap(masked, 2)
    relayed = send(masked, FAR_WIDE, lambda layer, row: row % 2 != layer // 2)
    beside = swap(masked, 1)
    crossed = swap(thin, 2)
    wide = call(functools.partial(relay_kernel, g), bf16(slab), [], 1, device_arg, masked, relayed, after=(thin,))
    wide = lax.ppermute(wide, "row", [(r, r ^ 1) for r in range(ring)])
    far_wide = call(
        functools.partial(pack_far_kernel, g),
        bf16(message_shape(g, FAR_WIDE)), [scratch(half_rows, 2 * cols)],
        1, layer_arg, masked, beside, other,
    )
    far_wide = send(far_wide, FAR_WIDE)

    early, late, far = (g.inner_count(part) * g.size for part in ("early", "late", "far"))
    (high_a, wide_a), (high_b, wide_b) = (tuple(n * g.size for n in g.group(name)) for name in "AB")
    span = g.span * g.size
    f32 = functools.partial(jax.ShapeDtypeStruct, dtype=jnp.float32)
    keep = pltpu.VMEM((even_up(g.rows + 6), cols), jnp.float32)

    inner_early, sum_a, sum_b, late_a, late_b, far_b = call(
        functools.partial(early_kernel, g),
        [
            bf16((early, span)), f32((high_a, wide_a)), f32((high_b, wide_b)), bf16((high_a, late)),
            bf16((high_b, late)), bf16((high_b, far)),
        ],
        [
            scratch(rows_dev, layers * cols), scratch(high_a, early), scratch(high_b, early),
            scratch(rows_dev, 2 * cols),
        ],
        1, layer_arg, masked, beside, other, swap(other, 1), thin, swap(thin, 1),
    )
    crossed, wide = (put_after(value, sum_a) for value in (crossed, wide))
    far_wide, far_thin = call(
        functools.partial(pass_far_kernel, g),
        [bf16(far_wide.shape), bf16(message_shape(g, FAR_THIN))], [], 1, layer_arg, far_wide, after=(sum_a,),
    )
    far_thin = lax.ppermute(far_thin, "layer", [(1, 2), (2, 1)])
    pieces = sum(([value, swap(value, 1)] for value in (crossed, wide, far_wide)), [])
    square_a, inner_late = call(
        functools.partial(late_kernel, g),
        [bf16((high_a, cols)), bf16((late, span))],
        [scratch(rows_dev, 2 * cols), scratch(rows_dev, 2 * cols), scratch(cross_shape[0], 2 * cols), keep],
        1, layer_arg, pattern, *pieces, sum_a, late_a,
    )
    across_a, beside_a = swap(square_a, 2), swap(square_a, 1)
    square_b, inner_far = call(
        functools.partial(square_kernel, g),
        [bf16((high_b, cols)), bf16((far, span))],
        [keep],
        1, layer_arg, pattern, far_thin, sum_b, late_b, far_b, inner_late,
    )
    across_b, beside_b = swap(square_b, 2), swap(square_b, 1)
    partial = call(
        functools.partial(cubic_kernel, g),
        f32(slab),
        [scratch(rows_dev, 2 * cols), scratch(*slab), keep] + 2 * left_scratch(g, "own", (g.rows + 1) // 2),
        1, layer_arg, pattern, square_a, beside_a, square_b, beside_b, inner_early, inner_late,
    )
    done = call(
        functools.partial(other_kernel, g),
        f32((high_a, cols)), [scratch(high_a, 2 * cols), keep] + left_scratch(g, "A", g.group("A")[0]),
        1, layer_arg, pattern, across_a, swap(across_a, 1), inner_early, inner_far, partial,
    )
    across_b = put_after(across_b, done)
    return call(
        functools.partial(last_kernel, g),
        f32(slab), [scratch(high_b, 2 * cols), keep] + left_scratch(g, "B", g.group("B")[0]),
        1, layer_arg, pattern, across_b, swap(across_b, 1), inner_early, inner_far, partial, done,
    )


def solution(mesh):
    placed = (P("row", "layer"), P("row", "layer"))
    return jax.shard_map(
        body, mesh=mesh, in_specs=placed, out_specs=P("row", "layer"), check_vma=False
    )
```

time: 614 us -> 69.1 us (0.11)
  local copies, waits for them, and re-layouts: 260 us -> 1.78 us
  waiting for transfers between devices: 198 us -> 32 us
  matrix products: 70.5 us -> 0 us
  loops' own time: 55.6 us -> 0 us
  Pallas kernels: 0 us -> 15.9 us
  between operations: 13.5 us -> 0.19 us
  starting transfers between devices: 6.79 us -> 19 us
    ppermute x4 -> x19, waiting for transfers between devices: 146 us -> 32 us  [the longest x14 15 us: swap(): return lax.ppermute(value, 'layer', [(s, s ^ bit) for s in range(layers)])]
    gather x20 -> x0, local copies, waits for them, and re-layouts: 102 us -> none  [piece(): lax.dynamic_slice(padded, (start_row, 0, start_col, 0), (1, tile_size, sl...]
    dot_general x20 -> x0, matrix products: 70.5 us -> none  [row_product(): jnp.einsum('xay,ayoz->xoz', left_row, windows, preferred_element_type=jnp...]
    reshape x5 -> x0, local copies, waits for them, and re-layouts: 59 us -> none  [the longest x1 37.5 us: body(): margin.reshape(-1, tile_size, offsets, tile_size)]
    another operation x2 -> x0, loops' own time: 55.6 us -> none  [products(): lax.map(lambda row_idx: row_product(left_blocks[row_idx], offsets, first_...]
    all_gather x2 -> x0, waiting for transfers between devices: 52.3 us -> none  [the longest x1 28.4 us: body(): own_band = lax.all_gather(masked, 'layer', axis=1, tiled=True)]
    dynamic_slice x40 -> x0, local copies, waits for them, and re-layouts: 34.9 us -> none  [the longest x20 21.6 us: products(): left_blocks[row_idx]]
    unnamed x9 -> x6, local copies, waits for them, and re-layouts: 31.3 us -> 1.78 us
  transfers between devices with their start and end apart: 6 -> 19, of which waited for: 5 -> 7; matrix products, arithmetic and copies ran while one was open for 3% -> 0% of each run, Pallas kernels for 0% -> 18%
where the time goes in v2:
time: 69.1 us; the launch traced here: 68.9 us
  waiting for transfers between devices  32 us (46%)
  starting transfers between devices  19 us (27%)
  Pallas kernels  15.9 us (23%)
  local copies, waits for them, and re-layouts  1.78 us (3%)
    pallas_call x13, Pallas kernels, call(): pl.pallas_call(kernel, out_shape=out_shape, in_specs=specs, out_specs=jax...  15.9 us
    ppermute x14, waiting for transfers between devices, swap(): return lax.ppermute(value, 'layer', [(s, s ^ bit) for s in range(layers)])  15 us
    ppermute x3, waiting for transfers between devices, send(): return lax.ppermute(value, ('layer', 'row'), pairs)  13.2 us
    ppermute x14, starting transfers between devices, swap(): return lax.ppermute(value, 'layer', [(s, s ^ bit) for s in range(layers)])  8.74 us
    ppermute x3, starting transfers between devices, send(): return lax.ppermute(value, ('layer', 'row'), pairs)  6.81 us
    ppermute x1, waiting for transfers between devices, body(): wide = lax.ppermute(wide, 'row', [(r, r ^ 1) for r in range(ring)])  3.76 us
    ppermute x1, starting transfers between devices, body(): wide = lax.ppermute(wide, 'row', [(r, r ^ 1) for r in range(ring)])  2.81 us
    unnamed x6, local copies, waits for them, and re-layouts  1.78 us
  transfers between devices with their start and end apart: 19, of which 7 were waited for; matrix products, arithmetic and copies ran while one was open for 0% of the time, Pallas kernels for 18%

profile of v2, /device:TPU:0, one launch (start us, length us, event | category | flops | bytes accessed | tf_op | source)
XLA Modules:
  0.0 68.9 jit_solution(10628151196370581366)
XLA Ops:
  0.0 1.1 %copy-done = bf16[640,512]{1,0:T(8,128)(2,1)S(1)} copy-done((bf16[640,512]{1,0:T(8,128)(2,1)S(1)}, bf16[640,512]{1,0:T(8,128)(2,1)}, u32[]{:S(2)}) %copy-start) | copy-done | bytes 655384
  1.1 0.7 copy-done.1
  1.8 0.2 shard_map.28.own_ref.own
  2.0 6.1 %collective-permute-start.4 = (bf16[640,512]{1,0:T(8,128)(2,1)S(1)}, bf16[640,512]{1,0:T(8,128)(2,1)S(1)}, u32[]{:S(2)}, u32[]{:S(2)}) collective-permute-start(bf16[640,512]{1,0:T(8,128)(2,1)S(1)} %shard_map.28.own_ref.own), channel_id=1, source_target_pairs={{0,7},{1,0},{2,1},{3,2},{4,3},{5,4},{6,5},{7,6},{8,15},{9,8},{10,9... | collective-permute-start | bytes 1966088 | tf_op jit(solution)/shard_map/ppermute | solution.py:539
  8.1 0.0 collective-permute-start.1
  8.1 0.7 %collective-permute-start.9 = (bf16[640,512]{1,0:T(8,128)(2,1)S(1)}, bf16[640,512]{1,0:T(8,128)(2,1)S(1)}, u32[]{:S(2)}, u32[]{:S(2)}) collective-permute-start(bf16[640,512]{1,0:T(8,128)(2,1)S(1)} %shard_map.28.own_ref.own), channel_id=1, source_target_pairs={{1,3},{3,5},{5,7},{7,1},{9,11},{11,13},{13,15},{15,9},{16,22},{18,... | collective-permute-start | bytes 1966088 | tf_op jit(solution)/shard_map/ppermute | solution.py:539
  8.8 0.1 collective-permute-start
  8.9 13.2 %collective-permute-done.4.refs_2_.after_ref = bf16[640,512]{1,0:T(8,128)(2,1)S(1)} collective-permute-done((bf16[640,512]{1,0:T(8,128)(2,1)S(1)}, bf16[640,512]{1,0:T(8,128)(2,1)S(1)}, u32[]{:S(2)}, u32[]{:S(2)}) %collective-permute-start.4) | collective-permute-done | bytes 655392 | tf_op jit(solution)/shard_map/ppermute | solution.py:539
  22.1 2.2 %collective-permute-start.7 = (bf16[640,512]{1,0:T(8,128)(2,1)S(1)}, bf16[640,512]{1,0:T(8,128)(2,1)S(1)}, u32[]{:S(2)}, u32[]{:S(2)}) collective-permute-start(bf16[640,512]{1,0:T(8,128)(2,1)S(1)} %collective-permute-done.4.refs_2_.after_ref), channel_id=1, source_target_pairs={{0,16},{8,24},{16,0},{24,8},{1,17},{9,25},{17,1},{25,9},{2,18},{10... | collective-permute-start | bytes 1966088 | tf_op jit(solution)/shard_map/ppermute | solution.py:530
  24.3 0.0 collective-permute-start.5
  24.3 0.0 collective-permute-done.1.other_ref.refs_0_
  24.3 0.5 collective-permute-start.3
  24.8 0.1 pad_add_fusion.device_ref
  24.9 0.0 collective-permute-done.9.relayed_ref
  24.9 0.6 shard_map.33
  25.5 2.8 %collective-permute-start.10 = (bf16[640,512]{1,0:T(8,128)(2,1)S(1)}, bf16[640,512]{1,0:T(8,128)(2,1)S(1)}, u32[]{:S(2)}, u32[]{:S(2)}) collective-permute-start(bf16[640,512]{1,0:T(8,128)(2,1)S(1)} %shard_map.33), channel_id=1, source_target_pairs={{0,1},{1,0},{2,3},{3,2},{4,5},{5,4},{6,7},{7,6},{8,9},{9,8},{10,11... | collective-permute-start | bytes 1966088 | tf_op jit(solution)/shard_map/ppermute | solution.py:555
  28.3 0.0 collective-permute-done.beside_ref.beside
  28.3 0.1 shard_map.29
  28.4 0.1 collective-permute-start.2
  28.5 0.0 collective-permute-done.5.refs_3_
  28.5 0.0 collective-permute-done.3.refs_1_
  28.5 3.1 %shard_map.30 = (bf16[1280,1664]{1,0:T(8,128)(2,1)S(1)}, f32[256,768]{1,0:T(8,128)S(1)}, f32[384,896]{1,0:T(8,128)S(1)}, bf16[256,1024]{1,0:T(8,128)(2,1)S(1)}, ...) custom-call(s32[1]{0:T(128)} %bitcast.layer_ref, bf16[640,512]{1,0:T(8,128)(2,1)S(1)} %shard_map.28.own_ref.own, ...), custom_call_target="tpu_custom_call" | custom-call | tf_op jit(solution)/shard_map/pallas_call | solution.py:509
  31.6 6.7 %collective-permute-done.7.in_ref = bf16[640,512]{1,0:T(8,128)(2,1)S(1)} collective-permute-done((bf16[640,512]{1,0:T(8,128)(2,1)S(1)}, bf16[640,512]{1,0:T(8,128)(2,1)S(1)}, u32[]{:S(2)}, u32[]{:S(2)}) %collective-permute-start.7) | collective-permute-done | bytes 655392 | tf_op jit(solution)/shard_map/ppermute | solution.py:530
  38.4 0.0 copy-start.2
  38.4 0.1 collective-permute-start.8
  38.4 3.8 %collective-permute-done.10.in_ref = bf16[640,512]{1,0:T(8,128)(2,1)S(1)} collective-permute-done((bf16[640,512]{1,0:T(8,128)(2,1)S(1)}, bf16[640,512]{1,0:T(8,128)(2,1)S(1)}, u32[]{:S(2)}, u32[]{:S(2)}) %collective-permute-start.10) | collective-permute-done | bytes 655392 | tf_op jit(solution)/shard_map/ppermute | solution.py:555
  42.2 0.1 collective-permute-start.11
  42.3 0.1 shard_map.31
  42.4 0.5 collective-permute-start.12
  43.0 0.7 collective-permute-start.6
  43.6 1.5 %collective-permute-done.12.refs_5_ = bf16[480,512]{1,0:T(8,128)(2,1)S(1)} collective-permute-done((bf16[480,512]{1,0:T(8,128)(2,1)S(1)}, bf16[480,512]{1,0:T(8,128)(2,1)S(1)}, u32[]{:S(2)}, u32[]{:S(2)}) %collective-permute-start.12) | collective-permute-done | bytes 491552 | tf_op jit(solution)/shard_map/ppermute | solution.py:530
  45.1 0.0 collective-permute-done.8.refs_1_
  45.1 0.0 collective-permute-done.11.refs_3_
  45.1 1.5 %shard_map.35 = (bf16[256,512]{1,0:T(8,128)(2,1)S(1)}, bf16[1024,1664]{1,0:T(8,128)(2,1)S(1)}) custom-call(s32[1]{0:T(128)} %bitcast.layer_ref, s32[8,10]{1,0:T(8,128)S(1)} %bitcast.4, bf16[640,512]{1,0:T(8,128)(2,1)S(1)} %shard_map.32.refs_0_, bf16[640,512]{1,0:T(8,128)(2,1)S(1)} %collective-permute-done.8.refs_1_, bf16[640,512]{1,0:T(8,128)(2,1)S(1)} %shard_map.34.refs_2_, ...), custom_call_target="tpu_custom_call" | custom-call | tf_op jit(solution)/shard_map/pallas_call | solution.py:509
  46.7 1.5 %collective-permute-start.14 = (bf16[256,512]{1,0:T(8,128)(2,1)S(1)}, bf16[256,512]{1,0:T(8,128)(2,1)S(1)}, u32[]{:S(2)}, u32[]{:S(2)}) collective-permute-start(bf16[256,512]{1,0:T(8,128)(2,1)S(1)} %get-tuple-element.26.refs_0_), channel_id=1, source_target_pairs={{0,16},{8,24},{16,0},{24,8},{1,17},{9,25},{17,1},{25,9},{2,18},{10... | collective-permute-start | bytes 786440 | tf_op jit(solution)/shard_map/ppermute | solution.py:530
  48.1 0.0 collective-permute-done.6.far
  48.1 1.6 %shard_map.36 = (bf16[384,512]{1,0:T(8,128)(2,1)S(1)}, bf16[384,1664]{1,0:T(8,128)(2,1)S(1)}) custom-call(s32[1]{0:T(128)} %bitcast.layer_ref, s32[8,10]{1,0:T(8,128)S(1)} %bitcast.5, bf16[192,384]{1,0:T(8,128)(2,1)S(1)} %collective-permute-done.6.far, f32[384,896]{1,0:T(8,128)S(1)} %get-tuple-element.19.total, ...), custom_call_target="tpu_custom_call" | custom-call | tf_op jit(solution)/shard_map/pallas_call | solution.py:509
  49.7 1.4 %collective-permute-start.17 = (bf16[384,512]{1,0:T(8,128)(2,1)S(1)}, bf16[384,512]{1,0:T(8,128)(2,1)S(1)}, u32[]{:S(2)}, u32[]{:S(2)}) collective-permute-start(bf16[384,512]{1,0:T(8,128)(2,1)S(1)} %get-tuple-element.25.refs_2_), channel_id=1, source_target_pairs={{0,8},{8,0},{16,24},{24,16},{1,9},{9,1},{17,25},{25,17},{2,10},{10... | collective-permute-start | bytes 1179656 | tf_op jit(solution)/shard_map/ppermute | solution.py:530
  51.1 1.4 %collective-permute-start.13 = (bf16[384,512]{1,0:T(8,128)(2,1)S(1)}, bf16[384,512]{1,0:T(8,128)(2,1)S(1)}, u32[]{:S(2)}, u32[]{:S(2)}) collective-permute-start(bf16[384,512]{1,0:T(8,128)(2,1)S(1)} %get-tuple-element.25.refs_2_), channel_id=1, source_target_pairs={{0,16},{8,24},{16,0},{24,8},{1,17},{9,25},{17,1},{25,9},{2,18},{10... | collective-permute-start | bytes 1179656 | tf_op jit(solution)/shard_map/ppermute | solution.py:530
  52.5 0.2 collective-permute-start.16
  52.7 3.0 %collective-permute-done.14.refs_0_ = bf16[256,512]{1,0:T(8,128)(2,1)S(1)} collective-permute-done((bf16[256,512]{1,0:T(8,128)(2,1)S(1)}, bf16[256,512]{1,0:T(8,128)(2,1)S(1)}, u32[]{:S(2)}, u32[]{:S(2)}) %collective-permute-start.14) | collective-permute-done | bytes 262176 | tf_op jit(solution)/shard_map/ppermute | solution.py:530
  55.6 0.7 collective-permute-start.15
  56.3 4.3 %shard_map.37.refs_4_ = f32[640,512]{1,0:T(8,128)S(1)} custom-call(s32[1]{0:T(128)} %bitcast.layer_ref, s32[8,10]{1,0:T(8,128)S(1)} %bitcast.6, bf16[256,512]{1,0:T(8,128)(2,1)S(1)} %get-tuple-element.26.refs_0_, bf16[256,512]{1,0:T(8,128)(2,1)S(1)} %collective-permute-done.16.refs_1_, bf16[384,512]{1,0:T(8,128)(2,1)S(1)} %get-tuple-element.25.refs_2_, ...), custom_call_target="tpu_custom_call" | custom-call | tf_op jit(solution)/shard_map/pallas_call | solution.py:509
  60.7 1.2 %shard_map.38.refs_0_.refs_5_ = f32[256,512]{1,0:T(8,128)S(1)} custom-call(s32[1]{0:T(128)} %bitcast.layer_ref, s32[8,10]{1,0:T(8,128)S(1)} %bitcast.7, bf16[256,512]{1,0:T(8,128)(2,1)S(1)} %collective-permute-done.14.refs_0_, bf16[256,512]{1,0:T(8,128)(2,1)S(1)} %collective-permute-done.15.refs_1_, ...), custom_call_target="tpu_custom_call" | custom-call | tf_op jit(solution)/shard_map/pallas_call | solution.py:509
  61.8 2.2 %collective-permute-done.13.in_ref = bf16[384,512]{1,0:T(8,128)(2,1)S(1)} collective-permute-done((bf16[384,512]{1,0:T(8,128)(2,1)S(1)}, bf16[384,512]{1,0:T(8,128)(2,1)S(1)}, u32[]{:S(2)}, u32[]{:S(2)}) %collective-permute-start.13) | collective-permute-done | bytes 393248 | tf_op jit(solution)/shard_map/ppermute | solution.py:530
  64.1 0.2 collective-permute-start.18
  64.3 1.6 %collective-permute-done.18.refs_1_ = bf16[384,512]{1,0:T(8,128)(2,1)S(1)} collective-permute-done((bf16[384,512]{1,0:T(8,128)(2,1)S(1)}, bf16[384,512]{1,0:T(8,128)(2,1)S(1)}, u32[]{:S(2)}, u32[]{:S(2)}) %collective-permute-start.18) | collective-permute-done | bytes 393248 | tf_op jit(solution)/shard_map/ppermute | solution.py:530
  65.9 3.0 %shard_map.40 = f32[640,512]{1,0:T(8,128)} custom-call(s32[1]{0:T(128)} %bitcast.layer_ref, s32[8,10]{1,0:T(8,128)S(1)} %bitcast.8, bf16[384,512]{1,0:T(8,128)(2,1)S(1)} %shard_map.39.refs_0_, bf16[384,512]{1,0:T(8,128)(2,1)S(1)} %collective-permute-done.18.refs_1_, bf16[1280,1664]{1,0:T(8,128)(2,1)S(1)} %get-tuple-element.27.refs_4_.refs_2_, ...), custom_call_target="tpu_custom_call" | custom-call | tf_op jit(solution)/shard_map/pallas_call | solution.py:509
  (10 shorter events, 0.1 us)
Async XLA Ops:
  0.0 1.1 %copy-start = (bf16[640,512]{1,0:T(8,128)(2,1)S(1)}, bf16[640,512]{1,0:T(8,128)(2,1)}, u32[]{:S(2)}) copy-start(bf16[640,512]{1,0:T(8,128)(2,1)} %density_ref.1) | copy-start | bytes 1966084
  1.1 0.7 copy-start.1
  2.0 20.0 %collective-permute-start.4 = (bf16[640,512]{1,0:T(8,128)(2,1)S(1)}, bf16[640,512]{1,0:T(8,128)(2,1)S(1)}, u32[]{:S(2)}, u32[]{:S(2)}) collective-permute-start(bf16[640,512]{1,0:T(8,128)(2,1)S(1)} %shard_map.28.own_ref.own), channel_id=1, source_target_pairs={{0,7},{1,0},{2,1},{3,2},{4,3},{5,4},{6,5},{7,6},{8,15},{9,8},{10,9... | collective-permute-start | bytes 1966088 | tf_op jit(solution)/shard_map/ppermute | solution.py:539
  8.1 16.2 %collective-permute-start.1 = (bf16[640,512]{1,0:T(8,128)(2,1)S(1)}, bf16[640,512]{1,0:T(8,128)(2,1)S(1)}, u32[]{:S(2)}, u32[]{:S(2)}) collective-permute-start(bf16[640,512]{1,0:T(8,128)(2,1)S(1)} %shard_map.28.own_ref.own), channel_id=1, source_target_pairs={{0,16},{8,24},{16,0},{24,8},{1,17},{9,25},{17,1},{25,9},{2,18},{10... | collective-permute-start | bytes 1966088 | tf_op jit(solution)/shard_map/ppermute | solution.py:530
  8.1 16.8 %collective-permute-start.9 = (bf16[640,512]{1,0:T(8,128)(2,1)S(1)}, bf16[640,512]{1,0:T(8,128)(2,1)S(1)}, u32[]{:S(2)}, u32[]{:S(2)}) collective-permute-start(bf16[640,512]{1,0:T(8,128)(2,1)S(1)} %shard_map.28.own_ref.own), channel_id=1, source_target_pairs={{1,3},{3,5},{5,7},{7,1},{9,11},{11,13},{13,15},{15,9},{16,22},{18,... | collective-permute-start | bytes 1966088 | tf_op jit(solution)/shard_map/ppermute | solution.py:539
  8.8 19.5 %collective-permute-start = (bf16[640,512]{1,0:T(8,128)(2,1)S(1)}, bf16[640,512]{1,0:T(8,128)(2,1)S(1)}, u32[]{:S(2)}, u32[]{:S(2)}) collective-permute-start(bf16[640,512]{1,0:T(8,128)(2,1)S(1)} %shard_map.28.own_ref.own), channel_id=1, source_target_pairs={{0,8},{8,0},{16,24},{24,16},{1,9},{9,1},{17,25},{25,17},{2,10},{10... | collective-permute-start | bytes 1966088 | tf_op jit(solution)/shard_map/ppermute | solution.py:530
  22.1 16.2 %collective-permute-start.7 = (bf16[640,512]{1,0:T(8,128)(2,1)S(1)}, bf16[640,512]{1,0:T(8,128)(2,1)S(1)}, u32[]{:S(2)}, u32[]{:S(2)}) collective-permute-start(bf16[640,512]{1,0:T(8,128)(2,1)S(1)} %collective-permute-done.4.refs_2_.after_ref), channel_id=1, source_target_pairs={{0,16},{8,24},{16,0},{24,8},{1,17},{9,25},{17,1},{25,9},{2,18},{10... | collective-permute-start | bytes 1966088 | tf_op jit(solution)/shard_map/ppermute | solution.py:530
  24.3 4.2 %collective-permute-start.5 = (bf16[640,512]{1,0:T(8,128)(2,1)S(1)}, bf16[640,512]{1,0:T(8,128)(2,1)S(1)}, u32[]{:S(2)}, u32[]{:S(2)}) collective-permute-start(bf16[640,512]{1,0:T(8,128)(2,1)S(1)} %collective-permute-done.4.refs_2_.after_ref), channel_id=1, source_target_pairs={{0,8},{8,0},{16,24},{24,16},{1,9},{9,1},{17,25},{25,17},{2,10},{10... | collective-permute-start | bytes 1966088 | tf_op jit(solution)/shard_map/ppermute | solution.py:530
  24.3 4.2 %collective-permute-start.3 = (bf16[640,512]{1,0:T(8,128)(2,1)S(1)}, bf16[640,512]{1,0:T(8,128)(2,1)S(1)}, u32[]{:S(2)}, u32[]{:S(2)}) collective-permute-start(bf16[640,512]{1,0:T(8,128)(2,1)S(1)} %collective-permute-done.1.other_ref.refs_0_), channel_id=1, source_target_pairs={{0,8},{8,0},{16,24},{24,16},{1,9},{9,1},{17,25},{25,17},{2,10},{10... | collective-permute-start | bytes 1966088 | tf_op jit(solution)/shard_map/ppermute | solution.py:530
  25.5 16.7 %collective-permute-start.10 = (bf16[640,512]{1,0:T(8,128)(2,1)S(1)}, bf16[640,512]{1,0:T(8,128)(2,1)S(1)}, u32[]{:S(2)}, u32[]{:S(2)}) collective-permute-start(bf16[640,512]{1,0:T(8,128)(2,1)S(1)} %shard_map.33), channel_id=1, source_target_pairs={{0,1},{1,0},{2,3},{3,2},{4,5},{5,4},{6,7},{7,6},{8,9},{9,8},{10,11... | collective-permute-start | bytes 1966088 | tf_op jit(solution)/shard_map/ppermute | solution.py:555
  28.4 13.9 %collective-permute-start.2 = (bf16[480,512]{1,0:T(8,128)(2,1)S(1)}, bf16[480,512]{1,0:T(8,128)(2,1)S(1)}, u32[]{:S(2)}, u32[]{:S(2)}) collective-permute-start(bf16[480,512]{1,0:T(8,128)(2,1)S(1)} %shard_map.29), channel_id=1, source_target_pairs={{0,2},{1,3},{2,4},{3,5},{4,6},{5,7},{6,0},{7,1},{8,10},{9,11},{10,... | collective-permute-start | bytes 1474568 | tf_op jit(solution)/shard_map/ppermute | solution.py:539
  38.4 6.8 %copy-start.2 = (s32[10,8]{0,1:T(8,128)S(1)}, s32[10,8]{0,1:T(8,128)}, u32[]{:S(2)}) copy-start(s32[10,8]{0,1:T(8,128)} %param.3) | copy-start | bytes 964
  38.4 6.8 %collective-permute-start.8 = (bf16[640,512]{1,0:T(8,128)(2,1)S(1)}, bf16[640,512]{1,0:T(8,128)(2,1)S(1)}, u32[]{:S(2)}, u32[]{:S(2)}) collective-permute-start(bf16[640,512]{1,0:T(8,128)(2,1)S(1)} %shard_map.32.refs_0_), channel_id=1, source_target_pairs={{0,8},{8,0},{16,24},{24,16},{1,9},{9,1},{17,25},{25,17},{2,10},{10... | collective-permute-start | bytes 1966088 | tf_op jit(solution)/shard_map/ppermute | solution.py:530
  42.2 2.9 %collective-permute-start.11 = (bf16[640,512]{1,0:T(8,128)(2,1)S(1)}, bf16[640,512]{1,0:T(8,128)(2,1)S(1)}, u32[]{:S(2)}, u32[]{:S(2)}) collective-permute-start(bf16[640,512]{1,0:T(8,128)(2,1)S(1)} %shard_map.34.refs_2_), channel_id=1, source_target_pairs={{0,8},{8,0},{16,24},{24,16},{1,9},{9,1},{17,25},{25,17},{2,10},{10... | collective-permute-start | bytes 1966088 | tf_op jit(solution)/shard_map/ppermute | solution.py:530
  42.4 2.7 %collective-permute-start.12 = (bf16[480,512]{1,0:T(8,128)(2,1)S(1)}, bf16[480,512]{1,0:T(8,128)(2,1)S(1)}, u32[]{:S(2)}, u32[]{:S(2)}) collective-permute-start(bf16[480,512]{1,0:T(8,128)(2,1)S(1)} %get-tuple-element.22.refs_4_), channel_id=1, source_target_pairs={{0,8},{8,0},{16,24},{24,16},{1,9},{9,1},{17,25},{25,17},{2,10},{10... | collective-permute-start | bytes 1474568 | tf_op jit(solution)/shard_map/ppermute | solution.py:530
  43.0 5.2 %collective-permute-start.6 = (bf16[192,384]{1,0:T(8,128)(2,1)S(1)}, bf16[192,384]{1,0:T(8,128)(2,1)S(1)}, u32[]{:S(2)}, u32[]{:S(2)}) collective-permute-start(bf16[192,384]{1,0:T(8,128)(2,1)S(1)} %get-tuple-element.18), channel_id=1, source_target_pairs={{8,16},{16,8},{9,17},{17,9},{10,18},{18,10},{11,19},{19,11},{12,20... | collective-permute-start | bytes 442376 | tf_op jit(solution)/shard_map/ppermute | solution.py:586
  46.7 9.0 %collective-permute-start.14 = (bf16[256,512]{1,0:T(8,128)(2,1)S(1)}, bf16[256,512]{1,0:T(8,128)(2,1)S(1)}, u32[]{:S(2)}, u32[]{:S(2)}) collective-permute-start(bf16[256,512]{1,0:T(8,128)(2,1)S(1)} %get-tuple-element.26.refs_0_), channel_id=1, source_target_pairs={{0,16},{8,24},{16,0},{24,8},{1,17},{9,25},{17,1},{25,9},{2,18},{10... | collective-permute-start | bytes 786440 | tf_op jit(solution)/shard_map/ppermute | solution.py:530
  49.7 6.5 %collective-permute-start.17 = (bf16[384,512]{1,0:T(8,128)(2,1)S(1)}, bf16[384,512]{1,0:T(8,128)(2,1)S(1)}, u32[]{:S(2)}, u32[]{:S(2)}) collective-permute-start(bf16[384,512]{1,0:T(8,128)(2,1)S(1)} %get-tuple-element.25.refs_2_), channel_id=1, source_target_pairs={{0,8},{8,0},{16,24},{24,16},{1,9},{9,1},{17,25},{25,17},{2,10},{10... | collective-permute-start | bytes 1179656 | tf_op jit(solution)/shard_map/ppermute | solution.py:530
  51.1 13.0 %collective-permute-start.13 = (bf16[384,512]{1,0:T(8,128)(2,1)S(1)}, bf16[384,512]{1,0:T(8,128)(2,1)S(1)}, u32[]{:S(2)}, u32[]{:S(2)}) collective-permute-start(bf16[384,512]{1,0:T(8,128)(2,1)S(1)} %get-tuple-element.25.refs_2_), channel_id=1, source_target_pairs={{0,16},{8,24},{16,0},{24,8},{1,17},{9,25},{17,1},{25,9},{2,18},{10... | collective-permute-start | bytes 1179656 | tf_op jit(solution)/shard_map/ppermute | solution.py:530
  52.5 3.8 %collective-permute-start.16 = (bf16[256,512]{1,0:T(8,128)(2,1)S(1)}, bf16[256,512]{1,0:T(8,128)(2,1)S(1)}, u32[]{:S(2)}, u32[]{:S(2)}) collective-permute-start(bf16[256,512]{1,0:T(8,128)(2,1)S(1)} %get-tuple-element.26.refs_0_), channel_id=1, source_target_pairs={{0,8},{8,0},{16,24},{24,16},{1,9},{9,1},{17,25},{25,17},{2,10},{10... | collective-permute-start | bytes 786440 | tf_op jit(solution)/shard_map/ppermute | solution.py:530
  55.6 5.0 %collective-permute-start.15 = (bf16[256,512]{1,0:T(8,128)(2,1)S(1)}, bf16[256,512]{1,0:T(8,128)(2,1)S(1)}, u32[]{:S(2)}, u32[]{:S(2)}) collective-permute-start(bf16[256,512]{1,0:T(8,128)(2,1)S(1)} %collective-permute-done.14.refs_0_), channel_id=1, source_target_pairs={{0,8},{8,0},{16,24},{24,16},{1,9},{9,1},{17,25},{25,17},{2,10},{10... | collective-permute-start | bytes 786440 | tf_op jit(solution)/shard_map/ppermute | solution.py:530
  64.1 1.8 %collective-permute-start.18 = (bf16[384,512]{1,0:T(8,128)(2,1)S(1)}, bf16[384,512]{1,0:T(8,128)(2,1)S(1)}, u32[]{:S(2)}, u32[]{:S(2)}) collective-permute-start(bf16[384,512]{1,0:T(8,128)(2,1)S(1)} %shard_map.39.refs_0_), channel_id=1, source_target_pairs={{0,8},{8,0},{16,24},{24,16},{1,9},{9,1},{17,25},{25,17},{2,10},{10... | collective-permute-start | bytes 1179656 | tf_op jit(solution)/shard_map/ppermute | solution.py:530

commit v3 on v2

--- a/solution.py
+++ b/solution.py
@@ -8,6 +8,7 @@
 from jax.sharding import PartitionSpec as P
 
 VMEM = pl.BlockSpec(memory_space=pltpu.VMEM)
+HBM = pl.BlockSpec(memory_space=pltpu.HBM)
 LIMIT = 12 * 1024 * 1024
 
 
@@ -105,15 +106,20 @@
     return (2 * rows, cols) if name == FAR_THIN else (rows, cols)
 
 
-def expand_pattern(pattern_ref, slab_cols, size):
-    offsets = pattern_ref.shape[0]
-    block = lax.broadcasted_iota(jnp.int32, (offsets, slab_cols), 1) // size
-    row = lax.broadcasted_iota(jnp.int32, (offsets, slab_cols), 0)
+def layer_index():
+    return lax.axis_index("layer").astype(jnp.int32)
+
+
+def keep_kernel(g, pattern_ref, keep):
+    offsets, cols = pattern_ref.shape[0], keep.shape[1]
+    block = lax.broadcasted_iota(jnp.int32, (offsets, cols), 1) // g.size
+    row = lax.broadcasted_iota(jnp.int32, (offsets, cols), 0)
     spread = jnp.where(block == row, 1.0, 0.0).astype(jnp.float32)
-    return lax.dot_general(
+    keep[: g.rows, :] = lax.dot_general(
         pattern_ref[...].astype(jnp.float32), spread, (((0,), (0,)), ((), ())),
         preferred_element_type=jnp.float32,
     )
+    keep[g.rows :, :] = jnp.zeros((keep.shape[0] - g.rows, cols), keep.dtype)
 
 
 def cross_rows(g, side):
@@ -122,8 +128,7 @@
     return min(rows[0], g.rows - count), count
 
 
-def mask_kernel(g, density_ref, pattern_ref, out_ref):
-    keep = expand_pattern(pattern_ref, density_ref.shape[1], g.size)
+def mask_kernel(g, density_ref, keep, out_ref):
     for t in range(g.rows):
         rows = slice(t * g.size, (t + 1) * g.size)
         out_ref[rows, :] = density_ref[rows, :] * keep[t : t + 1, :].astype(jnp.bfloat16)
@@ -176,32 +181,37 @@
             near[t * half : (t + 1) * half, pl.ds(start, cols)] = slab[pl.ds(src, half), :]
 
 
-def pack_far_kernel(g, layer_ref, own_ref, beside_ref, other_ref, message, near):
-    side, core = layer_ref[0] // 2, layer_ref[0] % 2
+def pack_kernel(g, own_ref, beside_ref, wide, far, near):
+    side, core = layer_index() // 2, layer_index() % 2
     half = g.size // 2
     fill_near(g, core, (own_ref, beside_ref), near)
 
     def fill(side):
-        pack(g, side, FAR_WIDE, near, lambda row: row * half, side * g.pair, half, message)
-        first, count = cross_rows(g, side)
-        message[message.shape[0] - count * g.size :, :] = other_ref[first * g.size : (first + count) * g.size, :]
+        for name, out in ((NEAR_WIDE, wide), (FAR_WIDE, far)):
+            pack(g, side, name, near, lambda row: row * half, side * g.pair, half, out)
 
     for value in (0, 1):
         pl.when(side == value)(functools.partial(fill, value))
 
 
-def relay_kernel(g, device_ref, own_ref, relayed_ref, after_ref, out_ref):
-    side, row = device_ref[0] // 2, device_ref[1]
+def relay_kernel(g, own_ref, relayed_ref, far_ref, other_ref, after_ref, out_ref, message):
+    side, row = layer_index() // 2, lax.axis_index("row")
     pick((row % 2) == side, own_ref, relayed_ref, out_ref)
+    message[: far_ref.shape[0], :] = far_ref[...]
+
+    def fill(side):
+        first, count = cross_rows(g, side)
+        message[far_ref.shape[0] :, :] = other_ref[first * g.size : (first + count) * g.size, :]
+
+    for value in (0, 1):
+        pl.when(side == value)(functools.partial(fill, value))
 
 
 def pass_kernel(in_ref, *refs):
     refs[-1][...] = in_ref[...]
 
 
-def pass_far_kernel(g, layer_ref, in_ref, after_ref, out_ref, message):
-    out_ref[...] = in_ref[...]
-
+def pass_far_kernel(g, in_ref, message):
     def fill(side):
         first, count = cross_rows(g, side)
         start = in_ref.shape[0] - (count + first) * g.size
@@ -209,7 +219,7 @@
         pack(g, 1 - side, FAR_THIN, in_ref, lambda row: start + row * g.size, lead, g.size, message)
 
     for value in (0, 1):
-        pl.when(layer_ref[0] // 2 == value)(functools.partial(fill, value))
+        pl.when(layer_index() // 2 == value)(functools.partial(fill, value))
 
 
 def fill_pair(g, core, slabs, pair):
@@ -299,10 +309,10 @@
     return range(first, first + g.group(name)[0])
 
 
-def early_kernel(g, layer_ref, own, beside, *refs):
+def early_kernel(g, own, beside, *refs):
     others, thins = refs[:2], refs[2:4]
-    inner, sum_a, sum_b, late_a, late_b, far_b, band, left_a, left_b, pair = refs[4:]
-    layer = layer_ref[0]
+    inner, sum_a, left_b, late_a, late_b, far_b, band, left_a, pair = refs[4:]
+    layer = layer_index()
     side, core = layer // 2, layer % 2
     cols = g.slab * g.size
     for q, slab in enumerate((own, beside, *others)):
@@ -327,28 +337,24 @@
 
     for value in (0, 1):
         pl.when(side == value)(functools.partial(gather, value))
-    for name, left, out in (("A", left_a, sum_a), ("B", left_b, sum_b)):
-        col, (_, cols) = group_first(g, side, name), g.group(name)
-        out[...] = dot(left[...], window_of(g, core, inner, col, cols))
-
-
-def square_of(g, name, side, core, pattern_ref, total, lefts, inners, keep):
-    keep[: g.rows, :] = expand_pattern(pattern_ref, keep.shape[1], g.size)
+    col, (_, cols) = group_first(g, side, "A"), g.group("A")
+    sum_a[...] = dot(left_a[...], window_of(g, core, inner, col, cols))
+
+
+def square_of(g, name, side, core, keep, lefts, inners, product=0.0):
     first, (_, cols) = group_first(g, side, name), g.group(name)
-    product = total[...]
     for left, inner in zip(lefts, inners):
-        product += dot(left[...], window_of(g, core, inner, first, cols))
+        product = product + dot(left[...], window_of(g, core, inner, first, cols))
     return lambda n: (own_columns(g, product, n) * keep[pl.ds(first + n, 1), :]).astype(jnp.bfloat16)
 
 
-def late_kernel(g, layer_ref, pattern_ref, *refs):
+def late_kernel(g, keep, *refs):
     crossed, wides, wide_fars = (refs[2 * n : 2 * n + 2] for n in range(3))
-    total, left, square, inner, pair, own_pair, far_pair, keep = refs[6:]
-    layer = layer_ref[0]
+    total, left, square, inner, pair, far_pair = refs[6:]
+    layer = layer_index()
     side, core = layer // 2, layer % 2
     half = g.size // 2
     fill_pair(g, core, crossed, pair)
-    fill_pair(g, core, wides, own_pair)
     tail = far_pair.shape[0]
     fill_pair(g, core, [piece.at[piece.shape[0] - tail :, :] for piece in wide_fars], far_pair)
 
@@ -357,29 +363,29 @@
         for k, t in enumerate(g.inner_rows(side, "late")):
             if t is None:
                 inner[k * g.size : (k + 1) * g.size, :] = jnp.zeros((g.size, inner.shape[1]), inner.dtype)
-            elif t in near:
-                row = (t - near[0]) * g.size
-                parts = [pair_part(g, value, own_pair if value == side else pair, row, g.size) for value in (0, 1)]
-                place_parts(g, inner, k * g.size, g.size, t, side, parts)
+                continue
+            if t in near:
+                name, pieces, source, row = NEAR_WIDE, wides, pair, t - near[0]
             else:
-                row = (t - step_of(side, FAR_WIDE) * g.rows - cross_rows(g, side)[0]) * g.size
-                for q, piece in enumerate(wide_fars):
-                    at = half * (core ^ q)
-                    parts = message_part(g, side, FAR_WIDE, t, piece, half)
-                    parts.append(pair_part(g, 1 - side, far_pair, pl.multiple_of(row + at, half), half))
-                    parts.sort(key=lambda part: part[0])
-                    place_parts(g, inner, pl.multiple_of(k * g.size + at, half), half, t, side, parts)
+                name, pieces, source = FAR_WIDE, wide_fars, far_pair
+                row = t - step_of(side, FAR_WIDE) * g.rows - cross_rows(g, side)[0]
+            for q, piece in enumerate(pieces):
+                at = half * (core ^ q)
+                parts = message_part(g, side, name, t, piece, half)
+                parts.append(pair_part(g, 1 - side, source, pl.multiple_of(row * g.size + at, half), half))
+                parts.sort(key=lambda part: part[0])
+                place_parts(g, inner, pl.multiple_of(k * g.size + at, half), half, t, side, parts)
 
     for value in (0, 1):
         pl.when(side == value)(functools.partial(gather, value))
-    row_of = square_of(g, "A", side, core, pattern_ref, total, [left], [inner], keep)
+    row_of = square_of(g, "A", side, core, keep, [left], [inner], total[...])
     for n in range(g.group("A")[0]):
         square[n * g.size : (n + 1) * g.size, :] = row_of(n)
 
 
-def square_kernel(g, layer_ref, pattern_ref, far, total, left, far_left, late, *refs):
-    square, inner, keep = refs
-    side, core = layer_ref[0] // 2, layer_ref[0] % 2
+def square_kernel(g, keep, far, early_left, left, far_left, early, late, *refs):
+    square, inner = refs
+    side, core = layer_index() // 2, layer_index() % 2
 
     def gather(side):
         for k, t in enumerate(g.inner_rows(side, "far")):
@@ -388,7 +394,7 @@
 
     for value in (0, 1):
         pl.when(side == value)(functools.partial(gather, value))
-    row_of = square_of(g, "B", side, core, pattern_ref, total, [left, far_left], [late, inner], keep)
+    row_of = square_of(g, "B", side, core, keep, [early_left, left, far_left], [early, late, inner])
     for n in range(g.group("B")[0]):
         square[n * g.size : (n + 1) * g.size, :] = row_of(n)
 
@@ -414,29 +420,51 @@
     return [min(lo, total - count) for lo, _ in spans], count
 
 
+def far_span(g, part):
+    spans = []
+    for side in (0, 1):
+        rows = group_rows(g, 1 - side, part)
+        lo = rows[0] - g.reach_low + g.pair * (1 - side)
+        hi = rows[-1] - g.reach_low + g.pair * (2 - side)
+        met = [k for k, t in enumerate(g.inner_rows(side, "far")) if t is not None and lo <= t < hi]
+        spans.append((even_down(met[0]), met[-1] + 1) if met else (0, 0))
+    count = even_up(max(hi - lo for lo, hi in spans))
+    return [min(lo, g.inner_count("far") - count) for lo, _ in spans], count
+
+
 def cubic_left(g, side, part, rows, band, band_first, lefts):
     pair = side if part == "own" else 1 - side
     starts, count = early_span(g, part)
-    early = g.inner_rows(side, "early")[starts[side] : starts[side] + count]
-    rest = g.inner_rows(side, "late" if part == "own" else "far")
-    for dst, inner_rows in zip(lefts, (early, rest)):
+    lists = [g.inner_rows(side, "early")[starts[side] : starts[side] + count]]
+    if part == "own":
+        lists.append(g.inner_rows(side, "late"))
+    else:
+        starts, count = far_span(g, part)
+        lists.append(g.inner_rows(side, "far")[starts[side] : starts[side] + count])
+    for dst, inner_rows in zip(lefts, lists):
         left_rows(g, dst, inner_rows, rows, band, band_first, g.pair * pair, g.pair)
 
 
 def cubic_right(g, side, part, inners):
-    starts, count = early_span(g, part)
-    start = pl.multiple_of(by_side(side, starts) * g.size, 2 * g.size)
-    return [inners[0].at[pl.ds(start, count * g.size), :], inners[1]]
+    rights = []
+    for inner, span in zip(inners, (early_span, far_span)):
+        if span == far_span and part == "own":
+            rights.append(inner)
+            continue
+        starts, count = span(g, part)
+        start = pl.multiple_of(by_side(side, starts) * g.size, 2 * g.size)
+        rights.append(inner.at[pl.ds(start, count * g.size), :])
+    return rights
 
 
 def left_scratch(g, part, count):
-    sizes = [early_span(g, part)[1], g.inner_count("late" if part == "own" else "far")]
+    sizes = [early_span(g, part)[1], g.inner_count("late") if part == "own" else far_span(g, part)[1]]
     return [pltpu.VMEM((count * g.size, n * g.size), jnp.bfloat16) for n in sizes]
 
 
-def cubic_kernel(g, layer_ref, pattern_ref, *refs):
-    squares, inners, (out, band, own, keep, *lefts) = refs[:4], refs[4:6], refs[6:]
-    layer = layer_ref[0]
+def cubic_kernel(g, keep, *refs):
+    squares, inners, (out, band, own, *lefts) = refs[:4], refs[4:6], refs[6:]
+    layer = layer_index()
     side, core = layer // 2, layer % 2
     cols = g.slab * g.size
     for n, name in enumerate("AB"):
@@ -445,7 +473,6 @@
         for q in range(2):
             column = pl.ds(pl.multiple_of((core ^ q) * cols, cols), cols)
             band[rows, column] = squares[2 * n + q][...]
-    keep[: g.rows, :] = expand_pattern(pattern_ref, cols, g.size)
     rights = cubic_right(g, side, "own", inners)
     size = (g.rows + 1) // 2
     for n, first in enumerate(range(0, g.rows, size)):
@@ -483,34 +510,43 @@
     )
 
 
-def other_kernel(g, layer_ref, pattern_ref, *refs):
-    squares, inners, (partial, out, band, keep, *lefts) = refs[:2], refs[2:4], refs[4:]
-    keep[: g.rows, :] = expand_pattern(pattern_ref, out.shape[1], g.size)
-    first, product = other_part(g, layer_ref[0], "A", squares, inners, band, lefts)
+def other_kernel(g, keep, *refs):
+    squares, inners, (partial, out, band, *lefts) = refs[:2], refs[2:4], refs[4:]
+    first, product = other_part(g, layer_index(), "A", squares, inners, band, lefts)
     for n in range(g.group("A")[0]):
         out[n * g.size : (n + 1) * g.size, :] = partial[block_rows(g, first + n), :] - 2.0 * (
             own_columns(g, product, n) * keep[pl.ds(first + n, 1), :]
         )
 
 
-def last_kernel(g, layer_ref, pattern_ref, *refs):
-    squares, inners, (partial, done, out, band, keep, *lefts) = refs[:2], refs[2:4], refs[4:]
-    keep[: g.rows, :] = expand_pattern(pattern_ref, out.shape[1], g.size)
-    out[band_rows(g, 1 - layer_ref[0] // 2, "A"), :] = done[...]
-    first, product = other_part(g, layer_ref[0], "B", squares, inners, band, lefts)
-    for n in range(g.group("B")[0]):
-        rows = block_rows(g, first + n)
-        out[rows, :] = partial[rows, :] - 2.0 * (own_columns(g, product, n) * keep[pl.ds(first + n, 1), :])
-
-
-def call(kernel, out_shape, scratch, smem, *args, flops=0, after=()):
-    specs = [pl.BlockSpec(memory_space=pltpu.SMEM)] * smem + [VMEM] * (len(args) - smem)
-    specs += [pl.BlockSpec(memory_space=pl.ANY)] * len(after)
+def last_kernel(g, keep, *refs):
+    squares, inners, (partial, done, out, band, rows, sems, *lefts) = refs[:2], refs[2:4], refs[4:]
+    side = layer_index() // 2
+    copies = [pltpu.make_async_copy(done, out.at[band_rows(g, 1 - side, "A"), :], sems.at[0])]
+    copies[0].start()
+    first, product = other_part(g, layer_index(), "B", squares, inners, band, lefts)
+    count = g.group("B")[0]
+    step = count // 2
+    for n in range(count):
+        rows[n * g.size : (n + 1) * g.size, :] = partial[block_rows(g, first + n), :] - 2.0 * (
+            own_columns(g, product, n) * keep[pl.ds(first + n, 1), :]
+        )
+        if n + 1 in (step, count):
+            begin, end = (0 if n + 1 == step else step) * g.size, (n + 1) * g.size
+            to = pl.ds(pl.multiple_of(first * g.size + begin, g.size), end - begin)
+            copies.append(pltpu.make_async_copy(rows.at[begin:end, :], out.at[to, :], sems.at[len(copies)]))
+            copies[-1].start()
+    for copy in copies:
+        copy.wait()
+
+
+def call(kernel, out_shape, scratch, *args, after=(), place=VMEM):
+    specs = [VMEM] * len(args) + [pl.BlockSpec(memory_space=pl.ANY)] * len(after)
     return pl.pallas_call(
         kernel,
         out_shape=out_shape,
         in_specs=specs,
-        out_specs=jax.tree.map(lambda _: VMEM, out_shape),
+        out_specs=jax.tree.map(lambda _: place, out_shape),
         scratch_shapes=scratch,
         compiler_params=pltpu.CompilerParams(vmem_limit_bytes=LIMIT),
         cost_estimate=pl.CostEstimate(flops=0, bytes_accessed=0, transcendentals=0),
@@ -520,9 +556,11 @@
 def body(density, pattern):
     layers, ring = lax.axis_size("layer"), lax.axis_size("row")
     g = Geometry(*density.shape, *pattern.shape, layers)
-    pattern = pattern.T
+    keep = call(
+        functools.partial(keep_kernel, g),
+        jax.ShapeDtypeStruct(((g.rows + 7) // 8 * 8, density.shape[1]), jnp.float32), [], pattern.T,
+    )
     rows_dev, cols = density.shape
-    layer_arg = lax.axis_index("layer").astype(jnp.int32)[None]
     bf16 = functools.partial(jax.ShapeDtypeStruct, dtype=jnp.bfloat16)
     scratch = lambda *shape: pltpu.VMEM(shape, jnp.bfloat16)
 
@@ -540,81 +578,88 @@
 
     half_rows, slab = rows_dev // 2, (rows_dev, cols)
     cross_shape = (g.far * g.size, cols)
-    device_arg = jnp.stack([layer_arg[0], lax.axis_index("row").astype(jnp.int32)])
 
     def put_after(value, *after):
-        return call(pass_kernel, bf16(value.shape), [], 0, value, after=after)
-
-    masked = call(functools.partial(mask_kernel, g), bf16(slab), [], 0, density, pattern)
+        return call(pass_kernel, bf16(value.shape), [], value, after=after)
+
+    masked = call(functools.partial(mask_kernel, g), bf16(slab), [], density, keep)
     thin = send(masked, NEAR_THIN)
     other = swap(masked, 2)
-    relayed = send(masked, FAR_WIDE, lambda layer, row: row % 2 != layer // 2)
     beside = swap(masked, 1)
+    far_shape = message_shape(g, FAR_WIDE)
+    head_shape = (far_shape[0] - cross_shape[0], cols)
+    wide, far_wide = call(
+        functools.partial(pack_kernel, g),
+        [bf16(message_shape(g, NEAR_WIDE)), bf16(head_shape)], [scratch(half_rows, 2 * cols)],
+        masked, beside,
+    )
+    relayed = send(wide, FAR_WIDE, lambda layer, row: row % 2 != layer // 2)
     crossed = swap(thin, 2)
-    wide = call(functools.partial(relay_kernel, g), bf16(slab), [], 1, device_arg, masked, relayed, after=(thin,))
+    wide, far_wide = call(
+        functools.partial(relay_kernel, g),
+        [bf16(wide.shape), bf16(far_shape)], [], wide, relayed, far_wide, other, after=(thin,),
+    )
     wide = lax.ppermute(wide, "row", [(r, r ^ 1) for r in range(ring)])
-    far_wide = call(
-        functools.partial(pack_far_kernel, g),
-        bf16(message_shape(g, FAR_WIDE)), [scratch(half_rows, 2 * cols)],
-        1, layer_arg, masked, beside, other,
-    )
     far_wide = send(far_wide, FAR_WIDE)
 
     early, late, far = (g.inner_count(part) * g.size for part in ("early", "late", "far"))
     (high_a, wide_a), (high_b, wide_b) = (tuple(n * g.size for n in g.group(name)) for name in "AB")
     span = g.span * g.size
     f32 = functools.partial(jax.ShapeDtypeStruct, dtype=jnp.float32)
-    keep = pltpu.VMEM((even_up(g.rows + 6), cols), jnp.float32)
-
-    inner_early, sum_a, sum_b, late_a, late_b, far_b = call(
+
+    inner_early, sum_a, left_b, late_a, late_b, far_b = call(
         functools.partial(early_kernel, g),
         [
-            bf16((early, span)), f32((high_a, wide_a)), f32((high_b, wide_b)), bf16((high_a, late)),
+            bf16((early, span)), f32((high_a, wide_a)), bf16((high_b, early)), bf16((high_a, late)),
             bf16((high_b, late)), bf16((high_b, far)),
         ],
         [
-            scratch(rows_dev, layers * cols), scratch(high_a, early), scratch(high_b, early),
+            scratch(rows_dev, layers * cols), scratch(high_a, early),
             scratch(rows_dev, 2 * cols),
         ],
-        1, layer_arg, masked, beside, other, swap(other, 1), thin, swap(thin, 1),
-    )
-    crossed, wide = (put_after(value, sum_a) for value in (crossed, wide))
-    far_wide, far_thin = call(
-        functools.partial(pass_far_kernel, g),
-        [bf16(far_wide.shape), bf16(message_shape(g, FAR_THIN))], [], 1, layer_arg, far_wide, after=(sum_a,),
+        masked, beside, other, swap(other, 1), thin, swap(thin, 1),
+    )
+    far_thin = call(
+        functools.partial(pass_far_kernel, g), bf16(message_shape(g, FAR_THIN)), [], far_wide,
     )
     far_thin = lax.ppermute(far_thin, "layer", [(1, 2), (2, 1)])
     pieces = sum(([value, swap(value, 1)] for value in (crossed, wide, far_wide)), [])
     square_a, inner_late = call(
         functools.partial(late_kernel, g),
         [bf16((high_a, cols)), bf16((late, span))],
-        [scratch(rows_dev, 2 * cols), scratch(rows_dev, 2 * cols), scratch(cross_shape[0], 2 * cols), keep],
-        1, layer_arg, pattern, *pieces, sum_a, late_a,
+        [scratch(rows_dev, 2 * cols), scratch(cross_shape[0], 2 * cols)],
+        keep, *pieces, sum_a, late_a,
     )
     across_a, beside_a = swap(square_a, 2), swap(square_a, 1)
     square_b, inner_far = call(
         functools.partial(square_kernel, g),
         [bf16((high_b, cols)), bf16((far, span))],
-        [keep],
-        1, layer_arg, pattern, far_thin, sum_b, late_b, far_b, inner_late,
+        [],
+        keep, far_thin, left_b, late_b, far_b, inner_early, inner_late,
     )
     across_b, beside_b = swap(square_b, 2), swap(square_b, 1)
     partial = call(
         functools.partial(cubic_kernel, g),
         f32(slab),
-        [scratch(rows_dev, 2 * cols), scratch(*slab), keep] + 2 * left_scratch(g, "own", (g.rows + 1) // 2),
-        1, layer_arg, pattern, square_a, beside_a, square_b, beside_b, inner_early, inner_late,
+        [scratch(rows_dev, 2 * cols), scratch(*slab)] + 2 * left_scratch(g, "own", (g.rows + 1) // 2),
+        keep, square_a, beside_a, square_b, beside_b, inner_early, inner_late,
     )
     done = call(
         functools.partial(other_kernel, g),
-        f32((high_a, cols)), [scratch(high_a, 2 * cols), keep] + left_scratch(g, "A", g.group("A")[0]),
-        1, layer_arg, pattern, across_a, swap(across_a, 1), inner_early, inner_far, partial,
+        f32((high_a, cols)), [scratch(high_a, 2 * cols)] + left_scratch(g, "A", g.group("A")[0]),
+        keep, across_a, swap(across_a, 1), inner_early, inner_far, partial,
     )
     across_b = put_after(across_b, done)
     return call(
         functools.partial(last_kernel, g),
-        f32(slab), [scratch(high_b, 2 * cols), keep] + left_scratch(g, "B", g.group("B")[0]),
-        1, layer_arg, pattern, across_b, swap(across_b, 1), inner_early, inner_far, partial, done,
+        f32(slab),
+        [
+            scratch(high_b, 2 * cols), pltpu.VMEM((high_b, cols), jnp.float32),
+            pltpu.SemaphoreType.DMA((3,)),
+        ]
+        + left_scratch(g, "B", g.group("B")[0]),
+        keep, across_b, swap(across_b, 1), inner_early, inner_far, partial, done,
+        place=HBM,
     )
 
 

time: 69.1 us -> 67.6 us (0.978)
  Pallas kernels: 15.9 us -> 14.3 us
  starting transfers between devices: 19 us -> 18.2 us
  waiting for transfers between devices: 32 us -> 32.7 us
    ppermute x14, waiting for transfers between devices: 15 us -> 19 us  [swap(): return lax.ppermute(value, 'layer', [(s, s ^ bit) for s in range(layers)])]
    ppermute x1, waiting for transfers between devices: 3.76 us -> 0.01 us  [body(): wide = lax.ppermute(wide, 'row', [(r, r ^ 1) for r in range(ring)])]
    ppermute x1, starting transfers between devices: 2.81 us -> 0.26 us  [body(): wide = lax.ppermute(wide, 'row', [(r, r ^ 1) for r in range(ring)])]
    ppermute x14, starting transfers between devices: 8.74 us -> 10.9 us  [swap(): return lax.ppermute(value, 'layer', [(s, s ^ bit) for s in range(layers)])]
    pallas_call x13 -> x12, Pallas kernels: 15.9 us -> 14.3 us  [call(): pl.pallas_call(kernel, out_shape=out_shape, in_specs=specs, out_specs=jax...]
    unnamed x6 -> x4, local copies, waits for them, and re-layouts: 1.78 us -> 1.77 us
  transfers between devices with their start and end apart: 19 -> 19, of which waited for: 7 -> 6; matrix products, arithmetic and copies ran while one was open for 0% -> 0% of each run, Pallas kernels for 18% -> 17%
where the time goes in v3:
time: 67.6 us; the launch traced here: 67.4 us
  waiting for transfers between devices  32.7 us (48%)
  starting transfers between devices  18.2 us (27%)
  Pallas kernels  14.3 us (21%)
  local copies, waits for them, and re-layouts  1.77 us (3%)
    ppermute x14, waiting for transfers between devices, swap(): return lax.ppermute(value, 'layer', [(s, s ^ bit) for s in range(layers)])  19 us
    pallas_call x12, Pallas kernels, call(): pl.pallas_call(kernel, out_shape=out_shape, in_specs=specs, out_specs=jax...  14.3 us
    ppermute x3, waiting for transfers between devices, send(): return lax.ppermute(value, ('layer', 'row'), pairs)  13.8 us
    ppermute x14, starting transfers between devices, swap(): return lax.ppermute(value, 'layer', [(s, s ^ bit) for s in range(layers)])  10.9 us
    ppermute x3, starting transfers between devices, send(): return lax.ppermute(value, ('layer', 'row'), pairs)  6.37 us
    unnamed x4, local copies, waits for them, and re-layouts  1.77 us
  transfers between devices with their start and end apart: 19, of which 6 were waited for; matrix products, arithmetic and copies ran while one was open for 0% of the time, Pallas kernels for 17%

profile of v3, /device:TPU:0, one launch (start us, length us, event | category | flops | bytes accessed | tf_op | source)
XLA Modules:
  0.0 67.4 jit_solution(1135258626504666143)
XLA Ops:
  0.0 0.7 %copy-done.1 = s32[10,8]{0,1:T(8,128)S(1)} copy-done((s32[10,8]{0,1:T(8,128)S(1)}, s32[10,8]{0,1:T(8,128)}, u32[]{:S(2)}) %copy-start.1) | copy-done | bytes 344
  0.7 0.2 shard_map.28.keep
  0.9 1.1 %copy-done = bf16[640,512]{1,0:T(8,128)(2,1)S(1)} copy-done((bf16[640,512]{1,0:T(8,128)(2,1)S(1)}, bf16[640,512]{1,0:T(8,128)(2,1)}, u32[]{:S(2)}) %copy-start) | copy-done | bytes 655384
  2.0 0.1 shard_map.29.own_ref.own
  2.0 0.5 collective-permute-start
  2.5 5.6 %collective-permute-start.3 = (bf16[640,512]{1,0:T(8,128)(2,1)S(1)}, bf16[640,512]{1,0:T(8,128)(2,1)S(1)}, u32[]{:S(2)}, u32[]{:S(2)}) collective-permute-start(bf16[640,512]{1,0:T(8,128)(2,1)S(1)} %shard_map.29.own_ref.own), channel_id=1, source_target_pairs={{0,7},{1,0},{2,1},{3,2},{4,3},{5,4},{6,5},{7,6},{8,15},{9,8},{10,9... | collective-permute-start | bytes 1966088 | tf_op jit(solution)/shard_map/ppermute | solution.py:577
  8.2 0.0 collective-permute-start.2
  8.2 0.0 collective-permute-done.beside_ref.beside
  8.2 0.1 shard_map.30
  8.3 0.7 %collective-permute-start.1 = (bf16[160,1408]{1,0:T(8,128)(2,1)S(1)}, bf16[160,1408]{1,0:T(8,128)(2,1)S(1)}, u32[]{:S(2)}, u32[]{:S(2)}) collective-permute-start(bf16[160,1408]{1,0:T(8,128)(2,1)S(1)} %get-tuple-element.19.own_ref), channel_id=1, source_target_pairs={{1,3},{3,5},{5,7},{7,1},{9,11},{11,13},{13,15},{15,9},{16,22},{18,... | collective-permute-start | bytes 1351688 | tf_op jit(solution)/shard_map/ppermute | solution.py:577
  9.0 13.8 %collective-permute-done.3.after_ref.refs_2_ = bf16[640,512]{1,0:T(8,128)(2,1)S(1)} collective-permute-done((bf16[640,512]{1,0:T(8,128)(2,1)S(1)}, bf16[640,512]{1,0:T(8,128)(2,1)S(1)}, u32[]{:S(2)}, u32[]{:S(2)}) %collective-permute-start.3) | collective-permute-done | bytes 655392 | tf_op jit(solution)/shard_map/ppermute | solution.py:577
  22.8 2.2 %collective-permute-start.8 = (bf16[640,512]{1,0:T(8,128)(2,1)S(1)}, bf16[640,512]{1,0:T(8,128)(2,1)S(1)}, u32[]{:S(2)}, u32[]{:S(2)}) collective-permute-start(bf16[640,512]{1,0:T(8,128)(2,1)S(1)} %collective-permute-done.3.after_ref.refs_2_), channel_id=1, source_target_pairs={{0,16},{8,24},{16,0},{24,8},{1,17},{9,25},{17,1},{25,9},{2,18},{10... | collective-permute-start | bytes 1966088 | tf_op jit(solution)/shard_map/ppermute | solution.py:568
  25.0 0.0 collective-permute-done.2.other_ref.refs_0_
  25.0 0.0 collective-permute-done.1.relayed_ref
  25.0 0.1 shard_map.31
  25.1 0.1 collective-permute-start.4
  25.1 0.3 collective-permute-start.10
  25.4 0.0 collective-permute-start.7
  25.4 0.5 collective-permute-start.6
  25.9 13.8 %collective-permute-done.8.refs_0_ = bf16[640,512]{1,0:T(8,128)(2,1)S(1)} collective-permute-done((bf16[640,512]{1,0:T(8,128)(2,1)S(1)}, bf16[640,512]{1,0:T(8,128)(2,1)S(1)}, u32[]{:S(2)}, u32[]{:S(2)}) %collective-permute-start.8) | collective-permute-done | bytes 655392 | tf_op jit(solution)/shard_map/ppermute | solution.py:568
  39.7 0.0 collective-permute-start.9
  39.7 0.0 collective-permute-done.4.in_ref.refs_4_
  39.7 0.5 collective-permute-start.12
  40.2 0.0 collective-permute-done.10.refs_2_
  40.2 0.1 collective-permute-start.11
  40.3 0.0 collective-permute-done.7.refs_3_
  40.3 0.7 collective-permute-start.5
  41.0 0.0 collective-permute-done.6.refs_1_
  41.0 2.0 %shard_map.33 = (bf16[1280,1664]{1,0:T(8,128)(2,1)S(1)}, f32[256,768]{1,0:T(8,128)S(1)}, bf16[384,1280]{1,0:T(8,128)(2,1)S(1)}, bf16[256,1024]{1,0:T(8,128)(2,1)...) custom-call(bf16[640,512]{1,0:T(8,128)(2,1)S(1)} %shard_map.29.own_ref.own, ...), custom_call_target="tpu_custom_call" | custom-call | tf_op jit(solution)/shard_map/pallas_call | solution.py:545
  43.0 0.1 collective-permute-done.11.refs_3_
  43.1 0.0 collective-permute-done.12.refs_5_
  43.1 1.4 %shard_map.34 = (bf16[256,512]{1,0:T(8,128)(2,1)S(1)}, bf16[1024,1664]{1,0:T(8,128)(2,1)S(1)}) custom-call(f32[16,512]{1,0:T(8,128)S(1)} %shard_map.28.keep, bf16[640,512]{1,0:T(8,128)(2,1)S(1)} %collective-permute-done.8.refs_0_, bf16[640,512]{1,0:T(8,128)(2,1)S(1)} %collective-permute-done.9.refs_1_, ...), custom_call_target="tpu_custom_call" | custom-call | tf_op jit(solution)/shard_map/pallas_call | solution.py:545
  44.5 3.3 %collective-permute-start.14 = (bf16[256,512]{1,0:T(8,128)(2,1)S(1)}, bf16[256,512]{1,0:T(8,128)(2,1)S(1)}, u32[]{:S(2)}, u32[]{:S(2)}) collective-permute-start(bf16[256,512]{1,0:T(8,128)(2,1)S(1)} %get-tuple-element.31.refs_0_), channel_id=1, source_target_pairs={{0,16},{8,24},{16,0},{24,8},{1,17},{9,25},{17,1},{25,9},{2,18},{10... | collective-permute-start | bytes 786440 | tf_op jit(solution)/shard_map/ppermute | solution.py:568
  47.8 0.0 collective-permute-done.5.far
  47.8 2.6 %shard_map.35 = (bf16[384,512]{1,0:T(8,128)(2,1)S(1)}, bf16[384,1664]{1,0:T(8,128)(2,1)S(1)}) custom-call(f32[16,512]{1,0:T(8,128)S(1)} %shard_map.28.keep, bf16[192,384]{1,0:T(8,128)(2,1)S(1)} %collective-permute-done.5.far, bf16[384,1280]{1,0:T(8,128)(2,1)S(1)} %get-tuple-element.22.early_left, bf16[384,1024]{1,0:T(8,128)(2,1)S(1)} %get-tuple-element.23.left, ...), custom_call_target="tpu_custom_call" | custom-call | tf_op jit(solution)/shard_map/pallas_call | solution.py:545
  50.4 0.1 collective-permute-start.17
  50.5 1.5 %collective-permute-start.13 = (bf16[384,512]{1,0:T(8,128)(2,1)S(1)}, bf16[384,512]{1,0:T(8,128)(2,1)S(1)}, u32[]{:S(2)}, u32[]{:S(2)}) collective-permute-start(bf16[384,512]{1,0:T(8,128)(2,1)S(1)} %get-tuple-element.30.refs_2_), channel_id=1, source_target_pairs={{0,16},{8,24},{16,0},{24,8},{1,17},{9,25},{17,1},{25,9},{2,18},{10... | collective-permute-start | bytes 1179656 | tf_op jit(solution)/shard_map/ppermute | solution.py:568
  52.1 2.5 %collective-permute-done.14.refs_0_ = bf16[256,512]{1,0:T(8,128)(2,1)S(1)} collective-permute-done((bf16[256,512]{1,0:T(8,128)(2,1)S(1)}, bf16[256,512]{1,0:T(8,128)(2,1)S(1)}, u32[]{:S(2)}, u32[]{:S(2)}) %collective-permute-start.14) | collective-permute-done | bytes 262176 | tf_op jit(solution)/shard_map/ppermute | solution.py:568
  54.5 1.4 %collective-permute-start.15 = (bf16[256,512]{1,0:T(8,128)(2,1)S(1)}, bf16[256,512]{1,0:T(8,128)(2,1)S(1)}, u32[]{:S(2)}, u32[]{:S(2)}) collective-permute-start(bf16[256,512]{1,0:T(8,128)(2,1)S(1)} %collective-permute-done.14.refs_0_), channel_id=1, source_target_pairs={{0,8},{8,0},{16,24},{24,16},{1,9},{9,1},{17,25},{25,17},{2,10},{10... | collective-permute-start | bytes 786440 | tf_op jit(solution)/shard_map/ppermute | solution.py:568
  55.9 0.0 collective-permute-done.16.refs_1_
  55.9 0.0 collective-permute-done.17.refs_3_
  55.9 4.3 %shard_map.36.refs_4_ = f32[640,512]{1,0:T(8,128)S(1)} custom-call(f32[16,512]{1,0:T(8,128)S(1)} %shard_map.28.keep, bf16[256,512]{1,0:T(8,128)(2,1)S(1)} %get-tuple-element.31.refs_0_, bf16[256,512]{1,0:T(8,128)(2,1)S(1)} %collective-permute-done.16.refs_1_, bf16[384,512]{1,0:T(8,128)(2,1)S(1)} %get-tuple-element.30.refs_2_, ...), custom_call_target="tpu_custom_call" | custom-call | tf_op jit(solution)/shard_map/pallas_call | solution.py:545
  60.2 0.0 collective-permute-done.15.refs_1_
  60.2 1.1 %shard_map.37.refs_0_.refs_5_ = f32[256,512]{1,0:T(8,128)S(1)} custom-call(f32[16,512]{1,0:T(8,128)S(1)} %shard_map.28.keep, bf16[256,512]{1,0:T(8,128)(2,1)S(1)} %collective-permute-done.14.refs_0_, bf16[256,512]{1,0:T(8,128)(2,1)S(1)} %collective-permute-done.15.refs_1_, bf16[1280,1664]{1,0:T(8,128)(2,1)S(1)} %get-tuple-element.25.early.refs_4_.refs_2_, ...), custom_call_target="tpu_custom_call" | custom-call | tf_op jit(solution)/shard_map/pallas_call | solution.py:545
  61.3 1.3 %collective-permute-done.13.in_ref = bf16[384,512]{1,0:T(8,128)(2,1)S(1)} collective-permute-done((bf16[384,512]{1,0:T(8,128)(2,1)S(1)}, bf16[384,512]{1,0:T(8,128)(2,1)S(1)}, u32[]{:S(2)}, u32[]{:S(2)}) %collective-permute-start.13) | collective-permute-done | bytes 393248 | tf_op jit(solution)/shard_map/ppermute | solution.py:568
  62.6 0.7 %collective-permute-start.18 = (bf16[384,512]{1,0:T(8,128)(2,1)S(1)}, bf16[384,512]{1,0:T(8,128)(2,1)S(1)}, u32[]{:S(2)}, u32[]{:S(2)}) collective-permute-start(bf16[384,512]{1,0:T(8,128)(2,1)S(1)} %shard_map.38.refs_0_), channel_id=1, source_target_pairs={{0,8},{8,0},{16,24},{24,16},{1,9},{9,1},{17,25},{25,17},{2,10},{10... | collective-permute-start | bytes 1179656 | tf_op jit(solution)/shard_map/ppermute | solution.py:568
  63.3 1.3 %collective-permute-done.18.refs_1_ = bf16[384,512]{1,0:T(8,128)(2,1)S(1)} collective-permute-done((bf16[384,512]{1,0:T(8,128)(2,1)S(1)}, bf16[384,512]{1,0:T(8,128)(2,1)S(1)}, u32[]{:S(2)}, u32[]{:S(2)}) %collective-permute-start.18) | collective-permute-done | bytes 393248 | tf_op jit(solution)/shard_map/ppermute | solution.py:568
  64.7 2.5 %shard_map.39 = f32[640,512]{1,0:T(8,128)} custom-call(f32[16,512]{1,0:T(8,128)S(1)} %shard_map.28.keep, bf16[384,512]{1,0:T(8,128)(2,1)S(1)} %shard_map.38.refs_0_, bf16[384,512]{1,0:T(8,128)(2,1)S(1)} %collective-permute-done.18.refs_1_, bf16[1280,1664]{1,0:T(8,128)(2,1)S(1)} %get-tuple-element.25.early.refs_4_.refs_2_, ...), custom_call_target="tpu_custom_call" | custom-call | tf_op jit(solution)/shard_map/pallas_call | solution.py:545
  (6 shorter events, 0.0 us)
Async XLA Ops:
  0.0 0.7 %copy-start.1 = (s32[10,8]{0,1:T(8,128)S(1)}, s32[10,8]{0,1:T(8,128)}, u32[]{:S(2)}) copy-start(s32[10,8]{0,1:T(8,128)} %param.3) | copy-start | bytes 964
  0.9 1.1 %copy-start = (bf16[640,512]{1,0:T(8,128)(2,1)S(1)}, bf16[640,512]{1,0:T(8,128)(2,1)}, u32[]{:S(2)}) copy-start(bf16[640,512]{1,0:T(8,128)(2,1)} %density_ref.1) | copy-start | bytes 1966084
  2.0 6.1 %collective-permute-start = (bf16[640,512]{1,0:T(8,128)(2,1)S(1)}, bf16[640,512]{1,0:T(8,128)(2,1)S(1)}, u32[]{:S(2)}, u32[]{:S(2)}) collective-permute-start(bf16[640,512]{1,0:T(8,128)(2,1)S(1)} %shard_map.29.own_ref.own), channel_id=1, source_target_pairs={{0,8},{8,0},{16,24},{24,16},{1,9},{9,1},{17,25},{25,17},{2,10},{10... | collective-permute-start | bytes 1966088 | tf_op jit(solution)/shard_map/ppermute | solution.py:568
  2.5 20.2 %collective-permute-start.3 = (bf16[640,512]{1,0:T(8,128)(2,1)S(1)}, bf16[640,512]{1,0:T(8,128)(2,1)S(1)}, u32[]{:S(2)}, u32[]{:S(2)}) collective-permute-start(bf16[640,512]{1,0:T(8,128)(2,1)S(1)} %shard_map.29.own_ref.own), channel_id=1, source_target_pairs={{0,7},{1,0},{2,1},{3,2},{4,3},{5,4},{6,5},{7,6},{8,15},{9,8},{10,9... | collective-permute-start | bytes 1966088 | tf_op jit(solution)/shard_map/ppermute | solution.py:577
  8.2 16.8 %collective-permute-start.2 = (bf16[640,512]{1,0:T(8,128)(2,1)S(1)}, bf16[640,512]{1,0:T(8,128)(2,1)S(1)}, u32[]{:S(2)}, u32[]{:S(2)}) collective-permute-start(bf16[640,512]{1,0:T(8,128)(2,1)S(1)} %shard_map.29.own_ref.own), channel_id=1, source_target_pairs={{0,16},{8,24},{16,0},{24,8},{1,17},{9,25},{17,1},{25,9},{2,18},{10... | collective-permute-start | bytes 1966088 | tf_op jit(solution)/shard_map/ppermute | solution.py:568
  8.3 16.7 %collective-permute-start.1 = (bf16[160,1408]{1,0:T(8,128)(2,1)S(1)}, bf16[160,1408]{1,0:T(8,128)(2,1)S(1)}, u32[]{:S(2)}, u32[]{:S(2)}) collective-permute-start(bf16[160,1408]{1,0:T(8,128)(2,1)S(1)} %get-tuple-element.19.own_ref), channel_id=1, source_target_pairs={{1,3},{3,5},{5,7},{7,1},{9,11},{11,13},{13,15},{15,9},{16,22},{18,... | collective-permute-start | bytes 1351688 | tf_op jit(solution)/shard_map/ppermute | solution.py:577
  22.8 16.9 %collective-permute-start.8 = (bf16[640,512]{1,0:T(8,128)(2,1)S(1)}, bf16[640,512]{1,0:T(8,128)(2,1)S(1)}, u32[]{:S(2)}, u32[]{:S(2)}) collective-permute-start(bf16[640,512]{1,0:T(8,128)(2,1)S(1)} %collective-permute-done.3.after_ref.refs_2_), channel_id=1, source_target_pairs={{0,16},{8,24},{16,0},{24,8},{1,17},{9,25},{17,1},{25,9},{2,18},{10... | collective-permute-start | bytes 1966088 | tf_op jit(solution)/shard_map/ppermute | solution.py:568
  25.1 14.6 %collective-permute-start.4 = (bf16[480,512]{1,0:T(8,128)(2,1)S(1)}, bf16[480,512]{1,0:T(8,128)(2,1)S(1)}, u32[]{:S(2)}, u32[]{:S(2)}) collective-permute-start(bf16[480,512]{1,0:T(8,128)(2,1)S(1)} %get-tuple-element.21), channel_id=1, source_target_pairs={{0,2},{1,3},{2,4},{3,5},{4,6},{5,7},{6,0},{7,1},{8,10},{9,11},{10,... | collective-permute-start | bytes 1474568 | tf_op jit(solution)/shard_map/ppermute | solution.py:577
  25.1 15.1 %collective-permute-start.10 = (bf16[160,1408]{1,0:T(8,128)(2,1)S(1)}, bf16[160,1408]{1,0:T(8,128)(2,1)S(1)}, u32[]{:S(2)}, u32[]{:S(2)}) collective-permute-start(bf16[160,1408]{1,0:T(8,128)(2,1)S(1)} %get-tuple-element.26), channel_id=1, source_target_pairs={{0,1},{1,0},{2,3},{3,2},{4,5},{5,4},{6,7},{7,6},{8,9},{9,8},{10,11... | collective-permute-start | bytes 1351688 | tf_op jit(solution)/shard_map/ppermute | solution.py:602
  25.4 14.9 %collective-permute-start.7 = (bf16[640,512]{1,0:T(8,128)(2,1)S(1)}, bf16[640,512]{1,0:T(8,128)(2,1)S(1)}, u32[]{:S(2)}, u32[]{:S(2)}) collective-permute-start(bf16[640,512]{1,0:T(8,128)(2,1)S(1)} %collective-permute-done.3.after_ref.refs_2_), channel_id=1, source_target_pairs={{0,8},{8,0},{16,24},{24,16},{1,9},{9,1},{17,25},{25,17},{2,10},{10... | collective-permute-start | bytes 1966088 | tf_op jit(solution)/shard_map/ppermute | solution.py:568
  25.4 15.6 %collective-permute-start.6 = (bf16[640,512]{1,0:T(8,128)(2,1)S(1)}, bf16[640,512]{1,0:T(8,128)(2,1)S(1)}, u32[]{:S(2)}, u32[]{:S(2)}) collective-permute-start(bf16[640,512]{1,0:T(8,128)(2,1)S(1)} %collective-permute-done.2.other_ref.refs_0_), channel_id=1, source_target_pairs={{0,8},{8,0},{16,24},{24,16},{1,9},{9,1},{17,25},{25,17},{2,10},{10... | collective-permute-start | bytes 1966088 | tf_op jit(solution)/shard_map/ppermute | solution.py:568
  39.7 3.4 %collective-permute-start.9 = (bf16[640,512]{1,0:T(8,128)(2,1)S(1)}, bf16[640,512]{1,0:T(8,128)(2,1)S(1)}, u32[]{:S(2)}, u32[]{:S(2)}) collective-permute-start(bf16[640,512]{1,0:T(8,128)(2,1)S(1)} %collective-permute-done.8.refs_0_), channel_id=1, source_target_pairs={{0,8},{8,0},{16,24},{24,16},{1,9},{9,1},{17,25},{25,17},{2,10},{10... | collective-permute-start | bytes 1966088 | tf_op jit(solution)/shard_map/ppermute | solution.py:568
  39.7 3.4 %collective-permute-start.12 = (bf16[480,512]{1,0:T(8,128)(2,1)S(1)}, bf16[480,512]{1,0:T(8,128)(2,1)S(1)}, u32[]{:S(2)}, u32[]{:S(2)}) collective-permute-start(bf16[480,512]{1,0:T(8,128)(2,1)S(1)} %collective-permute-done.4.in_ref.refs_4_), channel_id=1, source_target_pairs={{0,8},{8,0},{16,24},{24,16},{1,9},{9,1},{17,25},{25,17},{2,10},{10... | collective-permute-start | bytes 1474568 | tf_op jit(solution)/shard_map/ppermute | solution.py:568
  40.2 2.9 %collective-permute-start.11 = (bf16[160,1408]{1,0:T(8,128)(2,1)S(1)}, bf16[160,1408]{1,0:T(8,128)(2,1)S(1)}, u32[]{:S(2)}, u32[]{:S(2)}) collective-permute-start(bf16[160,1408]{1,0:T(8,128)(2,1)S(1)} %collective-permute-done.10.refs_2_), channel_id=1, source_target_pairs={{0,8},{8,0},{16,24},{24,16},{1,9},{9,1},{17,25},{25,17},{2,10},{10... | collective-permute-start | bytes 1351688 | tf_op jit(solution)/shard_map/ppermute | solution.py:568
  40.3 7.5 %collective-permute-start.5 = (bf16[192,384]{1,0:T(8,128)(2,1)S(1)}, bf16[192,384]{1,0:T(8,128)(2,1)S(1)}, u32[]{:S(2)}, u32[]{:S(2)}) collective-permute-start(bf16[192,384]{1,0:T(8,128)(2,1)S(1)} %shard_map.32), channel_id=1, source_target_pairs={{8,16},{16,8},{9,17},{17,9},{10,18},{18,10},{11,19},{19,11},{12,20... | collective-permute-start | bytes 442376 | tf_op jit(solution)/shard_map/ppermute | solution.py:625
  44.5 10.0 %collective-permute-start.14 = (bf16[256,512]{1,0:T(8,128)(2,1)S(1)}, bf16[256,512]{1,0:T(8,128)(2,1)S(1)}, u32[]{:S(2)}, u32[]{:S(2)}) collective-permute-start(bf16[256,512]{1,0:T(8,128)(2,1)S(1)} %get-tuple-element.31.refs_0_), channel_id=1, source_target_pairs={{0,16},{8,24},{16,0},{24,8},{1,17},{9,25},{17,1},{25,9},{2,18},{10... | collective-permute-start | bytes 786440 | tf_op jit(solution)/shard_map/ppermute | solution.py:568
  50.4 5.5 %collective-permute-start.17 = (bf16[384,512]{1,0:T(8,128)(2,1)S(1)}, bf16[384,512]{1,0:T(8,128)(2,1)S(1)}, u32[]{:S(2)}, u32[]{:S(2)}) collective-permute-start(bf16[384,512]{1,0:T(8,128)(2,1)S(1)} %get-tuple-element.30.refs_2_), channel_id=1, source_target_pairs={{0,8},{8,0},{16,24},{24,16},{1,9},{9,1},{17,25},{25,17},{2,10},{10... | collective-permute-start | bytes 1179656 | tf_op jit(solution)/shard_map/ppermute | solution.py:568
  50.5 12.1 %collective-permute-start.13 = (bf16[384,512]{1,0:T(8,128)(2,1)S(1)}, bf16[384,512]{1,0:T(8,128)(2,1)S(1)}, u32[]{:S(2)}, u32[]{:S(2)}) collective-permute-start(bf16[384,512]{1,0:T(8,128)(2,1)S(1)} %get-tuple-element.30.refs_2_), channel_id=1, source_target_pairs={{0,16},{8,24},{16,0},{24,8},{1,17},{9,25},{17,1},{25,9},{2,18},{10... | collective-permute-start | bytes 1179656 | tf_op jit(solution)/shard_map/ppermute | solution.py:568
  52.1 3.9 %collective-permute-start.16 = (bf16[256,512]{1,0:T(8,128)(2,1)S(1)}, bf16[256,512]{1,0:T(8,128)(2,1)S(1)}, u32[]{:S(2)}, u32[]{:S(2)}) collective-permute-start(bf16[256,512]{1,0:T(8,128)(2,1)S(1)} %get-tuple-element.31.refs_0_), channel_id=1, source_target_pairs={{0,8},{8,0},{16,24},{24,16},{1,9},{9,1},{17,25},{25,17},{2,10},{10... | collective-permute-start | bytes 786440 | tf_op jit(solution)/shard_map/ppermute | solution.py:568
  54.5 5.7 %collective-permute-start.15 = (bf16[256,512]{1,0:T(8,128)(2,1)S(1)}, bf16[256,512]{1,0:T(8,128)(2,1)S(1)}, u32[]{:S(2)}, u32[]{:S(2)}) collective-permute-start(bf16[256,512]{1,0:T(8,128)(2,1)S(1)} %collective-permute-done.14.refs_0_), channel_id=1, source_target_pairs={{0,8},{8,0},{16,24},{24,16},{1,9},{9,1},{17,25},{25,17},{2,10},{10... | collective-permute-start | bytes 786440 | tf_op jit(solution)/shard_map/ppermute | solution.py:568
  62.6 2.1 %collective-permute-start.18 = (bf16[384,512]{1,0:T(8,128)(2,1)S(1)}, bf16[384,512]{1,0:T(8,128)(2,1)S(1)}, u32[]{:S(2)}, u32[]{:S(2)}) collective-permute-start(bf16[384,512]{1,0:T(8,128)(2,1)S(1)} %shard_map.38.refs_0_), channel_id=1, source_target_pairs={{0,8},{8,0},{16,24},{24,16},{1,9},{9,1},{17,25},{25,17},{2,10},{10... | collective-permute-start | bytes 1179656 | tf_op jit(solution)/shard_map/ppermute | solution.py:568

commit v4 on v3

--- a/solution.py
+++ b/solution.py
@@ -103,35 +103,40 @@
     rows, cols = max(f[1] for f in layouts) * g.size // 2, max(f[2] for f in layouts) * g.size
     if name == FAR_WIDE:
         return rows + g.far * g.size, g.slab * g.size
-    return (2 * rows, cols) if name == FAR_THIN else (rows, cols)
+    return rows, cols
 
 
 def layer_index():
     return lax.axis_index("layer").astype(jnp.int32)
 
 
-def keep_kernel(g, pattern_ref, keep):
-    offsets, cols = pattern_ref.shape[0], keep.shape[1]
+def mask_kernel(g, density_ref, pattern_ref, out_ref, keep, density, pattern, sems):
+    copies = [
+        pltpu.make_async_copy(source, target, sems.at[n])
+        for n, (source, target) in enumerate(((pattern_ref, pattern), (density_ref, density)))
+    ]
+    for copy in copies:
+        copy.start()
+    copies[0].wait()
+    offsets, cols = pattern.shape[0], keep.shape[1]
     block = lax.broadcasted_iota(jnp.int32, (offsets, cols), 1) // g.size
     row = lax.broadcasted_iota(jnp.int32, (offsets, cols), 0)
     spread = jnp.where(block == row, 1.0, 0.0).astype(jnp.float32)
     keep[: g.rows, :] = lax.dot_general(
-        pattern_ref[...].astype(jnp.float32), spread, (((0,), (0,)), ((), ())),
+        pattern[...].astype(jnp.float32), spread, (((0,), (0,)), ((), ())),
         preferred_element_type=jnp.float32,
     )
     keep[g.rows :, :] = jnp.zeros((keep.shape[0] - g.rows, cols), keep.dtype)
+    copies[1].wait()
+    for t in range(g.rows):
+        rows = slice(t * g.size, (t + 1) * g.size)
+        out_ref[rows, :] = density[rows, :] * keep[t : t + 1, :].astype(jnp.bfloat16)
 
 
 def cross_rows(g, side):
     rows = [t - step_of(side, FAR_WIDE) * g.rows for t in g.reached(step_of(side, FAR_WIDE))]
     count = g.far
     return min(rows[0], g.rows - count), count
-
-
-def mask_kernel(g, density_ref, keep, out_ref):
-    for t in range(g.rows):
-        rows = slice(t * g.size, (t + 1) * g.size)
-        out_ref[rows, :] = density_ref[rows, :] * keep[t : t + 1, :].astype(jnp.bfloat16)
 
 
 def place_row(dst_ref, dst_row, dst_lo, src_ref, src_row, height, lo, hi, shift, size, limit):
@@ -211,15 +216,20 @@
     refs[-1][...] = in_ref[...]
 
 
-def pass_far_kernel(g, in_ref, message):
-    def fill(side):
+def far_thin_kernel(g, far_own, far_beside, after_ref, message):
+    side, core = layer_index() // 2, layer_index() % 2
+    half = g.size // 2
+
+    def fill(side, source):
         first, count = cross_rows(g, side)
-        start = in_ref.shape[0] - (count + first) * g.size
-        lead = (1 - side) * (g.offsets - g.slab)
-        pack(g, 1 - side, FAR_THIN, in_ref, lambda row: start + row * g.size, lead, g.size, message)
+        start = source.shape[0] - (count + first) * g.size
+        row_of = lambda row: pl.multiple_of(start + row * g.size + half * core, half)
+        pack(g, 1 - side, FAR_THIN, source, row_of, (1 - side) * (g.offsets - g.slab), half, message)
 
     for value in (0, 1):
-        pl.when(layer_index() // 2 == value)(functools.partial(fill, value))
+        for held, source in ((True, far_own), (False, far_beside)):
+            here = jnp.logical_and(side == value, (core == 1 - value) == held)
+            pl.when(here)(functools.partial(fill, value, source))
 
 
 def fill_pair(g, core, slabs, pair):
@@ -383,18 +393,28 @@
         square[n * g.size : (n + 1) * g.size, :] = row_of(n)
 
 
-def square_kernel(g, keep, far, early_left, left, far_left, early, late, *refs):
+def sum_kernel(g, early_left, late_left, early, late, out):
+    side, core = layer_index() // 2, layer_index() % 2
+    first, (_, cols) = group_first(g, side, "B"), g.group("B")
+    out[...] = dot(early_left[...], window_of(g, core, early, first, cols))
+    out[...] += dot(late_left[...], window_of(g, core, late, first, cols))
+
+
+def square_kernel(g, keep, far, far_beside, total, far_left, *refs):
     square, inner = refs
     side, core = layer_index() // 2, layer_index() % 2
+    half = g.size // 2
 
     def gather(side):
         for k, t in enumerate(g.inner_rows(side, "far")):
-            parts = [] if t is None else message_part(g, side, FAR_THIN, t, far, g.size)
-            place_parts(g, inner, k * g.size, g.size, t or 0, side, parts)
+            for q, piece in enumerate((far, far_beside)):
+                at = pl.multiple_of(k * g.size + half * (core ^ q), half)
+                parts = [] if t is None else message_part(g, side, FAR_THIN, t, piece, half)
+                place_parts(g, inner, at, half, t or 0, side, parts)
 
     for value in (0, 1):
         pl.when(side == value)(functools.partial(gather, value))
-    row_of = square_of(g, "B", side, core, keep, [early_left, left, far_left], [early, late, inner])
+    row_of = square_of(g, "B", side, core, keep, [far_left], [inner], total[...])
     for n in range(g.group("B")[0]):
         square[n * g.size : (n + 1) * g.size, :] = row_of(n)
 
@@ -519,29 +539,74 @@
         )
 
 
-def last_kernel(g, keep, *refs):
-    squares, inners, (partial, done, out, band, rows, sems, *lefts) = refs[:2], refs[2:4], refs[4:]
+def slab_early(g, slab):
+    side = 1 - slab // 2
+    rows = group_rows(g, 1 - side, "B")
+    early = g.inner_rows(side, "early")
+    lo, hi = rows[0] - g.reach_low + g.slab * slab, rows[-1] - g.reach_low + g.slab * (slab + 1)
+    met = [k for k, t in enumerate(early) if lo <= t < hi]
+    count = even_up(len(rows) + g.slab - 1)
+    return min(even_down(met[0]), len(early) - count), count
+
+
+def slab_part(g, slab, square, early, far, lefts):
+    side, core = layer_index() // 2, layer_index() % 2
+    _, width = g.group("B")
+    far_starts, far_count = far_span(g, "B")
+
+    def gather(slab):
+        here = 1 - slab // 2
+        rows = group_rows(g, 1 - here, "B")
+        start, count = slab_early(g, slab)
+        far_start = far_starts[here]
+        lists = (
+            g.inner_rows(here, "early")[start : start + count],
+            g.inner_rows(here, "far")[far_start : far_start + far_count],
+        )
+        for dst, inner_rows in zip(lefts, lists):
+            left_rows(g, dst, inner_rows, rows, square, 0, g.slab * slab, g.slab)
+
+    start = jnp.int32(0)
+    for value in range(g.layers):
+        pl.when(slab == value)(functools.partial(gather, value))
+        start = jnp.where(slab == value, slab_early(g, value)[0], start)
+    count = slab_early(g, 0)[1]
+    first = group_first(g, 1 - side, "B")
+    at = lambda start, count: pl.ds(pl.multiple_of(start * g.size, 2 * g.size), count * g.size)
+    rights = early.at[at(start, count), :], far.at[at(by_side(side, far_starts), far_count), :]
+    windows = [window_of(g, core, right, first, width) for right in rights]
+    return first, lambda rows: sum(dot(left[rows, :], window) for left, window in zip(lefts, windows))
+
+
+def slab_kernel(g, square, early, far, out, *lefts):
+    out[...] = slab_part(g, layer_index() ^ 2, square, early, far, lefts)[1](slice(None))
+
+
+def last_kernel(g, keep, square, early, far, partial, done, total, *refs):
+    out, rows, sems, *lefts = refs
     side = layer_index() // 2
     copies = [pltpu.make_async_copy(done, out.at[band_rows(g, 1 - side, "A"), :], sems.at[0])]
     copies[0].start()
-    first, product = other_part(g, layer_index(), "B", squares, inners, band, lefts)
+    first, product = slab_part(g, layer_index() ^ 3, square, early, far, lefts)
     count = g.group("B")[0]
     step = count // 2
-    for n in range(count):
-        rows[n * g.size : (n + 1) * g.size, :] = partial[block_rows(g, first + n), :] - 2.0 * (
-            own_columns(g, product, n) * keep[pl.ds(first + n, 1), :]
-        )
-        if n + 1 in (step, count):
-            begin, end = (0 if n + 1 == step else step) * g.size, (n + 1) * g.size
-            to = pl.ds(pl.multiple_of(first * g.size + begin, g.size), end - begin)
-            copies.append(pltpu.make_async_copy(rows.at[begin:end, :], out.at[to, :], sems.at[len(copies)]))
-            copies[-1].start()
+    for begin in range(0, count, step):
+        here = slice(begin * g.size, (begin + step) * g.size)
+        part = product(here) + total[here, :]
+        for n in range(begin, begin + step):
+            value = part[(n - begin) * g.size : (n - begin + 1) * g.size, n * g.size : (n + g.slab) * g.size]
+            rows[n * g.size : (n + 1) * g.size, :] = partial[block_rows(g, first + n), :] - 2.0 * (
+                value * keep[pl.ds(first + n, 1), :]
+            )
+        to = pl.ds(pl.multiple_of((first + begin) * g.size, g.size), step * g.size)
+        copies.append(pltpu.make_async_copy(rows.at[here, :], out.at[to, :], sems.at[len(copies)]))
+        copies[-1].start()
     for copy in copies:
         copy.wait()
 
 
-def call(kernel, out_shape, scratch, *args, after=(), place=VMEM):
-    specs = [VMEM] * len(args) + [pl.BlockSpec(memory_space=pl.ANY)] * len(after)
+def call(kernel, out_shape, scratch, *args, after=(), placed=(), place=VMEM):
+    specs = [VMEM] * len(args) + [pl.BlockSpec(memory_space=pl.ANY)] * len(after) + [HBM] * len(placed)
     return pl.pallas_call(
         kernel,
         out_shape=out_shape,
@@ -550,16 +615,12 @@
         scratch_shapes=scratch,
         compiler_params=pltpu.CompilerParams(vmem_limit_bytes=LIMIT),
         cost_estimate=pl.CostEstimate(flops=0, bytes_accessed=0, transcendentals=0),
-    )(*args, *after)
+    )(*args, *after, *placed)
 
 
 def body(density, pattern):
     layers, ring = lax.axis_size("layer"), lax.axis_size("row")
     g = Geometry(*density.shape, *pattern.shape, layers)
-    keep = call(
-        functools.partial(keep_kernel, g),
-        jax.ShapeDtypeStruct(((g.rows + 7) // 8 * 8, density.shape[1]), jnp.float32), [], pattern.T,
-    )
     rows_dev, cols = density.shape
     bf16 = functools.partial(jax.ShapeDtypeStruct, dtype=jnp.bfloat16)
     scratch = lambda *shape: pltpu.VMEM(shape, jnp.bfloat16)
@@ -582,7 +643,13 @@
     def put_after(value, *after):
         return call(pass_kernel, bf16(value.shape), [], value, after=after)
 
-    masked = call(functools.partial(mask_kernel, g), bf16(slab), [], density, keep)
+    sources = [pltpu.with_memory_space_constraint(value, pltpu.HBM) for value in (density, pattern.T)]
+    masked, keep = call(
+        functools.partial(mask_kernel, g),
+        [bf16(slab), jax.ShapeDtypeStruct(((g.rows + 7) // 8 * 8, cols), jnp.float32)],
+        [scratch(*slab), pltpu.VMEM(pattern.T.shape, pattern.dtype), pltpu.SemaphoreType.DMA((2,))],
+        placed=sources,
+    )
     thin = send(masked, NEAR_THIN)
     other = swap(masked, 2)
     beside = swap(masked, 1)
@@ -619,11 +686,13 @@
         ],
         masked, beside, other, swap(other, 1), thin, swap(thin, 1),
     )
+    far_beside = swap(far_wide, 1)
     far_thin = call(
-        functools.partial(pass_far_kernel, g), bf16(message_shape(g, FAR_THIN)), [], far_wide,
-    )
-    far_thin = lax.ppermute(far_thin, "layer", [(1, 2), (2, 1)])
-    pieces = sum(([value, swap(value, 1)] for value in (crossed, wide, far_wide)), [])
+        functools.partial(far_thin_kernel, g),
+        bf16(message_shape(g, FAR_THIN)), [], far_wide, far_beside, after=(sum_a,),
+    )
+    far_thin = swap(far_thin, 2)
+    pieces = [crossed, swap(crossed, 1), wide, swap(wide, 1), far_wide, far_beside]
     square_a, inner_late = call(
         functools.partial(late_kernel, g),
         [bf16((high_a, cols)), bf16((late, span))],
@@ -631,11 +700,13 @@
         keep, *pieces, sum_a, late_a,
     )
     across_a, beside_a = swap(square_a, 2), swap(square_a, 1)
+    sum_b = call(
+        functools.partial(sum_kernel, g), f32((high_b, wide_b)), [], left_b, late_b, inner_early, inner_late
+    )
     square_b, inner_far = call(
         functools.partial(square_kernel, g),
-        [bf16((high_b, cols)), bf16((far, span))],
-        [],
-        keep, far_thin, left_b, late_b, far_b, inner_early, inner_late,
+        [bf16((high_b, cols)), bf16((far, span))], [],
+        keep, far_thin, swap(far_thin, 1), sum_b, far_b,
     )
     across_b, beside_b = swap(square_b, 2), swap(square_b, 1)
     partial = call(
@@ -650,15 +721,15 @@
         keep, across_a, swap(across_a, 1), inner_early, inner_far, partial,
     )
     across_b = put_after(across_b, done)
+    lefts = [scratch(high_b, n * g.size) for n in (slab_early(g, 0)[1], far_span(g, "B")[1])]
+    total = call(
+        functools.partial(slab_kernel, g), f32((high_b, wide_b)), lefts, across_b, inner_early, inner_far
+    )
     return call(
         functools.partial(last_kernel, g),
         f32(slab),
-        [
-            scratch(high_b, 2 * cols), pltpu.VMEM((high_b, cols), jnp.float32),
-            pltpu.SemaphoreType.DMA((3,)),
-        ]
-        + left_scratch(g, "B", g.group("B")[0]),
-        keep, across_b, swap(across_b, 1), inner_early, inner_far, partial, done,
+        [pltpu.VMEM((high_b, cols), jnp.float32), pltpu.SemaphoreType.DMA((3,))] + lefts,
+        keep, swap(across_b, 1), inner_early, inner_far, partial, done, total,
         place=HBM,
     )
 

time: 67.6 us -> 65.9 us (0.975)
  starting transfers between devices: 18.2 us -> 15.3 us
  Pallas kernels: 14.3 us -> 16.2 us
  local copies, waits for them, and re-layouts: 1.77 us -> 0 us
  waiting for transfers between devices: 32.7 us -> 33.9 us
    ppermute x14 -> x16, starting transfers between devices: 10.9 us -> 8.64 us  [swap(): return lax.ppermute(value, 'layer', [(s, s ^ bit) for s in range(layers)])]
    pallas_call x12 -> x13, Pallas kernels: 14.3 us -> 16.2 us  [call(): pl.pallas_call(kernel, out_shape=out_shape, in_specs=specs, out_specs=jax...]
    unnamed x4 -> x0, local copies, waits for them, and re-layouts: 1.77 us -> none
    ppermute x14 -> x16, waiting for transfers between devices: 19 us -> 20.2 us  [swap(): return lax.ppermute(value, 'layer', [(s, s ^ bit) for s in range(layers)])]
  transfers between devices with their start and end apart: 19 -> 20, of which waited for: 6 -> 7; matrix products, arithmetic and copies ran while one was open for 0% -> 0% of each run, Pallas kernels for 17% -> 20%
where the time goes in v4:
time: 65.9 us; the launch traced here: 65.7 us
  waiting for transfers between devices  33.9 us (51%)
  Pallas kernels  16.2 us (25%)
  starting transfers between devices  15.3 us (23%)
    ppermute x16, waiting for transfers between devices, swap(): return lax.ppermute(value, 'layer', [(s, s ^ bit) for s in range(layers)])  20.2 us
    pallas_call x13, Pallas kernels, call(): pl.pallas_call(kernel, out_shape=out_shape, in_specs=specs, out_specs=jax...  16.2 us
    ppermute x3, waiting for transfers between devices, send(): return lax.ppermute(value, ('layer', 'row'), pairs)  13.8 us
    ppermute x16, starting transfers between devices, swap(): return lax.ppermute(value, 'layer', [(s, s ^ bit) for s in range(layers)])  8.64 us
    ppermute x3, starting transfers between devices, send(): return lax.ppermute(value, ('layer', 'row'), pairs)  6.37 us
  transfers between devices with their start and end apart: 20, of which 7 were waited for; matrix products, arithmetic and copies ran while one was open for 0% of the time, Pallas kernels for 20%

profile of v4, /device:TPU:0, one launch (start us, length us, event | category | flops | bytes accessed | tf_op | source)
XLA Modules:
  0.0 65.7 jit_solution(17921620308454291926)
XLA Ops:
  0.0 1.2 %shard_map.28 = (bf16[640,512]{1,0:T(8,128)(2,1)S(1)}, f32[16,512]{1,0:T(8,128)S(1)}) custom-call(bf16[640,512]{1,0:T(8,128)(2,1)} %density_ref.1, s32[8,10]{1,0:T(8,128)} %bitcast.1), custom_call_target="tpu_custom_call" | custom-call | tf_op jit(solution)/shard_map/pallas_call | solution.py:610
  1.2 0.5 collective-permute-start
  1.7 5.6 %collective-permute-start.3 = (bf16[640,512]{1,0:T(8,128)(2,1)S(1)}, bf16[640,512]{1,0:T(8,128)(2,1)S(1)}, u32[]{:S(2)}, u32[]{:S(2)}) collective-permute-start(bf16[640,512]{1,0:T(8,128)(2,1)S(1)} %get-tuple-element.22.own_ref.own), channel_id=1, source_target_pairs={{0,7},{1,0},{2,1},{3,2},{4,3},{5,4},{6,5},{7,6},{8,15},{9,8},{10,9... | collective-permute-start | bytes 1966088 | tf_op jit(solution)/shard_map/ppermute | solution.py:638
  7.3 0.0 collective-permute-start.2
  7.3 0.0 collective-permute-done.beside_ref.beside
  7.3 0.1 shard_map.29
  7.4 0.7 %collective-permute-start.1 = (bf16[160,1408]{1,0:T(8,128)(2,1)S(1)}, bf16[160,1408]{1,0:T(8,128)(2,1)S(1)}, u32[]{:S(2)}, u32[]{:S(2)}) collective-permute-start(bf16[160,1408]{1,0:T(8,128)(2,1)S(1)} %get-tuple-element.23.own_ref), channel_id=1, source_target_pairs={{1,3},{3,5},{5,7},{7,1},{9,11},{11,13},{13,15},{15,9},{16,22},{18,... | collective-permute-start | bytes 1351688 | tf_op jit(solution)/shard_map/ppermute | solution.py:638
  8.1 13.8 %collective-permute-done.3.after_ref.refs_2_ = bf16[640,512]{1,0:T(8,128)(2,1)S(1)} collective-permute-done((bf16[640,512]{1,0:T(8,128)(2,1)S(1)}, bf16[640,512]{1,0:T(8,128)(2,1)S(1)}, u32[]{:S(2)}, u32[]{:S(2)}) %collective-permute-start.3) | collective-permute-done | bytes 655392 | tf_op jit(solution)/shard_map/ppermute | solution.py:638
  21.9 2.2 %collective-permute-start.10 = (bf16[640,512]{1,0:T(8,128)(2,1)S(1)}, bf16[640,512]{1,0:T(8,128)(2,1)S(1)}, u32[]{:S(2)}, u32[]{:S(2)}) collective-permute-start(bf16[640,512]{1,0:T(8,128)(2,1)S(1)} %collective-permute-done.3.after_ref.refs_2_), channel_id=1, source_target_pairs={{0,16},{8,24},{16,0},{24,8},{1,17},{9,25},{17,1},{25,9},{2,18},{10... | collective-permute-start | bytes 1966088 | tf_op jit(solution)/shard_map/ppermute | solution.py:629
  24.1 0.0 collective-permute-done.2.other_ref.refs_0_
  24.2 0.0 collective-permute-done.1.relayed_ref
  24.2 0.1 shard_map.30
  24.2 0.1 collective-permute-start.4
  24.3 0.3 collective-permute-start.12
  24.6 0.0 collective-permute-start.7
  24.6 0.5 collective-permute-start.6
  25.1 13.8 %collective-permute-done.10.refs_0_ = bf16[640,512]{1,0:T(8,128)(2,1)S(1)} collective-permute-done((bf16[640,512]{1,0:T(8,128)(2,1)S(1)}, bf16[640,512]{1,0:T(8,128)(2,1)S(1)}, u32[]{:S(2)}, u32[]{:S(2)}) %collective-permute-start.10) | collective-permute-done | bytes 655392 | tf_op jit(solution)/shard_map/ppermute | solution.py:629
  38.8 0.0 collective-permute-start.11
  38.8 0.0 collective-permute-done.4.far_own.refs_4_
  38.8 0.5 collective-permute-start.5
  39.3 0.0 collective-permute-done.12.refs_2_
  39.4 0.1 collective-permute-start.13
  39.4 0.0 collective-permute-done.7.refs_3_
  39.4 0.0 collective-permute-done.6.refs_1_
  39.4 2.0 %shard_map.31 = (bf16[1280,1664]{1,0:T(8,128)(2,1)S(1)}, f32[256,768]{1,0:T(8,128)S(1)}, bf16[384,1280]{1,0:T(8,128)(2,1)S(1)}, bf16[256,1024]{1,0:T(8,128)(2,1)...) custom-call(bf16[640,512]{1,0:T(8,128)(2,1)S(1)} %get-tuple-element.22.own_ref.own, ...), custom_call_target="tpu_custom_call" | custom-call | tf_op jit(solution)/shard_map/pallas_call | solution.py:610
  41.5 0.2 collective-permute-done.5.far_beside.refs_5_
  41.7 1.8 %collective-permute-start.8 = (bf16[96,384]{1,0:T(8,128)(2,1)S(1)}, bf16[96,384]{1,0:T(8,128)(2,1)S(1)}, u32[]{:S(2)}, u32[]{:S(2)}) collective-permute-start(bf16[96,384]{1,0:T(8,128)(2,1)S(1)} %shard_map.32), channel_id=1, source_target_pairs={{0,16},{8,24},{16,0},{24,8},{1,17},{9,25},{17,1},{25,9},{2,18},{10... | collective-permute-start | bytes 221192 | tf_op jit(solution)/shard_map/ppermute | solution.py:629
  43.5 0.0 collective-permute-done.11.refs_1_
  43.5 0.0 collective-permute-done.13.refs_3_
  43.5 1.4 %shard_map.33 = (bf16[256,512]{1,0:T(8,128)(2,1)S(1)}, bf16[1024,1664]{1,0:T(8,128)(2,1)S(1)}) custom-call(f32[16,512]{1,0:T(8,128)S(1)} %get-tuple-element.21.keep, bf16[640,512]{1,0:T(8,128)(2,1)S(1)} %collective-permute-done.10.refs_0_, bf16[640,512]{1,0:T(8,128)(2,1)S(1)} %collective-permute-done.11.refs_1_, ...), custom_call_target="tpu_custom_call" | custom-call | tf_op jit(solution)/shard_map/pallas_call | solution.py:610
  44.9 0.6 collective-permute-start.15
  45.4 0.9 %collective-permute-done.8.far = bf16[96,384]{1,0:T(8,128)(2,1)S(1)} collective-permute-done((bf16[96,384]{1,0:T(8,128)(2,1)S(1)}, bf16[96,384]{1,0:T(8,128)(2,1)S(1)}, u32[]{:S(2)}, u32[]{:S(2)}) %collective-permute-start.8) | collective-permute-done | bytes 73760 | tf_op jit(solution)/shard_map/ppermute | solution.py:629
  46.3 0.0 collective-permute-start.9
  46.3 2.0 %shard_map.34.total = f32[384,896]{1,0:T(8,128)S(1)} custom-call(bf16[384,1280]{1,0:T(8,128)(2,1)S(1)} %get-tuple-element.27.early_left, bf16[384,1024]{1,0:T(8,128)(2,1)S(1)} %get-tuple-element.28.late_left, bf16[1280,1664]{1,0:T(8,128)(2,1)S(1)} %get-tuple-element.29.early.refs_4_.refs_2_, bf16[1024,1664]{1,0:T(8,128)(2,1)S(1)} %get-tuple-element.32.late.refs_5_), custom_call_target="tpu_custom_call" | custom-call | tf_op jit(solution)/shard_map/pallas_call | solution.py:610
  48.3 0.8 %shard_map.35 = (bf16[384,512]{1,0:T(8,128)(2,1)S(1)}, bf16[384,1664]{1,0:T(8,128)(2,1)S(1)}) custom-call(f32[16,512]{1,0:T(8,128)S(1)} %get-tuple-element.21.keep, bf16[96,384]{1,0:T(8,128)(2,1)S(1)} %collective-permute-done.8.far, bf16[96,384]{1,0:T(8,128)(2,1)S(1)} %collective-permute-done.9.far_beside, f32[384,896]{1,0:T(8,128)S(1)} %shard_map.34.total, ...), custom_call_target="tpu_custom_call" | custom-call | tf_op jit(solution)/shard_map/pallas_call | solution.py:610
  49.1 0.6 collective-permute-start.18
  49.7 1.8 %collective-permute-start.14 = (bf16[384,512]{1,0:T(8,128)(2,1)S(1)}, bf16[384,512]{1,0:T(8,128)(2,1)S(1)}, u32[]{:S(2)}, u32[]{:S(2)}) collective-permute-start(bf16[384,512]{1,0:T(8,128)(2,1)S(1)} %get-tuple-element.34.refs_2_), channel_id=1, source_target_pairs={{0,16},{8,24},{16,0},{24,8},{1,17},{9,25},{17,1},{25,9},{2,18},{10... | collective-permute-start | bytes 1179656 | tf_op jit(solution)/shard_map/ppermute | solution.py:629
  51.4 2.6 %collective-permute-done.15.refs_0_ = bf16[256,512]{1,0:T(8,128)(2,1)S(1)} collective-permute-done((bf16[256,512]{1,0:T(8,128)(2,1)S(1)}, bf16[256,512]{1,0:T(8,128)(2,1)S(1)}, u32[]{:S(2)}, u32[]{:S(2)}) %collective-permute-start.15) | collective-permute-done | bytes 262176 | tf_op jit(solution)/shard_map/ppermute | solution.py:629
  54.1 0.0 collective-permute-start.16
  54.1 0.0 collective-permute-done.17.refs_1_
  54.1 0.0 collective-permute-done.18.refs_3_
  54.1 4.1 %shard_map.36.refs_4_.partial = f32[640,512]{1,0:T(8,128)S(1)} custom-call(f32[16,512]{1,0:T(8,128)S(1)} %get-tuple-element.21.keep, bf16[256,512]{1,0:T(8,128)(2,1)S(1)} %get-tuple-element.35.refs_0_, bf16[256,512]{1,0:T(8,128)(2,1)S(1)} %collective-permute-done.17.refs_1_, bf16[384,512]{1,0:T(8,128)(2,1)S(1)} %get-tuple-element.34.refs_2_, ...), custom_call_target="tpu_custom_call" | custom-call | tf_op jit(solution)/shard_map/pallas_call | solution.py:610
  58.2 1.2 %shard_map.37.refs_0_.done = f32[256,512]{1,0:T(8,128)S(1)} custom-call(f32[16,512]{1,0:T(8,128)S(1)} %get-tuple-element.21.keep, bf16[256,512]{1,0:T(8,128)(2,1)S(1)} %collective-permute-done.15.refs_0_, bf16[256,512]{1,0:T(8,128)(2,1)S(1)} %collective-permute-done.16.refs_1_, bf16[1280,1664]{1,0:T(8,128)(2,1)S(1)} %get-tuple-element.29.early.refs_4_.refs_2_, ...), custom_call_target="tpu_custom_call" | custom-call | tf_op jit(solution)/shard_map/pallas_call | solution.py:610
  59.4 2.3 %collective-permute-done.14.in_ref = bf16[384,512]{1,0:T(8,128)(2,1)S(1)} collective-permute-done((bf16[384,512]{1,0:T(8,128)(2,1)S(1)}, bf16[384,512]{1,0:T(8,128)(2,1)S(1)}, u32[]{:S(2)}, u32[]{:S(2)}) %collective-permute-start.14) | collective-permute-done | bytes 393248 | tf_op jit(solution)/shard_map/ppermute | solution.py:629
  61.7 0.1 collective-permute-start.19
  61.8 1.3 %shard_map.39.total = f32[384,896]{1,0:T(8,128)S(1)} custom-call(bf16[384,512]{1,0:T(8,128)(2,1)S(1)} %shard_map.38.square, bf16[1280,1664]{1,0:T(8,128)(2,1)S(1)} %get-tuple-element.29.early.refs_4_.refs_2_, bf16[384,1664]{1,0:T(8,128)(2,1)S(1)} %get-tuple-element.36.refs_3_.far), custom_call_target="tpu_custom_call" | custom-call | tf_op jit(solution)/shard_map/pallas_call | solution.py:610
  63.1 0.4 collective-permute-done.19.square
  63.5 2.0 %shard_map.40 = f32[640,512]{1,0:T(8,128)} custom-call(f32[16,512]{1,0:T(8,128)S(1)} %get-tuple-element.21.keep, bf16[384,512]{1,0:T(8,128)(2,1)S(1)} %collective-permute-done.19.square, bf16[1280,1664]{1,0:T(8,128)(2,1)S(1)} %get-tuple-element.29.early.refs_4_.refs_2_, bf16[384,1664]{1,0:T(8,128)(2,1)S(1)} %get-tuple-element.36.refs_3_.far, ...), custom_call_target="tpu_custom_call" | custom-call | tf_op jit(solution)/shard_map/pallas_call | solution.py:610
  (5 shorter events, 0.1 us)
Async XLA Ops:
  1.2 6.1 %collective-permute-start = (bf16[640,512]{1,0:T(8,128)(2,1)S(1)}, bf16[640,512]{1,0:T(8,128)(2,1)S(1)}, u32[]{:S(2)}, u32[]{:S(2)}) collective-permute-start(bf16[640,512]{1,0:T(8,128)(2,1)S(1)} %get-tuple-element.22.own_ref.own), channel_id=1, source_target_pairs={{0,8},{8,0},{16,24},{24,16},{1,9},{9,1},{17,25},{25,17},{2,10},{10... | collective-permute-start | bytes 1966088 | tf_op jit(solution)/shard_map/ppermute | solution.py:629
  1.7 20.2 %collective-permute-start.3 = (bf16[640,512]{1,0:T(8,128)(2,1)S(1)}, bf16[640,512]{1,0:T(8,128)(2,1)S(1)}, u32[]{:S(2)}, u32[]{:S(2)}) collective-permute-start(bf16[640,512]{1,0:T(8,128)(2,1)S(1)} %get-tuple-element.22.own_ref.own), channel_id=1, source_target_pairs={{0,7},{1,0},{2,1},{3,2},{4,3},{5,4},{6,5},{7,6},{8,15},{9,8},{10,9... | collective-permute-start | bytes 1966088 | tf_op jit(solution)/shard_map/ppermute | solution.py:638
  7.3 16.8 %collective-permute-start.2 = (bf16[640,512]{1,0:T(8,128)(2,1)S(1)}, bf16[640,512]{1,0:T(8,128)(2,1)S(1)}, u32[]{:S(2)}, u32[]{:S(2)}) collective-permute-start(bf16[640,512]{1,0:T(8,128)(2,1)S(1)} %get-tuple-element.22.own_ref.own), channel_id=1, source_target_pairs={{0,16},{8,24},{16,0},{24,8},{1,17},{9,25},{17,1},{25,9},{2,18},{10... | collective-permute-start | bytes 1966088 | tf_op jit(solution)/shard_map/ppermute | solution.py:629
  7.4 16.7 %collective-permute-start.1 = (bf16[160,1408]{1,0:T(8,128)(2,1)S(1)}, bf16[160,1408]{1,0:T(8,128)(2,1)S(1)}, u32[]{:S(2)}, u32[]{:S(2)}) collective-permute-start(bf16[160,1408]{1,0:T(8,128)(2,1)S(1)} %get-tuple-element.23.own_ref), channel_id=1, source_target_pairs={{1,3},{3,5},{5,7},{7,1},{9,11},{11,13},{13,15},{15,9},{16,22},{18,... | collective-permute-start | bytes 1351688 | tf_op jit(solution)/shard_map/ppermute | solution.py:638
  21.9 16.9 %collective-permute-start.10 = (bf16[640,512]{1,0:T(8,128)(2,1)S(1)}, bf16[640,512]{1,0:T(8,128)(2,1)S(1)}, u32[]{:S(2)}, u32[]{:S(2)}) collective-permute-start(bf16[640,512]{1,0:T(8,128)(2,1)S(1)} %collective-permute-done.3.after_ref.refs_2_), channel_id=1, source_target_pairs={{0,16},{8,24},{16,0},{24,8},{1,17},{9,25},{17,1},{25,9},{2,18},{10... | collective-permute-start | bytes 1966088 | tf_op jit(solution)/shard_map/ppermute | solution.py:629
  24.2 14.6 %collective-permute-start.4 = (bf16[480,512]{1,0:T(8,128)(2,1)S(1)}, bf16[480,512]{1,0:T(8,128)(2,1)S(1)}, u32[]{:S(2)}, u32[]{:S(2)}) collective-permute-start(bf16[480,512]{1,0:T(8,128)(2,1)S(1)} %get-tuple-element.25), channel_id=1, source_target_pairs={{0,2},{1,3},{2,4},{3,5},{4,6},{5,7},{6,0},{7,1},{8,10},{9,11},{10,... | collective-permute-start | bytes 1474568 | tf_op jit(solution)/shard_map/ppermute | solution.py:638
  24.3 15.1 %collective-permute-start.12 = (bf16[160,1408]{1,0:T(8,128)(2,1)S(1)}, bf16[160,1408]{1,0:T(8,128)(2,1)S(1)}, u32[]{:S(2)}, u32[]{:S(2)}) collective-permute-start(bf16[160,1408]{1,0:T(8,128)(2,1)S(1)} %get-tuple-element.30), channel_id=1, source_target_pairs={{0,1},{1,0},{2,3},{3,2},{4,5},{5,4},{6,7},{7,6},{8,9},{9,8},{10,11... | collective-permute-start | bytes 1351688 | tf_op jit(solution)/shard_map/ppermute | solution.py:669
  24.6 14.9 %collective-permute-start.7 = (bf16[640,512]{1,0:T(8,128)(2,1)S(1)}, bf16[640,512]{1,0:T(8,128)(2,1)S(1)}, u32[]{:S(2)}, u32[]{:S(2)}) collective-permute-start(bf16[640,512]{1,0:T(8,128)(2,1)S(1)} %collective-permute-done.3.after_ref.refs_2_), channel_id=1, source_target_pairs={{0,8},{8,0},{16,24},{24,16},{1,9},{9,1},{17,25},{25,17},{2,10},{10... | collective-permute-start | bytes 1966088 | tf_op jit(solution)/shard_map/ppermute | solution.py:629
  24.6 14.9 %collective-permute-start.6 = (bf16[640,512]{1,0:T(8,128)(2,1)S(1)}, bf16[640,512]{1,0:T(8,128)(2,1)S(1)}, u32[]{:S(2)}, u32[]{:S(2)}) collective-permute-start(bf16[640,512]{1,0:T(8,128)(2,1)S(1)} %collective-permute-done.2.other_ref.refs_0_), channel_id=1, source_target_pairs={{0,8},{8,0},{16,24},{24,16},{1,9},{9,1},{17,25},{25,17},{2,10},{10... | collective-permute-start | bytes 1966088 | tf_op jit(solution)/shard_map/ppermute | solution.py:629
  38.8 4.6 %collective-permute-start.11 = (bf16[640,512]{1,0:T(8,128)(2,1)S(1)}, bf16[640,512]{1,0:T(8,128)(2,1)S(1)}, u32[]{:S(2)}, u32[]{:S(2)}) collective-permute-start(bf16[640,512]{1,0:T(8,128)(2,1)S(1)} %collective-permute-done.10.refs_0_), channel_id=1, source_target_pairs={{0,8},{8,0},{16,24},{24,16},{1,9},{9,1},{17,25},{25,17},{2,10},{10... | collective-permute-start | bytes 1966088 | tf_op jit(solution)/shard_map/ppermute | solution.py:629
  38.8 2.8 %collective-permute-start.5 = (bf16[480,512]{1,0:T(8,128)(2,1)S(1)}, bf16[480,512]{1,0:T(8,128)(2,1)S(1)}, u32[]{:S(2)}, u32[]{:S(2)}) collective-permute-start(bf16[480,512]{1,0:T(8,128)(2,1)S(1)} %collective-permute-done.4.far_own.refs_4_), channel_id=1, source_target_pairs={{0,8},{8,0},{16,24},{24,16},{1,9},{9,1},{17,25},{25,17},{2,10},{10... | collective-permute-start | bytes 1474568 | tf_op jit(solution)/shard_map/ppermute | solution.py:629
  39.4 4.1 %collective-permute-start.13 = (bf16[160,1408]{1,0:T(8,128)(2,1)S(1)}, bf16[160,1408]{1,0:T(8,128)(2,1)S(1)}, u32[]{:S(2)}, u32[]{:S(2)}) collective-permute-start(bf16[160,1408]{1,0:T(8,128)(2,1)S(1)} %collective-permute-done.12.refs_2_), channel_id=1, source_target_pairs={{0,8},{8,0},{16,24},{24,16},{1,9},{9,1},{17,25},{25,17},{2,10},{10... | collective-permute-start | bytes 1351688 | tf_op jit(solution)/shard_map/ppermute | solution.py:629
  41.7 4.6 %collective-permute-start.8 = (bf16[96,384]{1,0:T(8,128)(2,1)S(1)}, bf16[96,384]{1,0:T(8,128)(2,1)S(1)}, u32[]{:S(2)}, u32[]{:S(2)}) collective-permute-start(bf16[96,384]{1,0:T(8,128)(2,1)S(1)} %shard_map.32), channel_id=1, source_target_pairs={{0,16},{8,24},{16,0},{24,8},{1,17},{9,25},{17,1},{25,9},{2,18},{10... | collective-permute-start | bytes 221192 | tf_op jit(solution)/shard_map/ppermute | solution.py:629
  44.9 9.2 %collective-permute-start.15 = (bf16[256,512]{1,0:T(8,128)(2,1)S(1)}, bf16[256,512]{1,0:T(8,128)(2,1)S(1)}, u32[]{:S(2)}, u32[]{:S(2)}) collective-permute-start(bf16[256,512]{1,0:T(8,128)(2,1)S(1)} %get-tuple-element.35.refs_0_), channel_id=1, source_target_pairs={{0,16},{8,24},{16,0},{24,8},{1,17},{9,25},{17,1},{25,9},{2,18},{10... | collective-permute-start | bytes 786440 | tf_op jit(solution)/shard_map/ppermute | solution.py:629
  46.3 2.0 %collective-permute-start.9 = (bf16[96,384]{1,0:T(8,128)(2,1)S(1)}, bf16[96,384]{1,0:T(8,128)(2,1)S(1)}, u32[]{:S(2)}, u32[]{:S(2)}) collective-permute-start(bf16[96,384]{1,0:T(8,128)(2,1)S(1)} %collective-permute-done.8.far), channel_id=1, source_target_pairs={{0,8},{8,0},{16,24},{24,16},{1,9},{9,1},{17,25},{25,17},{2,10},{10... | collective-permute-start | bytes 221192 | tf_op jit(solution)/shard_map/ppermute | solution.py:629
  49.1 5.0 %collective-permute-start.18 = (bf16[384,512]{1,0:T(8,128)(2,1)S(1)}, bf16[384,512]{1,0:T(8,128)(2,1)S(1)}, u32[]{:S(2)}, u32[]{:S(2)}) collective-permute-start(bf16[384,512]{1,0:T(8,128)(2,1)S(1)} %get-tuple-element.34.refs_2_), channel_id=1, source_target_pairs={{0,8},{8,0},{16,24},{24,16},{1,9},{9,1},{17,25},{25,17},{2,10},{10... | collective-permute-start | bytes 1179656 | tf_op jit(solution)/shard_map/ppermute | solution.py:629
  49.7 12.0 %collective-permute-start.14 = (bf16[384,512]{1,0:T(8,128)(2,1)S(1)}, bf16[384,512]{1,0:T(8,128)(2,1)S(1)}, u32[]{:S(2)}, u32[]{:S(2)}) collective-permute-start(bf16[384,512]{1,0:T(8,128)(2,1)S(1)} %get-tuple-element.34.refs_2_), channel_id=1, source_target_pairs={{0,16},{8,24},{16,0},{24,8},{1,17},{9,25},{17,1},{25,9},{2,18},{10... | collective-permute-start | bytes 1179656 | tf_op jit(solution)/shard_map/ppermute | solution.py:629
  51.4 2.7 %collective-permute-start.17 = (bf16[256,512]{1,0:T(8,128)(2,1)S(1)}, bf16[256,512]{1,0:T(8,128)(2,1)S(1)}, u32[]{:S(2)}, u32[]{:S(2)}) collective-permute-start(bf16[256,512]{1,0:T(8,128)(2,1)S(1)} %get-tuple-element.35.refs_0_), channel_id=1, source_target_pairs={{0,8},{8,0},{16,24},{24,16},{1,9},{9,1},{17,25},{25,17},{2,10},{10... | collective-permute-start | bytes 786440 | tf_op jit(solution)/shard_map/ppermute | solution.py:629
  54.1 4.1 %collective-permute-start.16 = (bf16[256,512]{1,0:T(8,128)(2,1)S(1)}, bf16[256,512]{1,0:T(8,128)(2,1)S(1)}, u32[]{:S(2)}, u32[]{:S(2)}) collective-permute-start(bf16[256,512]{1,0:T(8,128)(2,1)S(1)} %collective-permute-done.15.refs_0_), channel_id=1, source_target_pairs={{0,8},{8,0},{16,24},{24,16},{1,9},{9,1},{17,25},{25,17},{2,10},{10... | collective-permute-start | bytes 786440 | tf_op jit(solution)/shard_map/ppermute | solution.py:629
  61.7 1.8 %collective-permute-start.19 = (bf16[384,512]{1,0:T(8,128)(2,1)S(1)}, bf16[384,512]{1,0:T(8,128)(2,1)S(1)}, u32[]{:S(2)}, u32[]{:S(2)}) collective-permute-start(bf16[384,512]{1,0:T(8,128)(2,1)S(1)} %shard_map.38.square), channel_id=1, source_target_pairs={{0,8},{8,0},{16,24},{24,16},{1,9},{9,1},{17,25},{25,17},{2,10},{10... | collective-permute-start | bytes 1179656 | tf_op jit(solution)/shard_map/ppermute | solution.py:629

commit v5 on v4

--- a/solution.py
+++ b/solution.py
@@ -321,7 +321,7 @@
 
 def early_kernel(g, own, beside, *refs):
     others, thins = refs[:2], refs[2:4]
-    inner, sum_a, left_b, late_a, late_b, far_b, band, left_a, pair = refs[4:]
+    inner, sum_a, late_a, band, left_a, pair = refs[4:]
     layer = layer_index()
     side, core = layer // 2, layer % 2
     cols = g.slab * g.size
@@ -331,7 +331,7 @@
 
     def gather(side):
         near = g.reached(step_of(side, NEAR_THIN))
-        early, late, far = (g.inner_rows(side, part) for part in ("early", "late", "far"))
+        early, late = (g.inner_rows(side, part) for part in ("early", "late"))
         for k, t in enumerate(early):
             if 0 <= t < g.rows:
                 part = (0, g.offsets, lambda a, b, t=t: band[
@@ -340,10 +340,9 @@
             else:
                 part = pair_part(g, side, pair, (t - near[0]) * g.size, g.size)
             place_parts(g, inner, k * g.size, g.size, t, side, [part])
-        for name, lefts in (("A", ((left_a, early), (late_a, late))), ("B", ((left_b, early), (late_b, late), (far_b, far)))):
-            rows = group_rows(g, side, name)
-            for left, inner_rows in lefts:
-                left_rows(g, left, inner_rows, rows, band, rows[0], 0, g.offsets)
+        rows = group_rows(g, side, "A")
+        for left, inner_rows in ((left_a, early), (late_a, late)):
+            left_rows(g, left, inner_rows, rows, band, rows[0], 0, g.offsets)
 
     for value in (0, 1):
         pl.when(side == value)(functools.partial(gather, value))
@@ -360,41 +359,58 @@
 
 def late_kernel(g, keep, *refs):
     crossed, wides, wide_fars = (refs[2 * n : 2 * n + 2] for n in range(3))
-    total, left, square, inner, pair, far_pair = refs[6:]
+    total, left, square, inner = refs[6:]
     layer = layer_index()
     side, core = layer // 2, layer % 2
     half = g.size // 2
-    fill_pair(g, core, crossed, pair)
-    tail = far_pair.shape[0]
-    fill_pair(g, core, [piece.at[piece.shape[0] - tail :, :] for piece in wide_fars], far_pair)
-
-    def gather(side):
+
+    def slab_parts(side, core, slabs, row, height):
+        base = g.pair * (1 - side)
+        parts = []
+        for c in (0, 1):
+            lo, slab = base + c * g.slab, slabs[core ^ c]
+            parts.append((lo, lo + g.slab, lambda a, b, lo=lo, slab=slab: slab[
+                row : row + height, (a - lo) * g.size : (b - lo) * g.size
+            ]))
+        return parts
+
+    def gather(layer):
+        side, core = layer // 2, layer % 2
         near = g.reached(step_of(side, NEAR_WIDE))
+        tail = wide_fars[0].shape[0] - g.far * g.size
         for k, t in enumerate(g.inner_rows(side, "late")):
             if t is None:
                 inner[k * g.size : (k + 1) * g.size, :] = jnp.zeros((g.size, inner.shape[1]), inner.dtype)
                 continue
             if t in near:
-                name, pieces, source, row = NEAR_WIDE, wides, pair, t - near[0]
+                name, pieces, slabs, row = NEAR_WIDE, wides, crossed, (t - near[0]) * g.size
             else:
-                name, pieces, source = FAR_WIDE, wide_fars, far_pair
-                row = t - step_of(side, FAR_WIDE) * g.rows - cross_rows(g, side)[0]
+                name, pieces, slabs = FAR_WIDE, wide_fars, wide_fars
+                row = tail + (t - step_of(side, FAR_WIDE) * g.rows - cross_rows(g, side)[0]) * g.size
             for q, piece in enumerate(pieces):
                 at = half * (core ^ q)
                 parts = message_part(g, side, name, t, piece, half)
-                parts.append(pair_part(g, 1 - side, source, pl.multiple_of(row * g.size + at, half), half))
+                parts += slab_parts(side, core, slabs, row + at, half)
                 parts.sort(key=lambda part: part[0])
-                place_parts(g, inner, pl.multiple_of(k * g.size + at, half), half, t, side, parts)
-
-    for value in (0, 1):
-        pl.when(side == value)(functools.partial(gather, value))
+                place_parts(g, inner, k * g.size + at, half, t, side, parts)
+
+    for value in range(g.layers):
+        pl.when(layer == value)(functools.partial(gather, value))
     row_of = square_of(g, "A", side, core, keep, [left], [inner], total[...])
     for n in range(g.group("A")[0]):
         square[n * g.size : (n + 1) * g.size, :] = row_of(n)
 
 
-def sum_kernel(g, early_left, late_left, early, late, out):
+def sum_kernel(g, band, early, late, out, far_left, early_left, late_left):
     side, core = layer_index() // 2, layer_index() % 2
+
+    def fill(side):
+        rows = group_rows(g, side, "B")
+        for left, part in ((early_left, "early"), (late_left, "late"), (far_left, "far")):
+            left_rows(g, left, g.inner_rows(side, part), rows, band, rows[0], 0, g.offsets)
+
+    for value in (0, 1):
+        pl.when(side == value)(functools.partial(fill, value))
     first, (_, cols) = group_first(g, side, "B"), g.group("B")
     out[...] = dot(early_left[...], window_of(g, core, early, first, cols))
     out[...] += dot(late_left[...], window_of(g, core, late, first, cols))
@@ -530,15 +546,6 @@
     )
 
 
-def other_kernel(g, keep, *refs):
-    squares, inners, (partial, out, band, *lefts) = refs[:2], refs[2:4], refs[4:]
-    first, product = other_part(g, layer_index(), "A", squares, inners, band, lefts)
-    for n in range(g.group("A")[0]):
-        out[n * g.size : (n + 1) * g.size, :] = partial[block_rows(g, first + n), :] - 2.0 * (
-            own_columns(g, product, n) * keep[pl.ds(first + n, 1), :]
-        )
-
-
 def slab_early(g, slab):
     side = 1 - slab // 2
     rows = group_rows(g, 1 - side, "B")
@@ -549,55 +556,69 @@
     return min(even_down(met[0]), len(early) - count), count
 
 
-def slab_part(g, slab, square, early, far, lefts):
+def slab_rights(g, slab, early, far, out):
     side, core = layer_index() // 2, layer_index() % 2
     _, width = g.group("B")
+    first = group_first(g, 1 - side, "B")
+    start, count = jnp.int32(0), slab_early(g, 0)[1]
+    for value in range(g.layers):
+        start = jnp.where(slab == value, slab_early(g, value)[0], start)
+    far_starts, far_count = far_span(g, "B")
+    split = count * g.size
+    at = lambda start, count: pl.ds(pl.multiple_of(start * g.size, 2 * g.size), count * g.size)
+    out[:split, :] = window_of(g, core, early.at[at(start, count), :], first, width)
+    out[split:, :] = window_of(g, core, far.at[at(by_side(side, far_starts), far_count), :], first, width)
+
+
+def slab_left(g, slab, square, left):
     far_starts, far_count = far_span(g, "B")
 
     def gather(slab):
         here = 1 - slab // 2
-        rows = group_rows(g, 1 - here, "B")
         start, count = slab_early(g, slab)
-        far_start = far_starts[here]
-        lists = (
-            g.inner_rows(here, "early")[start : start + count],
-            g.inner_rows(here, "far")[far_start : far_start + far_count],
-        )
-        for dst, inner_rows in zip(lefts, lists):
-            left_rows(g, dst, inner_rows, rows, square, 0, g.slab * slab, g.slab)
-
-    start = jnp.int32(0)
+        inner_rows = g.inner_rows(here, "early")[start : start + count]
+        inner_rows = inner_rows + g.inner_rows(here, "far")[far_starts[here] : far_starts[here] + far_count]
+        left_rows(g, left, inner_rows, group_rows(g, 1 - here, "B"), square, 0, g.slab * slab, g.slab)
+
     for value in range(g.layers):
         pl.when(slab == value)(functools.partial(gather, value))
-        start = jnp.where(slab == value, slab_early(g, value)[0], start)
-    count = slab_early(g, 0)[1]
-    first = group_first(g, 1 - side, "B")
-    at = lambda start, count: pl.ds(pl.multiple_of(start * g.size, 2 * g.size), count * g.size)
-    rights = early.at[at(start, count), :], far.at[at(by_side(side, far_starts), far_count), :]
-    windows = [window_of(g, core, right, first, width) for right in rights]
-    return first, lambda rows: sum(dot(left[rows, :], window) for left, window in zip(lefts, windows))
-
-
-def slab_kernel(g, square, early, far, out, *lefts):
-    out[...] = slab_part(g, layer_index() ^ 2, square, early, far, lefts)[1](slice(None))
-
-
-def last_kernel(g, keep, square, early, far, partial, done, total, *refs):
-    out, rows, sems, *lefts = refs
+
+
+def other_kernel(g, keep, *refs):
+    squares, inners, (partial, out, straight, beside, band, *lefts) = refs[:2], refs[2:4], refs[4:]
+    first, product = other_part(g, layer_index(), "A", squares, inners, band, lefts)
+    for n in range(g.group("A")[0]):
+        out[n * g.size : (n + 1) * g.size, :] = partial[block_rows(g, first + n), :] - 2.0 * (
+            own_columns(g, product, n) * keep[pl.ds(first + n, 1), :]
+        )
+    for q, right in ((2, straight), (3, beside)):
+        slab_rights(g, layer_index() ^ q, *inners, right)
+
+
+def slab_kernel(g, keep, square, right, partial, out, left):
+    slab_left(g, layer_index() ^ 2, square, left)
+    first = group_first(g, 1 - layer_index() // 2, "B")
+    product = dot(left[...], right[...])
+    for n in range(g.group("B")[0]):
+        out[n * g.size : (n + 1) * g.size, :] = partial[block_rows(g, first + n), :] - 2.0 * (
+            own_columns(g, product, n) * keep[pl.ds(first + n, 1), :]
+        )
+
+
+def last_kernel(g, keep, square, right, partial, done, out, rows, sems, left):
     side = layer_index() // 2
     copies = [pltpu.make_async_copy(done, out.at[band_rows(g, 1 - side, "A"), :], sems.at[0])]
     copies[0].start()
-    first, product = slab_part(g, layer_index() ^ 3, square, early, far, lefts)
-    count = g.group("B")[0]
+    slab_left(g, layer_index() ^ 3, square, left)
+    first, count = group_first(g, 1 - side, "B"), g.group("B")[0]
     step = count // 2
     for begin in range(0, count, step):
         here = slice(begin * g.size, (begin + step) * g.size)
-        part = product(here) + total[here, :]
+        part = dot(left[here, :], right[...])
         for n in range(begin, begin + step):
             value = part[(n - begin) * g.size : (n - begin + 1) * g.size, n * g.size : (n + g.slab) * g.size]
-            rows[n * g.size : (n + 1) * g.size, :] = partial[block_rows(g, first + n), :] - 2.0 * (
-                value * keep[pl.ds(first + n, 1), :]
-            )
+            row = slice(n * g.size, (n + 1) * g.size)
+            rows[row, :] = partial[row, :] - 2.0 * (value * keep[pl.ds(first + n, 1), :])
         to = pl.ds(pl.multiple_of((first + begin) * g.size, g.size), step * g.size)
         copies.append(pltpu.make_async_copy(rows.at[here, :], out.at[to, :], sems.at[len(copies)]))
         copies[-1].start()
@@ -674,16 +695,13 @@
     span = g.span * g.size
     f32 = functools.partial(jax.ShapeDtypeStruct, dtype=jnp.float32)
 
-    inner_early, sum_a, left_b, late_a, late_b, far_b = call(
+    inner_early, sum_a, late_a, band = call(
         functools.partial(early_kernel, g),
         [
-            bf16((early, span)), f32((high_a, wide_a)), bf16((high_b, early)), bf16((high_a, late)),
-            bf16((high_b, late)), bf16((high_b, far)),
+            bf16((early, span)), f32((high_a, wide_a)), bf16((high_a, late)),
+            bf16((rows_dev, layers * cols)),
         ],
-        [
-            scratch(rows_dev, layers * cols), scratch(high_a, early),
-            scratch(rows_dev, 2 * cols),
-        ],
+        [scratch(high_a, early), scratch(rows_dev, 2 * cols)],
         masked, beside, other, swap(other, 1), thin, swap(thin, 1),
     )
     far_beside = swap(far_wide, 1)
@@ -696,12 +714,14 @@
     square_a, inner_late = call(
         functools.partial(late_kernel, g),
         [bf16((high_a, cols)), bf16((late, span))],
-        [scratch(rows_dev, 2 * cols), scratch(cross_shape[0], 2 * cols)],
+        [],
         keep, *pieces, sum_a, late_a,
     )
     across_a, beside_a = swap(square_a, 2), swap(square_a, 1)
-    sum_b = call(
-        functools.partial(sum_kernel, g), f32((high_b, wide_b)), [], left_b, late_b, inner_early, inner_late
+    sum_b, far_b = call(
+        functools.partial(sum_kernel, g),
+        [f32((high_b, wide_b)), bf16((high_b, far))], [scratch(high_b, early), scratch(high_b, late)],
+        band, inner_early, inner_late,
     )
     square_b, inner_far = call(
         functools.partial(square_kernel, g),
@@ -715,21 +735,23 @@
         [scratch(rows_dev, 2 * cols), scratch(*slab)] + 2 * left_scratch(g, "own", (g.rows + 1) // 2),
         keep, square_a, beside_a, square_b, beside_b, inner_early, inner_late,
     )
-    done = call(
+    meet = (slab_early(g, 0)[1] + far_span(g, "B")[1]) * g.size
+    done, straight, next_to = call(
         functools.partial(other_kernel, g),
-        f32((high_a, cols)), [scratch(high_a, 2 * cols)] + left_scratch(g, "A", g.group("A")[0]),
+        [f32((high_a, cols)), bf16((meet, wide_b)), bf16((meet, wide_b))],
+        [scratch(high_a, 2 * cols)] + left_scratch(g, "A", g.group("A")[0]),
         keep, across_a, swap(across_a, 1), inner_early, inner_far, partial,
     )
     across_b = put_after(across_b, done)
-    lefts = [scratch(high_b, n * g.size) for n in (slab_early(g, 0)[1], far_span(g, "B")[1])]
-    total = call(
-        functools.partial(slab_kernel, g), f32((high_b, wide_b)), lefts, across_b, inner_early, inner_far
+    left = scratch(high_b, meet)
+    partial = call(
+        functools.partial(slab_kernel, g), f32((high_b, cols)), [left], keep, across_b, straight, partial
     )
     return call(
         functools.partial(last_kernel, g),
         f32(slab),
-        [pltpu.VMEM((high_b, cols), jnp.float32), pltpu.SemaphoreType.DMA((3,))] + lefts,
-        keep, swap(across_b, 1), inner_early, inner_far, partial, done, total,
+        [pltpu.VMEM((high_b, cols), jnp.float32), pltpu.SemaphoreType.DMA((3,)), left],
+        keep, swap(across_b, 1), next_to, partial, done,
         place=HBM,
     )
 

time: 65.9 us -> 65.3 us (level)
  no operation moved by 1% of the time
where the time goes in v5:
time: 65.3 us; the launch traced here: 65.1 us
  waiting for transfers between devices  33.4 us (51%)
  Pallas kernels  16.2 us (25%)
  starting transfers between devices  15.2 us (23%)
    ppermute x16, waiting for transfers between devices, swap(): return lax.ppermute(value, 'layer', [(s, s ^ bit) for s in range(layers)])  19.6 us
    pallas_call x13, Pallas kernels, call(): pl.pallas_call(kernel, out_shape=out_shape, in_specs=specs, out_specs=jax...  16.2 us
    ppermute x3, waiting for transfers between devices, send(): return lax.ppermute(value, ('layer', 'row'), pairs)  13.8 us
    ppermute x16, starting transfers between devices, swap(): return lax.ppermute(value, 'layer', [(s, s ^ bit) for s in range(layers)])  8.59 us
    ppermute x3, starting transfers between devices, send(): return lax.ppermute(value, ('layer', 'row'), pairs)  6.37 us
  transfers between devices with their start and end apart: 20, of which 7 were waited for; matrix products, arithmetic and copies ran while one was open for 0% of the time, Pallas kernels for 20%

profile of v5, /device:TPU:0, one launch (start us, length us, event | category | flops | bytes accessed | tf_op | source)
XLA Modules:
  0.0 65.1 jit_solution(17601657177035407469)
XLA Ops:
  0.0 1.2 %shard_map.28 = (bf16[640,512]{1,0:T(8,128)(2,1)S(1)}, f32[16,512]{1,0:T(8,128)S(1)}) custom-call(bf16[640,512]{1,0:T(8,128)(2,1)} %density_ref.1, s32[8,10]{1,0:T(8,128)} %bitcast.1), custom_call_target="tpu_custom_call" | custom-call | tf_op jit(solution)/shard_map/pallas_call | solution.py:631
  1.2 0.5 collective-permute-start
  1.7 5.6 %collective-permute-start.3 = (bf16[640,512]{1,0:T(8,128)(2,1)S(1)}, bf16[640,512]{1,0:T(8,128)(2,1)S(1)}, u32[]{:S(2)}, u32[]{:S(2)}) collective-permute-start(bf16[640,512]{1,0:T(8,128)(2,1)S(1)} %get-tuple-element.25.own_ref.own), channel_id=1, source_target_pairs={{0,7},{1,0},{2,1},{3,2},{4,3},{5,4},{6,5},{7,6},{8,15},{9,8},{10,9... | collective-permute-start | bytes 1966088 | tf_op jit(solution)/shard_map/ppermute | solution.py:659
  7.3 0.0 collective-permute-start.2
  7.3 0.0 collective-permute-done.beside_ref.beside
  7.3 0.1 shard_map.29
  7.4 0.7 %collective-permute-start.1 = (bf16[160,1408]{1,0:T(8,128)(2,1)S(1)}, bf16[160,1408]{1,0:T(8,128)(2,1)S(1)}, u32[]{:S(2)}, u32[]{:S(2)}) collective-permute-start(bf16[160,1408]{1,0:T(8,128)(2,1)S(1)} %get-tuple-element.26.own_ref), channel_id=1, source_target_pairs={{1,3},{3,5},{5,7},{7,1},{9,11},{11,13},{13,15},{15,9},{16,22},{18,... | collective-permute-start | bytes 1351688 | tf_op jit(solution)/shard_map/ppermute | solution.py:659
  8.1 13.8 %collective-permute-done.3.after_ref.refs_2_ = bf16[640,512]{1,0:T(8,128)(2,1)S(1)} collective-permute-done((bf16[640,512]{1,0:T(8,128)(2,1)S(1)}, bf16[640,512]{1,0:T(8,128)(2,1)S(1)}, u32[]{:S(2)}, u32[]{:S(2)}) %collective-permute-start.3) | collective-permute-done | bytes 655392 | tf_op jit(solution)/shard_map/ppermute | solution.py:659
  21.9 2.2 %collective-permute-start.10 = (bf16[640,512]{1,0:T(8,128)(2,1)S(1)}, bf16[640,512]{1,0:T(8,128)(2,1)S(1)}, u32[]{:S(2)}, u32[]{:S(2)}) collective-permute-start(bf16[640,512]{1,0:T(8,128)(2,1)S(1)} %collective-permute-done.3.after_ref.refs_2_), channel_id=1, source_target_pairs={{0,16},{8,24},{16,0},{24,8},{1,17},{9,25},{17,1},{25,9},{2,18},{10... | collective-permute-start | bytes 1966088 | tf_op jit(solution)/shard_map/ppermute | solution.py:650
  24.1 0.0 collective-permute-done.2.other_ref.refs_0_
  24.2 0.0 collective-permute-done.1.relayed_ref
  24.2 0.1 shard_map.30
  24.2 0.1 collective-permute-start.4
  24.3 0.3 collective-permute-start.12
  24.6 0.0 collective-permute-start.7
  24.6 0.5 collective-permute-start.6
  25.1 13.8 %collective-permute-done.10.refs_0_ = bf16[640,512]{1,0:T(8,128)(2,1)S(1)} collective-permute-done((bf16[640,512]{1,0:T(8,128)(2,1)S(1)}, bf16[640,512]{1,0:T(8,128)(2,1)S(1)}, u32[]{:S(2)}, u32[]{:S(2)}) %collective-permute-start.10) | collective-permute-done | bytes 655392 | tf_op jit(solution)/shard_map/ppermute | solution.py:650
  38.8 0.0 collective-permute-start.11
  38.8 0.0 collective-permute-done.4.far_own.refs_4_
  38.8 0.5 collective-permute-start.5
  39.3 0.0 collective-permute-done.12.refs_2_
  39.4 0.1 collective-permute-start.13
  39.4 0.0 collective-permute-done.7.refs_3_
  39.4 0.0 collective-permute-done.6.refs_1_
  39.4 1.7 %shard_map.31 = (bf16[1280,1664]{1,0:T(8,128)(2,1)S(1)}, f32[256,768]{1,0:T(8,128)S(1)}, bf16[256,1024]{1,0:T(8,128)(2,1)S(1)}, bf16[640,2048]{1,0:T(8,128)(2,1)S(1)}) custom-call(bf16[640,512]{1,0:T(8,128)(2,1)S(1)} %get-tuple-element.25.own_ref.own, bf16[640,512]{1,0:T(8,128)(2,1)S(1)} %collective-permute-done.beside_ref.beside, ...), custom_call_target="tpu_custom_call" | custom-call | tf_op jit(solution)/shard_map/pallas_call | solution.py:631
  41.2 0.5 collective-permute-done.5.far_beside.refs_5_
  41.7 1.8 %collective-permute-start.8 = (bf16[96,384]{1,0:T(8,128)(2,1)S(1)}, bf16[96,384]{1,0:T(8,128)(2,1)S(1)}, u32[]{:S(2)}, u32[]{:S(2)}) collective-permute-start(bf16[96,384]{1,0:T(8,128)(2,1)S(1)} %shard_map.32), channel_id=1, source_target_pairs={{0,16},{8,24},{16,0},{24,8},{1,17},{9,25},{17,1},{25,9},{2,18},{10... | collective-permute-start | bytes 221192 | tf_op jit(solution)/shard_map/ppermute | solution.py:650
  43.5 0.0 collective-permute-done.11.refs_1_
  43.5 1.2 %shard_map.33 = (bf16[256,512]{1,0:T(8,128)(2,1)S(1)}, bf16[1024,1664]{1,0:T(8,128)(2,1)S(1)}) custom-call(f32[16,512]{1,0:T(8,128)S(1)} %get-tuple-element.24.keep, bf16[640,512]{1,0:T(8,128)(2,1)S(1)} %collective-permute-done.10.refs_0_, bf16[640,512]{1,0:T(8,128)(2,1)S(1)} %collective-permute-done.11.refs_1_, ...), custom_call_target="tpu_custom_call" | custom-call | tf_op jit(solution)/shard_map/pallas_call | solution.py:631
  44.7 0.5 collective-permute-start.15
  45.2 0.8 %collective-permute-done.8.far = bf16[96,384]{1,0:T(8,128)(2,1)S(1)} collective-permute-done((bf16[96,384]{1,0:T(8,128)(2,1)S(1)}, bf16[96,384]{1,0:T(8,128)(2,1)S(1)}, u32[]{:S(2)}, u32[]{:S(2)}) %collective-permute-start.8) | collective-permute-done | bytes 73760 | tf_op jit(solution)/shard_map/ppermute | solution.py:650
  46.1 0.0 collective-permute-start.9
  46.1 2.3 %shard_map.34 = (f32[384,896]{1,0:T(8,128)S(1)}, bf16[384,384]{1,0:T(8,128)(2,1)S(1)}) custom-call(bf16[640,2048]{1,0:T(8,128)(2,1)S(1)} %get-tuple-element.30.band, bf16[1280,1664]{1,0:T(8,128)(2,1)S(1)} %get-tuple-element.31.early.refs_4_.refs_2_, bf16[1024,1664]{1,0:T(8,128)(2,1)S(1)} %get-tuple-element.34.late.refs_5_), custom_call_target="tpu_custom_call" | custom-call | tf_op jit(solution)/shard_map/pallas_call | solution.py:631
  48.4 0.0 collective-permute-done.9.far_beside
  48.4 0.8 %shard_map.35 = (bf16[384,512]{1,0:T(8,128)(2,1)S(1)}, bf16[384,1664]{1,0:T(8,128)(2,1)S(1)}) custom-call(f32[16,512]{1,0:T(8,128)S(1)} %get-tuple-element.24.keep, bf16[96,384]{1,0:T(8,128)(2,1)S(1)} %collective-permute-done.8.far, bf16[96,384]{1,0:T(8,128)(2,1)S(1)} %collective-permute-done.9.far_beside, f32[384,896]{1,0:T(8,128)S(1)} %get-tuple-element.35.total, ...), custom_call_target="tpu_custom_call" | custom-call | tf_op jit(solution)/shard_map/pallas_call | solution.py:631
  49.2 0.6 collective-permute-start.18
  49.8 1.7 %collective-permute-start.14 = (bf16[384,512]{1,0:T(8,128)(2,1)S(1)}, bf16[384,512]{1,0:T(8,128)(2,1)S(1)}, u32[]{:S(2)}, u32[]{:S(2)}) collective-permute-start(bf16[384,512]{1,0:T(8,128)(2,1)S(1)} %get-tuple-element.37.refs_2_), channel_id=1, source_target_pairs={{0,16},{8,24},{16,0},{24,8},{1,17},{9,25},{17,1},{25,9},{2,18},{10... | collective-permute-start | bytes 1179656 | tf_op jit(solution)/shard_map/ppermute | solution.py:650
  51.5 0.0 collective-permute-start.17
  51.5 1.5 %collective-permute-done.15.refs_0_ = bf16[256,512]{1,0:T(8,128)(2,1)S(1)} collective-permute-done((bf16[256,512]{1,0:T(8,128)(2,1)S(1)}, bf16[256,512]{1,0:T(8,128)(2,1)S(1)}, u32[]{:S(2)}, u32[]{:S(2)}) %collective-permute-start.15) | collective-permute-done | bytes 262176 | tf_op jit(solution)/shard_map/ppermute | solution.py:650
  53.1 0.0 collective-permute-start.16
  53.1 0.0 collective-permute-done.17.refs_1_
  53.1 4.3 %shard_map.36.refs_4_.partial = f32[640,512]{1,0:T(8,128)S(1)} custom-call(f32[16,512]{1,0:T(8,128)S(1)} %get-tuple-element.24.keep, bf16[256,512]{1,0:T(8,128)(2,1)S(1)} %get-tuple-element.38.refs_0_, bf16[256,512]{1,0:T(8,128)(2,1)S(1)} %collective-permute-done.17.refs_1_, bf16[384,512]{1,0:T(8,128)(2,1)S(1)} %get-tuple-element.37.refs_2_, ...), custom_call_target="tpu_custom_call" | custom-call | tf_op jit(solution)/shard_map/pallas_call | solution.py:631
  57.4 1.3 %shard_map.37 = (f32[256,512]{1,0:T(8,128)S(1)}, bf16[1024,896]{1,0:T(8,128)(2,1)S(1)}, bf16[1024,896]{1,0:T(8,128)(2,1)S(1)}) custom-call(f32[16,512]{1,0:T(8,128)S(1)} %get-tuple-element.24.keep, bf16[256,512]{1,0:T(8,128)(2,1)S(1)} %collective-permute-done.15.refs_0_, bf16[256,512]{1,0:T(8,128)(2,1)S(1)} %collective-permute-done.16.refs_1_, ...), custom_call_target="tpu_custom_call" | custom-call | tf_op jit(solution)/shard_map/pallas_call | solution.py:631
  58.7 2.5 %collective-permute-done.14.in_ref = bf16[384,512]{1,0:T(8,128)(2,1)S(1)} collective-permute-done((bf16[384,512]{1,0:T(8,128)(2,1)S(1)}, bf16[384,512]{1,0:T(8,128)(2,1)S(1)}, u32[]{:S(2)}, u32[]{:S(2)}) %collective-permute-start.14) | collective-permute-done | bytes 393248 | tf_op jit(solution)/shard_map/ppermute | solution.py:650
  61.3 0.1 collective-permute-start.19
  61.3 1.2 %shard_map.39.partial = f32[384,512]{1,0:T(8,128)S(1)} custom-call(f32[16,512]{1,0:T(8,128)S(1)} %get-tuple-element.24.keep, bf16[384,512]{1,0:T(8,128)(2,1)S(1)} %shard_map.38.square, bf16[1024,896]{1,0:T(8,128)(2,1)S(1)} %get-tuple-element.42.right, f32[640,512]{1,0:T(8,128)S(1)} %shard_map.36.refs_4_.partial), custom_call_target="tpu_custom_call" | custom-call | tf_op jit(solution)/shard_map/pallas_call | solution.py:631
  62.6 0.5 collective-permute-done.19.square
  63.1 1.9 %shard_map.40 = f32[640,512]{1,0:T(8,128)} custom-call(f32[16,512]{1,0:T(8,128)S(1)} %get-tuple-element.24.keep, bf16[384,512]{1,0:T(8,128)(2,1)S(1)} %collective-permute-done.19.square, bf16[1024,896]{1,0:T(8,128)(2,1)S(1)} %get-tuple-element.41.right, f32[384,512]{1,0:T(8,128)S(1)} %shard_map.39.partial, f32[256,512]{1,0:T(8,128)S(1)} %get-tuple-element.40.refs_0_.done), custom_call_target="tpu_custom_call" | custom-call | tf_op jit(solution)/shard_map/pallas_call | solution.py:631
  (5 shorter events, 0.1 us)
Async XLA Ops:
  1.2 6.1 %collective-permute-start = (bf16[640,512]{1,0:T(8,128)(2,1)S(1)}, bf16[640,512]{1,0:T(8,128)(2,1)S(1)}, u32[]{:S(2)}, u32[]{:S(2)}) collective-permute-start(bf16[640,512]{1,0:T(8,128)(2,1)S(1)} %get-tuple-element.25.own_ref.own), channel_id=1, source_target_pairs={{0,8},{8,0},{16,24},{24,16},{1,9},{9,1},{17,25},{25,17},{2,10},{10... | collective-permute-start | bytes 1966088 | tf_op jit(solution)/shard_map/ppermute | solution.py:650
  1.7 20.2 %collective-permute-start.3 = (bf16[640,512]{1,0:T(8,128)(2,1)S(1)}, bf16[640,512]{1,0:T(8,128)(2,1)S(1)}, u32[]{:S(2)}, u32[]{:S(2)}) collective-permute-start(bf16[640,512]{1,0:T(8,128)(2,1)S(1)} %get-tuple-element.25.own_ref.own), channel_id=1, source_target_pairs={{0,7},{1,0},{2,1},{3,2},{4,3},{5,4},{6,5},{7,6},{8,15},{9,8},{10,9... | collective-permute-start | bytes 1966088 | tf_op jit(solution)/shard_map/ppermute | solution.py:659
  7.3 16.8 %collective-permute-start.2 = (bf16[640,512]{1,0:T(8,128)(2,1)S(1)}, bf16[640,512]{1,0:T(8,128)(2,1)S(1)}, u32[]{:S(2)}, u32[]{:S(2)}) collective-permute-start(bf16[640,512]{1,0:T(8,128)(2,1)S(1)} %get-tuple-element.25.own_ref.own), channel_id=1, source_target_pairs={{0,16},{8,24},{16,0},{24,8},{1,17},{9,25},{17,1},{25,9},{2,18},{10... | collective-permute-start | bytes 1966088 | tf_op jit(solution)/shard_map/ppermute | solution.py:650
  7.4 16.7 %collective-permute-start.1 = (bf16[160,1408]{1,0:T(8,128)(2,1)S(1)}, bf16[160,1408]{1,0:T(8,128)(2,1)S(1)}, u32[]{:S(2)}, u32[]{:S(2)}) collective-permute-start(bf16[160,1408]{1,0:T(8,128)(2,1)S(1)} %get-tuple-element.26.own_ref), channel_id=1, source_target_pairs={{1,3},{3,5},{5,7},{7,1},{9,11},{11,13},{13,15},{15,9},{16,22},{18,... | collective-permute-start | bytes 1351688 | tf_op jit(solution)/shard_map/ppermute | solution.py:659
  21.9 16.9 %collective-permute-start.10 = (bf16[640,512]{1,0:T(8,128)(2,1)S(1)}, bf16[640,512]{1,0:T(8,128)(2,1)S(1)}, u32[]{:S(2)}, u32[]{:S(2)}) collective-permute-start(bf16[640,512]{1,0:T(8,128)(2,1)S(1)} %collective-permute-done.3.after_ref.refs_2_), channel_id=1, source_target_pairs={{0,16},{8,24},{16,0},{24,8},{1,17},{9,25},{17,1},{25,9},{2,18},{10... | collective-permute-start | bytes 1966088 | tf_op jit(solution)/shard_map/ppermute | solution.py:650
  24.2 14.6 %collective-permute-start.4 = (bf16[480,512]{1,0:T(8,128)(2,1)S(1)}, bf16[480,512]{1,0:T(8,128)(2,1)S(1)}, u32[]{:S(2)}, u32[]{:S(2)}) collective-permute-start(bf16[480,512]{1,0:T(8,128)(2,1)S(1)} %get-tuple-element.28), channel_id=1, source_target_pairs={{0,2},{1,3},{2,4},{3,5},{4,6},{5,7},{6,0},{7,1},{8,10},{9,11},{10,... | collective-permute-start | bytes 1474568 | tf_op jit(solution)/shard_map/ppermute | solution.py:659
  24.3 15.1 %collective-permute-start.12 = (bf16[160,1408]{1,0:T(8,128)(2,1)S(1)}, bf16[160,1408]{1,0:T(8,128)(2,1)S(1)}, u32[]{:S(2)}, u32[]{:S(2)}) collective-permute-start(bf16[160,1408]{1,0:T(8,128)(2,1)S(1)} %get-tuple-element.32), channel_id=1, source_target_pairs={{0,1},{1,0},{2,3},{3,2},{4,5},{5,4},{6,7},{7,6},{8,9},{9,8},{10,11... | collective-permute-start | bytes 1351688 | tf_op jit(solution)/shard_map/ppermute | solution.py:690
  24.6 14.9 %collective-permute-start.7 = (bf16[640,512]{1,0:T(8,128)(2,1)S(1)}, bf16[640,512]{1,0:T(8,128)(2,1)S(1)}, u32[]{:S(2)}, u32[]{:S(2)}) collective-permute-start(bf16[640,512]{1,0:T(8,128)(2,1)S(1)} %collective-permute-done.3.after_ref.refs_2_), channel_id=1, source_target_pairs={{0,8},{8,0},{16,24},{24,16},{1,9},{9,1},{17,25},{25,17},{2,10},{10... | collective-permute-start | bytes 1966088 | tf_op jit(solution)/shard_map/ppermute | solution.py:650
  24.6 14.9 %collective-permute-start.6 = (bf16[640,512]{1,0:T(8,128)(2,1)S(1)}, bf16[640,512]{1,0:T(8,128)(2,1)S(1)}, u32[]{:S(2)}, u32[]{:S(2)}) collective-permute-start(bf16[640,512]{1,0:T(8,128)(2,1)S(1)} %collective-permute-done.2.other_ref.refs_0_), channel_id=1, source_target_pairs={{0,8},{8,0},{16,24},{24,16},{1,9},{9,1},{17,25},{25,17},{2,10},{10... | collective-permute-start | bytes 1966088 | tf_op jit(solution)/shard_map/ppermute | solution.py:650
  38.8 4.6 %collective-permute-start.11 = (bf16[640,512]{1,0:T(8,128)(2,1)S(1)}, bf16[640,512]{1,0:T(8,128)(2,1)S(1)}, u32[]{:S(2)}, u32[]{:S(2)}) collective-permute-start(bf16[640,512]{1,0:T(8,128)(2,1)S(1)} %collective-permute-done.10.refs_0_), channel_id=1, source_target_pairs={{0,8},{8,0},{16,24},{24,16},{1,9},{9,1},{17,25},{25,17},{2,10},{10... | collective-permute-start | bytes 1966088 | tf_op jit(solution)/shard_map/ppermute | solution.py:650
  38.8 2.8 %collective-permute-start.5 = (bf16[480,512]{1,0:T(8,128)(2,1)S(1)}, bf16[480,512]{1,0:T(8,128)(2,1)S(1)}, u32[]{:S(2)}, u32[]{:S(2)}) collective-permute-start(bf16[480,512]{1,0:T(8,128)(2,1)S(1)} %collective-permute-done.4.far_own.refs_4_), channel_id=1, source_target_pairs={{0,8},{8,0},{16,24},{24,16},{1,9},{9,1},{17,25},{25,17},{2,10},{10... | collective-permute-start | bytes 1474568 | tf_op jit(solution)/shard_map/ppermute | solution.py:650
  39.4 4.1 %collective-permute-start.13 = (bf16[160,1408]{1,0:T(8,128)(2,1)S(1)}, bf16[160,1408]{1,0:T(8,128)(2,1)S(1)}, u32[]{:S(2)}, u32[]{:S(2)}) collective-permute-start(bf16[160,1408]{1,0:T(8,128)(2,1)S(1)} %collective-permute-done.12.refs_2_), channel_id=1, source_target_pairs={{0,8},{8,0},{16,24},{24,16},{1,9},{9,1},{17,25},{25,17},{2,10},{10... | collective-permute-start | bytes 1351688 | tf_op jit(solution)/shard_map/ppermute | solution.py:650
  41.7 4.4 %collective-permute-start.8 = (bf16[96,384]{1,0:T(8,128)(2,1)S(1)}, bf16[96,384]{1,0:T(8,128)(2,1)S(1)}, u32[]{:S(2)}, u32[]{:S(2)}) collective-permute-start(bf16[96,384]{1,0:T(8,128)(2,1)S(1)} %shard_map.32), channel_id=1, source_target_pairs={{0,16},{8,24},{16,0},{24,8},{1,17},{9,25},{17,1},{25,9},{2,18},{10... | collective-permute-start | bytes 221192 | tf_op jit(solution)/shard_map/ppermute | solution.py:650
  44.7 8.4 %collective-permute-start.15 = (bf16[256,512]{1,0:T(8,128)(2,1)S(1)}, bf16[256,512]{1,0:T(8,128)(2,1)S(1)}, u32[]{:S(2)}, u32[]{:S(2)}) collective-permute-start(bf16[256,512]{1,0:T(8,128)(2,1)S(1)} %get-tuple-element.38.refs_0_), channel_id=1, source_target_pairs={{0,16},{8,24},{16,0},{24,8},{1,17},{9,25},{17,1},{25,9},{2,18},{10... | collective-permute-start | bytes 786440 | tf_op jit(solution)/shard_map/ppermute | solution.py:650
  46.1 2.4 %collective-permute-start.9 = (bf16[96,384]{1,0:T(8,128)(2,1)S(1)}, bf16[96,384]{1,0:T(8,128)(2,1)S(1)}, u32[]{:S(2)}, u32[]{:S(2)}) collective-permute-start(bf16[96,384]{1,0:T(8,128)(2,1)S(1)} %collective-permute-done.8.far), channel_id=1, source_target_pairs={{0,8},{8,0},{16,24},{24,16},{1,9},{9,1},{17,25},{25,17},{2,10},{10... | collective-permute-start | bytes 221192 | tf_op jit(solution)/shard_map/ppermute | solution.py:650
  49.2 3.9 %collective-permute-start.18 = (bf16[384,512]{1,0:T(8,128)(2,1)S(1)}, bf16[384,512]{1,0:T(8,128)(2,1)S(1)}, u32[]{:S(2)}, u32[]{:S(2)}) collective-permute-start(bf16[384,512]{1,0:T(8,128)(2,1)S(1)} %get-tuple-element.37.refs_2_), channel_id=1, source_target_pairs={{0,8},{8,0},{16,24},{24,16},{1,9},{9,1},{17,25},{25,17},{2,10},{10... | collective-permute-start | bytes 1179656 | tf_op jit(solution)/shard_map/ppermute | solution.py:650
  49.8 11.4 %collective-permute-start.14 = (bf16[384,512]{1,0:T(8,128)(2,1)S(1)}, bf16[384,512]{1,0:T(8,128)(2,1)S(1)}, u32[]{:S(2)}, u32[]{:S(2)}) collective-permute-start(bf16[384,512]{1,0:T(8,128)(2,1)S(1)} %get-tuple-element.37.refs_2_), channel_id=1, source_target_pairs={{0,16},{8,24},{16,0},{24,8},{1,17},{9,25},{17,1},{25,9},{2,18},{10... | collective-permute-start | bytes 1179656 | tf_op jit(solution)/shard_map/ppermute | solution.py:650
  51.5 1.5 %collective-permute-start.17 = (bf16[256,512]{1,0:T(8,128)(2,1)S(1)}, bf16[256,512]{1,0:T(8,128)(2,1)S(1)}, u32[]{:S(2)}, u32[]{:S(2)}) collective-permute-start(bf16[256,512]{1,0:T(8,128)(2,1)S(1)} %get-tuple-element.38.refs_0_), channel_id=1, source_target_pairs={{0,8},{8,0},{16,24},{24,16},{1,9},{9,1},{17,25},{25,17},{2,10},{10... | collective-permute-start | bytes 786440 | tf_op jit(solution)/shard_map/ppermute | solution.py:650
  53.1 4.3 %collective-permute-start.16 = (bf16[256,512]{1,0:T(8,128)(2,1)S(1)}, bf16[256,512]{1,0:T(8,128)(2,1)S(1)}, u32[]{:S(2)}, u32[]{:S(2)}) collective-permute-start(bf16[256,512]{1,0:T(8,128)(2,1)S(1)} %collective-permute-done.15.refs_0_), channel_id=1, source_target_pairs={{0,8},{8,0},{16,24},{24,16},{1,9},{9,1},{17,25},{25,17},{2,10},{10... | collective-permute-start | bytes 786440 | tf_op jit(solution)/shard_map/ppermute | solution.py:650
  61.3 1.8 %collective-permute-start.19 = (bf16[384,512]{1,0:T(8,128)(2,1)S(1)}, bf16[384,512]{1,0:T(8,128)(2,1)S(1)}, u32[]{:S(2)}, u32[]{:S(2)}) collective-permute-start(bf16[384,512]{1,0:T(8,128)(2,1)S(1)} %shard_map.38.square), channel_id=1, source_target_pairs={{0,8},{8,0},{16,24},{24,16},{1,9},{9,1},{17,25},{25,17},{2,10},{10... | collective-permute-start | bytes 1179656 | tf_op jit(solution)/shard_map/ppermute | solution.py:650

commit v6 on v5

--- a/solution.py
+++ b/solution.py
@@ -110,7 +110,7 @@
     return lax.axis_index("layer").astype(jnp.int32)
 
 
-def mask_kernel(g, density_ref, pattern_ref, out_ref, keep, density, pattern, sems):
+def mask_kernel(g, density_ref, pattern_ref, out_ref, keep, give, density, pattern, sems):
     copies = [
         pltpu.make_async_copy(source, target, sems.at[n])
         for n, (source, target) in enumerate(((pattern_ref, pattern), (density_ref, density)))
@@ -128,9 +128,12 @@
     )
     keep[g.rows :, :] = jnp.zeros((keep.shape[0] - g.rows, cols), keep.dtype)
     copies[1].wait()
+    half = g.size // 2
     for t in range(g.rows):
         rows = slice(t * g.size, (t + 1) * g.size)
         out_ref[rows, :] = density[rows, :] * keep[t : t + 1, :].astype(jnp.bfloat16)
+        start = pl.multiple_of(t * g.size + half * (1 - layer_index() % 2), half)
+        give[t * half : (t + 1) * half, :] = out_ref[pl.ds(start, half), :]
 
 
 def cross_rows(g, side):
@@ -177,19 +180,19 @@
         out[slots * height :, :] = jnp.zeros((out.shape[0] - slots * height, out.shape[1]), out.dtype)
 
 
-def fill_near(g, core, slabs, near):
+def fill_near(g, core, own, given, near):
     half, cols = g.size // 2, g.slab * g.size
-    for q, slab in enumerate(slabs):
-        start = pl.multiple_of((core ^ q) * cols, cols)
-        for t in range(g.rows):
-            src = pl.multiple_of(t * g.size + half * core, half)
-            near[t * half : (t + 1) * half, pl.ds(start, cols)] = slab[pl.ds(src, half), :]
-
-
-def pack_kernel(g, own_ref, beside_ref, wide, far, near):
+    here, there = (pl.ds(pl.multiple_of(c * cols, cols), cols) for c in (core, 1 - core))
+    for t in range(g.rows):
+        src = pl.multiple_of(t * g.size + half * core, half)
+        near[t * half : (t + 1) * half, here] = own[pl.ds(src, half), :]
+    near[:, there] = given[...]
+
+
+def pack_kernel(g, own_ref, given_ref, wide, far, near):
     side, core = layer_index() // 2, layer_index() % 2
     half = g.size // 2
-    fill_near(g, core, (own_ref, beside_ref), near)
+    fill_near(g, core, own_ref, given_ref, near)
 
     def fill(side):
         for name, out in ((NEAR_WIDE, wide), (FAR_WIDE, far)):
@@ -665,9 +668,12 @@
         return call(pass_kernel, bf16(value.shape), [], value, after=after)
 
     sources = [pltpu.with_memory_space_constraint(value, pltpu.HBM) for value in (density, pattern.T)]
-    masked, keep = call(
+    masked, keep, give = call(
         functools.partial(mask_kernel, g),
-        [bf16(slab), jax.ShapeDtypeStruct(((g.rows + 7) // 8 * 8, cols), jnp.float32)],
+        [
+            bf16(slab), jax.ShapeDtypeStruct(((g.rows + 7) // 8 * 8, cols), jnp.float32),
+            bf16((half_rows, cols)),
+        ],
         [scratch(*slab), pltpu.VMEM(pattern.T.shape, pattern.dtype), pltpu.SemaphoreType.DMA((2,))],
         placed=sources,
     )
@@ -679,7 +685,7 @@
     wide, far_wide = call(
         functools.partial(pack_kernel, g),
         [bf16(message_shape(g, NEAR_WIDE)), bf16(head_shape)], [scratch(half_rows, 2 * cols)],
-        masked, beside,
+        masked, swap(give, 1),
     )
     relayed = send(wide, FAR_WIDE, lambda layer, row: row % 2 != layer // 2)
     crossed = swap(thin, 2)

time: 65.3 us -> 64.9 us (level)
  starting transfers between devices: 15.2 us -> 13.5 us
  waiting for transfers between devices: 33.4 us -> 34.6 us
    ppermute x16 -> x17, waiting for transfers between devices: 19.6 us -> 22.5 us  [swap(): return lax.ppermute(value, 'layer', [(s, s ^ bit) for s in range(layers)])]
    ppermute x16 -> x17, starting transfers between devices: 8.59 us -> 6.67 us  [swap(): return lax.ppermute(value, 'layer', [(s, s ^ bit) for s in range(layers)])]
    ppermute x3, waiting for transfers between devices: 13.8 us -> 12.1 us  [send(): return lax.ppermute(value, ('layer', 'row'), pairs)]
  transfers between devices with their start and end apart: 20 -> 21, of which waited for: 7 -> 10; matrix products, arithmetic and copies ran while one was open for 0% -> 0% of each run, Pallas kernels for 20% -> 20%
where the time goes in v6:
time: 64.9 us; the launch traced here: 64.8 us
  waiting for transfers between devices  34.6 us (53%)
  Pallas kernels  16.2 us (25%)
  starting transfers between devices  13.5 us (21%)
    ppermute x17, waiting for transfers between devices, swap(): return lax.ppermute(value, 'layer', [(s, s ^ bit) for s in range(layers)])  22.5 us
    pallas_call x13, Pallas kernels, call(): pl.pallas_call(kernel, out_shape=out_shape, in_specs=specs, out_specs=jax...  16.2 us
    ppermute x3, waiting for transfers between devices, send(): return lax.ppermute(value, ('layer', 'row'), pairs)  12.1 us
    ppermute x3, starting transfers between devices, send(): return lax.ppermute(value, ('layer', 'row'), pairs)  6.81 us
    ppermute x17, starting transfers between devices, swap(): return lax.ppermute(value, 'layer', [(s, s ^ bit) for s in range(layers)])  6.67 us
  transfers between devices with their start and end apart: 21, of which 10 were waited for; matrix products, arithmetic and copies ran while one was open for 0% of the time, Pallas kernels for 20%

profile of v6, /device:TPU:0, one launch (start us, length us, event | category | flops | bytes accessed | tf_op | source)
XLA Modules:
  0.0 64.8 jit_solution(6410923493817842752)
XLA Ops:
  0.0 1.2 %shard_map.28 = (bf16[640,512]{1,0:T(8,128)(2,1)S(1)}, f32[16,512]{1,0:T(8,128)S(1)}, bf16[320,512]{1,0:T(8,128)(2,1)S(1)}) custom-call(bf16[640,512]{1,0:T(8,128)(2,1)} %density_ref.1, s32[8,10]{1,0:T(8,128)} %bitcast.1), custom_call_target="tpu_custom_call" | custom-call | tf_op jit(solution)/shard_map/pallas_call | solution.py:634
  1.3 6.1 %collective-permute-start.3 = (bf16[640,512]{1,0:T(8,128)(2,1)S(1)}, bf16[640,512]{1,0:T(8,128)(2,1)S(1)}, u32[]{:S(2)}, u32[]{:S(2)}) collective-permute-start(bf16[640,512]{1,0:T(8,128)(2,1)S(1)} %get-tuple-element.26.own_ref.own), channel_id=1, source_target_pairs={{0,7},{1,0},{2,1},{3,2},{4,3},{5,4},{6,5},{7,6},{8,15},{9,8},{10,9... | collective-permute-start | bytes 1966088 | tf_op jit(solution)/shard_map/ppermute | solution.py:662
  7.3 0.0 collective-permute-start
  7.3 0.0 collective-permute-start.2
  7.3 1.6 %collective-permute-done.given_ref = bf16[320,512]{1,0:T(8,128)(2,1)S(1)} collective-permute-done((bf16[320,512]{1,0:T(8,128)(2,1)S(1)}, bf16[320,512]{1,0:T(8,128)(2,1)S(1)}, u32[]{:S(2)}, u32[]{:S(2)}) %collective-permute-start) | collective-permute-done | bytes 327712 | tf_op jit(solution)/shard_map/ppermute | solution.py:653
  8.9 0.1 shard_map.29
  9.0 0.7 %collective-permute-start.1 = (bf16[160,1408]{1,0:T(8,128)(2,1)S(1)}, bf16[160,1408]{1,0:T(8,128)(2,1)S(1)}, u32[]{:S(2)}, u32[]{:S(2)}) collective-permute-start(bf16[160,1408]{1,0:T(8,128)(2,1)S(1)} %get-tuple-element.28.own_ref), channel_id=1, source_target_pairs={{1,3},{3,5},{5,7},{7,1},{9,11},{11,13},{13,15},{15,9},{16,22},{18,... | collective-permute-start | bytes 1351688 | tf_op jit(solution)/shard_map/ppermute | solution.py:662
  9.7 0.2 collective-permute-start.6
  9.9 11.4 %collective-permute-done.3.after_ref.refs_2_ = bf16[640,512]{1,0:T(8,128)(2,1)S(1)} collective-permute-done((bf16[640,512]{1,0:T(8,128)(2,1)S(1)}, bf16[640,512]{1,0:T(8,128)(2,1)S(1)}, u32[]{:S(2)}, u32[]{:S(2)}) %collective-permute-start.3) | collective-permute-done | bytes 655392 | tf_op jit(solution)/shard_map/ppermute | solution.py:662
  21.3 2.2 %collective-permute-start.11 = (bf16[640,512]{1,0:T(8,128)(2,1)S(1)}, bf16[640,512]{1,0:T(8,128)(2,1)S(1)}, u32[]{:S(2)}, u32[]{:S(2)}) collective-permute-start(bf16[640,512]{1,0:T(8,128)(2,1)S(1)} %collective-permute-done.3.after_ref.refs_2_), channel_id=1, source_target_pairs={{0,16},{8,24},{16,0},{24,8},{1,17},{9,25},{17,1},{25,9},{2,18},{10... | collective-permute-start | bytes 1966088 | tf_op jit(solution)/shard_map/ppermute | solution.py:653
  23.5 1.3 %collective-permute-done.2.other_ref.refs_0_ = bf16[640,512]{1,0:T(8,128)(2,1)S(1)} collective-permute-done((bf16[640,512]{1,0:T(8,128)(2,1)S(1)}, bf16[640,512]{1,0:T(8,128)(2,1)S(1)}, u32[]{:S(2)}, u32[]{:S(2)}) %collective-permute-start.2) | collective-permute-done | bytes 655392 | tf_op jit(solution)/shard_map/ppermute | solution.py:653
  24.8 0.0 collective-permute-done.1.relayed_ref
  24.8 0.1 shard_map.30
  24.9 0.1 collective-permute-start.4
  25.0 0.1 collective-permute-start.13
  25.1 0.1 collective-permute-start.8
  25.1 0.0 collective-permute-done.6.beside
  25.2 0.5 collective-permute-start.7
  25.6 12.9 %collective-permute-done.11.refs_0_ = bf16[640,512]{1,0:T(8,128)(2,1)S(1)} collective-permute-done((bf16[640,512]{1,0:T(8,128)(2,1)S(1)}, bf16[640,512]{1,0:T(8,128)(2,1)S(1)}, u32[]{:S(2)}, u32[]{:S(2)}) %collective-permute-start.11) | collective-permute-done | bytes 655392 | tf_op jit(solution)/shard_map/ppermute | solution.py:653
  38.5 0.0 collective-permute-start.12
  38.5 0.7 %collective-permute-done.4.far_own.refs_4_ = bf16[480,512]{1,0:T(8,128)(2,1)S(1)} collective-permute-done((bf16[480,512]{1,0:T(8,128)(2,1)S(1)}, bf16[480,512]{1,0:T(8,128)(2,1)S(1)}, u32[]{:S(2)}, u32[]{:S(2)}) %collective-permute-start.4) | collective-permute-done | bytes 491552 | tf_op jit(solution)/shard_map/ppermute | solution.py:662
  39.2 0.0 collective-permute-start.5
  39.2 0.0 collective-permute-done.13.refs_2_
  39.2 0.5 collective-permute-start.14
  39.8 0.0 collective-permute-done.8.refs_3_
  39.8 0.0 collective-permute-done.7.refs_1_
  39.8 1.7 %shard_map.31 = (bf16[1280,1664]{1,0:T(8,128)(2,1)S(1)}, f32[256,768]{1,0:T(8,128)S(1)}, bf16[256,1024]{1,0:T(8,128)(2,1)S(1)}, bf16[640,2048]{1,0:T(8,128)(2,1)S(1)}) custom-call(bf16[640,512]{1,0:T(8,128)(2,1)S(1)} %get-tuple-element.26.own_ref.own, bf16[640,512]{1,0:T(8,128)(2,1)S(1)} %collective-permute-done.6.beside, ...), custom_call_target="tpu_custom_call" | custom-call | tf_op jit(solution)/shard_map/pallas_call | solution.py:634
  41.5 0.0 collective-permute-done.5.far_beside.refs_5_
  41.6 0.6 collective-permute-start.9
  42.1 0.0 collective-permute-done.14.refs_3_
  42.1 1.2 %shard_map.33 = (bf16[256,512]{1,0:T(8,128)(2,1)S(1)}, bf16[1024,1664]{1,0:T(8,128)(2,1)S(1)}) custom-call(f32[16,512]{1,0:T(8,128)S(1)} %get-tuple-element.25.keep, bf16[640,512]{1,0:T(8,128)(2,1)S(1)} %collective-permute-done.11.refs_0_, bf16[640,512]{1,0:T(8,128)(2,1)S(1)} %collective-permute-done.12.refs_1_, ...), custom_call_target="tpu_custom_call" | custom-call | tf_op jit(solution)/shard_map/pallas_call | solution.py:634
  43.4 1.5 %collective-permute-start.16 = (bf16[256,512]{1,0:T(8,128)(2,1)S(1)}, bf16[256,512]{1,0:T(8,128)(2,1)S(1)}, u32[]{:S(2)}, u32[]{:S(2)}) collective-permute-start(bf16[256,512]{1,0:T(8,128)(2,1)S(1)} %get-tuple-element.40.refs_0_), channel_id=1, source_target_pairs={{0,16},{8,24},{16,0},{24,8},{1,17},{9,25},{17,1},{25,9},{2,18},{10... | collective-permute-start | bytes 786440 | tf_op jit(solution)/shard_map/ppermute | solution.py:653
  44.9 1.2 %collective-permute-done.9.far = bf16[96,384]{1,0:T(8,128)(2,1)S(1)} collective-permute-done((bf16[96,384]{1,0:T(8,128)(2,1)S(1)}, bf16[96,384]{1,0:T(8,128)(2,1)S(1)}, u32[]{:S(2)}, u32[]{:S(2)}) %collective-permute-start.9) | collective-permute-done | bytes 73760 | tf_op jit(solution)/shard_map/ppermute | solution.py:653
  46.1 0.0 collective-permute-start.10
  46.1 2.3 %shard_map.34 = (f32[384,896]{1,0:T(8,128)S(1)}, bf16[384,384]{1,0:T(8,128)(2,1)S(1)}) custom-call(bf16[640,2048]{1,0:T(8,128)(2,1)S(1)} %get-tuple-element.32.band, bf16[1280,1664]{1,0:T(8,128)(2,1)S(1)} %get-tuple-element.33.early.refs_4_.refs_2_, bf16[1024,1664]{1,0:T(8,128)(2,1)S(1)} %get-tuple-element.36.late.refs_5_), custom_call_target="tpu_custom_call" | custom-call | tf_op jit(solution)/shard_map/pallas_call | solution.py:634
  48.4 0.0 collective-permute-done.10.far_beside
  48.4 0.8 %shard_map.35 = (bf16[384,512]{1,0:T(8,128)(2,1)S(1)}, bf16[384,1664]{1,0:T(8,128)(2,1)S(1)}) custom-call(f32[16,512]{1,0:T(8,128)S(1)} %get-tuple-element.25.keep, bf16[96,384]{1,0:T(8,128)(2,1)S(1)} %collective-permute-done.9.far, bf16[96,384]{1,0:T(8,128)(2,1)S(1)} %collective-permute-done.10.far_beside, f32[384,896]{1,0:T(8,128)S(1)} %get-tuple-element.37.total, ...), custom_call_target="tpu_custom_call" | custom-call | tf_op jit(solution)/shard_map/pallas_call | solution.py:634
  49.2 0.6 collective-permute-start.19
  49.8 0.4 collective-permute-start.15
  50.2 1.4 %collective-permute-done.16.refs_0_ = bf16[256,512]{1,0:T(8,128)(2,1)S(1)} collective-permute-done((bf16[256,512]{1,0:T(8,128)(2,1)S(1)}, bf16[256,512]{1,0:T(8,128)(2,1)S(1)}, u32[]{:S(2)}, u32[]{:S(2)}) %collective-permute-start.16) | collective-permute-done | bytes 262176 | tf_op jit(solution)/shard_map/ppermute | solution.py:653
  51.6 0.1 collective-permute-done.18.refs_1_
  51.8 4.3 %shard_map.36.refs_4_.partial = f32[640,512]{1,0:T(8,128)S(1)} custom-call(f32[16,512]{1,0:T(8,128)S(1)} %get-tuple-element.25.keep, bf16[256,512]{1,0:T(8,128)(2,1)S(1)} %get-tuple-element.40.refs_0_, bf16[256,512]{1,0:T(8,128)(2,1)S(1)} %collective-permute-done.18.refs_1_, bf16[384,512]{1,0:T(8,128)(2,1)S(1)} %get-tuple-element.39.refs_2_, ...), custom_call_target="tpu_custom_call" | custom-call | tf_op jit(solution)/shard_map/pallas_call | solution.py:634
  56.0 1.3 %shard_map.37 = (f32[256,512]{1,0:T(8,128)S(1)}, bf16[1024,896]{1,0:T(8,128)(2,1)S(1)}, bf16[1024,896]{1,0:T(8,128)(2,1)S(1)}) custom-call(f32[16,512]{1,0:T(8,128)S(1)} %get-tuple-element.25.keep, bf16[256,512]{1,0:T(8,128)(2,1)S(1)} %collective-permute-done.16.refs_0_, bf16[256,512]{1,0:T(8,128)(2,1)S(1)} %collective-permute-done.17.refs_1_, ...), custom_call_target="tpu_custom_call" | custom-call | tf_op jit(solution)/shard_map/pallas_call | solution.py:634
  57.4 3.5 %collective-permute-done.15.in_ref = bf16[384,512]{1,0:T(8,128)(2,1)S(1)} collective-permute-done((bf16[384,512]{1,0:T(8,128)(2,1)S(1)}, bf16[384,512]{1,0:T(8,128)(2,1)S(1)}, u32[]{:S(2)}, u32[]{:S(2)}) %collective-permute-start.15) | collective-permute-done | bytes 393248 | tf_op jit(solution)/shard_map/ppermute | solution.py:653
  60.9 0.1 collective-permute-start.20
  61.0 1.2 %shard_map.39.partial = f32[384,512]{1,0:T(8,128)S(1)} custom-call(f32[16,512]{1,0:T(8,128)S(1)} %get-tuple-element.25.keep, bf16[384,512]{1,0:T(8,128)(2,1)S(1)} %shard_map.38.square, bf16[1024,896]{1,0:T(8,128)(2,1)S(1)} %get-tuple-element.44.right, f32[640,512]{1,0:T(8,128)S(1)} %shard_map.36.refs_4_.partial), custom_call_target="tpu_custom_call" | custom-call | tf_op jit(solution)/shard_map/pallas_call | solution.py:634
  62.3 0.5 collective-permute-done.20.square
  62.7 1.9 %shard_map.40 = f32[640,512]{1,0:T(8,128)} custom-call(f32[16,512]{1,0:T(8,128)S(1)} %get-tuple-element.25.keep, bf16[384,512]{1,0:T(8,128)(2,1)S(1)} %collective-permute-done.20.square, bf16[1024,896]{1,0:T(8,128)(2,1)S(1)} %get-tuple-element.43.right, f32[384,512]{1,0:T(8,128)S(1)} %shard_map.39.partial, f32[256,512]{1,0:T(8,128)S(1)} %get-tuple-element.42.refs_0_.done), custom_call_target="tpu_custom_call" | custom-call | tf_op jit(solution)/shard_map/pallas_call | solution.py:634
  (7 shorter events, 0.1 us)
Async XLA Ops:
  1.3 20.0 %collective-permute-start.3 = (bf16[640,512]{1,0:T(8,128)(2,1)S(1)}, bf16[640,512]{1,0:T(8,128)(2,1)S(1)}, u32[]{:S(2)}, u32[]{:S(2)}) collective-permute-start(bf16[640,512]{1,0:T(8,128)(2,1)S(1)} %get-tuple-element.26.own_ref.own), channel_id=1, source_target_pairs={{0,7},{1,0},{2,1},{3,2},{4,3},{5,4},{6,5},{7,6},{8,15},{9,8},{10,9... | collective-permute-start | bytes 1966088 | tf_op jit(solution)/shard_map/ppermute | solution.py:662
  7.3 1.6 %collective-permute-start = (bf16[320,512]{1,0:T(8,128)(2,1)S(1)}, bf16[320,512]{1,0:T(8,128)(2,1)S(1)}, u32[]{:S(2)}, u32[]{:S(2)}) collective-permute-start(bf16[320,512]{1,0:T(8,128)(2,1)S(1)} %get-tuple-element.27), channel_id=1, source_target_pairs={{0,8},{8,0},{16,24},{24,16},{1,9},{9,1},{17,25},{25,17},{2,10},{10... | collective-permute-start | bytes 983048 | tf_op jit(solution)/shard_map/ppermute | solution.py:653
  7.3 17.5 %collective-permute-start.2 = (bf16[640,512]{1,0:T(8,128)(2,1)S(1)}, bf16[640,512]{1,0:T(8,128)(2,1)S(1)}, u32[]{:S(2)}, u32[]{:S(2)}) collective-permute-start(bf16[640,512]{1,0:T(8,128)(2,1)S(1)} %get-tuple-element.26.own_ref.own), channel_id=1, source_target_pairs={{0,16},{8,24},{16,0},{24,8},{1,17},{9,25},{17,1},{25,9},{2,18},{10... | collective-permute-start | bytes 1966088 | tf_op jit(solution)/shard_map/ppermute | solution.py:653
  9.0 15.8 %collective-permute-start.1 = (bf16[160,1408]{1,0:T(8,128)(2,1)S(1)}, bf16[160,1408]{1,0:T(8,128)(2,1)S(1)}, u32[]{:S(2)}, u32[]{:S(2)}) collective-permute-start(bf16[160,1408]{1,0:T(8,128)(2,1)S(1)} %get-tuple-element.28.own_ref), channel_id=1, source_target_pairs={{1,3},{3,5},{5,7},{7,1},{9,11},{11,13},{13,15},{15,9},{16,22},{18,... | collective-permute-start | bytes 1351688 | tf_op jit(solution)/shard_map/ppermute | solution.py:662
  9.7 15.4 %collective-permute-start.6 = (bf16[640,512]{1,0:T(8,128)(2,1)S(1)}, bf16[640,512]{1,0:T(8,128)(2,1)S(1)}, u32[]{:S(2)}, u32[]{:S(2)}) collective-permute-start(bf16[640,512]{1,0:T(8,128)(2,1)S(1)} %get-tuple-element.26.own_ref.own), channel_id=1, source_target_pairs={{0,8},{8,0},{16,24},{24,16},{1,9},{9,1},{17,25},{25,17},{2,10},{10... | collective-permute-start | bytes 1966088 | tf_op jit(solution)/shard_map/ppermute | solution.py:653
  21.3 17.2 %collective-permute-start.11 = (bf16[640,512]{1,0:T(8,128)(2,1)S(1)}, bf16[640,512]{1,0:T(8,128)(2,1)S(1)}, u32[]{:S(2)}, u32[]{:S(2)}) collective-permute-start(bf16[640,512]{1,0:T(8,128)(2,1)S(1)} %collective-permute-done.3.after_ref.refs_2_), channel_id=1, source_target_pairs={{0,16},{8,24},{16,0},{24,8},{1,17},{9,25},{17,1},{25,9},{2,18},{10... | collective-permute-start | bytes 1966088 | tf_op jit(solution)/shard_map/ppermute | solution.py:653
  24.9 14.3 %collective-permute-start.4 = (bf16[480,512]{1,0:T(8,128)(2,1)S(1)}, bf16[480,512]{1,0:T(8,128)(2,1)S(1)}, u32[]{:S(2)}, u32[]{:S(2)}) collective-permute-start(bf16[480,512]{1,0:T(8,128)(2,1)S(1)} %get-tuple-element.30), channel_id=1, source_target_pairs={{0,2},{1,3},{2,4},{3,5},{4,6},{5,7},{6,0},{7,1},{8,10},{9,11},{10,... | collective-permute-start | bytes 1474568 | tf_op jit(solution)/shard_map/ppermute | solution.py:662
  25.0 14.3 %collective-permute-start.13 = (bf16[160,1408]{1,0:T(8,128)(2,1)S(1)}, bf16[160,1408]{1,0:T(8,128)(2,1)S(1)}, u32[]{:S(2)}, u32[]{:S(2)}) collective-permute-start(bf16[160,1408]{1,0:T(8,128)(2,1)S(1)} %get-tuple-element.34), channel_id=1, source_target_pairs={{0,1},{1,0},{2,3},{3,2},{4,5},{5,4},{6,7},{7,6},{8,9},{9,8},{10,11... | collective-permute-start | bytes 1351688 | tf_op jit(solution)/shard_map/ppermute | solution.py:696
  25.1 14.7 %collective-permute-start.8 = (bf16[640,512]{1,0:T(8,128)(2,1)S(1)}, bf16[640,512]{1,0:T(8,128)(2,1)S(1)}, u32[]{:S(2)}, u32[]{:S(2)}) collective-permute-start(bf16[640,512]{1,0:T(8,128)(2,1)S(1)} %collective-permute-done.3.after_ref.refs_2_), channel_id=1, source_target_pairs={{0,8},{8,0},{16,24},{24,16},{1,9},{9,1},{17,25},{25,17},{2,10},{10... | collective-permute-start | bytes 1966088 | tf_op jit(solution)/shard_map/ppermute | solution.py:653
  25.2 14.6 %collective-permute-start.7 = (bf16[640,512]{1,0:T(8,128)(2,1)S(1)}, bf16[640,512]{1,0:T(8,128)(2,1)S(1)}, u32[]{:S(2)}, u32[]{:S(2)}) collective-permute-start(bf16[640,512]{1,0:T(8,128)(2,1)S(1)} %collective-permute-done.2.other_ref.refs_0_), channel_id=1, source_target_pairs={{0,8},{8,0},{16,24},{24,16},{1,9},{9,1},{17,25},{25,17},{2,10},{10... | collective-permute-start | bytes 1966088 | tf_op jit(solution)/shard_map/ppermute | solution.py:653
  38.5 3.6 %collective-permute-start.12 = (bf16[640,512]{1,0:T(8,128)(2,1)S(1)}, bf16[640,512]{1,0:T(8,128)(2,1)S(1)}, u32[]{:S(2)}, u32[]{:S(2)}) collective-permute-start(bf16[640,512]{1,0:T(8,128)(2,1)S(1)} %collective-permute-done.11.refs_0_), channel_id=1, source_target_pairs={{0,8},{8,0},{16,24},{24,16},{1,9},{9,1},{17,25},{25,17},{2,10},{10... | collective-permute-start | bytes 1966088 | tf_op jit(solution)/shard_map/ppermute | solution.py:653
  39.2 2.3 %collective-permute-start.5 = (bf16[480,512]{1,0:T(8,128)(2,1)S(1)}, bf16[480,512]{1,0:T(8,128)(2,1)S(1)}, u32[]{:S(2)}, u32[]{:S(2)}) collective-permute-start(bf16[480,512]{1,0:T(8,128)(2,1)S(1)} %collective-permute-done.4.far_own.refs_4_), channel_id=1, source_target_pairs={{0,8},{8,0},{16,24},{24,16},{1,9},{9,1},{17,25},{25,17},{2,10},{10... | collective-permute-start | bytes 1474568 | tf_op jit(solution)/shard_map/ppermute | solution.py:653
  39.2 2.9 %collective-permute-start.14 = (bf16[160,1408]{1,0:T(8,128)(2,1)S(1)}, bf16[160,1408]{1,0:T(8,128)(2,1)S(1)}, u32[]{:S(2)}, u32[]{:S(2)}) collective-permute-start(bf16[160,1408]{1,0:T(8,128)(2,1)S(1)} %collective-permute-done.13.refs_2_), channel_id=1, source_target_pairs={{0,8},{8,0},{16,24},{24,16},{1,9},{9,1},{17,25},{25,17},{2,10},{10... | collective-permute-start | bytes 1351688 | tf_op jit(solution)/shard_map/ppermute | solution.py:653
  41.6 4.5 %collective-permute-start.9 = (bf16[96,384]{1,0:T(8,128)(2,1)S(1)}, bf16[96,384]{1,0:T(8,128)(2,1)S(1)}, u32[]{:S(2)}, u32[]{:S(2)}) collective-permute-start(bf16[96,384]{1,0:T(8,128)(2,1)S(1)} %shard_map.32), channel_id=1, source_target_pairs={{0,16},{8,24},{16,0},{24,8},{1,17},{9,25},{17,1},{25,9},{2,18},{10... | collective-permute-start | bytes 221192 | tf_op jit(solution)/shard_map/ppermute | solution.py:653
  43.4 8.3 %collective-permute-start.16 = (bf16[256,512]{1,0:T(8,128)(2,1)S(1)}, bf16[256,512]{1,0:T(8,128)(2,1)S(1)}, u32[]{:S(2)}, u32[]{:S(2)}) collective-permute-start(bf16[256,512]{1,0:T(8,128)(2,1)S(1)} %get-tuple-element.40.refs_0_), channel_id=1, source_target_pairs={{0,16},{8,24},{16,0},{24,8},{1,17},{9,25},{17,1},{25,9},{2,18},{10... | collective-permute-start | bytes 786440 | tf_op jit(solution)/shard_map/ppermute | solution.py:653
  46.1 2.4 %collective-permute-start.10 = (bf16[96,384]{1,0:T(8,128)(2,1)S(1)}, bf16[96,384]{1,0:T(8,128)(2,1)S(1)}, u32[]{:S(2)}, u32[]{:S(2)}) collective-permute-start(bf16[96,384]{1,0:T(8,128)(2,1)S(1)} %collective-permute-done.9.far), channel_id=1, source_target_pairs={{0,8},{8,0},{16,24},{24,16},{1,9},{9,1},{17,25},{25,17},{2,10},{10... | collective-permute-start | bytes 221192 | tf_op jit(solution)/shard_map/ppermute | solution.py:653
  49.2 2.5 %collective-permute-start.19 = (bf16[384,512]{1,0:T(8,128)(2,1)S(1)}, bf16[384,512]{1,0:T(8,128)(2,1)S(1)}, u32[]{:S(2)}, u32[]{:S(2)}) collective-permute-start(bf16[384,512]{1,0:T(8,128)(2,1)S(1)} %get-tuple-element.39.refs_2_), channel_id=1, source_target_pairs={{0,8},{8,0},{16,24},{24,16},{1,9},{9,1},{17,25},{25,17},{2,10},{10... | collective-permute-start | bytes 1179656 | tf_op jit(solution)/shard_map/ppermute | solution.py:653
  49.8 11.1 %collective-permute-start.15 = (bf16[384,512]{1,0:T(8,128)(2,1)S(1)}, bf16[384,512]{1,0:T(8,128)(2,1)S(1)}, u32[]{:S(2)}, u32[]{:S(2)}) collective-permute-start(bf16[384,512]{1,0:T(8,128)(2,1)S(1)} %get-tuple-element.39.refs_2_), channel_id=1, source_target_pairs={{0,16},{8,24},{16,0},{24,8},{1,17},{9,25},{17,1},{25,9},{2,18},{10... | collective-permute-start | bytes 1179656 | tf_op jit(solution)/shard_map/ppermute | solution.py:653
  50.2 1.5 %collective-permute-start.18 = (bf16[256,512]{1,0:T(8,128)(2,1)S(1)}, bf16[256,512]{1,0:T(8,128)(2,1)S(1)}, u32[]{:S(2)}, u32[]{:S(2)}) collective-permute-start(bf16[256,512]{1,0:T(8,128)(2,1)S(1)} %get-tuple-element.40.refs_0_), channel_id=1, source_target_pairs={{0,8},{8,0},{16,24},{24,16},{1,9},{9,1},{17,25},{25,17},{2,10},{10... | collective-permute-start | bytes 786440 | tf_op jit(solution)/shard_map/ppermute | solution.py:653
  51.6 4.4 %collective-permute-start.17 = (bf16[256,512]{1,0:T(8,128)(2,1)S(1)}, bf16[256,512]{1,0:T(8,128)(2,1)S(1)}, u32[]{:S(2)}, u32[]{:S(2)}) collective-permute-start(bf16[256,512]{1,0:T(8,128)(2,1)S(1)} %collective-permute-done.16.refs_0_), channel_id=1, source_target_pairs={{0,8},{8,0},{16,24},{24,16},{1,9},{9,1},{17,25},{25,17},{2,10},{10... | collective-permute-start | bytes 786440 | tf_op jit(solution)/shard_map/ppermute | solution.py:653
  60.9 1.8 %collective-permute-start.20 = (bf16[384,512]{1,0:T(8,128)(2,1)S(1)}, bf16[384,512]{1,0:T(8,128)(2,1)S(1)}, u32[]{:S(2)}, u32[]{:S(2)}) collective-permute-start(bf16[384,512]{1,0:T(8,128)(2,1)S(1)} %shard_map.38.square), channel_id=1, source_target_pairs={{0,8},{8,0},{16,24},{24,16},{1,9},{9,1},{17,25},{25,17},{2,10},{10... | collective-permute-start | bytes 1179656 | tf_op jit(solution)/shard_map/ppermute | solution.py:653

commit v7 on v6

--- a/solution.py
+++ b/solution.py
@@ -322,33 +322,47 @@
     return range(first, first + g.group(name)[0])
 
 
-def early_kernel(g, own, beside, *refs):
-    others, thins = refs[:2], refs[2:4]
-    inner, sum_a, late_a, band, left_a, pair = refs[4:]
-    layer = layer_index()
-    side, core = layer // 2, layer % 2
-    cols = g.slab * g.size
-    for q, slab in enumerate((own, beside, *others)):
-        band[:, pl.ds(pl.multiple_of((layer ^ q) * cols, cols), cols)] = slab[...]
-    fill_pair(g, core, thins, pair)
-
-    def gather(side):
+class Slabs:
+    def __init__(self, g, layer, slabs):
+        self.width, self.slabs, self.layer = g.slab * g.size, slabs, layer
+
+    def __getitem__(self, at):
+        rows, cols = at
+        found = []
+        for place in range(len(self.slabs)):
+            lo, hi = max(cols.start, place * self.width), min(cols.stop, (place + 1) * self.width)
+            if lo < hi:
+                here = slice(lo - place * self.width, hi - place * self.width)
+                found.append(self.slabs[self.layer ^ place][rows, here])
+        return found[0] if len(found) == 1 else jnp.concatenate(found, axis=1)
+
+
+def early_kernel(g, *refs):
+    owns, thins = refs[:4], refs[4:6]
+    inner, sum_a, late_a, left_a = refs[6:]
+    side, core = layer_index() // 2, layer_index() % 2
+
+    def gather(layer):
+        side, core = layer // 2, layer % 2
+        band, pair = Slabs(g, layer, owns), Slabs(g, core, thins)
         near = g.reached(step_of(side, NEAR_THIN))
         early, late = (g.inner_rows(side, part) for part in ("early", "late"))
         for k, t in enumerate(early):
             if 0 <= t < g.rows:
-                part = (0, g.offsets, lambda a, b, t=t: band[
-                    t * g.size : (t + 1) * g.size, a * g.size : b * g.size
-                ])
+                source, row, lead, limit = band, t, 0, g.offsets
             else:
-                part = pair_part(g, side, pair, (t - near[0]) * g.size, g.size)
+                source, row, lead, limit = pair, t - near[0], g.pair * side, g.pair
+            rows = slice(row * g.size, (row + 1) * g.size)
+            part = (lead, lead + limit, lambda a, b, source=source, rows=rows, lead=lead: source[
+                rows, (a - lead) * g.size : (b - lead) * g.size
+            ])
             place_parts(g, inner, k * g.size, g.size, t, side, [part])
         rows = group_rows(g, side, "A")
         for left, inner_rows in ((left_a, early), (late_a, late)):
             left_rows(g, left, inner_rows, rows, band, rows[0], 0, g.offsets)
 
-    for value in (0, 1):
-        pl.when(side == value)(functools.partial(gather, value))
+    for value in range(g.layers):
+        pl.when(layer_index() == value)(functools.partial(gather, value))
     col, (_, cols) = group_first(g, side, "A"), g.group("A")
     sum_a[...] = dot(left_a[...], window_of(g, core, inner, col, cols))
 
@@ -404,16 +418,19 @@
         square[n * g.size : (n + 1) * g.size, :] = row_of(n)
 
 
-def sum_kernel(g, band, early, late, out, far_left, early_left, late_left):
+def sum_kernel(g, *refs):
+    owns, (early, late, out, far_left, early_left, late_left) = refs[:4], refs[4:]
     side, core = layer_index() // 2, layer_index() % 2
 
-    def fill(side):
+    def fill(layer):
+        side = layer // 2
         rows = group_rows(g, side, "B")
         for left, part in ((early_left, "early"), (late_left, "late"), (far_left, "far")):
-            left_rows(g, left, g.inner_rows(side, part), rows, band, rows[0], 0, g.offsets)
-
-    for value in (0, 1):
-        pl.when(side == value)(functools.partial(fill, value))
+            inner_rows = g.inner_rows(side, part)
+            left_rows(g, left, inner_rows, rows, Slabs(g, layer, owns), rows[0], 0, g.offsets)
+
+    for value in range(g.layers):
+        pl.when(layer_index() == value)(functools.partial(fill, value))
     first, (_, cols) = group_first(g, side, "B"), g.group("B")
     out[...] = dot(early_left[...], window_of(g, core, early, first, cols))
     out[...] += dot(late_left[...], window_of(g, core, late, first, cols))
@@ -701,14 +718,11 @@
     span = g.span * g.size
     f32 = functools.partial(jax.ShapeDtypeStruct, dtype=jnp.float32)
 
-    inner_early, sum_a, late_a, band = call(
+    slabs = (masked, beside, other, swap(other, 1))
+    inner_early, sum_a, late_a = call(
         functools.partial(early_kernel, g),
-        [
-            bf16((early, span)), f32((high_a, wide_a)), bf16((high_a, late)),
-            bf16((rows_dev, layers * cols)),
-        ],
-        [scratch(high_a, early), scratch(rows_dev, 2 * cols)],
-        masked, beside, other, swap(other, 1), thin, swap(thin, 1),
+        [bf16((early, span)), f32((high_a, wide_a)), bf16((high_a, late))], [scratch(high_a, early)],
+        *slabs, thin, swap(thin, 1),
     )
     far_beside = swap(far_wide, 1)
     far_thin = call(
@@ -727,7 +741,7 @@
     sum_b, far_b = call(
         functools.partial(sum_kernel, g),
         [f32((high_b, wide_b)), bf16((high_b, far))], [scratch(high_b, early), scratch(high_b, late)],
-        band, inner_early, inner_late,
+        *slabs, inner_early, inner_late,
     )
     square_b, inner_far = call(
         functools.partial(square_kernel, g),

time: 64.9 us -> 64.6 us (level)
  transfers between devices with their start and end apart: 21 -> 21, of which waited for: 10 -> 11; matrix products, arithmetic and copies ran while one was open for 0% -> 0% of each run, Pallas kernels for 20% -> 20%
where the time goes in v7:
time: 64.6 us; the launch traced here: 64.4 us
  waiting for transfers between devices  34.3 us (53%)
  Pallas kernels  15.9 us (25%)
  starting transfers between devices  13.9 us (22%)
    ppermute x17, waiting for transfers between devices, swap(): return lax.ppermute(value, 'layer', [(s, s ^ bit) for s in range(layers)])  22.2 us
    pallas_call x13, Pallas kernels, call(): pl.pallas_call(kernel, out_shape=out_shape, in_specs=specs, out_specs=jax...  15.9 us
    ppermute x3, waiting for transfers between devices, send(): return lax.ppermute(value, ('layer', 'row'), pairs)  12.1 us
    ppermute x17, starting transfers between devices, swap(): return lax.ppermute(value, 'layer', [(s, s ^ bit) for s in range(layers)])  7 us
    ppermute x3, starting transfers between devices, send(): return lax.ppermute(value, ('layer', 'row'), pairs)  6.81 us
  transfers between devices with their start and end apart: 21, of which 11 were waited for; matrix products, arithmetic and copies ran while one was open for 0% of the time, Pallas kernels for 20%

profile of v7, /device:TPU:0, one launch (start us, length us, event | category | flops | bytes accessed | tf_op | source)
XLA Modules:
  0.0 64.4 jit_solution(4933172230796882404)
XLA Ops:
  0.0 1.2 %shard_map.28 = (bf16[640,512]{1,0:T(8,128)(2,1)S(1)}, f32[16,512]{1,0:T(8,128)S(1)}, bf16[320,512]{1,0:T(8,128)(2,1)S(1)}) custom-call(bf16[640,512]{1,0:T(8,128)(2,1)} %density_ref.1, s32[8,10]{1,0:T(8,128)} %bitcast.1), custom_call_target="tpu_custom_call" | custom-call | tf_op jit(solution)/shard_map/pallas_call | solution.py:651
  1.3 6.1 %collective-permute-start.3 = (bf16[640,512]{1,0:T(8,128)(2,1)S(1)}, bf16[640,512]{1,0:T(8,128)(2,1)S(1)}, u32[]{:S(2)}, u32[]{:S(2)}) collective-permute-start(bf16[640,512]{1,0:T(8,128)(2,1)S(1)} %get-tuple-element.25.own_ref.refs_0_), channel_id=1, source_target_pairs={{0,7},{1,0},{2,1},{3,2},{4,3},{5,4},{6,5},{7,6},{8,15},{9,8},{10,9... | collective-permute-start | bytes 1966088 | tf_op jit(solution)/shard_map/ppermute | solution.py:679
  7.3 0.0 collective-permute-start
  7.3 0.0 collective-permute-start.2
  7.3 1.6 %collective-permute-done.given_ref = bf16[320,512]{1,0:T(8,128)(2,1)S(1)} collective-permute-done((bf16[320,512]{1,0:T(8,128)(2,1)S(1)}, bf16[320,512]{1,0:T(8,128)(2,1)S(1)}, u32[]{:S(2)}, u32[]{:S(2)}) %collective-permute-start) | collective-permute-done | bytes 327712 | tf_op jit(solution)/shard_map/ppermute | solution.py:670
  8.9 0.1 shard_map.29
  9.0 0.7 %collective-permute-start.1 = (bf16[160,1408]{1,0:T(8,128)(2,1)S(1)}, bf16[160,1408]{1,0:T(8,128)(2,1)S(1)}, u32[]{:S(2)}, u32[]{:S(2)}) collective-permute-start(bf16[160,1408]{1,0:T(8,128)(2,1)S(1)} %get-tuple-element.27.own_ref), channel_id=1, source_target_pairs={{1,3},{3,5},{5,7},{7,1},{9,11},{11,13},{13,15},{15,9},{16,22},{18,... | collective-permute-start | bytes 1351688 | tf_op jit(solution)/shard_map/ppermute | solution.py:679
  9.7 0.2 collective-permute-start.6
  9.9 11.3 %collective-permute-done.3.after_ref.refs_4_ = bf16[640,512]{1,0:T(8,128)(2,1)S(1)} collective-permute-done((bf16[640,512]{1,0:T(8,128)(2,1)S(1)}, bf16[640,512]{1,0:T(8,128)(2,1)S(1)}, u32[]{:S(2)}, u32[]{:S(2)}) %collective-permute-start.3) | collective-permute-done | bytes 655392 | tf_op jit(solution)/shard_map/ppermute | solution.py:679
  21.3 2.2 %collective-permute-start.11 = (bf16[640,512]{1,0:T(8,128)(2,1)S(1)}, bf16[640,512]{1,0:T(8,128)(2,1)S(1)}, u32[]{:S(2)}, u32[]{:S(2)}) collective-permute-start(bf16[640,512]{1,0:T(8,128)(2,1)S(1)} %collective-permute-done.3.after_ref.refs_4_), channel_id=1, source_target_pairs={{0,16},{8,24},{16,0},{24,8},{1,17},{9,25},{17,1},{25,9},{2,18},{10... | collective-permute-start | bytes 1966088 | tf_op jit(solution)/shard_map/ppermute | solution.py:670
  23.5 1.3 %collective-permute-done.2.other_ref.refs_2_ = bf16[640,512]{1,0:T(8,128)(2,1)S(1)} collective-permute-done((bf16[640,512]{1,0:T(8,128)(2,1)S(1)}, bf16[640,512]{1,0:T(8,128)(2,1)S(1)}, u32[]{:S(2)}, u32[]{:S(2)}) %collective-permute-start.2) | collective-permute-done | bytes 655392 | tf_op jit(solution)/shard_map/ppermute | solution.py:670
  24.8 0.0 collective-permute-done.1.relayed_ref
  24.8 0.1 shard_map.30
  24.9 0.1 collective-permute-start.4
  25.0 0.1 collective-permute-start.13
  25.1 0.1 collective-permute-start.7
  25.1 0.0 collective-permute-done.6.refs_1_
  25.2 0.5 collective-permute-start.8
  25.7 12.9 %collective-permute-done.11.refs_0_ = bf16[640,512]{1,0:T(8,128)(2,1)S(1)} collective-permute-done((bf16[640,512]{1,0:T(8,128)(2,1)S(1)}, bf16[640,512]{1,0:T(8,128)(2,1)S(1)}, u32[]{:S(2)}, u32[]{:S(2)}) %collective-permute-start.11) | collective-permute-done | bytes 655392 | tf_op jit(solution)/shard_map/ppermute | solution.py:670
  38.5 0.0 collective-permute-start.12
  38.5 0.7 %collective-permute-done.4.far_own.refs_4_ = bf16[480,512]{1,0:T(8,128)(2,1)S(1)} collective-permute-done((bf16[480,512]{1,0:T(8,128)(2,1)S(1)}, bf16[480,512]{1,0:T(8,128)(2,1)S(1)}, u32[]{:S(2)}, u32[]{:S(2)}) %collective-permute-start.4) | collective-permute-done | bytes 491552 | tf_op jit(solution)/shard_map/ppermute | solution.py:679
  39.2 0.0 collective-permute-start.5
  39.2 0.0 collective-permute-done.13.refs_2_
  39.3 0.5 collective-permute-start.14
  39.8 0.0 collective-permute-done.7.refs_3_
  39.8 1.4 %shard_map.31 = (bf16[1280,1664]{1,0:T(8,128)(2,1)S(1)}, f32[256,768]{1,0:T(8,128)S(1)}, bf16[256,1024]{1,0:T(8,128)(2,1)S(1)}) custom-call(bf16[640,512]{1,0:T(8,128)(2,1)S(1)} %get-tuple-element.25.own_ref.refs_0_, bf16[640,512]{1,0:T(8,128)(2,1)S(1)} %collective-permute-done.6.refs_1_, bf16[640,512]{1,0:T(8,128)(2,1)S(1)} %collective-permute-done.2.other_ref.refs_2_, ...), custom_call_target="tpu_custom_call" | custom-call | tf_op jit(solution)/shard_map/pallas_call | solution.py:651
  41.2 0.1 collective-permute-done.5.far_beside.refs_5_
  41.3 0.8 %collective-permute-start.9 = (bf16[96,384]{1,0:T(8,128)(2,1)S(1)}, bf16[96,384]{1,0:T(8,128)(2,1)S(1)}, u32[]{:S(2)}, u32[]{:S(2)}) collective-permute-start(bf16[96,384]{1,0:T(8,128)(2,1)S(1)} %shard_map.32), channel_id=1, source_target_pairs={{0,16},{8,24},{16,0},{24,8},{1,17},{9,25},{17,1},{25,9},{2,18},{10... | collective-permute-start | bytes 221192 | tf_op jit(solution)/shard_map/ppermute | solution.py:670
  42.1 0.0 collective-permute-done.12.refs_1_
  42.1 1.2 %shard_map.33 = (bf16[256,512]{1,0:T(8,128)(2,1)S(1)}, bf16[1024,1664]{1,0:T(8,128)(2,1)S(1)}) custom-call(f32[16,512]{1,0:T(8,128)S(1)} %get-tuple-element.24.keep, bf16[640,512]{1,0:T(8,128)(2,1)S(1)} %collective-permute-done.11.refs_0_, bf16[640,512]{1,0:T(8,128)(2,1)S(1)} %collective-permute-done.12.refs_1_, ...), custom_call_target="tpu_custom_call" | custom-call | tf_op jit(solution)/shard_map/pallas_call | solution.py:651
  43.4 1.3 %collective-permute-start.16 = (bf16[256,512]{1,0:T(8,128)(2,1)S(1)}, bf16[256,512]{1,0:T(8,128)(2,1)S(1)}, u32[]{:S(2)}, u32[]{:S(2)}) collective-permute-start(bf16[256,512]{1,0:T(8,128)(2,1)S(1)} %get-tuple-element.38.refs_0_), channel_id=1, source_target_pairs={{0,16},{8,24},{16,0},{24,8},{1,17},{9,25},{17,1},{25,9},{2,18},{10... | collective-permute-start | bytes 786440 | tf_op jit(solution)/shard_map/ppermute | solution.py:670
  44.6 1.1 %collective-permute-done.9.far = bf16[96,384]{1,0:T(8,128)(2,1)S(1)} collective-permute-done((bf16[96,384]{1,0:T(8,128)(2,1)S(1)}, bf16[96,384]{1,0:T(8,128)(2,1)S(1)}, u32[]{:S(2)}, u32[]{:S(2)}) %collective-permute-start.9) | collective-permute-done | bytes 73760 | tf_op jit(solution)/shard_map/ppermute | solution.py:670
  45.8 2.3 %shard_map.34 = (f32[384,896]{1,0:T(8,128)S(1)}, bf16[384,384]{1,0:T(8,128)(2,1)S(1)}) custom-call(bf16[640,512]{1,0:T(8,128)(2,1)S(1)} %get-tuple-element.25.own_ref.refs_0_, bf16[640,512]{1,0:T(8,128)(2,1)S(1)} %collective-permute-done.6.refs_1_, bf16[640,512]{1,0:T(8,128)(2,1)S(1)} %collective-permute-done.2.other_ref.refs_2_, ...), custom_call_target="tpu_custom_call" | custom-call | tf_op jit(solution)/shard_map/pallas_call | solution.py:651
  48.1 0.0 collective-permute-done.10.far_beside
  48.1 0.8 %shard_map.35 = (bf16[384,512]{1,0:T(8,128)(2,1)S(1)}, bf16[384,1664]{1,0:T(8,128)(2,1)S(1)}) custom-call(f32[16,512]{1,0:T(8,128)S(1)} %get-tuple-element.24.keep, bf16[96,384]{1,0:T(8,128)(2,1)S(1)} %collective-permute-done.9.far, bf16[96,384]{1,0:T(8,128)(2,1)S(1)} %collective-permute-done.10.far_beside, f32[384,896]{1,0:T(8,128)S(1)} %get-tuple-element.35.total, ...), custom_call_target="tpu_custom_call" | custom-call | tf_op jit(solution)/shard_map/pallas_call | solution.py:651
  48.9 0.6 collective-permute-start.19
  49.5 0.7 %collective-permute-start.15 = (bf16[384,512]{1,0:T(8,128)(2,1)S(1)}, bf16[384,512]{1,0:T(8,128)(2,1)S(1)}, u32[]{:S(2)}, u32[]{:S(2)}) collective-permute-start(bf16[384,512]{1,0:T(8,128)(2,1)S(1)} %get-tuple-element.37.refs_2_), channel_id=1, source_target_pairs={{0,16},{8,24},{16,0},{24,8},{1,17},{9,25},{17,1},{25,9},{2,18},{10... | collective-permute-start | bytes 1179656 | tf_op jit(solution)/shard_map/ppermute | solution.py:670
  50.2 0.0 collective-permute-start.18
  50.2 1.4 %collective-permute-done.16.refs_0_ = bf16[256,512]{1,0:T(8,128)(2,1)S(1)} collective-permute-done((bf16[256,512]{1,0:T(8,128)(2,1)S(1)}, bf16[256,512]{1,0:T(8,128)(2,1)S(1)}, u32[]{:S(2)}, u32[]{:S(2)}) %collective-permute-start.16) | collective-permute-done | bytes 262176 | tf_op jit(solution)/shard_map/ppermute | solution.py:670
  51.6 0.0 collective-permute-start.17
  51.6 0.2 collective-permute-done.18.refs_1_
  51.8 4.3 %shard_map.36.refs_4_.partial = f32[640,512]{1,0:T(8,128)S(1)} custom-call(f32[16,512]{1,0:T(8,128)S(1)} %get-tuple-element.24.keep, bf16[256,512]{1,0:T(8,128)(2,1)S(1)} %get-tuple-element.38.refs_0_, bf16[256,512]{1,0:T(8,128)(2,1)S(1)} %collective-permute-done.18.refs_1_, bf16[384,512]{1,0:T(8,128)(2,1)S(1)} %get-tuple-element.37.refs_2_, ...), custom_call_target="tpu_custom_call" | custom-call | tf_op jit(solution)/shard_map/pallas_call | solution.py:651
  56.0 1.3 %shard_map.37 = (f32[256,512]{1,0:T(8,128)S(1)}, bf16[1024,896]{1,0:T(8,128)(2,1)S(1)}, bf16[1024,896]{1,0:T(8,128)(2,1)S(1)}) custom-call(f32[16,512]{1,0:T(8,128)S(1)} %get-tuple-element.24.keep, bf16[256,512]{1,0:T(8,128)(2,1)S(1)} %collective-permute-done.16.refs_0_, bf16[256,512]{1,0:T(8,128)(2,1)S(1)} %collective-permute-done.17.refs_1_, ...), custom_call_target="tpu_custom_call" | custom-call | tf_op jit(solution)/shard_map/pallas_call | solution.py:651
  57.4 3.2 %collective-permute-done.15.in_ref = bf16[384,512]{1,0:T(8,128)(2,1)S(1)} collective-permute-done((bf16[384,512]{1,0:T(8,128)(2,1)S(1)}, bf16[384,512]{1,0:T(8,128)(2,1)S(1)}, u32[]{:S(2)}, u32[]{:S(2)}) %collective-permute-start.15) | collective-permute-done | bytes 393248 | tf_op jit(solution)/shard_map/ppermute | solution.py:670
  60.6 0.1 collective-permute-start.20
  60.7 1.2 %shard_map.39.partial = f32[384,512]{1,0:T(8,128)S(1)} custom-call(f32[16,512]{1,0:T(8,128)S(1)} %get-tuple-element.24.keep, bf16[384,512]{1,0:T(8,128)(2,1)S(1)} %shard_map.38.square, bf16[1024,896]{1,0:T(8,128)(2,1)S(1)} %get-tuple-element.42.right, f32[640,512]{1,0:T(8,128)S(1)} %shard_map.36.refs_4_.partial), custom_call_target="tpu_custom_call" | custom-call | tf_op jit(solution)/shard_map/pallas_call | solution.py:651
  61.9 0.5 collective-permute-done.20.square
  62.4 1.9 %shard_map.40 = f32[640,512]{1,0:T(8,128)} custom-call(f32[16,512]{1,0:T(8,128)S(1)} %get-tuple-element.24.keep, bf16[384,512]{1,0:T(8,128)(2,1)S(1)} %collective-permute-done.20.square, bf16[1024,896]{1,0:T(8,128)(2,1)S(1)} %get-tuple-element.41.right, f32[384,512]{1,0:T(8,128)S(1)} %shard_map.39.partial, f32[256,512]{1,0:T(8,128)S(1)} %get-tuple-element.40.refs_0_.done), custom_call_target="tpu_custom_call" | custom-call | tf_op jit(solution)/shard_map/pallas_call | solution.py:651
  (7 shorter events, 0.1 us)
Async XLA Ops:
  1.3 20.0 %collective-permute-start.3 = (bf16[640,512]{1,0:T(8,128)(2,1)S(1)}, bf16[640,512]{1,0:T(8,128)(2,1)S(1)}, u32[]{:S(2)}, u32[]{:S(2)}) collective-permute-start(bf16[640,512]{1,0:T(8,128)(2,1)S(1)} %get-tuple-element.25.own_ref.refs_0_), channel_id=1, source_target_pairs={{0,7},{1,0},{2,1},{3,2},{4,3},{5,4},{6,5},{7,6},{8,15},{9,8},{10,9... | collective-permute-start | bytes 1966088 | tf_op jit(solution)/shard_map/ppermute | solution.py:679
  7.3 1.6 %collective-permute-start = (bf16[320,512]{1,0:T(8,128)(2,1)S(1)}, bf16[320,512]{1,0:T(8,128)(2,1)S(1)}, u32[]{:S(2)}, u32[]{:S(2)}) collective-permute-start(bf16[320,512]{1,0:T(8,128)(2,1)S(1)} %get-tuple-element.26), channel_id=1, source_target_pairs={{0,8},{8,0},{16,24},{24,16},{1,9},{9,1},{17,25},{25,17},{2,10},{10... | collective-permute-start | bytes 983048 | tf_op jit(solution)/shard_map/ppermute | solution.py:670
  7.3 17.5 %collective-permute-start.2 = (bf16[640,512]{1,0:T(8,128)(2,1)S(1)}, bf16[640,512]{1,0:T(8,128)(2,1)S(1)}, u32[]{:S(2)}, u32[]{:S(2)}) collective-permute-start(bf16[640,512]{1,0:T(8,128)(2,1)S(1)} %get-tuple-element.25.own_ref.refs_0_), channel_id=1, source_target_pairs={{0,16},{8,24},{16,0},{24,8},{1,17},{9,25},{17,1},{25,9},{2,18},{10... | collective-permute-start | bytes 1966088 | tf_op jit(solution)/shard_map/ppermute | solution.py:670
  9.0 15.8 %collective-permute-start.1 = (bf16[160,1408]{1,0:T(8,128)(2,1)S(1)}, bf16[160,1408]{1,0:T(8,128)(2,1)S(1)}, u32[]{:S(2)}, u32[]{:S(2)}) collective-permute-start(bf16[160,1408]{1,0:T(8,128)(2,1)S(1)} %get-tuple-element.27.own_ref), channel_id=1, source_target_pairs={{1,3},{3,5},{5,7},{7,1},{9,11},{11,13},{13,15},{15,9},{16,22},{18,... | collective-permute-start | bytes 1351688 | tf_op jit(solution)/shard_map/ppermute | solution.py:679
  9.7 15.4 %collective-permute-start.6 = (bf16[640,512]{1,0:T(8,128)(2,1)S(1)}, bf16[640,512]{1,0:T(8,128)(2,1)S(1)}, u32[]{:S(2)}, u32[]{:S(2)}) collective-permute-start(bf16[640,512]{1,0:T(8,128)(2,1)S(1)} %get-tuple-element.25.own_ref.refs_0_), channel_id=1, source_target_pairs={{0,8},{8,0},{16,24},{24,16},{1,9},{9,1},{17,25},{25,17},{2,10},{10... | collective-permute-start | bytes 1966088 | tf_op jit(solution)/shard_map/ppermute | solution.py:670
  21.3 17.2 %collective-permute-start.11 = (bf16[640,512]{1,0:T(8,128)(2,1)S(1)}, bf16[640,512]{1,0:T(8,128)(2,1)S(1)}, u32[]{:S(2)}, u32[]{:S(2)}) collective-permute-start(bf16[640,512]{1,0:T(8,128)(2,1)S(1)} %collective-permute-done.3.after_ref.refs_4_), channel_id=1, source_target_pairs={{0,16},{8,24},{16,0},{24,8},{1,17},{9,25},{17,1},{25,9},{2,18},{10... | collective-permute-start | bytes 1966088 | tf_op jit(solution)/shard_map/ppermute | solution.py:670
  24.9 14.3 %collective-permute-start.4 = (bf16[480,512]{1,0:T(8,128)(2,1)S(1)}, bf16[480,512]{1,0:T(8,128)(2,1)S(1)}, u32[]{:S(2)}, u32[]{:S(2)}) collective-permute-start(bf16[480,512]{1,0:T(8,128)(2,1)S(1)} %get-tuple-element.29), channel_id=1, source_target_pairs={{0,2},{1,3},{2,4},{3,5},{4,6},{5,7},{6,0},{7,1},{8,10},{9,11},{10,... | collective-permute-start | bytes 1474568 | tf_op jit(solution)/shard_map/ppermute | solution.py:679
  25.0 14.3 %collective-permute-start.13 = (bf16[160,1408]{1,0:T(8,128)(2,1)S(1)}, bf16[160,1408]{1,0:T(8,128)(2,1)S(1)}, u32[]{:S(2)}, u32[]{:S(2)}) collective-permute-start(bf16[160,1408]{1,0:T(8,128)(2,1)S(1)} %get-tuple-element.32), channel_id=1, source_target_pairs={{0,1},{1,0},{2,3},{3,2},{4,5},{5,4},{6,7},{7,6},{8,9},{9,8},{10,11... | collective-permute-start | bytes 1351688 | tf_op jit(solution)/shard_map/ppermute | solution.py:713
  25.1 14.7 %collective-permute-start.7 = (bf16[640,512]{1,0:T(8,128)(2,1)S(1)}, bf16[640,512]{1,0:T(8,128)(2,1)S(1)}, u32[]{:S(2)}, u32[]{:S(2)}) collective-permute-start(bf16[640,512]{1,0:T(8,128)(2,1)S(1)} %collective-permute-done.2.other_ref.refs_2_), channel_id=1, source_target_pairs={{0,8},{8,0},{16,24},{24,16},{1,9},{9,1},{17,25},{25,17},{2,10},{10... | collective-permute-start | bytes 1966088 | tf_op jit(solution)/shard_map/ppermute | solution.py:670
  25.2 14.6 %collective-permute-start.8 = (bf16[640,512]{1,0:T(8,128)(2,1)S(1)}, bf16[640,512]{1,0:T(8,128)(2,1)S(1)}, u32[]{:S(2)}, u32[]{:S(2)}) collective-permute-start(bf16[640,512]{1,0:T(8,128)(2,1)S(1)} %collective-permute-done.3.after_ref.refs_4_), channel_id=1, source_target_pairs={{0,8},{8,0},{16,24},{24,16},{1,9},{9,1},{17,25},{25,17},{2,10},{10... | collective-permute-start | bytes 1966088 | tf_op jit(solution)/shard_map/ppermute | solution.py:670
  38.5 3.6 %collective-permute-start.12 = (bf16[640,512]{1,0:T(8,128)(2,1)S(1)}, bf16[640,512]{1,0:T(8,128)(2,1)S(1)}, u32[]{:S(2)}, u32[]{:S(2)}) collective-permute-start(bf16[640,512]{1,0:T(8,128)(2,1)S(1)} %collective-permute-done.11.refs_0_), channel_id=1, source_target_pairs={{0,8},{8,0},{16,24},{24,16},{1,9},{9,1},{17,25},{25,17},{2,10},{10... | collective-permute-start | bytes 1966088 | tf_op jit(solution)/shard_map/ppermute | solution.py:670
  39.2 2.1 %collective-permute-start.5 = (bf16[480,512]{1,0:T(8,128)(2,1)S(1)}, bf16[480,512]{1,0:T(8,128)(2,1)S(1)}, u32[]{:S(2)}, u32[]{:S(2)}) collective-permute-start(bf16[480,512]{1,0:T(8,128)(2,1)S(1)} %collective-permute-done.4.far_own.refs_4_), channel_id=1, source_target_pairs={{0,8},{8,0},{16,24},{24,16},{1,9},{9,1},{17,25},{25,17},{2,10},{10... | collective-permute-start | bytes 1474568 | tf_op jit(solution)/shard_map/ppermute | solution.py:670
  39.3 2.9 %collective-permute-start.14 = (bf16[160,1408]{1,0:T(8,128)(2,1)S(1)}, bf16[160,1408]{1,0:T(8,128)(2,1)S(1)}, u32[]{:S(2)}, u32[]{:S(2)}) collective-permute-start(bf16[160,1408]{1,0:T(8,128)(2,1)S(1)} %collective-permute-done.13.refs_2_), channel_id=1, source_target_pairs={{0,8},{8,0},{16,24},{24,16},{1,9},{9,1},{17,25},{25,17},{2,10},{10... | collective-permute-start | bytes 1351688 | tf_op jit(solution)/shard_map/ppermute | solution.py:670
  41.3 4.4 %collective-permute-start.9 = (bf16[96,384]{1,0:T(8,128)(2,1)S(1)}, bf16[96,384]{1,0:T(8,128)(2,1)S(1)}, u32[]{:S(2)}, u32[]{:S(2)}) collective-permute-start(bf16[96,384]{1,0:T(8,128)(2,1)S(1)} %shard_map.32), channel_id=1, source_target_pairs={{0,16},{8,24},{16,0},{24,8},{1,17},{9,25},{17,1},{25,9},{2,18},{10... | collective-permute-start | bytes 221192 | tf_op jit(solution)/shard_map/ppermute | solution.py:670
  43.4 8.2 %collective-permute-start.16 = (bf16[256,512]{1,0:T(8,128)(2,1)S(1)}, bf16[256,512]{1,0:T(8,128)(2,1)S(1)}, u32[]{:S(2)}, u32[]{:S(2)}) collective-permute-start(bf16[256,512]{1,0:T(8,128)(2,1)S(1)} %get-tuple-element.38.refs_0_), channel_id=1, source_target_pairs={{0,16},{8,24},{16,0},{24,8},{1,17},{9,25},{17,1},{25,9},{2,18},{10... | collective-permute-start | bytes 786440 | tf_op jit(solution)/shard_map/ppermute | solution.py:670
  45.7 2.3 %collective-permute-start.10 = (bf16[96,384]{1,0:T(8,128)(2,1)S(1)}, bf16[96,384]{1,0:T(8,128)(2,1)S(1)}, u32[]{:S(2)}, u32[]{:S(2)}) collective-permute-start(bf16[96,384]{1,0:T(8,128)(2,1)S(1)} %collective-permute-done.9.far), channel_id=1, source_target_pairs={{0,8},{8,0},{16,24},{24,16},{1,9},{9,1},{17,25},{25,17},{2,10},{10... | collective-permute-start | bytes 221192 | tf_op jit(solution)/shard_map/ppermute | solution.py:670
  48.9 2.9 %collective-permute-start.19 = (bf16[384,512]{1,0:T(8,128)(2,1)S(1)}, bf16[384,512]{1,0:T(8,128)(2,1)S(1)}, u32[]{:S(2)}, u32[]{:S(2)}) collective-permute-start(bf16[384,512]{1,0:T(8,128)(2,1)S(1)} %get-tuple-element.37.refs_2_), channel_id=1, source_target_pairs={{0,8},{8,0},{16,24},{24,16},{1,9},{9,1},{17,25},{25,17},{2,10},{10... | collective-permute-start | bytes 1179656 | tf_op jit(solution)/shard_map/ppermute | solution.py:670
  49.5 11.1 %collective-permute-start.15 = (bf16[384,512]{1,0:T(8,128)(2,1)S(1)}, bf16[384,512]{1,0:T(8,128)(2,1)S(1)}, u32[]{:S(2)}, u32[]{:S(2)}) collective-permute-start(bf16[384,512]{1,0:T(8,128)(2,1)S(1)} %get-tuple-element.37.refs_2_), channel_id=1, source_target_pairs={{0,16},{8,24},{16,0},{24,8},{1,17},{9,25},{17,1},{25,9},{2,18},{10... | collective-permute-start | bytes 1179656 | tf_op jit(solution)/shard_map/ppermute | solution.py:670
  50.2 1.5 %collective-permute-start.18 = (bf16[256,512]{1,0:T(8,128)(2,1)S(1)}, bf16[256,512]{1,0:T(8,128)(2,1)S(1)}, u32[]{:S(2)}, u32[]{:S(2)}) collective-permute-start(bf16[256,512]{1,0:T(8,128)(2,1)S(1)} %get-tuple-element.38.refs_0_), channel_id=1, source_target_pairs={{0,8},{8,0},{16,24},{24,16},{1,9},{9,1},{17,25},{25,17},{2,10},{10... | collective-permute-start | bytes 786440 | tf_op jit(solution)/shard_map/ppermute | solution.py:670
  51.6 4.5 %collective-permute-start.17 = (bf16[256,512]{1,0:T(8,128)(2,1)S(1)}, bf16[256,512]{1,0:T(8,128)(2,1)S(1)}, u32[]{:S(2)}, u32[]{:S(2)}) collective-permute-start(bf16[256,512]{1,0:T(8,128)(2,1)S(1)} %collective-permute-done.16.refs_0_), channel_id=1, source_target_pairs={{0,8},{8,0},{16,24},{24,16},{1,9},{9,1},{17,25},{25,17},{2,10},{10... | collective-permute-start | bytes 786440 | tf_op jit(solution)/shard_map/ppermute | solution.py:670
  60.6 1.8 %collective-permute-start.20 = (bf16[384,512]{1,0:T(8,128)(2,1)S(1)}, bf16[384,512]{1,0:T(8,128)(2,1)S(1)}, u32[]{:S(2)}, u32[]{:S(2)}) collective-permute-start(bf16[384,512]{1,0:T(8,128)(2,1)S(1)} %shard_map.38.square), channel_id=1, source_target_pairs={{0,8},{8,0},{16,24},{24,16},{1,9},{9,1},{17,25},{25,17},{2,10},{10... | collective-permute-start | bytes 1179656 | tf_op jit(solution)/shard_map/ppermute | solution.py:670

commit v8 on v7

--- a/solution.py
+++ b/solution.py
@@ -69,8 +69,19 @@
             lo, hi = self.needed(t, side)
             lo, hi = max(lo, self.pair * side), min(hi, self.pair * (side + 1))
             if hi > lo:
-                found.append((even_up(hi) - even_down(lo), t, even_down(lo), even_up(hi)))
+                if name != FAR_WIDE:
+                    lo, hi = even_down(lo), even_up(hi)
+                found.append((hi - lo, t, lo, hi))
         found.sort(reverse=True)
+        if name == FAR_WIDE:
+            places, used = {}, []
+            for width, t, lo, hi in found:
+                free = [n for n, taken in enumerate(used) if taken + width <= self.slab]
+                slot = free[0] if free else len(used)
+                used += [] if free else [0]
+                places[t] = (slot, used[slot], lo, hi)
+                used[slot] += width
+            return places, len(used), max(used)
         slots = (len(found) + 1) // 2
         used = [0] * slots
         places = {}

time: 64.6 us -> 64.6 us (level)
    ppermute x3, waiting for transfers between devices: 12.1 us -> 11.4 us  [send(): return lax.ppermute(value, ('layer', 'row'), pairs)]
  transfers between devices with their start and end apart: 21 -> 21, of which waited for: 11 -> 10; matrix products, arithmetic and copies ran while one was open for 0% -> 0% of each run, Pallas kernels for 20% -> 20%
where the time goes in v8:
time: 64.6 us; the launch traced here: 64.4 us
  waiting for transfers between devices  34.2 us (53%)
  Pallas kernels  15.9 us (25%)
  starting transfers between devices  13.9 us (22%)
    ppermute x17, waiting for transfers between devices, swap(): return lax.ppermute(value, 'layer', [(s, s ^ bit) for s in range(layers)])  22.8 us
    pallas_call x13, Pallas kernels, call(): pl.pallas_call(kernel, out_shape=out_shape, in_specs=specs, out_specs=jax...  15.9 us
    ppermute x3, waiting for transfers between devices, send(): return lax.ppermute(value, ('layer', 'row'), pairs)  11.4 us
    ppermute x17, starting transfers between devices, swap(): return lax.ppermute(value, 'layer', [(s, s ^ bit) for s in range(layers)])  7.05 us
    ppermute x3, starting transfers between devices, send(): return lax.ppermute(value, ('layer', 'row'), pairs)  6.81 us
  transfers between devices with their start and end apart: 21, of which 10 were waited for; matrix products, arithmetic and copies ran while one was open for 0% of the time, Pallas kernels for 20%

profile of v8, /device:TPU:0, one launch (start us, length us, event | category | flops | bytes accessed | tf_op | source)
XLA Modules:
  0.0 64.4 jit_solution(2297205590653765992)
XLA Ops:
  0.0 1.2 %shard_map.28 = (bf16[640,512]{1,0:T(8,128)(2,1)S(1)}, f32[16,512]{1,0:T(8,128)S(1)}, bf16[320,512]{1,0:T(8,128)(2,1)S(1)}) custom-call(bf16[640,512]{1,0:T(8,128)(2,1)} %density_ref.1, s32[8,10]{1,0:T(8,128)} %bitcast.1), custom_call_target="tpu_custom_call" | custom-call | tf_op jit(solution)/shard_map/pallas_call | solution.py:662
  1.3 6.1 %collective-permute-start.3 = (bf16[640,512]{1,0:T(8,128)(2,1)S(1)}, bf16[640,512]{1,0:T(8,128)(2,1)S(1)}, u32[]{:S(2)}, u32[]{:S(2)}) collective-permute-start(bf16[640,512]{1,0:T(8,128)(2,1)S(1)} %get-tuple-element.25.own_ref.refs_0_), channel_id=1, source_target_pairs={{0,7},{1,0},{2,1},{3,2},{4,3},{5,4},{6,5},{7,6},{8,15},{9,8},{10,9... | collective-permute-start | bytes 1966088 | tf_op jit(solution)/shard_map/ppermute | solution.py:690
  7.3 0.0 collective-permute-start
  7.3 0.0 collective-permute-start.2
  7.3 1.6 %collective-permute-done.given_ref = bf16[320,512]{1,0:T(8,128)(2,1)S(1)} collective-permute-done((bf16[320,512]{1,0:T(8,128)(2,1)S(1)}, bf16[320,512]{1,0:T(8,128)(2,1)S(1)}, u32[]{:S(2)}, u32[]{:S(2)}) %collective-permute-start) | collective-permute-done | bytes 327712 | tf_op jit(solution)/shard_map/ppermute | solution.py:681
  8.9 0.1 shard_map.29
  9.1 0.7 %collective-permute-start.1 = (bf16[160,1408]{1,0:T(8,128)(2,1)S(1)}, bf16[160,1408]{1,0:T(8,128)(2,1)S(1)}, u32[]{:S(2)}, u32[]{:S(2)}) collective-permute-start(bf16[160,1408]{1,0:T(8,128)(2,1)S(1)} %get-tuple-element.27.own_ref), channel_id=1, source_target_pairs={{1,3},{3,5},{5,7},{7,1},{9,11},{11,13},{13,15},{15,9},{16,22},{18,... | collective-permute-start | bytes 1351688 | tf_op jit(solution)/shard_map/ppermute | solution.py:690
  9.8 0.2 collective-permute-start.6
  10.0 11.3 %collective-permute-done.3.after_ref.refs_4_ = bf16[640,512]{1,0:T(8,128)(2,1)S(1)} collective-permute-done((bf16[640,512]{1,0:T(8,128)(2,1)S(1)}, bf16[640,512]{1,0:T(8,128)(2,1)S(1)}, u32[]{:S(2)}, u32[]{:S(2)}) %collective-permute-start.3) | collective-permute-done | bytes 655392 | tf_op jit(solution)/shard_map/ppermute | solution.py:690
  21.3 2.2 %collective-permute-start.11 = (bf16[640,512]{1,0:T(8,128)(2,1)S(1)}, bf16[640,512]{1,0:T(8,128)(2,1)S(1)}, u32[]{:S(2)}, u32[]{:S(2)}) collective-permute-start(bf16[640,512]{1,0:T(8,128)(2,1)S(1)} %collective-permute-done.3.after_ref.refs_4_), channel_id=1, source_target_pairs={{0,16},{8,24},{16,0},{24,8},{1,17},{9,25},{17,1},{25,9},{2,18},{10... | collective-permute-start | bytes 1966088 | tf_op jit(solution)/shard_map/ppermute | solution.py:681
  23.5 1.3 %collective-permute-done.2.other_ref.refs_2_ = bf16[640,512]{1,0:T(8,128)(2,1)S(1)} collective-permute-done((bf16[640,512]{1,0:T(8,128)(2,1)S(1)}, bf16[640,512]{1,0:T(8,128)(2,1)S(1)}, u32[]{:S(2)}, u32[]{:S(2)}) %collective-permute-start.2) | collective-permute-done | bytes 655392 | tf_op jit(solution)/shard_map/ppermute | solution.py:681
  24.8 0.0 collective-permute-done.1.relayed_ref
  24.8 0.1 shard_map.30
  24.9 0.1 collective-permute-start.4
  25.0 0.1 collective-permute-start.13
  25.1 0.1 collective-permute-start.7
  25.1 0.0 collective-permute-done.6.refs_1_
  25.2 0.5 collective-permute-start.8
  25.6 12.9 %collective-permute-done.11.refs_0_ = bf16[640,512]{1,0:T(8,128)(2,1)S(1)} collective-permute-done((bf16[640,512]{1,0:T(8,128)(2,1)S(1)}, bf16[640,512]{1,0:T(8,128)(2,1)S(1)}, u32[]{:S(2)}, u32[]{:S(2)}) %collective-permute-start.11) | collective-permute-done | bytes 655392 | tf_op jit(solution)/shard_map/ppermute | solution.py:681
  38.5 0.0 collective-permute-start.12
  38.5 0.0 collective-permute-done.4.far_own.refs_4_
  38.5 0.5 collective-permute-start.5
  39.0 0.0 collective-permute-done.13.refs_2_
  39.0 0.1 collective-permute-start.14
  39.1 1.4 %shard_map.31 = (bf16[1280,1664]{1,0:T(8,128)(2,1)S(1)}, f32[256,768]{1,0:T(8,128)S(1)}, bf16[256,1024]{1,0:T(8,128)(2,1)S(1)}) custom-call(bf16[640,512]{1,0:T(8,128)(2,1)S(1)} %get-tuple-element.25.own_ref.refs_0_, bf16[640,512]{1,0:T(8,128)(2,1)S(1)} %collective-permute-done.6.refs_1_, bf16[640,512]{1,0:T(8,128)(2,1)S(1)} %collective-permute-done.2.other_ref.refs_2_, ...), custom_call_target="tpu_custom_call" | custom-call | tf_op jit(solution)/shard_map/pallas_call | solution.py:662
  40.6 0.7 %collective-permute-done.5.far_beside.refs_5_ = bf16[448,512]{1,0:T(8,128)(2,1)S(1)} collective-permute-done((bf16[448,512]{1,0:T(8,128)(2,1)S(1)}, bf16[448,512]{1,0:T(8,128)(2,1)S(1)}, u32[]{:S(2)}, u32[]{:S(2)}) %collective-permute-start.5) | collective-permute-done | bytes 458784 | tf_op jit(solution)/shard_map/ppermute | solution.py:681
  41.3 0.8 %collective-permute-start.9 = (bf16[96,384]{1,0:T(8,128)(2,1)S(1)}, bf16[96,384]{1,0:T(8,128)(2,1)S(1)}, u32[]{:S(2)}, u32[]{:S(2)}) collective-permute-start(bf16[96,384]{1,0:T(8,128)(2,1)S(1)} %shard_map.32), channel_id=1, source_target_pairs={{0,16},{8,24},{16,0},{24,8},{1,17},{9,25},{17,1},{25,9},{2,18},{10... | collective-permute-start | bytes 221192 | tf_op jit(solution)/shard_map/ppermute | solution.py:681
  42.1 0.0 collective-permute-done.14.refs_3_
  42.1 1.2 %shard_map.33 = (bf16[256,512]{1,0:T(8,128)(2,1)S(1)}, bf16[1024,1664]{1,0:T(8,128)(2,1)S(1)}) custom-call(f32[16,512]{1,0:T(8,128)S(1)} %get-tuple-element.24.keep, bf16[640,512]{1,0:T(8,128)(2,1)S(1)} %collective-permute-done.11.refs_0_, bf16[640,512]{1,0:T(8,128)(2,1)S(1)} %collective-permute-done.12.refs_1_, ...), custom_call_target="tpu_custom_call" | custom-call | tf_op jit(solution)/shard_map/pallas_call | solution.py:662
  43.3 1.3 %collective-permute-start.16 = (bf16[256,512]{1,0:T(8,128)(2,1)S(1)}, bf16[256,512]{1,0:T(8,128)(2,1)S(1)}, u32[]{:S(2)}, u32[]{:S(2)}) collective-permute-start(bf16[256,512]{1,0:T(8,128)(2,1)S(1)} %get-tuple-element.38.refs_0_), channel_id=1, source_target_pairs={{0,16},{8,24},{16,0},{24,8},{1,17},{9,25},{17,1},{25,9},{2,18},{10... | collective-permute-start | bytes 786440 | tf_op jit(solution)/shard_map/ppermute | solution.py:681
  44.6 1.1 %collective-permute-done.9.far = bf16[96,384]{1,0:T(8,128)(2,1)S(1)} collective-permute-done((bf16[96,384]{1,0:T(8,128)(2,1)S(1)}, bf16[96,384]{1,0:T(8,128)(2,1)S(1)}, u32[]{:S(2)}, u32[]{:S(2)}) %collective-permute-start.9) | collective-permute-done | bytes 73760 | tf_op jit(solution)/shard_map/ppermute | solution.py:681
  45.7 0.0 collective-permute-start.10
  45.7 2.3 %shard_map.34 = (f32[384,896]{1,0:T(8,128)S(1)}, bf16[384,384]{1,0:T(8,128)(2,1)S(1)}) custom-call(bf16[640,512]{1,0:T(8,128)(2,1)S(1)} %get-tuple-element.25.own_ref.refs_0_, bf16[640,512]{1,0:T(8,128)(2,1)S(1)} %collective-permute-done.6.refs_1_, bf16[640,512]{1,0:T(8,128)(2,1)S(1)} %collective-permute-done.2.other_ref.refs_2_, ...), custom_call_target="tpu_custom_call" | custom-call | tf_op jit(solution)/shard_map/pallas_call | solution.py:662
  48.1 0.8 %shard_map.35 = (bf16[384,512]{1,0:T(8,128)(2,1)S(1)}, bf16[384,1664]{1,0:T(8,128)(2,1)S(1)}) custom-call(f32[16,512]{1,0:T(8,128)S(1)} %get-tuple-element.24.keep, bf16[96,384]{1,0:T(8,128)(2,1)S(1)} %collective-permute-done.9.far, bf16[96,384]{1,0:T(8,128)(2,1)S(1)} %collective-permute-done.10.far_beside, f32[384,896]{1,0:T(8,128)S(1)} %get-tuple-element.35.total, ...), custom_call_target="tpu_custom_call" | custom-call | tf_op jit(solution)/shard_map/pallas_call | solution.py:662
  48.8 0.6 collective-permute-start.19
  49.4 0.7 %collective-permute-start.15 = (bf16[384,512]{1,0:T(8,128)(2,1)S(1)}, bf16[384,512]{1,0:T(8,128)(2,1)S(1)}, u32[]{:S(2)}, u32[]{:S(2)}) collective-permute-start(bf16[384,512]{1,0:T(8,128)(2,1)S(1)} %get-tuple-element.37.refs_2_), channel_id=1, source_target_pairs={{0,16},{8,24},{16,0},{24,8},{1,17},{9,25},{17,1},{25,9},{2,18},{10... | collective-permute-start | bytes 1179656 | tf_op jit(solution)/shard_map/ppermute | solution.py:681
  50.2 0.0 collective-permute-start.18
  50.2 1.4 %collective-permute-done.16.refs_0_ = bf16[256,512]{1,0:T(8,128)(2,1)S(1)} collective-permute-done((bf16[256,512]{1,0:T(8,128)(2,1)S(1)}, bf16[256,512]{1,0:T(8,128)(2,1)S(1)}, u32[]{:S(2)}, u32[]{:S(2)}) %collective-permute-start.16) | collective-permute-done | bytes 262176 | tf_op jit(solution)/shard_map/ppermute | solution.py:681
  51.5 0.0 collective-permute-start.17
  51.5 0.2 collective-permute-done.18.refs_1_
  51.7 0.0 collective-permute-done.19.refs_3_
  51.7 4.3 %shard_map.36.refs_4_.partial = f32[640,512]{1,0:T(8,128)S(1)} custom-call(f32[16,512]{1,0:T(8,128)S(1)} %get-tuple-element.24.keep, bf16[256,512]{1,0:T(8,128)(2,1)S(1)} %get-tuple-element.38.refs_0_, bf16[256,512]{1,0:T(8,128)(2,1)S(1)} %collective-permute-done.18.refs_1_, bf16[384,512]{1,0:T(8,128)(2,1)S(1)} %get-tuple-element.37.refs_2_, ...), custom_call_target="tpu_custom_call" | custom-call | tf_op jit(solution)/shard_map/pallas_call | solution.py:662
  56.0 1.3 %shard_map.37 = (f32[256,512]{1,0:T(8,128)S(1)}, bf16[1024,896]{1,0:T(8,128)(2,1)S(1)}, bf16[1024,896]{1,0:T(8,128)(2,1)S(1)}) custom-call(f32[16,512]{1,0:T(8,128)S(1)} %get-tuple-element.24.keep, bf16[256,512]{1,0:T(8,128)(2,1)S(1)} %collective-permute-done.16.refs_0_, bf16[256,512]{1,0:T(8,128)(2,1)S(1)} %collective-permute-done.17.refs_1_, ...), custom_call_target="tpu_custom_call" | custom-call | tf_op jit(solution)/shard_map/pallas_call | solution.py:662
  57.3 3.2 %collective-permute-done.15.in_ref = bf16[384,512]{1,0:T(8,128)(2,1)S(1)} collective-permute-done((bf16[384,512]{1,0:T(8,128)(2,1)S(1)}, bf16[384,512]{1,0:T(8,128)(2,1)S(1)}, u32[]{:S(2)}, u32[]{:S(2)}) %collective-permute-start.15) | collective-permute-done | bytes 393248 | tf_op jit(solution)/shard_map/ppermute | solution.py:681
  60.5 0.1 collective-permute-start.20
  60.6 1.2 %shard_map.39.partial = f32[384,512]{1,0:T(8,128)S(1)} custom-call(f32[16,512]{1,0:T(8,128)S(1)} %get-tuple-element.24.keep, bf16[384,512]{1,0:T(8,128)(2,1)S(1)} %shard_map.38.square, bf16[1024,896]{1,0:T(8,128)(2,1)S(1)} %get-tuple-element.42.right, f32[640,512]{1,0:T(8,128)S(1)} %shard_map.36.refs_4_.partial), custom_call_target="tpu_custom_call" | custom-call | tf_op jit(solution)/shard_map/pallas_call | solution.py:662
  61.9 0.5 collective-permute-done.20.square
  62.3 1.9 %shard_map.40 = f32[640,512]{1,0:T(8,128)} custom-call(f32[16,512]{1,0:T(8,128)S(1)} %get-tuple-element.24.keep, bf16[384,512]{1,0:T(8,128)(2,1)S(1)} %collective-permute-done.20.square, bf16[1024,896]{1,0:T(8,128)(2,1)S(1)} %get-tuple-element.41.right, f32[384,512]{1,0:T(8,128)S(1)} %shard_map.39.partial, f32[256,512]{1,0:T(8,128)S(1)} %get-tuple-element.40.refs_0_.done), custom_call_target="tpu_custom_call" | custom-call | tf_op jit(solution)/shard_map/pallas_call | solution.py:662
  (7 shorter events, 0.1 us)
Async XLA Ops:
  1.3 20.0 %collective-permute-start.3 = (bf16[640,512]{1,0:T(8,128)(2,1)S(1)}, bf16[640,512]{1,0:T(8,128)(2,1)S(1)}, u32[]{:S(2)}, u32[]{:S(2)}) collective-permute-start(bf16[640,512]{1,0:T(8,128)(2,1)S(1)} %get-tuple-element.25.own_ref.refs_0_), channel_id=1, source_target_pairs={{0,7},{1,0},{2,1},{3,2},{4,3},{5,4},{6,5},{7,6},{8,15},{9,8},{10,9... | collective-permute-start | bytes 1966088 | tf_op jit(solution)/shard_map/ppermute | solution.py:690
  7.3 1.6 %collective-permute-start = (bf16[320,512]{1,0:T(8,128)(2,1)S(1)}, bf16[320,512]{1,0:T(8,128)(2,1)S(1)}, u32[]{:S(2)}, u32[]{:S(2)}) collective-permute-start(bf16[320,512]{1,0:T(8,128)(2,1)S(1)} %get-tuple-element.26), channel_id=1, source_target_pairs={{0,8},{8,0},{16,24},{24,16},{1,9},{9,1},{17,25},{25,17},{2,10},{10... | collective-permute-start | bytes 983048 | tf_op jit(solution)/shard_map/ppermute | solution.py:681
  7.3 17.5 %collective-permute-start.2 = (bf16[640,512]{1,0:T(8,128)(2,1)S(1)}, bf16[640,512]{1,0:T(8,128)(2,1)S(1)}, u32[]{:S(2)}, u32[]{:S(2)}) collective-permute-start(bf16[640,512]{1,0:T(8,128)(2,1)S(1)} %get-tuple-element.25.own_ref.refs_0_), channel_id=1, source_target_pairs={{0,16},{8,24},{16,0},{24,8},{1,17},{9,25},{17,1},{25,9},{2,18},{10... | collective-permute-start | bytes 1966088 | tf_op jit(solution)/shard_map/ppermute | solution.py:681
  9.1 15.8 %collective-permute-start.1 = (bf16[160,1408]{1,0:T(8,128)(2,1)S(1)}, bf16[160,1408]{1,0:T(8,128)(2,1)S(1)}, u32[]{:S(2)}, u32[]{:S(2)}) collective-permute-start(bf16[160,1408]{1,0:T(8,128)(2,1)S(1)} %get-tuple-element.27.own_ref), channel_id=1, source_target_pairs={{1,3},{3,5},{5,7},{7,1},{9,11},{11,13},{13,15},{15,9},{16,22},{18,... | collective-permute-start | bytes 1351688 | tf_op jit(solution)/shard_map/ppermute | solution.py:690
  9.8 15.4 %collective-permute-start.6 = (bf16[640,512]{1,0:T(8,128)(2,1)S(1)}, bf16[640,512]{1,0:T(8,128)(2,1)S(1)}, u32[]{:S(2)}, u32[]{:S(2)}) collective-permute-start(bf16[640,512]{1,0:T(8,128)(2,1)S(1)} %get-tuple-element.25.own_ref.refs_0_), channel_id=1, source_target_pairs={{0,8},{8,0},{16,24},{24,16},{1,9},{9,1},{17,25},{25,17},{2,10},{10... | collective-permute-start | bytes 1966088 | tf_op jit(solution)/shard_map/ppermute | solution.py:681
  21.3 17.2 %collective-permute-start.11 = (bf16[640,512]{1,0:T(8,128)(2,1)S(1)}, bf16[640,512]{1,0:T(8,128)(2,1)S(1)}, u32[]{:S(2)}, u32[]{:S(2)}) collective-permute-start(bf16[640,512]{1,0:T(8,128)(2,1)S(1)} %collective-permute-done.3.after_ref.refs_4_), channel_id=1, source_target_pairs={{0,16},{8,24},{16,0},{24,8},{1,17},{9,25},{17,1},{25,9},{2,18},{10... | collective-permute-start | bytes 1966088 | tf_op jit(solution)/shard_map/ppermute | solution.py:681
  24.9 13.6 %collective-permute-start.4 = (bf16[448,512]{1,0:T(8,128)(2,1)S(1)}, bf16[448,512]{1,0:T(8,128)(2,1)S(1)}, u32[]{:S(2)}, u32[]{:S(2)}) collective-permute-start(bf16[448,512]{1,0:T(8,128)(2,1)S(1)} %get-tuple-element.29), channel_id=1, source_target_pairs={{0,2},{1,3},{2,4},{3,5},{4,6},{5,7},{6,0},{7,1},{8,10},{9,11},{10,... | collective-permute-start | bytes 1376264 | tf_op jit(solution)/shard_map/ppermute | solution.py:690
  25.0 14.0 %collective-permute-start.13 = (bf16[160,1408]{1,0:T(8,128)(2,1)S(1)}, bf16[160,1408]{1,0:T(8,128)(2,1)S(1)}, u32[]{:S(2)}, u32[]{:S(2)}) collective-permute-start(bf16[160,1408]{1,0:T(8,128)(2,1)S(1)} %get-tuple-element.32), channel_id=1, source_target_pairs={{0,1},{1,0},{2,3},{3,2},{4,5},{5,4},{6,7},{7,6},{8,9},{9,8},{10,11... | collective-permute-start | bytes 1351688 | tf_op jit(solution)/shard_map/ppermute | solution.py:724
  25.1 14.0 %collective-permute-start.7 = (bf16[640,512]{1,0:T(8,128)(2,1)S(1)}, bf16[640,512]{1,0:T(8,128)(2,1)S(1)}, u32[]{:S(2)}, u32[]{:S(2)}) collective-permute-start(bf16[640,512]{1,0:T(8,128)(2,1)S(1)} %collective-permute-done.2.other_ref.refs_2_), channel_id=1, source_target_pairs={{0,8},{8,0},{16,24},{24,16},{1,9},{9,1},{17,25},{25,17},{2,10},{10... | collective-permute-start | bytes 1966088 | tf_op jit(solution)/shard_map/ppermute | solution.py:681
  25.2 13.9 %collective-permute-start.8 = (bf16[640,512]{1,0:T(8,128)(2,1)S(1)}, bf16[640,512]{1,0:T(8,128)(2,1)S(1)}, u32[]{:S(2)}, u32[]{:S(2)}) collective-permute-start(bf16[640,512]{1,0:T(8,128)(2,1)S(1)} %collective-permute-done.3.after_ref.refs_4_), channel_id=1, source_target_pairs={{0,8},{8,0},{16,24},{24,16},{1,9},{9,1},{17,25},{25,17},{2,10},{10... | collective-permute-start | bytes 1966088 | tf_op jit(solution)/shard_map/ppermute | solution.py:681
  38.5 3.6 %collective-permute-start.12 = (bf16[640,512]{1,0:T(8,128)(2,1)S(1)}, bf16[640,512]{1,0:T(8,128)(2,1)S(1)}, u32[]{:S(2)}, u32[]{:S(2)}) collective-permute-start(bf16[640,512]{1,0:T(8,128)(2,1)S(1)} %collective-permute-done.11.refs_0_), channel_id=1, source_target_pairs={{0,8},{8,0},{16,24},{24,16},{1,9},{9,1},{17,25},{25,17},{2,10},{10... | collective-permute-start | bytes 1966088 | tf_op jit(solution)/shard_map/ppermute | solution.py:681
  38.5 2.7 %collective-permute-start.5 = (bf16[448,512]{1,0:T(8,128)(2,1)S(1)}, bf16[448,512]{1,0:T(8,128)(2,1)S(1)}, u32[]{:S(2)}, u32[]{:S(2)}) collective-permute-start(bf16[448,512]{1,0:T(8,128)(2,1)S(1)} %collective-permute-done.4.far_own.refs_4_), channel_id=1, source_target_pairs={{0,8},{8,0},{16,24},{24,16},{1,9},{9,1},{17,25},{25,17},{2,10},{10... | collective-permute-start | bytes 1376264 | tf_op jit(solution)/shard_map/ppermute | solution.py:681
  39.0 3.1 %collective-permute-start.14 = (bf16[160,1408]{1,0:T(8,128)(2,1)S(1)}, bf16[160,1408]{1,0:T(8,128)(2,1)S(1)}, u32[]{:S(2)}, u32[]{:S(2)}) collective-permute-start(bf16[160,1408]{1,0:T(8,128)(2,1)S(1)} %collective-permute-done.13.refs_2_), channel_id=1, source_target_pairs={{0,8},{8,0},{16,24},{24,16},{1,9},{9,1},{17,25},{25,17},{2,10},{10... | collective-permute-start | bytes 1351688 | tf_op jit(solution)/shard_map/ppermute | solution.py:681
  41.3 4.4 %collective-permute-start.9 = (bf16[96,384]{1,0:T(8,128)(2,1)S(1)}, bf16[96,384]{1,0:T(8,128)(2,1)S(1)}, u32[]{:S(2)}, u32[]{:S(2)}) collective-permute-start(bf16[96,384]{1,0:T(8,128)(2,1)S(1)} %shard_map.32), channel_id=1, source_target_pairs={{0,16},{8,24},{16,0},{24,8},{1,17},{9,25},{17,1},{25,9},{2,18},{10... | collective-permute-start | bytes 221192 | tf_op jit(solution)/shard_map/ppermute | solution.py:681
  43.3 8.2 %collective-permute-start.16 = (bf16[256,512]{1,0:T(8,128)(2,1)S(1)}, bf16[256,512]{1,0:T(8,128)(2,1)S(1)}, u32[]{:S(2)}, u32[]{:S(2)}) collective-permute-start(bf16[256,512]{1,0:T(8,128)(2,1)S(1)} %get-tuple-element.38.refs_0_), channel_id=1, source_target_pairs={{0,16},{8,24},{16,0},{24,8},{1,17},{9,25},{17,1},{25,9},{2,18},{10... | collective-permute-start | bytes 786440 | tf_op jit(solution)/shard_map/ppermute | solution.py:681
  45.7 2.4 %collective-permute-start.10 = (bf16[96,384]{1,0:T(8,128)(2,1)S(1)}, bf16[96,384]{1,0:T(8,128)(2,1)S(1)}, u32[]{:S(2)}, u32[]{:S(2)}) collective-permute-start(bf16[96,384]{1,0:T(8,128)(2,1)S(1)} %collective-permute-done.9.far), channel_id=1, source_target_pairs={{0,8},{8,0},{16,24},{24,16},{1,9},{9,1},{17,25},{25,17},{2,10},{10... | collective-permute-start | bytes 221192 | tf_op jit(solution)/shard_map/ppermute | solution.py:681
  48.8 2.9 %collective-permute-start.19 = (bf16[384,512]{1,0:T(8,128)(2,1)S(1)}, bf16[384,512]{1,0:T(8,128)(2,1)S(1)}, u32[]{:S(2)}, u32[]{:S(2)}) collective-permute-start(bf16[384,512]{1,0:T(8,128)(2,1)S(1)} %get-tuple-element.37.refs_2_), channel_id=1, source_target_pairs={{0,8},{8,0},{16,24},{24,16},{1,9},{9,1},{17,25},{25,17},{2,10},{10... | collective-permute-start | bytes 1179656 | tf_op jit(solution)/shard_map/ppermute | solution.py:681
  49.4 11.1 %collective-permute-start.15 = (bf16[384,512]{1,0:T(8,128)(2,1)S(1)}, bf16[384,512]{1,0:T(8,128)(2,1)S(1)}, u32[]{:S(2)}, u32[]{:S(2)}) collective-permute-start(bf16[384,512]{1,0:T(8,128)(2,1)S(1)} %get-tuple-element.37.refs_2_), channel_id=1, source_target_pairs={{0,16},{8,24},{16,0},{24,8},{1,17},{9,25},{17,1},{25,9},{2,18},{10... | collective-permute-start | bytes 1179656 | tf_op jit(solution)/shard_map/ppermute | solution.py:681
  50.2 1.5 %collective-permute-start.18 = (bf16[256,512]{1,0:T(8,128)(2,1)S(1)}, bf16[256,512]{1,0:T(8,128)(2,1)S(1)}, u32[]{:S(2)}, u32[]{:S(2)}) collective-permute-start(bf16[256,512]{1,0:T(8,128)(2,1)S(1)} %get-tuple-element.38.refs_0_), channel_id=1, source_target_pairs={{0,8},{8,0},{16,24},{24,16},{1,9},{9,1},{17,25},{25,17},{2,10},{10... | collective-permute-start | bytes 786440 | tf_op jit(solution)/shard_map/ppermute | solution.py:681
  51.5 4.5 %collective-permute-start.17 = (bf16[256,512]{1,0:T(8,128)(2,1)S(1)}, bf16[256,512]{1,0:T(8,128)(2,1)S(1)}, u32[]{:S(2)}, u32[]{:S(2)}) collective-permute-start(bf16[256,512]{1,0:T(8,128)(2,1)S(1)} %collective-permute-done.16.refs_0_), channel_id=1, source_target_pairs={{0,8},{8,0},{16,24},{24,16},{1,9},{9,1},{17,25},{25,17},{2,10},{10... | collective-permute-start | bytes 786440 | tf_op jit(solution)/shard_map/ppermute | solution.py:681
  60.5 1.8 %collective-permute-start.20 = (bf16[384,512]{1,0:T(8,128)(2,1)S(1)}, bf16[384,512]{1,0:T(8,128)(2,1)S(1)}, u32[]{:S(2)}, u32[]{:S(2)}) collective-permute-start(bf16[384,512]{1,0:T(8,128)(2,1)S(1)} %shard_map.38.square), channel_id=1, source_target_pairs={{0,8},{8,0},{16,24},{24,16},{1,9},{9,1},{17,25},{25,17},{2,10},{10... | collective-permute-start | bytes 1179656 | tf_op jit(solution)/shard_map/ppermute | solution.py:681

commit v9 on v8

--- a/solution.py
+++ b/solution.py
@@ -69,11 +69,11 @@
             lo, hi = self.needed(t, side)
             lo, hi = max(lo, self.pair * side), min(hi, self.pair * (side + 1))
             if hi > lo:
-                if name != FAR_WIDE:
+                if name[0] == "near":
                     lo, hi = even_down(lo), even_up(hi)
                 found.append((hi - lo, t, lo, hi))
         found.sort(reverse=True)
-        if name == FAR_WIDE:
+        if name[0] == "far":
             places, used = {}, []
             for width, t, lo, hi in found:
                 free = [n for n, taken in enumerate(used) if taken + width <= self.slab]
@@ -650,9 +650,9 @@
             value = part[(n - begin) * g.size : (n - begin + 1) * g.size, n * g.size : (n + g.slab) * g.size]
             row = slice(n * g.size, (n + 1) * g.size)
             rows[row, :] = partial[row, :] - 2.0 * (value * keep[pl.ds(first + n, 1), :])
-        to = pl.ds(pl.multiple_of((first + begin) * g.size, g.size), step * g.size)
-        copies.append(pltpu.make_async_copy(rows.at[here, :], out.at[to, :], sems.at[len(copies)]))
-        copies[-1].start()
+            to = pl.ds(pl.multiple_of((first + n) * g.size, g.size), g.size)
+            copies.append(pltpu.make_async_copy(rows.at[row, :], out.at[to, :], sems.at[len(copies)]))
+            copies[-1].start()
     for copy in copies:
         copy.wait()
 
@@ -781,7 +781,7 @@
     return call(
         functools.partial(last_kernel, g),
         f32(slab),
-        [pltpu.VMEM((high_b, cols), jnp.float32), pltpu.SemaphoreType.DMA((3,)), left],
+        [pltpu.VMEM((high_b, cols), jnp.float32), pltpu.SemaphoreType.DMA((1 + g.group("B")[0],)), left],
         keep, swap(across_b, 1), next_to, partial, done,
         place=HBM,
     )

time: 64.6 us -> 64.5 us (level)
  no operation moved by 1% of the time
where the time goes in v9:
time: 64.5 us; the launch traced here: 64.3 us
  waiting for transfers between devices  34.2 us (53%)
  Pallas kernels  16 us (25%)
  starting transfers between devices  13.8 us (21%)
    ppermute x17, waiting for transfers between devices, swap(): return lax.ppermute(value, 'layer', [(s, s ^ bit) for s in range(layers)])  22.8 us
    pallas_call x13, Pallas kernels, call(): pl.pallas_call(kernel, out_shape=out_shape, in_specs=specs, out_specs=jax...  16 us
    ppermute x3, waiting for transfers between devices, send(): return lax.ppermute(value, ('layer', 'row'), pairs)  11.3 us
    ppermute x17, starting transfers between devices, swap(): return lax.ppermute(value, 'layer', [(s, s ^ bit) for s in range(layers)])  6.96 us
    ppermute x3, starting transfers between devices, send(): return lax.ppermute(value, ('layer', 'row'), pairs)  6.81 us
  transfers between devices with their start and end apart: 21, of which 10 were waited for; matrix products, arithmetic and copies ran while one was open for 0% of the time, Pallas kernels for 20%

profile of v9, /device:TPU:0, one launch (start us, length us, event | category | flops | bytes accessed | tf_op | source)
XLA Modules:
  0.0 64.3 jit_solution(1107177404156925446)
XLA Ops:
  0.0 1.2 %shard_map.28 = (bf16[640,512]{1,0:T(8,128)(2,1)S(1)}, f32[16,512]{1,0:T(8,128)S(1)}, bf16[320,512]{1,0:T(8,128)(2,1)S(1)}) custom-call(bf16[640,512]{1,0:T(8,128)(2,1)} %density_ref.1, s32[8,10]{1,0:T(8,128)} %bitcast.1), custom_call_target="tpu_custom_call" | custom-call | tf_op jit(solution)/shard_map/pallas_call | solution.py:662
  1.3 6.1 %collective-permute-start.3 = (bf16[640,512]{1,0:T(8,128)(2,1)S(1)}, bf16[640,512]{1,0:T(8,128)(2,1)S(1)}, u32[]{:S(2)}, u32[]{:S(2)}) collective-permute-start(bf16[640,512]{1,0:T(8,128)(2,1)S(1)} %get-tuple-element.25.own_ref.refs_0_), channel_id=1, source_target_pairs={{0,7},{1,0},{2,1},{3,2},{4,3},{5,4},{6,5},{7,6},{8,15},{9,8},{10,9... | collective-permute-start | bytes 1966088 | tf_op jit(solution)/shard_map/ppermute | solution.py:690
  7.3 0.0 collective-permute-start
  7.3 0.0 collective-permute-start.2
  7.3 1.6 %collective-permute-done.given_ref = bf16[320,512]{1,0:T(8,128)(2,1)S(1)} collective-permute-done((bf16[320,512]{1,0:T(8,128)(2,1)S(1)}, bf16[320,512]{1,0:T(8,128)(2,1)S(1)}, u32[]{:S(2)}, u32[]{:S(2)}) %collective-permute-start) | collective-permute-done | bytes 327712 | tf_op jit(solution)/shard_map/ppermute | solution.py:681
  8.9 0.1 shard_map.29
  9.1 0.7 %collective-permute-start.1 = (bf16[160,1408]{1,0:T(8,128)(2,1)S(1)}, bf16[160,1408]{1,0:T(8,128)(2,1)S(1)}, u32[]{:S(2)}, u32[]{:S(2)}) collective-permute-start(bf16[160,1408]{1,0:T(8,128)(2,1)S(1)} %get-tuple-element.27.own_ref), channel_id=1, source_target_pairs={{1,3},{3,5},{5,7},{7,1},{9,11},{11,13},{13,15},{15,9},{16,22},{18,... | collective-permute-start | bytes 1351688 | tf_op jit(solution)/shard_map/ppermute | solution.py:690
  9.8 0.2 collective-permute-start.6
  10.0 11.3 %collective-permute-done.3.after_ref.refs_4_ = bf16[640,512]{1,0:T(8,128)(2,1)S(1)} collective-permute-done((bf16[640,512]{1,0:T(8,128)(2,1)S(1)}, bf16[640,512]{1,0:T(8,128)(2,1)S(1)}, u32[]{:S(2)}, u32[]{:S(2)}) %collective-permute-start.3) | collective-permute-done | bytes 655392 | tf_op jit(solution)/shard_map/ppermute | solution.py:690
  21.3 2.2 %collective-permute-start.11 = (bf16[640,512]{1,0:T(8,128)(2,1)S(1)}, bf16[640,512]{1,0:T(8,128)(2,1)S(1)}, u32[]{:S(2)}, u32[]{:S(2)}) collective-permute-start(bf16[640,512]{1,0:T(8,128)(2,1)S(1)} %collective-permute-done.3.after_ref.refs_4_), channel_id=1, source_target_pairs={{0,16},{8,24},{16,0},{24,8},{1,17},{9,25},{17,1},{25,9},{2,18},{10... | collective-permute-start | bytes 1966088 | tf_op jit(solution)/shard_map/ppermute | solution.py:681
  23.5 1.3 %collective-permute-done.2.other_ref.refs_2_ = bf16[640,512]{1,0:T(8,128)(2,1)S(1)} collective-permute-done((bf16[640,512]{1,0:T(8,128)(2,1)S(1)}, bf16[640,512]{1,0:T(8,128)(2,1)S(1)}, u32[]{:S(2)}, u32[]{:S(2)}) %collective-permute-start.2) | collective-permute-done | bytes 655392 | tf_op jit(solution)/shard_map/ppermute | solution.py:681
  24.8 0.0 collective-permute-done.1.relayed_ref
  24.8 0.1 shard_map.30
  24.9 0.1 collective-permute-start.4
  25.0 0.1 collective-permute-start.13
  25.1 0.1 collective-permute-start.7
  25.1 0.0 collective-permute-done.6.refs_1_
  25.2 0.5 collective-permute-start.8
  25.6 12.9 %collective-permute-done.11.refs_0_ = bf16[640,512]{1,0:T(8,128)(2,1)S(1)} collective-permute-done((bf16[640,512]{1,0:T(8,128)(2,1)S(1)}, bf16[640,512]{1,0:T(8,128)(2,1)S(1)}, u32[]{:S(2)}, u32[]{:S(2)}) %collective-permute-start.11) | collective-permute-done | bytes 655392 | tf_op jit(solution)/shard_map/ppermute | solution.py:681
  38.5 0.0 collective-permute-start.12
  38.5 0.0 collective-permute-done.4.far_own.refs_4_
  38.5 0.5 collective-permute-start.5
  39.0 0.0 collective-permute-done.13.refs_2_
  39.0 0.1 collective-permute-start.14
  39.1 1.5 %shard_map.31 = (bf16[1280,1664]{1,0:T(8,128)(2,1)S(1)}, f32[256,768]{1,0:T(8,128)S(1)}, bf16[256,1024]{1,0:T(8,128)(2,1)S(1)}) custom-call(bf16[640,512]{1,0:T(8,128)(2,1)S(1)} %get-tuple-element.25.own_ref.refs_0_, bf16[640,512]{1,0:T(8,128)(2,1)S(1)} %collective-permute-done.6.refs_1_, bf16[640,512]{1,0:T(8,128)(2,1)S(1)} %collective-permute-done.2.other_ref.refs_2_, ...), custom_call_target="tpu_custom_call" | custom-call | tf_op jit(solution)/shard_map/pallas_call | solution.py:662
  40.6 0.7 %collective-permute-done.5.far_beside.refs_5_ = bf16[448,512]{1,0:T(8,128)(2,1)S(1)} collective-permute-done((bf16[448,512]{1,0:T(8,128)(2,1)S(1)}, bf16[448,512]{1,0:T(8,128)(2,1)S(1)}, u32[]{:S(2)}, u32[]{:S(2)}) %collective-permute-start.5) | collective-permute-done | bytes 458784 | tf_op jit(solution)/shard_map/ppermute | solution.py:681
  41.3 0.1 shard_map.32
  41.4 0.7 %collective-permute-start.9 = (bf16[64,512]{1,0:T(8,128)(2,1)S(1)}, bf16[64,512]{1,0:T(8,128)(2,1)S(1)}, u32[]{:S(2)}, u32[]{:S(2)}) collective-permute-start(bf16[64,512]{1,0:T(8,128)(2,1)S(1)} %shard_map.32), channel_id=1, source_target_pairs={{0,16},{8,24},{16,0},{24,8},{1,17},{9,25},{17,1},{25,9},{2,18},{10... | collective-permute-start | bytes 196616 | tf_op jit(solution)/shard_map/ppermute | solution.py:681
  42.1 1.2 %shard_map.33 = (bf16[256,512]{1,0:T(8,128)(2,1)S(1)}, bf16[1024,1664]{1,0:T(8,128)(2,1)S(1)}) custom-call(f32[16,512]{1,0:T(8,128)S(1)} %get-tuple-element.24.keep, bf16[640,512]{1,0:T(8,128)(2,1)S(1)} %collective-permute-done.11.refs_0_, bf16[640,512]{1,0:T(8,128)(2,1)S(1)} %collective-permute-done.12.refs_1_, ...), custom_call_target="tpu_custom_call" | custom-call | tf_op jit(solution)/shard_map/pallas_call | solution.py:662
  43.3 1.4 %collective-permute-start.16 = (bf16[256,512]{1,0:T(8,128)(2,1)S(1)}, bf16[256,512]{1,0:T(8,128)(2,1)S(1)}, u32[]{:S(2)}, u32[]{:S(2)}) collective-permute-start(bf16[256,512]{1,0:T(8,128)(2,1)S(1)} %get-tuple-element.38.refs_0_), channel_id=1, source_target_pairs={{0,16},{8,24},{16,0},{24,8},{1,17},{9,25},{17,1},{25,9},{2,18},{10... | collective-permute-start | bytes 786440 | tf_op jit(solution)/shard_map/ppermute | solution.py:681
  44.7 1.0 %collective-permute-done.9.far = bf16[64,512]{1,0:T(8,128)(2,1)S(1)} collective-permute-done((bf16[64,512]{1,0:T(8,128)(2,1)S(1)}, bf16[64,512]{1,0:T(8,128)(2,1)S(1)}, u32[]{:S(2)}, u32[]{:S(2)}) %collective-permute-start.9) | collective-permute-done | bytes 65568 | tf_op jit(solution)/shard_map/ppermute | solution.py:681
  45.7 2.3 %shard_map.34 = (f32[384,896]{1,0:T(8,128)S(1)}, bf16[384,384]{1,0:T(8,128)(2,1)S(1)}) custom-call(bf16[640,512]{1,0:T(8,128)(2,1)S(1)} %get-tuple-element.25.own_ref.refs_0_, bf16[640,512]{1,0:T(8,128)(2,1)S(1)} %collective-permute-done.6.refs_1_, bf16[640,512]{1,0:T(8,128)(2,1)S(1)} %collective-permute-done.2.other_ref.refs_2_, ...), custom_call_target="tpu_custom_call" | custom-call | tf_op jit(solution)/shard_map/pallas_call | solution.py:662
  48.0 0.0 collective-permute-done.10.far_beside
  48.0 0.8 %shard_map.35 = (bf16[384,512]{1,0:T(8,128)(2,1)S(1)}, bf16[384,1664]{1,0:T(8,128)(2,1)S(1)}) custom-call(f32[16,512]{1,0:T(8,128)S(1)} %get-tuple-element.24.keep, bf16[64,512]{1,0:T(8,128)(2,1)S(1)} %collective-permute-done.9.far, bf16[64,512]{1,0:T(8,128)(2,1)S(1)} %collective-permute-done.10.far_beside, f32[384,896]{1,0:T(8,128)S(1)} %get-tuple-element.35.total, ...), custom_call_target="tpu_custom_call" | custom-call | tf_op jit(solution)/shard_map/pallas_call | solution.py:662
  48.8 0.6 collective-permute-start.19
  49.4 0.7 %collective-permute-start.15 = (bf16[384,512]{1,0:T(8,128)(2,1)S(1)}, bf16[384,512]{1,0:T(8,128)(2,1)S(1)}, u32[]{:S(2)}, u32[]{:S(2)}) collective-permute-start(bf16[384,512]{1,0:T(8,128)(2,1)S(1)} %get-tuple-element.37.refs_2_), channel_id=1, source_target_pairs={{0,16},{8,24},{16,0},{24,8},{1,17},{9,25},{17,1},{25,9},{2,18},{10... | collective-permute-start | bytes 1179656 | tf_op jit(solution)/shard_map/ppermute | solution.py:681
  50.1 0.0 collective-permute-start.18
  50.1 1.5 %collective-permute-done.16.refs_0_ = bf16[256,512]{1,0:T(8,128)(2,1)S(1)} collective-permute-done((bf16[256,512]{1,0:T(8,128)(2,1)S(1)}, bf16[256,512]{1,0:T(8,128)(2,1)S(1)}, u32[]{:S(2)}, u32[]{:S(2)}) %collective-permute-start.16) | collective-permute-done | bytes 262176 | tf_op jit(solution)/shard_map/ppermute | solution.py:681
  51.5 0.1 collective-permute-done.18.refs_1_
  51.6 0.0 collective-permute-done.19.refs_3_
  51.6 4.3 %shard_map.36.refs_4_.partial = f32[640,512]{1,0:T(8,128)S(1)} custom-call(f32[16,512]{1,0:T(8,128)S(1)} %get-tuple-element.24.keep, bf16[256,512]{1,0:T(8,128)(2,1)S(1)} %get-tuple-element.38.refs_0_, bf16[256,512]{1,0:T(8,128)(2,1)S(1)} %collective-permute-done.18.refs_1_, bf16[384,512]{1,0:T(8,128)(2,1)S(1)} %get-tuple-element.37.refs_2_, ...), custom_call_target="tpu_custom_call" | custom-call | tf_op jit(solution)/shard_map/pallas_call | solution.py:662
  55.9 0.0 collective-permute-done.17.refs_1_
  55.9 1.3 %shard_map.37 = (f32[256,512]{1,0:T(8,128)S(1)}, bf16[1024,896]{1,0:T(8,128)(2,1)S(1)}, bf16[1024,896]{1,0:T(8,128)(2,1)S(1)}) custom-call(f32[16,512]{1,0:T(8,128)S(1)} %get-tuple-element.24.keep, bf16[256,512]{1,0:T(8,128)(2,1)S(1)} %collective-permute-done.16.refs_0_, bf16[256,512]{1,0:T(8,128)(2,1)S(1)} %collective-permute-done.17.refs_1_, ...), custom_call_target="tpu_custom_call" | custom-call | tf_op jit(solution)/shard_map/pallas_call | solution.py:662
  57.2 3.3 %collective-permute-done.15.in_ref = bf16[384,512]{1,0:T(8,128)(2,1)S(1)} collective-permute-done((bf16[384,512]{1,0:T(8,128)(2,1)S(1)}, bf16[384,512]{1,0:T(8,128)(2,1)S(1)}, u32[]{:S(2)}, u32[]{:S(2)}) %collective-permute-start.15) | collective-permute-done | bytes 393248 | tf_op jit(solution)/shard_map/ppermute | solution.py:681
  60.5 0.1 collective-permute-start.20
  60.6 1.2 %shard_map.39.partial = f32[384,512]{1,0:T(8,128)S(1)} custom-call(f32[16,512]{1,0:T(8,128)S(1)} %get-tuple-element.24.keep, bf16[384,512]{1,0:T(8,128)(2,1)S(1)} %shard_map.38.square, bf16[1024,896]{1,0:T(8,128)(2,1)S(1)} %get-tuple-element.42.right, f32[640,512]{1,0:T(8,128)S(1)} %shard_map.36.refs_4_.partial), custom_call_target="tpu_custom_call" | custom-call | tf_op jit(solution)/shard_map/pallas_call | solution.py:662
  61.9 0.5 collective-permute-done.20.square
  62.3 1.8 %shard_map.40 = f32[640,512]{1,0:T(8,128)} custom-call(f32[16,512]{1,0:T(8,128)S(1)} %get-tuple-element.24.keep, bf16[384,512]{1,0:T(8,128)(2,1)S(1)} %collective-permute-done.20.square, bf16[1024,896]{1,0:T(8,128)(2,1)S(1)} %get-tuple-element.41.right, f32[384,512]{1,0:T(8,128)S(1)} %shard_map.39.partial, f32[256,512]{1,0:T(8,128)S(1)} %get-tuple-element.40.refs_0_.done), custom_call_target="tpu_custom_call" | custom-call | tf_op jit(solution)/shard_map/pallas_call | solution.py:662
  (7 shorter events, 0.0 us)
Async XLA Ops:
  1.3 20.0 %collective-permute-start.3 = (bf16[640,512]{1,0:T(8,128)(2,1)S(1)}, bf16[640,512]{1,0:T(8,128)(2,1)S(1)}, u32[]{:S(2)}, u32[]{:S(2)}) collective-permute-start(bf16[640,512]{1,0:T(8,128)(2,1)S(1)} %get-tuple-element.25.own_ref.refs_0_), channel_id=1, source_target_pairs={{0,7},{1,0},{2,1},{3,2},{4,3},{5,4},{6,5},{7,6},{8,15},{9,8},{10,9... | collective-permute-start | bytes 1966088 | tf_op jit(solution)/shard_map/ppermute | solution.py:690
  7.3 1.6 %collective-permute-start = (bf16[320,512]{1,0:T(8,128)(2,1)S(1)}, bf16[320,512]{1,0:T(8,128)(2,1)S(1)}, u32[]{:S(2)}, u32[]{:S(2)}) collective-permute-start(bf16[320,512]{1,0:T(8,128)(2,1)S(1)} %get-tuple-element.26), channel_id=1, source_target_pairs={{0,8},{8,0},{16,24},{24,16},{1,9},{9,1},{17,25},{25,17},{2,10},{10... | collective-permute-start | bytes 983048 | tf_op jit(solution)/shard_map/ppermute | solution.py:681
  7.3 17.5 %collective-permute-start.2 = (bf16[640,512]{1,0:T(8,128)(2,1)S(1)}, bf16[640,512]{1,0:T(8,128)(2,1)S(1)}, u32[]{:S(2)}, u32[]{:S(2)}) collective-permute-start(bf16[640,512]{1,0:T(8,128)(2,1)S(1)} %get-tuple-element.25.own_ref.refs_0_), channel_id=1, source_target_pairs={{0,16},{8,24},{16,0},{24,8},{1,17},{9,25},{17,1},{25,9},{2,18},{10... | collective-permute-start | bytes 1966088 | tf_op jit(solution)/shard_map/ppermute | solution.py:681
  9.1 15.8 %collective-permute-start.1 = (bf16[160,1408]{1,0:T(8,128)(2,1)S(1)}, bf16[160,1408]{1,0:T(8,128)(2,1)S(1)}, u32[]{:S(2)}, u32[]{:S(2)}) collective-permute-start(bf16[160,1408]{1,0:T(8,128)(2,1)S(1)} %get-tuple-element.27.own_ref), channel_id=1, source_target_pairs={{1,3},{3,5},{5,7},{7,1},{9,11},{11,13},{13,15},{15,9},{16,22},{18,... | collective-permute-start | bytes 1351688 | tf_op jit(solution)/shard_map/ppermute | solution.py:690
  9.8 15.4 %collective-permute-start.6 = (bf16[640,512]{1,0:T(8,128)(2,1)S(1)}, bf16[640,512]{1,0:T(8,128)(2,1)S(1)}, u32[]{:S(2)}, u32[]{:S(2)}) collective-permute-start(bf16[640,512]{1,0:T(8,128)(2,1)S(1)} %get-tuple-element.25.own_ref.refs_0_), channel_id=1, source_target_pairs={{0,8},{8,0},{16,24},{24,16},{1,9},{9,1},{17,25},{25,17},{2,10},{10... | collective-permute-start | bytes 1966088 | tf_op jit(solution)/shard_map/ppermute | solution.py:681
  21.3 17.2 %collective-permute-start.11 = (bf16[640,512]{1,0:T(8,128)(2,1)S(1)}, bf16[640,512]{1,0:T(8,128)(2,1)S(1)}, u32[]{:S(2)}, u32[]{:S(2)}) collective-permute-start(bf16[640,512]{1,0:T(8,128)(2,1)S(1)} %collective-permute-done.3.after_ref.refs_4_), channel_id=1, source_target_pairs={{0,16},{8,24},{16,0},{24,8},{1,17},{9,25},{17,1},{25,9},{2,18},{10... | collective-permute-start | bytes 1966088 | tf_op jit(solution)/shard_map/ppermute | solution.py:681
  24.9 13.6 %collective-permute-start.4 = (bf16[448,512]{1,0:T(8,128)(2,1)S(1)}, bf16[448,512]{1,0:T(8,128)(2,1)S(1)}, u32[]{:S(2)}, u32[]{:S(2)}) collective-permute-start(bf16[448,512]{1,0:T(8,128)(2,1)S(1)} %get-tuple-element.29), channel_id=1, source_target_pairs={{0,2},{1,3},{2,4},{3,5},{4,6},{5,7},{6,0},{7,1},{8,10},{9,11},{10,... | collective-permute-start | bytes 1376264 | tf_op jit(solution)/shard_map/ppermute | solution.py:690
  25.0 14.0 %collective-permute-start.13 = (bf16[160,1408]{1,0:T(8,128)(2,1)S(1)}, bf16[160,1408]{1,0:T(8,128)(2,1)S(1)}, u32[]{:S(2)}, u32[]{:S(2)}) collective-permute-start(bf16[160,1408]{1,0:T(8,128)(2,1)S(1)} %get-tuple-element.32), channel_id=1, source_target_pairs={{0,1},{1,0},{2,3},{3,2},{4,5},{5,4},{6,7},{7,6},{8,9},{9,8},{10,11... | collective-permute-start | bytes 1351688 | tf_op jit(solution)/shard_map/ppermute | solution.py:724
  25.1 14.0 %collective-permute-start.7 = (bf16[640,512]{1,0:T(8,128)(2,1)S(1)}, bf16[640,512]{1,0:T(8,128)(2,1)S(1)}, u32[]{:S(2)}, u32[]{:S(2)}) collective-permute-start(bf16[640,512]{1,0:T(8,128)(2,1)S(1)} %collective-permute-done.2.other_ref.refs_2_), channel_id=1, source_target_pairs={{0,8},{8,0},{16,24},{24,16},{1,9},{9,1},{17,25},{25,17},{2,10},{10... | collective-permute-start | bytes 1966088 | tf_op jit(solution)/shard_map/ppermute | solution.py:681
  25.2 13.9 %collective-permute-start.8 = (bf16[640,512]{1,0:T(8,128)(2,1)S(1)}, bf16[640,512]{1,0:T(8,128)(2,1)S(1)}, u32[]{:S(2)}, u32[]{:S(2)}) collective-permute-start(bf16[640,512]{1,0:T(8,128)(2,1)S(1)} %collective-permute-done.3.after_ref.refs_4_), channel_id=1, source_target_pairs={{0,8},{8,0},{16,24},{24,16},{1,9},{9,1},{17,25},{25,17},{2,10},{10... | collective-permute-start | bytes 1966088 | tf_op jit(solution)/shard_map/ppermute | solution.py:681
  38.5 3.6 %collective-permute-start.12 = (bf16[640,512]{1,0:T(8,128)(2,1)S(1)}, bf16[640,512]{1,0:T(8,128)(2,1)S(1)}, u32[]{:S(2)}, u32[]{:S(2)}) collective-permute-start(bf16[640,512]{1,0:T(8,128)(2,1)S(1)} %collective-permute-done.11.refs_0_), channel_id=1, source_target_pairs={{0,8},{8,0},{16,24},{24,16},{1,9},{9,1},{17,25},{25,17},{2,10},{10... | collective-permute-start | bytes 1966088 | tf_op jit(solution)/shard_map/ppermute | solution.py:681
  38.5 2.7 %collective-permute-start.5 = (bf16[448,512]{1,0:T(8,128)(2,1)S(1)}, bf16[448,512]{1,0:T(8,128)(2,1)S(1)}, u32[]{:S(2)}, u32[]{:S(2)}) collective-permute-start(bf16[448,512]{1,0:T(8,128)(2,1)S(1)} %collective-permute-done.4.far_own.refs_4_), channel_id=1, source_target_pairs={{0,8},{8,0},{16,24},{24,16},{1,9},{9,1},{17,25},{25,17},{2,10},{10... | collective-permute-start | bytes 1376264 | tf_op jit(solution)/shard_map/ppermute | solution.py:681
  39.0 3.1 %collective-permute-start.14 = (bf16[160,1408]{1,0:T(8,128)(2,1)S(1)}, bf16[160,1408]{1,0:T(8,128)(2,1)S(1)}, u32[]{:S(2)}, u32[]{:S(2)}) collective-permute-start(bf16[160,1408]{1,0:T(8,128)(2,1)S(1)} %collective-permute-done.13.refs_2_), channel_id=1, source_target_pairs={{0,8},{8,0},{16,24},{24,16},{1,9},{9,1},{17,25},{25,17},{2,10},{10... | collective-permute-start | bytes 1351688 | tf_op jit(solution)/shard_map/ppermute | solution.py:681
  41.4 4.3 %collective-permute-start.9 = (bf16[64,512]{1,0:T(8,128)(2,1)S(1)}, bf16[64,512]{1,0:T(8,128)(2,1)S(1)}, u32[]{:S(2)}, u32[]{:S(2)}) collective-permute-start(bf16[64,512]{1,0:T(8,128)(2,1)S(1)} %shard_map.32), channel_id=1, source_target_pairs={{0,16},{8,24},{16,0},{24,8},{1,17},{9,25},{17,1},{25,9},{2,18},{10... | collective-permute-start | bytes 196616 | tf_op jit(solution)/shard_map/ppermute | solution.py:681
  43.3 8.2 %collective-permute-start.16 = (bf16[256,512]{1,0:T(8,128)(2,1)S(1)}, bf16[256,512]{1,0:T(8,128)(2,1)S(1)}, u32[]{:S(2)}, u32[]{:S(2)}) collective-permute-start(bf16[256,512]{1,0:T(8,128)(2,1)S(1)} %get-tuple-element.38.refs_0_), channel_id=1, source_target_pairs={{0,16},{8,24},{16,0},{24,8},{1,17},{9,25},{17,1},{25,9},{2,18},{10... | collective-permute-start | bytes 786440 | tf_op jit(solution)/shard_map/ppermute | solution.py:681
  45.7 2.4 %collective-permute-start.10 = (bf16[64,512]{1,0:T(8,128)(2,1)S(1)}, bf16[64,512]{1,0:T(8,128)(2,1)S(1)}, u32[]{:S(2)}, u32[]{:S(2)}) collective-permute-start(bf16[64,512]{1,0:T(8,128)(2,1)S(1)} %collective-permute-done.9.far), channel_id=1, source_target_pairs={{0,8},{8,0},{16,24},{24,16},{1,9},{9,1},{17,25},{25,17},{2,10},{10... | collective-permute-start | bytes 196616 | tf_op jit(solution)/shard_map/ppermute | solution.py:681
  48.8 2.8 %collective-permute-start.19 = (bf16[384,512]{1,0:T(8,128)(2,1)S(1)}, bf16[384,512]{1,0:T(8,128)(2,1)S(1)}, u32[]{:S(2)}, u32[]{:S(2)}) collective-permute-start(bf16[384,512]{1,0:T(8,128)(2,1)S(1)} %get-tuple-element.37.refs_2_), channel_id=1, source_target_pairs={{0,8},{8,0},{16,24},{24,16},{1,9},{9,1},{17,25},{25,17},{2,10},{10... | collective-permute-start | bytes 1179656 | tf_op jit(solution)/shard_map/ppermute | solution.py:681
  49.4 11.1 %collective-permute-start.15 = (bf16[384,512]{1,0:T(8,128)(2,1)S(1)}, bf16[384,512]{1,0:T(8,128)(2,1)S(1)}, u32[]{:S(2)}, u32[]{:S(2)}) collective-permute-start(bf16[384,512]{1,0:T(8,128)(2,1)S(1)} %get-tuple-element.37.refs_2_), channel_id=1, source_target_pairs={{0,16},{8,24},{16,0},{24,8},{1,17},{9,25},{17,1},{25,9},{2,18},{10... | collective-permute-start | bytes 1179656 | tf_op jit(solution)/shard_map/ppermute | solution.py:681
  50.1 1.5 %collective-permute-start.18 = (bf16[256,512]{1,0:T(8,128)(2,1)S(1)}, bf16[256,512]{1,0:T(8,128)(2,1)S(1)}, u32[]{:S(2)}, u32[]{:S(2)}) collective-permute-start(bf16[256,512]{1,0:T(8,128)(2,1)S(1)} %get-tuple-element.38.refs_0_), channel_id=1, source_target_pairs={{0,8},{8,0},{16,24},{24,16},{1,9},{9,1},{17,25},{25,17},{2,10},{10... | collective-permute-start | bytes 786440 | tf_op jit(solution)/shard_map/ppermute | solution.py:681
  51.5 4.4 %collective-permute-start.17 = (bf16[256,512]{1,0:T(8,128)(2,1)S(1)}, bf16[256,512]{1,0:T(8,128)(2,1)S(1)}, u32[]{:S(2)}, u32[]{:S(2)}) collective-permute-start(bf16[256,512]{1,0:T(8,128)(2,1)S(1)} %collective-permute-done.16.refs_0_), channel_id=1, source_target_pairs={{0,8},{8,0},{16,24},{24,16},{1,9},{9,1},{17,25},{25,17},{2,10},{10... | collective-permute-start | bytes 786440 | tf_op jit(solution)/shard_map/ppermute | solution.py:681
  60.5 1.8 %collective-permute-start.20 = (bf16[384,512]{1,0:T(8,128)(2,1)S(1)}, bf16[384,512]{1,0:T(8,128)(2,1)S(1)}, u32[]{:S(2)}, u32[]{:S(2)}) collective-permute-start(bf16[384,512]{1,0:T(8,128)(2,1)S(1)} %shard_map.38.square), channel_id=1, source_target_pairs={{0,8},{8,0},{16,24},{24,16},{1,9},{9,1},{17,25},{25,17},{2,10},{10... | collective-permute-start | bytes 1179656 | tf_op jit(solution)/shard_map/ppermute | solution.py:681

commit v10 on v9

--- a/solution.py
+++ b/solution.py
@@ -213,9 +213,7 @@
         pl.when(side == value)(functools.partial(fill, value))
 
 
-def relay_kernel(g, own_ref, relayed_ref, far_ref, other_ref, after_ref, out_ref, message):
-    side, row = layer_index() // 2, lax.axis_index("row")
-    pick((row % 2) == side, own_ref, relayed_ref, out_ref)
+def far_kernel(g, far_ref, other_ref, after_ref, message):
     message[: far_ref.shape[0], :] = far_ref[...]
 
     def fill(side):
@@ -223,7 +221,11 @@
         message[far_ref.shape[0] :, :] = other_ref[first * g.size : (first + count) * g.size, :]
 
     for value in (0, 1):
-        pl.when(side == value)(functools.partial(fill, value))
+        pl.when(layer_index() // 2 == value)(functools.partial(fill, value))
+
+
+def relay_kernel(g, own_ref, relayed_ref, after_ref, out_ref):
+    pick((lax.axis_index("row") % 2) == layer_index() // 2, own_ref, relayed_ref, out_ref)
 
 
 def pass_kernel(in_ref, *refs):
@@ -717,12 +719,10 @@
     )
     relayed = send(wide, FAR_WIDE, lambda layer, row: row % 2 != layer // 2)
     crossed = swap(thin, 2)
-    wide, far_wide = call(
-        functools.partial(relay_kernel, g),
-        [bf16(wide.shape), bf16(far_shape)], [], wide, relayed, far_wide, other, after=(thin,),
-    )
+    message = call(functools.partial(far_kernel, g), bf16(far_shape), [], far_wide, other, after=(thin,))
+    far_wide = send(message, FAR_WIDE)
+    wide = call(functools.partial(relay_kernel, g), bf16(wide.shape), [], wide, relayed, after=(message,))
     wide = lax.ppermute(wide, "row", [(r, r ^ 1) for r in range(ring)])
-    far_wide = send(far_wide, FAR_WIDE)
 
     early, late, far = (g.inner_count(part) * g.size for part in ("early", "late", "far"))
     (high_a, wide_a), (high_b, wide_b) = (tuple(n * g.size for n in g.group(name)) for name in "AB")

time: 64.5 us -> 64.5 us (level)
    pallas_call x13 -> x14, Pallas kernels: 16 us -> 16 us  [call(): pl.pallas_call(kernel, out_shape=out_shape, in_specs=specs, out_specs=jax...]
where the time goes in v10:
time: 64.5 us; the launch traced here: 64.3 us
  waiting for transfers between devices  34.1 us (53%)
  Pallas kernels  16 us (25%)
  starting transfers between devices  13.9 us (22%)
    ppermute x17, waiting for transfers between devices, swap(): return lax.ppermute(value, 'layer', [(s, s ^ bit) for s in range(layers)])  22.8 us
    pallas_call x14, Pallas kernels, call(): pl.pallas_call(kernel, out_shape=out_shape, in_specs=specs, out_specs=jax...  16 us
    ppermute x3, waiting for transfers between devices, send(): return lax.ppermute(value, ('layer', 'row'), pairs)  11.3 us
    ppermute x17, starting transfers between devices, swap(): return lax.ppermute(value, 'layer', [(s, s ^ bit) for s in range(layers)])  6.99 us
    ppermute x3, starting transfers between devices, send(): return lax.ppermute(value, ('layer', 'row'), pairs)  6.81 us
  transfers between devices with their start and end apart: 21, of which 10 were waited for; matrix products, arithmetic and copies ran while one was open for 0% of the time, Pallas kernels for 20%

profile of v10, /device:TPU:0, one launch (start us, length us, event | category | flops | bytes accessed | tf_op | source)
XLA Modules:
  0.0 64.3 jit_solution(16048785463480754526)
XLA Ops:
  0.0 1.2 %shard_map.28 = (bf16[640,512]{1,0:T(8,128)(2,1)S(1)}, f32[16,512]{1,0:T(8,128)S(1)}, bf16[320,512]{1,0:T(8,128)(2,1)S(1)}) custom-call(bf16[640,512]{1,0:T(8,128)(2,1)} %density_ref.1, s32[8,10]{1,0:T(8,128)} %bitcast.1), custom_call_target="tpu_custom_call" | custom-call | tf_op jit(solution)/shard_map/pallas_call | solution.py:664
  1.3 6.1 %collective-permute-start.2 = (bf16[640,512]{1,0:T(8,128)(2,1)S(1)}, bf16[640,512]{1,0:T(8,128)(2,1)S(1)}, u32[]{:S(2)}, u32[]{:S(2)}) collective-permute-start(bf16[640,512]{1,0:T(8,128)(2,1)S(1)} %get-tuple-element.23.own_ref.refs_0_), channel_id=1, source_target_pairs={{0,7},{1,0},{2,1},{3,2},{4,3},{5,4},{6,5},{7,6},{8,15},{9,8},{10,9... | collective-permute-start | bytes 1966088 | tf_op jit(solution)/shard_map/ppermute | solution.py:692
  7.3 0.0 collective-permute-start
  7.3 1.6 %collective-permute-done.given_ref = bf16[320,512]{1,0:T(8,128)(2,1)S(1)} collective-permute-done((bf16[320,512]{1,0:T(8,128)(2,1)S(1)}, bf16[320,512]{1,0:T(8,128)(2,1)S(1)}, u32[]{:S(2)}, u32[]{:S(2)}) %collective-permute-start) | collective-permute-done | bytes 327712 | tf_op jit(solution)/shard_map/ppermute | solution.py:683
  8.9 0.1 shard_map.29
  9.1 0.7 %collective-permute-start.12 = (bf16[160,1408]{1,0:T(8,128)(2,1)S(1)}, bf16[160,1408]{1,0:T(8,128)(2,1)S(1)}, u32[]{:S(2)}, u32[]{:S(2)}) collective-permute-start(bf16[160,1408]{1,0:T(8,128)(2,1)S(1)} %get-tuple-element.28.own_ref), channel_id=1, source_target_pairs={{1,3},{3,5},{5,7},{7,1},{9,11},{11,13},{13,15},{15,9},{16,22},{18,... | collective-permute-start | bytes 1351688 | tf_op jit(solution)/shard_map/ppermute | solution.py:692
  9.8 0.2 collective-permute-start.5
  10.0 11.3 %collective-permute-done.2.after_ref.refs_4_ = bf16[640,512]{1,0:T(8,128)(2,1)S(1)} collective-permute-done((bf16[640,512]{1,0:T(8,128)(2,1)S(1)}, bf16[640,512]{1,0:T(8,128)(2,1)S(1)}, u32[]{:S(2)}, u32[]{:S(2)}) %collective-permute-start.2) | collective-permute-done | bytes 655392 | tf_op jit(solution)/shard_map/ppermute | solution.py:692
  21.3 2.2 %collective-permute-start.10 = (bf16[640,512]{1,0:T(8,128)(2,1)S(1)}, bf16[640,512]{1,0:T(8,128)(2,1)S(1)}, u32[]{:S(2)}, u32[]{:S(2)}) collective-permute-start(bf16[640,512]{1,0:T(8,128)(2,1)S(1)} %collective-permute-done.2.after_ref.refs_4_), channel_id=1, source_target_pairs={{0,16},{8,24},{16,0},{24,8},{1,17},{9,25},{17,1},{25,9},{2,18},{10... | collective-permute-start | bytes 1966088 | tf_op jit(solution)/shard_map/ppermute | solution.py:683
  23.5 1.3 %collective-permute-done.1.other_ref.refs_2_ = bf16[640,512]{1,0:T(8,128)(2,1)S(1)} collective-permute-done((bf16[640,512]{1,0:T(8,128)(2,1)S(1)}, bf16[640,512]{1,0:T(8,128)(2,1)S(1)}, u32[]{:S(2)}, u32[]{:S(2)}) %collective-permute-start.1) | collective-permute-done | bytes 655392 | tf_op jit(solution)/shard_map/ppermute | solution.py:683
  24.9 0.1 collective-permute-start.3
  24.9 0.0 collective-permute-done.12.relayed_ref
  25.0 0.1 shard_map.33
  25.0 0.1 collective-permute-start.13
  25.1 0.1 collective-permute-start.6
  25.2 0.5 collective-permute-start.7
  25.7 12.8 %collective-permute-done.10.refs_0_ = bf16[640,512]{1,0:T(8,128)(2,1)S(1)} collective-permute-done((bf16[640,512]{1,0:T(8,128)(2,1)S(1)}, bf16[640,512]{1,0:T(8,128)(2,1)S(1)}, u32[]{:S(2)}, u32[]{:S(2)}) %collective-permute-start.10) | collective-permute-done | bytes 655392 | tf_op jit(solution)/shard_map/ppermute | solution.py:683
  38.5 0.0 collective-permute-done.3.far_own.refs_4_
  38.5 0.5 collective-permute-start.4
  39.0 0.0 collective-permute-done.13.refs_2_
  39.0 0.1 collective-permute-start.14
  39.1 0.0 collective-permute-done.7.refs_5_
  39.1 1.4 %shard_map.31 = (bf16[1280,1664]{1,0:T(8,128)(2,1)S(1)}, f32[256,768]{1,0:T(8,128)S(1)}, bf16[256,1024]{1,0:T(8,128)(2,1)S(1)}) custom-call(bf16[640,512]{1,0:T(8,128)(2,1)S(1)} %get-tuple-element.23.own_ref.refs_0_, bf16[640,512]{1,0:T(8,128)(2,1)S(1)} %collective-permute-done.5.refs_1_, bf16[640,512]{1,0:T(8,128)(2,1)S(1)} %collective-permute-done.1.other_ref.refs_2_, ...), custom_call_target="tpu_custom_call" | custom-call | tf_op jit(solution)/shard_map/pallas_call | solution.py:664
  40.6 0.7 %collective-permute-done.4.far_beside.refs_5_ = bf16[448,512]{1,0:T(8,128)(2,1)S(1)} collective-permute-done((bf16[448,512]{1,0:T(8,128)(2,1)S(1)}, bf16[448,512]{1,0:T(8,128)(2,1)S(1)}, u32[]{:S(2)}, u32[]{:S(2)}) %collective-permute-start.4) | collective-permute-done | bytes 458784 | tf_op jit(solution)/shard_map/ppermute | solution.py:683
  41.3 0.1 shard_map.32
  41.4 0.7 %collective-permute-start.8 = (bf16[64,512]{1,0:T(8,128)(2,1)S(1)}, bf16[64,512]{1,0:T(8,128)(2,1)S(1)}, u32[]{:S(2)}, u32[]{:S(2)}) collective-permute-start(bf16[64,512]{1,0:T(8,128)(2,1)S(1)} %shard_map.32), channel_id=1, source_target_pairs={{0,16},{8,24},{16,0},{24,8},{1,17},{9,25},{17,1},{25,9},{2,18},{10... | collective-permute-start | bytes 196616 | tf_op jit(solution)/shard_map/ppermute | solution.py:683
  42.1 0.0 collective-permute-done.14.refs_3_
  42.1 1.2 %shard_map.34 = (bf16[256,512]{1,0:T(8,128)(2,1)S(1)}, bf16[1024,1664]{1,0:T(8,128)(2,1)S(1)}) custom-call(f32[16,512]{1,0:T(8,128)S(1)} %get-tuple-element.22.keep, bf16[640,512]{1,0:T(8,128)(2,1)S(1)} %collective-permute-done.10.refs_0_, bf16[640,512]{1,0:T(8,128)(2,1)S(1)} %collective-permute-done.11.refs_1_, ...), custom_call_target="tpu_custom_call" | custom-call | tf_op jit(solution)/shard_map/pallas_call | solution.py:664
  43.3 1.4 %collective-permute-start.16 = (bf16[256,512]{1,0:T(8,128)(2,1)S(1)}, bf16[256,512]{1,0:T(8,128)(2,1)S(1)}, u32[]{:S(2)}, u32[]{:S(2)}) collective-permute-start(bf16[256,512]{1,0:T(8,128)(2,1)S(1)} %get-tuple-element.34.refs_0_), channel_id=1, source_target_pairs={{0,16},{8,24},{16,0},{24,8},{1,17},{9,25},{17,1},{25,9},{2,18},{10... | collective-permute-start | bytes 786440 | tf_op jit(solution)/shard_map/ppermute | solution.py:683
  44.7 1.0 %collective-permute-done.8.far = bf16[64,512]{1,0:T(8,128)(2,1)S(1)} collective-permute-done((bf16[64,512]{1,0:T(8,128)(2,1)S(1)}, bf16[64,512]{1,0:T(8,128)(2,1)S(1)}, u32[]{:S(2)}, u32[]{:S(2)}) %collective-permute-start.8) | collective-permute-done | bytes 65568 | tf_op jit(solution)/shard_map/ppermute | solution.py:683
  45.7 0.0 collective-permute-start.9
  45.7 2.3 %shard_map.35 = (f32[384,896]{1,0:T(8,128)S(1)}, bf16[384,384]{1,0:T(8,128)(2,1)S(1)}) custom-call(bf16[640,512]{1,0:T(8,128)(2,1)S(1)} %get-tuple-element.23.own_ref.refs_0_, bf16[640,512]{1,0:T(8,128)(2,1)S(1)} %collective-permute-done.5.refs_1_, bf16[640,512]{1,0:T(8,128)(2,1)S(1)} %collective-permute-done.1.other_ref.refs_2_, ...), custom_call_target="tpu_custom_call" | custom-call | tf_op jit(solution)/shard_map/pallas_call | solution.py:664
  48.0 0.0 collective-permute-done.9.far_beside
  48.0 0.8 %shard_map.36 = (bf16[384,512]{1,0:T(8,128)(2,1)S(1)}, bf16[384,1664]{1,0:T(8,128)(2,1)S(1)}) custom-call(f32[16,512]{1,0:T(8,128)S(1)} %get-tuple-element.22.keep, bf16[64,512]{1,0:T(8,128)(2,1)S(1)} %collective-permute-done.8.far, bf16[64,512]{1,0:T(8,128)(2,1)S(1)} %collective-permute-done.9.far_beside, f32[384,896]{1,0:T(8,128)S(1)} %get-tuple-element.31.total, ...), custom_call_target="tpu_custom_call" | custom-call | tf_op jit(solution)/shard_map/pallas_call | solution.py:664
  48.8 0.6 collective-permute-start.19
  49.4 0.7 %collective-permute-start.15 = (bf16[384,512]{1,0:T(8,128)(2,1)S(1)}, bf16[384,512]{1,0:T(8,128)(2,1)S(1)}, u32[]{:S(2)}, u32[]{:S(2)}) collective-permute-start(bf16[384,512]{1,0:T(8,128)(2,1)S(1)} %get-tuple-element.33.refs_2_), channel_id=1, source_target_pairs={{0,16},{8,24},{16,0},{24,8},{1,17},{9,25},{17,1},{25,9},{2,18},{10... | collective-permute-start | bytes 1179656 | tf_op jit(solution)/shard_map/ppermute | solution.py:683
  50.1 0.0 collective-permute-start.18
  50.1 1.5 %collective-permute-done.16.refs_0_ = bf16[256,512]{1,0:T(8,128)(2,1)S(1)} collective-permute-done((bf16[256,512]{1,0:T(8,128)(2,1)S(1)}, bf16[256,512]{1,0:T(8,128)(2,1)S(1)}, u32[]{:S(2)}, u32[]{:S(2)}) %collective-permute-start.16) | collective-permute-done | bytes 262176 | tf_op jit(solution)/shard_map/ppermute | solution.py:683
  51.5 0.0 collective-permute-start.17
  51.5 0.1 collective-permute-done.18.refs_1_
  51.6 4.3 %shard_map.37.refs_4_.partial = f32[640,512]{1,0:T(8,128)S(1)} custom-call(f32[16,512]{1,0:T(8,128)S(1)} %get-tuple-element.22.keep, bf16[256,512]{1,0:T(8,128)(2,1)S(1)} %get-tuple-element.34.refs_0_, bf16[256,512]{1,0:T(8,128)(2,1)S(1)} %collective-permute-done.18.refs_1_, bf16[384,512]{1,0:T(8,128)(2,1)S(1)} %get-tuple-element.33.refs_2_, ...), custom_call_target="tpu_custom_call" | custom-call | tf_op jit(solution)/shard_map/pallas_call | solution.py:664
  55.9 0.0 collective-permute-done.17.refs_1_
  55.9 1.3 %shard_map.38 = (f32[256,512]{1,0:T(8,128)S(1)}, bf16[1024,896]{1,0:T(8,128)(2,1)S(1)}, bf16[1024,896]{1,0:T(8,128)(2,1)S(1)}) custom-call(f32[16,512]{1,0:T(8,128)S(1)} %get-tuple-element.22.keep, bf16[256,512]{1,0:T(8,128)(2,1)S(1)} %collective-permute-done.16.refs_0_, bf16[256,512]{1,0:T(8,128)(2,1)S(1)} %collective-permute-done.17.refs_1_, ...), custom_call_target="tpu_custom_call" | custom-call | tf_op jit(solution)/shard_map/pallas_call | solution.py:664
  57.2 3.3 %collective-permute-done.15.in_ref = bf16[384,512]{1,0:T(8,128)(2,1)S(1)} collective-permute-done((bf16[384,512]{1,0:T(8,128)(2,1)S(1)}, bf16[384,512]{1,0:T(8,128)(2,1)S(1)}, u32[]{:S(2)}, u32[]{:S(2)}) %collective-permute-start.15) | collective-permute-done | bytes 393248 | tf_op jit(solution)/shard_map/ppermute | solution.py:683
  60.5 0.1 collective-permute-start.20
  60.6 1.2 %shard_map.40.partial = f32[384,512]{1,0:T(8,128)S(1)} custom-call(f32[16,512]{1,0:T(8,128)S(1)} %get-tuple-element.22.keep, bf16[384,512]{1,0:T(8,128)(2,1)S(1)} %shard_map.39.square, bf16[1024,896]{1,0:T(8,128)(2,1)S(1)} %get-tuple-element.38.right, f32[640,512]{1,0:T(8,128)S(1)} %shard_map.37.refs_4_.partial), custom_call_target="tpu_custom_call" | custom-call | tf_op jit(solution)/shard_map/pallas_call | solution.py:664
  61.9 0.5 collective-permute-done.20.square
  62.3 1.8 %shard_map.41 = f32[640,512]{1,0:T(8,128)} custom-call(f32[16,512]{1,0:T(8,128)S(1)} %get-tuple-element.22.keep, bf16[384,512]{1,0:T(8,128)(2,1)S(1)} %collective-permute-done.20.square, bf16[1024,896]{1,0:T(8,128)(2,1)S(1)} %get-tuple-element.37.right, f32[384,512]{1,0:T(8,128)S(1)} %shard_map.40.partial, f32[256,512]{1,0:T(8,128)S(1)} %get-tuple-element.36.refs_0_.done), custom_call_target="tpu_custom_call" | custom-call | tf_op jit(solution)/shard_map/pallas_call | solution.py:664
  (8 shorter events, 0.1 us)
Async XLA Ops:
  1.3 20.0 %collective-permute-start.2 = (bf16[640,512]{1,0:T(8,128)(2,1)S(1)}, bf16[640,512]{1,0:T(8,128)(2,1)S(1)}, u32[]{:S(2)}, u32[]{:S(2)}) collective-permute-start(bf16[640,512]{1,0:T(8,128)(2,1)S(1)} %get-tuple-element.23.own_ref.refs_0_), channel_id=1, source_target_pairs={{0,7},{1,0},{2,1},{3,2},{4,3},{5,4},{6,5},{7,6},{8,15},{9,8},{10,9... | collective-permute-start | bytes 1966088 | tf_op jit(solution)/shard_map/ppermute | solution.py:692
  7.3 1.6 %collective-permute-start = (bf16[320,512]{1,0:T(8,128)(2,1)S(1)}, bf16[320,512]{1,0:T(8,128)(2,1)S(1)}, u32[]{:S(2)}, u32[]{:S(2)}) collective-permute-start(bf16[320,512]{1,0:T(8,128)(2,1)S(1)} %get-tuple-element.24), channel_id=1, source_target_pairs={{0,8},{8,0},{16,24},{24,16},{1,9},{9,1},{17,25},{25,17},{2,10},{10... | collective-permute-start | bytes 983048 | tf_op jit(solution)/shard_map/ppermute | solution.py:683
  7.3 17.5 %collective-permute-start.1 = (bf16[640,512]{1,0:T(8,128)(2,1)S(1)}, bf16[640,512]{1,0:T(8,128)(2,1)S(1)}, u32[]{:S(2)}, u32[]{:S(2)}) collective-permute-start(bf16[640,512]{1,0:T(8,128)(2,1)S(1)} %get-tuple-element.23.own_ref.refs_0_), channel_id=1, source_target_pairs={{0,16},{8,24},{16,0},{24,8},{1,17},{9,25},{17,1},{25,9},{2,18},{10... | collective-permute-start | bytes 1966088 | tf_op jit(solution)/shard_map/ppermute | solution.py:683
  9.1 15.9 %collective-permute-start.12 = (bf16[160,1408]{1,0:T(8,128)(2,1)S(1)}, bf16[160,1408]{1,0:T(8,128)(2,1)S(1)}, u32[]{:S(2)}, u32[]{:S(2)}) collective-permute-start(bf16[160,1408]{1,0:T(8,128)(2,1)S(1)} %get-tuple-element.28.own_ref), channel_id=1, source_target_pairs={{1,3},{3,5},{5,7},{7,1},{9,11},{11,13},{13,15},{15,9},{16,22},{18,... | collective-permute-start | bytes 1351688 | tf_op jit(solution)/shard_map/ppermute | solution.py:692
  9.8 15.4 %collective-permute-start.5 = (bf16[640,512]{1,0:T(8,128)(2,1)S(1)}, bf16[640,512]{1,0:T(8,128)(2,1)S(1)}, u32[]{:S(2)}, u32[]{:S(2)}) collective-permute-start(bf16[640,512]{1,0:T(8,128)(2,1)S(1)} %get-tuple-element.23.own_ref.refs_0_), channel_id=1, source_target_pairs={{0,8},{8,0},{16,24},{24,16},{1,9},{9,1},{17,25},{25,17},{2,10},{10... | collective-permute-start | bytes 1966088 | tf_op jit(solution)/shard_map/ppermute | solution.py:683
  21.3 17.2 %collective-permute-start.10 = (bf16[640,512]{1,0:T(8,128)(2,1)S(1)}, bf16[640,512]{1,0:T(8,128)(2,1)S(1)}, u32[]{:S(2)}, u32[]{:S(2)}) collective-permute-start(bf16[640,512]{1,0:T(8,128)(2,1)S(1)} %collective-permute-done.2.after_ref.refs_4_), channel_id=1, source_target_pairs={{0,16},{8,24},{16,0},{24,8},{1,17},{9,25},{17,1},{25,9},{2,18},{10... | collective-permute-start | bytes 1966088 | tf_op jit(solution)/shard_map/ppermute | solution.py:683
  24.9 13.6 %collective-permute-start.3 = (bf16[448,512]{1,0:T(8,128)(2,1)S(1)}, bf16[448,512]{1,0:T(8,128)(2,1)S(1)}, u32[]{:S(2)}, u32[]{:S(2)}) collective-permute-start(bf16[448,512]{1,0:T(8,128)(2,1)S(1)} %shard_map.30.after_ref), channel_id=1, source_target_pairs={{0,2},{1,3},{2,4},{3,5},{4,6},{5,7},{6,0},{7,1},{8,10},{9,11},{10,... | collective-permute-start | bytes 1376264 | tf_op jit(solution)/shard_map/ppermute | solution.py:692
  25.0 14.0 %collective-permute-start.13 = (bf16[160,1408]{1,0:T(8,128)(2,1)S(1)}, bf16[160,1408]{1,0:T(8,128)(2,1)S(1)}, u32[]{:S(2)}, u32[]{:S(2)}) collective-permute-start(bf16[160,1408]{1,0:T(8,128)(2,1)S(1)} %shard_map.33), channel_id=1, source_target_pairs={{0,1},{1,0},{2,3},{3,2},{4,5},{5,4},{6,7},{7,6},{8,9},{9,8},{10,11... | collective-permute-start | bytes 1351688 | tf_op jit(solution)/shard_map/ppermute | solution.py:725
  25.1 14.0 %collective-permute-start.6 = (bf16[640,512]{1,0:T(8,128)(2,1)S(1)}, bf16[640,512]{1,0:T(8,128)(2,1)S(1)}, u32[]{:S(2)}, u32[]{:S(2)}) collective-permute-start(bf16[640,512]{1,0:T(8,128)(2,1)S(1)} %collective-permute-done.1.other_ref.refs_2_), channel_id=1, source_target_pairs={{0,8},{8,0},{16,24},{24,16},{1,9},{9,1},{17,25},{25,17},{2,10},{10... | collective-permute-start | bytes 1966088 | tf_op jit(solution)/shard_map/ppermute | solution.py:683
  25.2 13.9 %collective-permute-start.7 = (bf16[640,512]{1,0:T(8,128)(2,1)S(1)}, bf16[640,512]{1,0:T(8,128)(2,1)S(1)}, u32[]{:S(2)}, u32[]{:S(2)}) collective-permute-start(bf16[640,512]{1,0:T(8,128)(2,1)S(1)} %collective-permute-done.2.after_ref.refs_4_), channel_id=1, source_target_pairs={{0,8},{8,0},{16,24},{24,16},{1,9},{9,1},{17,25},{25,17},{2,10},{10... | collective-permute-start | bytes 1966088 | tf_op jit(solution)/shard_map/ppermute | solution.py:683
  38.5 3.6 %collective-permute-start.11 = (bf16[640,512]{1,0:T(8,128)(2,1)S(1)}, bf16[640,512]{1,0:T(8,128)(2,1)S(1)}, u32[]{:S(2)}, u32[]{:S(2)}) collective-permute-start(bf16[640,512]{1,0:T(8,128)(2,1)S(1)} %collective-permute-done.10.refs_0_), channel_id=1, source_target_pairs={{0,8},{8,0},{16,24},{24,16},{1,9},{9,1},{17,25},{25,17},{2,10},{10... | collective-permute-start | bytes 1966088 | tf_op jit(solution)/shard_map/ppermute | solution.py:683
  38.5 2.7 %collective-permute-start.4 = (bf16[448,512]{1,0:T(8,128)(2,1)S(1)}, bf16[448,512]{1,0:T(8,128)(2,1)S(1)}, u32[]{:S(2)}, u32[]{:S(2)}) collective-permute-start(bf16[448,512]{1,0:T(8,128)(2,1)S(1)} %collective-permute-done.3.far_own.refs_4_), channel_id=1, source_target_pairs={{0,8},{8,0},{16,24},{24,16},{1,9},{9,1},{17,25},{25,17},{2,10},{10... | collective-permute-start | bytes 1376264 | tf_op jit(solution)/shard_map/ppermute | solution.py:683
  39.0 3.1 %collective-permute-start.14 = (bf16[160,1408]{1,0:T(8,128)(2,1)S(1)}, bf16[160,1408]{1,0:T(8,128)(2,1)S(1)}, u32[]{:S(2)}, u32[]{:S(2)}) collective-permute-start(bf16[160,1408]{1,0:T(8,128)(2,1)S(1)} %collective-permute-done.13.refs_2_), channel_id=1, source_target_pairs={{0,8},{8,0},{16,24},{24,16},{1,9},{9,1},{17,25},{25,17},{2,10},{10... | collective-permute-start | bytes 1351688 | tf_op jit(solution)/shard_map/ppermute | solution.py:683
  41.4 4.3 %collective-permute-start.8 = (bf16[64,512]{1,0:T(8,128)(2,1)S(1)}, bf16[64,512]{1,0:T(8,128)(2,1)S(1)}, u32[]{:S(2)}, u32[]{:S(2)}) collective-permute-start(bf16[64,512]{1,0:T(8,128)(2,1)S(1)} %shard_map.32), channel_id=1, source_target_pairs={{0,16},{8,24},{16,0},{24,8},{1,17},{9,25},{17,1},{25,9},{2,18},{10... | collective-permute-start | bytes 196616 | tf_op jit(solution)/shard_map/ppermute | solution.py:683
  43.3 8.2 %collective-permute-start.16 = (bf16[256,512]{1,0:T(8,128)(2,1)S(1)}, bf16[256,512]{1,0:T(8,128)(2,1)S(1)}, u32[]{:S(2)}, u32[]{:S(2)}) collective-permute-start(bf16[256,512]{1,0:T(8,128)(2,1)S(1)} %get-tuple-element.34.refs_0_), channel_id=1, source_target_pairs={{0,16},{8,24},{16,0},{24,8},{1,17},{9,25},{17,1},{25,9},{2,18},{10... | collective-permute-start | bytes 786440 | tf_op jit(solution)/shard_map/ppermute | solution.py:683
  45.7 2.4 %collective-permute-start.9 = (bf16[64,512]{1,0:T(8,128)(2,1)S(1)}, bf16[64,512]{1,0:T(8,128)(2,1)S(1)}, u32[]{:S(2)}, u32[]{:S(2)}) collective-permute-start(bf16[64,512]{1,0:T(8,128)(2,1)S(1)} %collective-permute-done.8.far), channel_id=1, source_target_pairs={{0,8},{8,0},{16,24},{24,16},{1,9},{9,1},{17,25},{25,17},{2,10},{10... | collective-permute-start | bytes 196616 | tf_op jit(solution)/shard_map/ppermute | solution.py:683
  48.8 2.8 %collective-permute-start.19 = (bf16[384,512]{1,0:T(8,128)(2,1)S(1)}, bf16[384,512]{1,0:T(8,128)(2,1)S(1)}, u32[]{:S(2)}, u32[]{:S(2)}) collective-permute-start(bf16[384,512]{1,0:T(8,128)(2,1)S(1)} %get-tuple-element.33.refs_2_), channel_id=1, source_target_pairs={{0,8},{8,0},{16,24},{24,16},{1,9},{9,1},{17,25},{25,17},{2,10},{10... | collective-permute-start | bytes 1179656 | tf_op jit(solution)/shard_map/ppermute | solution.py:683
  49.4 11.1 %collective-permute-start.15 = (bf16[384,512]{1,0:T(8,128)(2,1)S(1)}, bf16[384,512]{1,0:T(8,128)(2,1)S(1)}, u32[]{:S(2)}, u32[]{:S(2)}) collective-permute-start(bf16[384,512]{1,0:T(8,128)(2,1)S(1)} %get-tuple-element.33.refs_2_), channel_id=1, source_target_pairs={{0,16},{8,24},{16,0},{24,8},{1,17},{9,25},{17,1},{25,9},{2,18},{10... | collective-permute-start | bytes 1179656 | tf_op jit(solution)/shard_map/ppermute | solution.py:683
  50.1 1.5 %collective-permute-start.18 = (bf16[256,512]{1,0:T(8,128)(2,1)S(1)}, bf16[256,512]{1,0:T(8,128)(2,1)S(1)}, u32[]{:S(2)}, u32[]{:S(2)}) collective-permute-start(bf16[256,512]{1,0:T(8,128)(2,1)S(1)} %get-tuple-element.34.refs_0_), channel_id=1, source_target_pairs={{0,8},{8,0},{16,24},{24,16},{1,9},{9,1},{17,25},{25,17},{2,10},{10... | collective-permute-start | bytes 786440 | tf_op jit(solution)/shard_map/ppermute | solution.py:683
  51.5 4.4 %collective-permute-start.17 = (bf16[256,512]{1,0:T(8,128)(2,1)S(1)}, bf16[256,512]{1,0:T(8,128)(2,1)S(1)}, u32[]{:S(2)}, u32[]{:S(2)}) collective-permute-start(bf16[256,512]{1,0:T(8,128)(2,1)S(1)} %collective-permute-done.16.refs_0_), channel_id=1, source_target_pairs={{0,8},{8,0},{16,24},{24,16},{1,9},{9,1},{17,25},{25,17},{2,10},{10... | collective-permute-start | bytes 786440 | tf_op jit(solution)/shard_map/ppermute | solution.py:683
  60.5 1.8 %collective-permute-start.20 = (bf16[384,512]{1,0:T(8,128)(2,1)S(1)}, bf16[384,512]{1,0:T(8,128)(2,1)S(1)}, u32[]{:S(2)}, u32[]{:S(2)}) collective-permute-start(bf16[384,512]{1,0:T(8,128)(2,1)S(1)} %shard_map.39.square), channel_id=1, source_target_pairs={{0,8},{8,0},{16,24},{24,16},{1,9},{9,1},{17,25},{25,17},{2,10},{10... | collective-permute-start | bytes 1179656 | tf_op jit(solution)/shard_map/ppermute | solution.py:683

commit v11 on v9

--- a/solution.py
+++ b/solution.py
@@ -719,7 +719,7 @@
     crossed = swap(thin, 2)
     wide, far_wide = call(
         functools.partial(relay_kernel, g),
-        [bf16(wide.shape), bf16(far_shape)], [], wide, relayed, far_wide, other, after=(thin,),
+        [bf16(wide.shape), bf16(far_shape)], [], wide, relayed, far_wide, other, after=(relayed,),
     )
     wide = lax.ppermute(wide, "row", [(r, r ^ 1) for r in range(ring)])
     far_wide = send(far_wide, FAR_WIDE)

time: 64.5 us -> 64.5 us (level)
  no operation moved by 1% of the time
where the time goes in v11:
time: 64.5 us; the launch traced here: 64.3 us
  waiting for transfers between devices  34.2 us (53%)
  Pallas kernels  15.9 us (25%)
  starting transfers between devices  13.8 us (21%)
    ppermute x17, waiting for transfers between devices, swap(): return lax.ppermute(value, 'layer', [(s, s ^ bit) for s in range(layers)])  22.8 us
    pallas_call x13, Pallas kernels, call(): pl.pallas_call(kernel, out_shape=out_shape, in_specs=specs, out_specs=jax...  15.9 us
    ppermute x3, waiting for transfers between devices, send(): return lax.ppermute(value, ('layer', 'row'), pairs)  11.4 us
    ppermute x17, starting transfers between devices, swap(): return lax.ppermute(value, 'layer', [(s, s ^ bit) for s in range(layers)])  6.96 us
    ppermute x3, starting transfers between devices, send(): return lax.ppermute(value, ('layer', 'row'), pairs)  6.81 us
  transfers between devices with their start and end apart: 21, of which 10 were waited for; matrix products, arithmetic and copies ran while one was open for 0% of the time, Pallas kernels for 20%

profile of v11, /device:TPU:0, one launch (start us, length us, event | category | flops | bytes accessed | tf_op | source)
XLA Modules:
  0.0 64.3 jit_solution(6845025163636737988)
XLA Ops:
  0.0 1.2 %shard_map.28 = (bf16[640,512]{1,0:T(8,128)(2,1)S(1)}, f32[16,512]{1,0:T(8,128)S(1)}, bf16[320,512]{1,0:T(8,128)(2,1)S(1)}) custom-call(bf16[640,512]{1,0:T(8,128)(2,1)} %density_ref.1, s32[8,10]{1,0:T(8,128)} %bitcast.1), custom_call_target="tpu_custom_call" | custom-call | tf_op jit(solution)/shard_map/pallas_call | solution.py:662
  1.3 6.1 %collective-permute-start.7 = (bf16[640,512]{1,0:T(8,128)(2,1)S(1)}, bf16[640,512]{1,0:T(8,128)(2,1)S(1)}, u32[]{:S(2)}, u32[]{:S(2)}) collective-permute-start(bf16[640,512]{1,0:T(8,128)(2,1)S(1)} %get-tuple-element.25.own_ref.refs_0_), channel_id=1, source_target_pairs={{0,7},{1,0},{2,1},{3,2},{4,3},{5,4},{6,5},{7,6},{8,15},{9,8},{10,9... | collective-permute-start | bytes 1966088 | tf_op jit(solution)/shard_map/ppermute | solution.py:690
  7.3 1.6 %collective-permute-done.given_ref = bf16[320,512]{1,0:T(8,128)(2,1)S(1)} collective-permute-done((bf16[320,512]{1,0:T(8,128)(2,1)S(1)}, bf16[320,512]{1,0:T(8,128)(2,1)S(1)}, u32[]{:S(2)}, u32[]{:S(2)}) %collective-permute-start) | collective-permute-done | bytes 327712 | tf_op jit(solution)/shard_map/ppermute | solution.py:681
  8.9 0.1 shard_map.29
  9.1 0.7 %collective-permute-start.1 = (bf16[160,1408]{1,0:T(8,128)(2,1)S(1)}, bf16[160,1408]{1,0:T(8,128)(2,1)S(1)}, u32[]{:S(2)}, u32[]{:S(2)}) collective-permute-start(bf16[160,1408]{1,0:T(8,128)(2,1)S(1)} %get-tuple-element.27.own_ref), channel_id=1, source_target_pairs={{1,3},{3,5},{5,7},{7,1},{9,11},{11,13},{13,15},{15,9},{16,22},{18,... | collective-permute-start | bytes 1351688 | tf_op jit(solution)/shard_map/ppermute | solution.py:690
  9.8 0.2 collective-permute-start.5
  10.0 11.3 %collective-permute-done.7.refs_4_ = bf16[640,512]{1,0:T(8,128)(2,1)S(1)} collective-permute-done((bf16[640,512]{1,0:T(8,128)(2,1)S(1)}, bf16[640,512]{1,0:T(8,128)(2,1)S(1)}, u32[]{:S(2)}, u32[]{:S(2)}) %collective-permute-start.7) | collective-permute-done | bytes 655392 | tf_op jit(solution)/shard_map/ppermute | solution.py:690
  21.3 2.2 %collective-permute-start.11 = (bf16[640,512]{1,0:T(8,128)(2,1)S(1)}, bf16[640,512]{1,0:T(8,128)(2,1)S(1)}, u32[]{:S(2)}, u32[]{:S(2)}) collective-permute-start(bf16[640,512]{1,0:T(8,128)(2,1)S(1)} %collective-permute-done.7.refs_4_), channel_id=1, source_target_pairs={{0,16},{8,24},{16,0},{24,8},{1,17},{9,25},{17,1},{25,9},{2,18},{10... | collective-permute-start | bytes 1966088 | tf_op jit(solution)/shard_map/ppermute | solution.py:681
  23.5 1.3 %collective-permute-done.2.other_ref.refs_2_ = bf16[640,512]{1,0:T(8,128)(2,1)S(1)} collective-permute-done((bf16[640,512]{1,0:T(8,128)(2,1)S(1)}, bf16[640,512]{1,0:T(8,128)(2,1)S(1)}, u32[]{:S(2)}, u32[]{:S(2)}) %collective-permute-start.2) | collective-permute-done | bytes 655392 | tf_op jit(solution)/shard_map/ppermute | solution.py:681
  24.8 0.0 collective-permute-done.1.relayed_ref.after_ref
  24.8 0.1 shard_map.30
  24.9 0.1 collective-permute-start.3
  25.0 0.1 collective-permute-start.13
  25.1 0.1 collective-permute-start.6
  25.1 0.0 collective-permute-done.5.refs_1_
  25.2 0.5 collective-permute-start.8
  25.6 12.9 %collective-permute-done.11.refs_0_ = bf16[640,512]{1,0:T(8,128)(2,1)S(1)} collective-permute-done((bf16[640,512]{1,0:T(8,128)(2,1)S(1)}, bf16[640,512]{1,0:T(8,128)(2,1)S(1)}, u32[]{:S(2)}, u32[]{:S(2)}) %collective-permute-start.11) | collective-permute-done | bytes 655392 | tf_op jit(solution)/shard_map/ppermute | solution.py:681
  38.5 0.0 collective-permute-done.3.far_own.refs_4_
  38.5 0.5 collective-permute-start.4
  39.0 0.0 collective-permute-done.13.refs_2_
  39.0 0.1 collective-permute-start.14
  39.1 0.0 collective-permute-done.8.refs_5_
  39.1 1.4 %shard_map.31 = (bf16[1280,1664]{1,0:T(8,128)(2,1)S(1)}, f32[256,768]{1,0:T(8,128)S(1)}, bf16[256,1024]{1,0:T(8,128)(2,1)S(1)}) custom-call(bf16[640,512]{1,0:T(8,128)(2,1)S(1)} %get-tuple-element.25.own_ref.refs_0_, bf16[640,512]{1,0:T(8,128)(2,1)S(1)} %collective-permute-done.5.refs_1_, bf16[640,512]{1,0:T(8,128)(2,1)S(1)} %collective-permute-done.2.other_ref.refs_2_, ...), custom_call_target="tpu_custom_call" | custom-call | tf_op jit(solution)/shard_map/pallas_call | solution.py:662
  40.6 0.7 %collective-permute-done.4.far_beside.refs_5_ = bf16[448,512]{1,0:T(8,128)(2,1)S(1)} collective-permute-done((bf16[448,512]{1,0:T(8,128)(2,1)S(1)}, bf16[448,512]{1,0:T(8,128)(2,1)S(1)}, u32[]{:S(2)}, u32[]{:S(2)}) %collective-permute-start.4) | collective-permute-done | bytes 458784 | tf_op jit(solution)/shard_map/ppermute | solution.py:681
  41.3 0.1 shard_map.32
  41.4 0.7 %collective-permute-start.9 = (bf16[64,512]{1,0:T(8,128)(2,1)S(1)}, bf16[64,512]{1,0:T(8,128)(2,1)S(1)}, u32[]{:S(2)}, u32[]{:S(2)}) collective-permute-start(bf16[64,512]{1,0:T(8,128)(2,1)S(1)} %shard_map.32), channel_id=1, source_target_pairs={{0,16},{8,24},{16,0},{24,8},{1,17},{9,25},{17,1},{25,9},{2,18},{10... | collective-permute-start | bytes 196616 | tf_op jit(solution)/shard_map/ppermute | solution.py:681
  42.1 0.0 collective-permute-done.14.refs_3_
  42.1 1.2 %shard_map.33 = (bf16[256,512]{1,0:T(8,128)(2,1)S(1)}, bf16[1024,1664]{1,0:T(8,128)(2,1)S(1)}) custom-call(f32[16,512]{1,0:T(8,128)S(1)} %get-tuple-element.24.keep, bf16[640,512]{1,0:T(8,128)(2,1)S(1)} %collective-permute-done.11.refs_0_, bf16[640,512]{1,0:T(8,128)(2,1)S(1)} %collective-permute-done.12.refs_1_, ...), custom_call_target="tpu_custom_call" | custom-call | tf_op jit(solution)/shard_map/pallas_call | solution.py:662
  43.3 1.4 %collective-permute-start.16 = (bf16[256,512]{1,0:T(8,128)(2,1)S(1)}, bf16[256,512]{1,0:T(8,128)(2,1)S(1)}, u32[]{:S(2)}, u32[]{:S(2)}) collective-permute-start(bf16[256,512]{1,0:T(8,128)(2,1)S(1)} %get-tuple-element.38.refs_0_), channel_id=1, source_target_pairs={{0,16},{8,24},{16,0},{24,8},{1,17},{9,25},{17,1},{25,9},{2,18},{10... | collective-permute-start | bytes 786440 | tf_op jit(solution)/shard_map/ppermute | solution.py:681
  44.7 1.0 %collective-permute-done.9.far = bf16[64,512]{1,0:T(8,128)(2,1)S(1)} collective-permute-done((bf16[64,512]{1,0:T(8,128)(2,1)S(1)}, bf16[64,512]{1,0:T(8,128)(2,1)S(1)}, u32[]{:S(2)}, u32[]{:S(2)}) %collective-permute-start.9) | collective-permute-done | bytes 65568 | tf_op jit(solution)/shard_map/ppermute | solution.py:681
  45.7 0.0 collective-permute-start.10
  45.7 2.3 %shard_map.34 = (f32[384,896]{1,0:T(8,128)S(1)}, bf16[384,384]{1,0:T(8,128)(2,1)S(1)}) custom-call(bf16[640,512]{1,0:T(8,128)(2,1)S(1)} %get-tuple-element.25.own_ref.refs_0_, bf16[640,512]{1,0:T(8,128)(2,1)S(1)} %collective-permute-done.5.refs_1_, bf16[640,512]{1,0:T(8,128)(2,1)S(1)} %collective-permute-done.2.other_ref.refs_2_, ...), custom_call_target="tpu_custom_call" | custom-call | tf_op jit(solution)/shard_map/pallas_call | solution.py:662
  48.0 0.0 collective-permute-done.10.far_beside
  48.0 0.8 %shard_map.35 = (bf16[384,512]{1,0:T(8,128)(2,1)S(1)}, bf16[384,1664]{1,0:T(8,128)(2,1)S(1)}) custom-call(f32[16,512]{1,0:T(8,128)S(1)} %get-tuple-element.24.keep, bf16[64,512]{1,0:T(8,128)(2,1)S(1)} %collective-permute-done.9.far, bf16[64,512]{1,0:T(8,128)(2,1)S(1)} %collective-permute-done.10.far_beside, f32[384,896]{1,0:T(8,128)S(1)} %get-tuple-element.35.total, ...), custom_call_target="tpu_custom_call" | custom-call | tf_op jit(solution)/shard_map/pallas_call | solution.py:662
  48.8 0.6 collective-permute-start.19
  49.4 0.7 %collective-permute-start.15 = (bf16[384,512]{1,0:T(8,128)(2,1)S(1)}, bf16[384,512]{1,0:T(8,128)(2,1)S(1)}, u32[]{:S(2)}, u32[]{:S(2)}) collective-permute-start(bf16[384,512]{1,0:T(8,128)(2,1)S(1)} %get-tuple-element.37.refs_2_), channel_id=1, source_target_pairs={{0,16},{8,24},{16,0},{24,8},{1,17},{9,25},{17,1},{25,9},{2,18},{10... | collective-permute-start | bytes 1179656 | tf_op jit(solution)/shard_map/ppermute | solution.py:681
  50.1 0.0 collective-permute-start.18
  50.1 1.5 %collective-permute-done.16.refs_0_ = bf16[256,512]{1,0:T(8,128)(2,1)S(1)} collective-permute-done((bf16[256,512]{1,0:T(8,128)(2,1)S(1)}, bf16[256,512]{1,0:T(8,128)(2,1)S(1)}, u32[]{:S(2)}, u32[]{:S(2)}) %collective-permute-start.16) | collective-permute-done | bytes 262176 | tf_op jit(solution)/shard_map/ppermute | solution.py:681
  51.5 0.0 collective-permute-start.17
  51.5 0.1 collective-permute-done.18.refs_1_
  51.6 4.3 %shard_map.36.refs_4_.partial = f32[640,512]{1,0:T(8,128)S(1)} custom-call(f32[16,512]{1,0:T(8,128)S(1)} %get-tuple-element.24.keep, bf16[256,512]{1,0:T(8,128)(2,1)S(1)} %get-tuple-element.38.refs_0_, bf16[256,512]{1,0:T(8,128)(2,1)S(1)} %collective-permute-done.18.refs_1_, bf16[384,512]{1,0:T(8,128)(2,1)S(1)} %get-tuple-element.37.refs_2_, ...), custom_call_target="tpu_custom_call" | custom-call | tf_op jit(solution)/shard_map/pallas_call | solution.py:662
  55.9 0.0 collective-permute-done.17.refs_1_
  55.9 1.3 %shard_map.37 = (f32[256,512]{1,0:T(8,128)S(1)}, bf16[1024,896]{1,0:T(8,128)(2,1)S(1)}, bf16[1024,896]{1,0:T(8,128)(2,1)S(1)}) custom-call(f32[16,512]{1,0:T(8,128)S(1)} %get-tuple-element.24.keep, bf16[256,512]{1,0:T(8,128)(2,1)S(1)} %collective-permute-done.16.refs_0_, bf16[256,512]{1,0:T(8,128)(2,1)S(1)} %collective-permute-done.17.refs_1_, ...), custom_call_target="tpu_custom_call" | custom-call | tf_op jit(solution)/shard_map/pallas_call | solution.py:662
  57.2 3.3 %collective-permute-done.15.in_ref = bf16[384,512]{1,0:T(8,128)(2,1)S(1)} collective-permute-done((bf16[384,512]{1,0:T(8,128)(2,1)S(1)}, bf16[384,512]{1,0:T(8,128)(2,1)S(1)}, u32[]{:S(2)}, u32[]{:S(2)}) %collective-permute-start.15) | collective-permute-done | bytes 393248 | tf_op jit(solution)/shard_map/ppermute | solution.py:681
  60.5 0.1 collective-permute-start.20
  60.6 1.2 %shard_map.39.partial = f32[384,512]{1,0:T(8,128)S(1)} custom-call(f32[16,512]{1,0:T(8,128)S(1)} %get-tuple-element.24.keep, bf16[384,512]{1,0:T(8,128)(2,1)S(1)} %shard_map.38.square, bf16[1024,896]{1,0:T(8,128)(2,1)S(1)} %get-tuple-element.42.right, f32[640,512]{1,0:T(8,128)S(1)} %shard_map.36.refs_4_.partial), custom_call_target="tpu_custom_call" | custom-call | tf_op jit(solution)/shard_map/pallas_call | solution.py:662
  61.9 0.5 collective-permute-done.20.square
  62.3 1.8 %shard_map.40 = f32[640,512]{1,0:T(8,128)} custom-call(f32[16,512]{1,0:T(8,128)S(1)} %get-tuple-element.24.keep, bf16[384,512]{1,0:T(8,128)(2,1)S(1)} %collective-permute-done.20.square, bf16[1024,896]{1,0:T(8,128)(2,1)S(1)} %get-tuple-element.41.right, f32[384,512]{1,0:T(8,128)S(1)} %shard_map.39.partial, f32[256,512]{1,0:T(8,128)S(1)} %get-tuple-element.40.refs_0_.done), custom_call_target="tpu_custom_call" | custom-call | tf_op jit(solution)/shard_map/pallas_call | solution.py:662
  (7 shorter events, 0.0 us)
Async XLA Ops:
  1.3 20.0 %collective-permute-start.7 = (bf16[640,512]{1,0:T(8,128)(2,1)S(1)}, bf16[640,512]{1,0:T(8,128)(2,1)S(1)}, u32[]{:S(2)}, u32[]{:S(2)}) collective-permute-start(bf16[640,512]{1,0:T(8,128)(2,1)S(1)} %get-tuple-element.25.own_ref.refs_0_), channel_id=1, source_target_pairs={{0,7},{1,0},{2,1},{3,2},{4,3},{5,4},{6,5},{7,6},{8,15},{9,8},{10,9... | collective-permute-start | bytes 1966088 | tf_op jit(solution)/shard_map/ppermute | solution.py:690
  7.3 1.6 %collective-permute-start = (bf16[320,512]{1,0:T(8,128)(2,1)S(1)}, bf16[320,512]{1,0:T(8,128)(2,1)S(1)}, u32[]{:S(2)}, u32[]{:S(2)}) collective-permute-start(bf16[320,512]{1,0:T(8,128)(2,1)S(1)} %get-tuple-element.26), channel_id=1, source_target_pairs={{0,8},{8,0},{16,24},{24,16},{1,9},{9,1},{17,25},{25,17},{2,10},{10... | collective-permute-start | bytes 983048 | tf_op jit(solution)/shard_map/ppermute | solution.py:681
  7.3 17.5 %collective-permute-start.2 = (bf16[640,512]{1,0:T(8,128)(2,1)S(1)}, bf16[640,512]{1,0:T(8,128)(2,1)S(1)}, u32[]{:S(2)}, u32[]{:S(2)}) collective-permute-start(bf16[640,512]{1,0:T(8,128)(2,1)S(1)} %get-tuple-element.25.own_ref.refs_0_), channel_id=1, source_target_pairs={{0,16},{8,24},{16,0},{24,8},{1,17},{9,25},{17,1},{25,9},{2,18},{10... | collective-permute-start | bytes 1966088 | tf_op jit(solution)/shard_map/ppermute | solution.py:681
  9.1 15.8 %collective-permute-start.1 = (bf16[160,1408]{1,0:T(8,128)(2,1)S(1)}, bf16[160,1408]{1,0:T(8,128)(2,1)S(1)}, u32[]{:S(2)}, u32[]{:S(2)}) collective-permute-start(bf16[160,1408]{1,0:T(8,128)(2,1)S(1)} %get-tuple-element.27.own_ref), channel_id=1, source_target_pairs={{1,3},{3,5},{5,7},{7,1},{9,11},{11,13},{13,15},{15,9},{16,22},{18,... | collective-permute-start | bytes 1351688 | tf_op jit(solution)/shard_map/ppermute | solution.py:690
  9.8 15.4 %collective-permute-start.5 = (bf16[640,512]{1,0:T(8,128)(2,1)S(1)}, bf16[640,512]{1,0:T(8,128)(2,1)S(1)}, u32[]{:S(2)}, u32[]{:S(2)}) collective-permute-start(bf16[640,512]{1,0:T(8,128)(2,1)S(1)} %get-tuple-element.25.own_ref.refs_0_), channel_id=1, source_target_pairs={{0,8},{8,0},{16,24},{24,16},{1,9},{9,1},{17,25},{25,17},{2,10},{10... | collective-permute-start | bytes 1966088 | tf_op jit(solution)/shard_map/ppermute | solution.py:681
  21.3 17.2 %collective-permute-start.11 = (bf16[640,512]{1,0:T(8,128)(2,1)S(1)}, bf16[640,512]{1,0:T(8,128)(2,1)S(1)}, u32[]{:S(2)}, u32[]{:S(2)}) collective-permute-start(bf16[640,512]{1,0:T(8,128)(2,1)S(1)} %collective-permute-done.7.refs_4_), channel_id=1, source_target_pairs={{0,16},{8,24},{16,0},{24,8},{1,17},{9,25},{17,1},{25,9},{2,18},{10... | collective-permute-start | bytes 1966088 | tf_op jit(solution)/shard_map/ppermute | solution.py:681
  24.9 13.6 %collective-permute-start.3 = (bf16[448,512]{1,0:T(8,128)(2,1)S(1)}, bf16[448,512]{1,0:T(8,128)(2,1)S(1)}, u32[]{:S(2)}, u32[]{:S(2)}) collective-permute-start(bf16[448,512]{1,0:T(8,128)(2,1)S(1)} %get-tuple-element.29), channel_id=1, source_target_pairs={{0,2},{1,3},{2,4},{3,5},{4,6},{5,7},{6,0},{7,1},{8,10},{9,11},{10,... | collective-permute-start | bytes 1376264 | tf_op jit(solution)/shard_map/ppermute | solution.py:690
  25.0 14.0 %collective-permute-start.13 = (bf16[160,1408]{1,0:T(8,128)(2,1)S(1)}, bf16[160,1408]{1,0:T(8,128)(2,1)S(1)}, u32[]{:S(2)}, u32[]{:S(2)}) collective-permute-start(bf16[160,1408]{1,0:T(8,128)(2,1)S(1)} %get-tuple-element.32), channel_id=1, source_target_pairs={{0,1},{1,0},{2,3},{3,2},{4,5},{5,4},{6,7},{7,6},{8,9},{9,8},{10,11... | collective-permute-start | bytes 1351688 | tf_op jit(solution)/shard_map/ppermute | solution.py:724
  25.1 14.0 %collective-permute-start.6 = (bf16[640,512]{1,0:T(8,128)(2,1)S(1)}, bf16[640,512]{1,0:T(8,128)(2,1)S(1)}, u32[]{:S(2)}, u32[]{:S(2)}) collective-permute-start(bf16[640,512]{1,0:T(8,128)(2,1)S(1)} %collective-permute-done.2.other_ref.refs_2_), channel_id=1, source_target_pairs={{0,8},{8,0},{16,24},{24,16},{1,9},{9,1},{17,25},{25,17},{2,10},{10... | collective-permute-start | bytes 1966088 | tf_op jit(solution)/shard_map/ppermute | solution.py:681
  25.2 13.9 %collective-permute-start.8 = (bf16[640,512]{1,0:T(8,128)(2,1)S(1)}, bf16[640,512]{1,0:T(8,128)(2,1)S(1)}, u32[]{:S(2)}, u32[]{:S(2)}) collective-permute-start(bf16[640,512]{1,0:T(8,128)(2,1)S(1)} %collective-permute-done.7.refs_4_), channel_id=1, source_target_pairs={{0,8},{8,0},{16,24},{24,16},{1,9},{9,1},{17,25},{25,17},{2,10},{10... | collective-permute-start | bytes 1966088 | tf_op jit(solution)/shard_map/ppermute | solution.py:681
  38.5 3.6 %collective-permute-start.12 = (bf16[640,512]{1,0:T(8,128)(2,1)S(1)}, bf16[640,512]{1,0:T(8,128)(2,1)S(1)}, u32[]{:S(2)}, u32[]{:S(2)}) collective-permute-start(bf16[640,512]{1,0:T(8,128)(2,1)S(1)} %collective-permute-done.11.refs_0_), channel_id=1, source_target_pairs={{0,8},{8,0},{16,24},{24,16},{1,9},{9,1},{17,25},{25,17},{2,10},{10... | collective-permute-start | bytes 1966088 | tf_op jit(solution)/shard_map/ppermute | solution.py:681
  38.5 2.7 %collective-permute-start.4 = (bf16[448,512]{1,0:T(8,128)(2,1)S(1)}, bf16[448,512]{1,0:T(8,128)(2,1)S(1)}, u32[]{:S(2)}, u32[]{:S(2)}) collective-permute-start(bf16[448,512]{1,0:T(8,128)(2,1)S(1)} %collective-permute-done.3.far_own.refs_4_), channel_id=1, source_target_pairs={{0,8},{8,0},{16,24},{24,16},{1,9},{9,1},{17,25},{25,17},{2,10},{10... | collective-permute-start | bytes 1376264 | tf_op jit(solution)/shard_map/ppermute | solution.py:681
  39.0 3.1 %collective-permute-start.14 = (bf16[160,1408]{1,0:T(8,128)(2,1)S(1)}, bf16[160,1408]{1,0:T(8,128)(2,1)S(1)}, u32[]{:S(2)}, u32[]{:S(2)}) collective-permute-start(bf16[160,1408]{1,0:T(8,128)(2,1)S(1)} %collective-permute-done.13.refs_2_), channel_id=1, source_target_pairs={{0,8},{8,0},{16,24},{24,16},{1,9},{9,1},{17,25},{25,17},{2,10},{10... | collective-permute-start | bytes 1351688 | tf_op jit(solution)/shard_map/ppermute | solution.py:681
  41.4 4.3 %collective-permute-start.9 = (bf16[64,512]{1,0:T(8,128)(2,1)S(1)}, bf16[64,512]{1,0:T(8,128)(2,1)S(1)}, u32[]{:S(2)}, u32[]{:S(2)}) collective-permute-start(bf16[64,512]{1,0:T(8,128)(2,1)S(1)} %shard_map.32), channel_id=1, source_target_pairs={{0,16},{8,24},{16,0},{24,8},{1,17},{9,25},{17,1},{25,9},{2,18},{10... | collective-permute-start | bytes 196616 | tf_op jit(solution)/shard_map/ppermute | solution.py:681
  43.3 8.2 %collective-permute-start.16 = (bf16[256,512]{1,0:T(8,128)(2,1)S(1)}, bf16[256,512]{1,0:T(8,128)(2,1)S(1)}, u32[]{:S(2)}, u32[]{:S(2)}) collective-permute-start(bf16[256,512]{1,0:T(8,128)(2,1)S(1)} %get-tuple-element.38.refs_0_), channel_id=1, source_target_pairs={{0,16},{8,24},{16,0},{24,8},{1,17},{9,25},{17,1},{25,9},{2,18},{10... | collective-permute-start | bytes 786440 | tf_op jit(solution)/shard_map/ppermute | solution.py:681
  45.7 2.4 %collective-permute-start.10 = (bf16[64,512]{1,0:T(8,128)(2,1)S(1)}, bf16[64,512]{1,0:T(8,128)(2,1)S(1)}, u32[]{:S(2)}, u32[]{:S(2)}) collective-permute-start(bf16[64,512]{1,0:T(8,128)(2,1)S(1)} %collective-permute-done.9.far), channel_id=1, source_target_pairs={{0,8},{8,0},{16,24},{24,16},{1,9},{9,1},{17,25},{25,17},{2,10},{10... | collective-permute-start | bytes 196616 | tf_op jit(solution)/shard_map/ppermute | solution.py:681
  48.8 2.8 %collective-permute-start.19 = (bf16[384,512]{1,0:T(8,128)(2,1)S(1)}, bf16[384,512]{1,0:T(8,128)(2,1)S(1)}, u32[]{:S(2)}, u32[]{:S(2)}) collective-permute-start(bf16[384,512]{1,0:T(8,128)(2,1)S(1)} %get-tuple-element.37.refs_2_), channel_id=1, source_target_pairs={{0,8},{8,0},{16,24},{24,16},{1,9},{9,1},{17,25},{25,17},{2,10},{10... | collective-permute-start | bytes 1179656 | tf_op jit(solution)/shard_map/ppermute | solution.py:681
  49.4 11.1 %collective-permute-start.15 = (bf16[384,512]{1,0:T(8,128)(2,1)S(1)}, bf16[384,512]{1,0:T(8,128)(2,1)S(1)}, u32[]{:S(2)}, u32[]{:S(2)}) collective-permute-start(bf16[384,512]{1,0:T(8,128)(2,1)S(1)} %get-tuple-element.37.refs_2_), channel_id=1, source_target_pairs={{0,16},{8,24},{16,0},{24,8},{1,17},{9,25},{17,1},{25,9},{2,18},{10... | collective-permute-start | bytes 1179656 | tf_op jit(solution)/shard_map/ppermute | solution.py:681
  50.1 1.5 %collective-permute-start.18 = (bf16[256,512]{1,0:T(8,128)(2,1)S(1)}, bf16[256,512]{1,0:T(8,128)(2,1)S(1)}, u32[]{:S(2)}, u32[]{:S(2)}) collective-permute-start(bf16[256,512]{1,0:T(8,128)(2,1)S(1)} %get-tuple-element.38.refs_0_), channel_id=1, source_target_pairs={{0,8},{8,0},{16,24},{24,16},{1,9},{9,1},{17,25},{25,17},{2,10},{10... | collective-permute-start | bytes 786440 | tf_op jit(solution)/shard_map/ppermute | solution.py:681
  51.5 4.4 %collective-permute-start.17 = (bf16[256,512]{1,0:T(8,128)(2,1)S(1)}, bf16[256,512]{1,0:T(8,128)(2,1)S(1)}, u32[]{:S(2)}, u32[]{:S(2)}) collective-permute-start(bf16[256,512]{1,0:T(8,128)(2,1)S(1)} %collective-permute-done.16.refs_0_), channel_id=1, source_target_pairs={{0,8},{8,0},{16,24},{24,16},{1,9},{9,1},{17,25},{25,17},{2,10},{10... | collective-permute-start | bytes 786440 | tf_op jit(solution)/shard_map/ppermute | solution.py:681
  60.5 1.8 %collective-permute-start.20 = (bf16[384,512]{1,0:T(8,128)(2,1)S(1)}, bf16[384,512]{1,0:T(8,128)(2,1)S(1)}, u32[]{:S(2)}, u32[]{:S(2)}) collective-permute-start(bf16[384,512]{1,0:T(8,128)(2,1)S(1)} %shard_map.38.square), channel_id=1, source_target_pairs={{0,8},{8,0},{16,24},{24,16},{1,9},{9,1},{17,25},{25,17},{2,10},{10... | collective-permute-start | bytes 1179656 | tf_op jit(solution)/shard_map/ppermute | solution.py:681
